TPU v7x, 32 devices: a whole 2x2x4 slice. The times are simulated.
32 devices in a mesh: blk: 8 (over z, x), head: 4 (over y, core).
Axes of the slice: x: 2, y: 2, z: 4, core: 2. Of those that a mesh axis runs over, the one named last changes fastest.
Arguments:
- tokens: bfloat16 [4096, 2048], P(('blk', 'head')), may hold values from -6 to 6
- seg_ids: int32 [4096], P('blk'), may hold values from 0 to 14, as said below
- cotangent: bfloat16 [4096, 2048], P(('blk', 'head')), may hold values from -6 to 6
- gain_mix: bfloat16 [2048], P(('blk', 'head')), may hold values from 0.25 to 1.75
- q_w: bfloat16 [2048, 1024], P('blk', 'head'), may hold values from -0.125 to 0.125
- kv_w: bfloat16 [2048, 2, 256], P(('blk', 'head')), may hold values from -0.125 to 0.125
- zx_w: bfloat16 [2048, 2, 3072], P('blk', None, 'head'), may hold values from -0.125 to 0.125
- dt_w: bfloat16 [2048, 48], P('blk', 'head'), may hold values from -0.125 to 0.125
- bc_w: bfloat16 [2048, 512], P(('blk', 'head')), may hold values from -0.125 to 0.125
- a_log: float32 [48], P('head'), may hold values from 0 to 2.77
- dt_bias: float32 [48], P('head'), may hold values from -6.9 to -2.3
- skip: float32 [48], P('head'), may hold values from 0.5 to 1.5
- wo_w: bfloat16 [2048, 1024], P('blk', 'head'), may hold values from -0.75 to 0.75
- wm_w: bfloat16 [2048, 3072], P('blk', 'head'), may hold values from -0.109375 to 0.109375
- gain_ff: bfloat16 [2048], P(('blk', 'head')), may hold values from 0.25 to 1.75
- gu_w: bfloat16 [2048, 2, 4096], P('blk', None, 'head'), may hold values from -0.125 to 0.125
- down_w: bfloat16 [2048, 4096], P('blk', 'head'), may hold values from -0.09375 to 0.09375
Outputs:
- layer_out: bfloat16 [4096, 2048], P(('blk', 'head'))
- input_grad: float32 [4096, 2048], P(('blk', 'head'))
- gain_mix_grad: float32 [2048], P(('blk', 'head'))
- q_grad: float32 [2048, 1024], P('blk', 'head')
- kv_grad: float32 [2048, 2, 256], P(('blk', 'head'))
- zx_grad: float32 [2048, 2, 3072], P('blk', None, 'head')
- dt_grad: float32 [2048, 48], P('blk', 'head')
- bc_grad: float32 [2048, 512], P(('blk', 'head'))
- a_log_grad: float32 [48], P('head')
- dt_bias_grad: float32 [48], P('head')
- skip_grad: float32 [48], P('head')
- wo_grad: float32 [2048, 1024], P('blk', 'head')
- wm_grad: float32 [2048, 3072], P('blk', 'head')
- gain_ff_grad: float32 [2048], P(('blk', 'head'))
- gu_grad: float32 [2048, 2, 4096], P('blk', None, 'head')
- down_grad: float32 [2048, 4096], P('blk', 'head')
Inputs may be any that keep to these rules, and one draw needn't show every extreme that they name: `seg_ids`: ids never fall along the stream, begin at 0 and use every number up to 14.
All inputs are finite; a program needn't handle non-finite values.
Results may differ from a plain program's by a relative error of at most 0.025.
Values may be sent and summed in bfloat16 or wider, within the bound.
No kernel may reach another device: no remote copies, remote signals or barrier semaphores. Data moves between devices by JAX's collectives and lax.ppermute only.
A program may use at most 256 MiB of HBM per device.

v0:
```python
import math

import jax
import jax.numpy as jnp
import numpy as np
from jax import lax
from jax.sharding import PartitionSpec as P

QH = 8
KVH = 2
HD = 128
MP = 64
STRETCH = 256


EPS = 1e-05
THETA = 100000000000.0
NEGATIVE = -1e30
NEARLY = lax.Precision.HIGH


def entering(shard, axis, join, neutral):
    place = lax.axis_index(axis)
    gathered = jax.tree.map(
        lambda a, kind: lax.all_gather(a.astype(kind), axis),
        shard,
        (jnp.bfloat16, jnp.bfloat16, jnp.bfloat16),
    )
    state = jax.tree.map(lambda a, e: jnp.zeros_like(a) + jnp.asarray(e, a.dtype), shard, neutral)

    def entering_one(step, state):
        return join(
            state,
            jax.tree.map(
                lambda a, own: lax.dynamic_index_in_dim(a, step, 0, False).astype(own.dtype),
                gathered,
                shard,
            ),
        )

    return lax.fori_loop(0, place, entering_one, state)


def carried_in(shard, axis, join, neutral):
    count = lax.axis_size(axis)
    place = lax.axis_index(axis)
    ahead = count - 1 - place
    gathered = jax.tree.map(
        lambda a, kind: lax.all_gather(a.astype(kind), axis),
        shard,
        jax.tree.map(lambda a: jnp.bfloat16 if a.dtype == jnp.float32 else a.dtype, shard),
    )
    state = jax.tree.map(lambda a, e: jnp.zeros_like(a) + jnp.asarray(e, a.dtype), shard, neutral)

    def carried_one(step, state):
        source = count - 1 - step
        return join(
            state,
            jax.tree.map(
                lambda a, own: lax.dynamic_index_in_dim(a, source, 0, False).astype(own.dtype),
                gathered,
                shard,
            ),
        )

    return lax.fori_loop(0, ahead, carried_one, state)


def rms_norm(values, gain):
    scale = lax.rsqrt(jnp.mean(values * values, axis=-1, keepdims=True) + EPS)
    return values * scale * gain


def rope(values, positions):
    half = values.shape[-1] // 2
    frequency = jnp.exp(
        jnp.arange(half, dtype=jnp.float32) * (-2.0 * math.log(THETA) / values.shape[-1])
    )
    angle = positions.astype(jnp.float32)[:, None] * frequency[None, :]
    cosine = jnp.cos(angle)[:, None, :]
    sine = jnp.sin(angle)[:, None, :]
    first = values[..., :half]
    second = values[..., half:]
    return jnp.concatenate(
        [first * cosine - second * sine, second * cosine + first * sine], axis=-1
    )


def stretch_step(carry, block, rates, skip):
    held, label = carry
    x_val, z_val, b_val, c_val, dt_val, segment = block
    length = segment.shape[0]
    running = jnp.cumsum(-dt_val * rates[None, :], axis=0)
    running_heads = running.T
    order = jnp.arange(length)
    allowed = (segment[:, None] == segment[None, :]) & (order[:, None] >= order[None, :])
    spread = running_heads[:, :, None] - running_heads[:, None, :]
    decay = jnp.where(allowed[None], jnp.exp(jnp.where(allowed[None], spread, 0.0)), 0.0)
    intersection = jnp.einsum("tn,sn->ts", c_val, b_val)
    mixing = decay * intersection[None] * dt_val.T[:, None, :]
    y_val = jnp.einsum("hts,shp->thp", mixing, x_val, precision=NEARLY)
    entry = jnp.where((segment == label)[:, None], jnp.exp(running), 0.0)
    y_val = y_val + entry[:, :, None] * jnp.einsum("hpn,tn->thp", held, c_val, precision=NEARLY)
    y_val = y_val + skip[None, :, None] * x_val
    gated = y_val * jax.nn.silu(z_val)
    final = segment[length - 1]
    tail = (
        jnp.where((segment == final)[:, None], jnp.exp(running[length - 1][None, :] - running), 0.0)
        * dt_val
    )
    fresh = jnp.einsum("shp,sn->hpn", tail[:, :, None] * x_val, b_val, precision=NEARLY)
    kept = jnp.where(label == final, jnp.exp(running[length - 1]), 0.0)
    return ((kept[:, None, None] * held + fresh, final), gated.reshape(length, -1))


def mamba_run(x_val, z_val, b_val, c_val, dt_raw, a_log, dt_bias, skip, segment, held, label):
    size = x_val.shape[0]
    count = size // STRETCH
    dt_val = jax.nn.softplus(dt_raw + dt_bias[None, :])
    rates = jnp.exp(a_log)
    blocks = tuple(
        (
            part.reshape((count, STRETCH) + part.shape[1:])
            for part in (x_val, z_val, b_val, c_val, dt_val, segment)
        )
    )
    step = jax.checkpoint(lambda carry, block: stretch_step(carry, block, rates, skip))
    (held, label), gated = lax.scan(step, (held, label), blocks)
    total = jnp.exp(-jnp.sum(dt_val * rates[None, :], axis=0))
    return (gated.reshape(size, -1), held, total)


def link_states(early, later):
    early_total, early_held, early_label = early
    later_total, later_held, later_label = later
    joined = ((early_label == later_label) | (early_label < 0) | (later_label < 0)).astype(
        jnp.float32
    )
    return (
        joined * early_total * later_total,
        joined * later_total[..., None, None] * early_held + later_held,
        jnp.where(later_label < 0, early_label, later_label),
    )


def link_grads(early, later):
    early_factor, early_grad = early
    later_factor, later_grad = later
    return (later_factor * early_factor, later_grad + later_factor[..., None, None] * early_grad)


def gather_rows(values):
    return lax.all_gather(values, "head", axis=0, tiled=True)


def reduce_rows(term):
    return lax.psum_scatter(
        term.astype(jnp.bfloat16), "head", scatter_dimension=0, tiled=True
    ).astype(jnp.float32)


def shards(
    tokens,
    seg_ids,
    cotangent,
    gain_mix,
    q_w,
    kv_w,
    zx_w,
    dt_w,
    bc_w,
    a_log,
    dt_bias,
    skip,
    wo_w,
    wm_w,
    gain_ff,
    gu_w,
    down_w,
):
    head_count = lax.axis_size("head")
    cycle_count = lax.axis_size("blk")
    head_pos = lax.axis_index("head")
    cycle_pos = lax.axis_index("blk")
    own_rows, width = tokens.shape
    group = own_rows * head_count
    q_cols, zx_cols, dt_cols, wo_cols, wm_cols, gu_cols, down_cols = (
        lax.all_gather(q_w, "blk", axis=0, tiled=True),
        lax.all_gather(zx_w, "blk", axis=0, tiled=True),
        lax.all_gather(dt_w, "blk", axis=0, tiled=True),
        lax.all_gather(wo_w, "blk", axis=0, tiled=True),
        lax.all_gather(wm_w, "blk", axis=0, tiled=True),
        lax.all_gather(gu_w, "blk", axis=0, tiled=True),
        lax.all_gather(down_w, "blk", axis=0, tiled=True),
    )
    kv_full, bc_full, gain_one, gain_two = (
        lax.all_gather(kv_w, ("blk", "head"), axis=0, tiled=True),
        lax.all_gather(bc_w, ("blk", "head"), axis=0, tiled=True),
        lax.all_gather(gain_mix, ("blk", "head"), axis=0, tiled=True),
        lax.all_gather(gain_ff, ("blk", "head"), axis=0, tiled=True),
    )
    local_heads = q_cols.shape[1] // HD
    local_ssm = dt_cols.shape[1]
    state_width = bc_full.shape[1] // 2
    kv_group = head_pos * local_heads // (QH // KVH)
    kv_sel = lax.dynamic_slice_in_dim(kv_full, kv_group * HD, HD, 2)
    group_pos = cycle_pos * group + jnp.arange(group, dtype=jnp.int32)
    own_pos = cycle_pos * group + head_pos * own_rows + jnp.arange(own_rows, dtype=jnp.int32)
    segment = seg_ids.astype(jnp.float32)
    stream_in = tokens.astype(jnp.float32)
    normed, norm_one_back = jax.vjp(rms_norm, stream_in, gain_one.astype(jnp.float32))
    normed = normed.astype(jnp.bfloat16)
    q_wide, zx_wide, dt_wide = (
        lax.all_gather(q_cols, "head", axis=1, tiled=True),
        lax.all_gather(zx_cols, "head", axis=2, tiled=True),
        lax.all_gather(dt_cols, "head", axis=1, tiled=True),
    )
    q_own = jnp.dot(normed, q_wide, preferred_element_type=jnp.float32).reshape(
        own_rows, head_count * local_heads, HD
    )
    q_send = (
        rope(q_own, own_pos).astype(jnp.bfloat16).reshape(own_rows, head_count, local_heads * HD)
    )
    slot_heads = np.array([slot * local_heads // (QH // KVH) for slot in range(head_count)])
    kv_slots = kv_full.reshape(width, 2, KVH, HD)[:, :, slot_heads, :]
    kv_own = jnp.einsum("td,dgah->tagh", normed, kv_slots, preferred_element_type=jnp.float32)
    kv_send = jnp.stack([rope(kv_own[:, :, 0], own_pos), kv_own[:, :, 1]], axis=2).astype(
        jnp.bfloat16
    )
    zx_send = jnp.einsum(
        "td,dgac->tagc",
        normed,
        zx_wide.reshape(width, 2, head_count, -1),
        preferred_element_type=jnp.float32,
    ).astype(jnp.bfloat16)
    dt_send = (
        jnp.dot(normed, dt_wide, preferred_element_type=jnp.float32)
        .astype(jnp.bfloat16)
        .reshape(own_rows, head_count, local_ssm)
    )
    bc_own = jnp.dot(normed, bc_full, preferred_element_type=jnp.float32).astype(jnp.bfloat16)
    bc_send = jnp.broadcast_to(bc_own[:, None, :], (own_rows, head_count, bc_own.shape[1]))
    q_recv, kv_recv, zx_recv, dt_recv, bc_recv = (
        lax.all_to_all(q_send, "head", split_axis=1, concat_axis=0, tiled=True),
        lax.all_to_all(kv_send, "head", split_axis=1, concat_axis=0, tiled=True),
        lax.all_to_all(zx_send, "head", split_axis=1, concat_axis=0, tiled=True),
        lax.all_to_all(dt_send, "head", split_axis=1, concat_axis=0, tiled=True),
        lax.all_to_all(bc_send, "head", split_axis=1, concat_axis=0, tiled=True),
    )
    q_heads = q_recv[:, 0].reshape(group, local_heads, HD)
    kv_heads = kv_recv[:, 0]
    zx_heads = zx_recv[:, 0]
    dt_heads = dt_recv[:, 0]
    bc_heads = bc_recv[:, 0]
    ssm_args = (
        zx_heads[:, 1].astype(jnp.float32).reshape(group, local_ssm, MP),
        zx_heads[:, 0].astype(jnp.float32).reshape(group, local_ssm, MP),
        bc_heads[:, :state_width].astype(jnp.float32),
        bc_heads[:, state_width:].astype(jnp.float32),
        dt_heads.astype(jnp.float32),
        a_log,
        dt_bias,
        skip,
    )
    empty_state = jnp.zeros((local_ssm, MP, state_width), jnp.float32)

    def summary_fn(*inputs):
        unused_gated, held, total = mamba_run(*inputs, segment, empty_state, jnp.float32(-1.0))
        return (held, total)

    (held_own, total_own), summary_back = jax.vjp(summary_fn, *ssm_args)
    last_label = segment[group - 1]
    chain_start = (jnp.ones((local_ssm,), jnp.float32), empty_state, jnp.float32(-1.0))
    in_total, in_held, in_label = entering(
        (total_own, held_own, last_label), "blk", link_states, chain_start
    )

    def output_fn(*inputs):
        gated, unused_held, unused_total = mamba_run(*inputs[:8], segment, inputs[8], in_label)
        return gated

    gated, output_back = jax.vjp(output_fn, *ssm_args, in_held)
    ssm_out = gated.astype(jnp.bfloat16)
    scale = HD ** (-0.5)
    q_last = group_pos[group - 1]
    seg_low = segment[0]
    seg_high = segment[group - 1]

    def key_mask(key_seg, first):
        key_pos = first + jnp.arange(group, dtype=jnp.int32)
        return (key_pos[None, :] <= group_pos[:, None]) & (key_seg[None, :] == segment[:, None])

    def sweep(block_fn, carry, piece, start):
        kv_piece, seg_piece = piece
        count = kv_piece.shape[0] // group
        items = (
            kv_piece.reshape(count, group, 2, HD),
            seg_piece.astype(jnp.float32).reshape(count, group),
            start + group * jnp.arange(count, dtype=jnp.int32),
        )

        def visit(state, item):
            kv_block, key_seg, first = item
            live = (first <= q_last) & (key_seg[group - 1] >= seg_low) & (key_seg[0] <= seg_high)
            return (
                lax.cond(
                    live,
                    lambda inner: block_fn(inner, kv_block, key_seg, first),
                    lambda inner: inner,
                    state,
                ),
                None,
            )

        carry, unused = lax.scan(visit, carry, items)
        return carry

    def attend_block(state, kv_block, key_seg, first):
        peak, total, weighted = state
        allowed = key_mask(key_seg, first)[None]
        scores = (
            jnp.einsum("qhd,kd->hqk", q_heads, kv_block[:, 0], preferred_element_type=jnp.float32)
            * scale
        )
        masked = jnp.where(allowed, scores, NEGATIVE)
        new_peak = jnp.maximum(peak, jnp.max(masked, axis=-1))
        weights = jnp.where(allowed, jnp.exp(masked - new_peak[:, :, None]), 0.0)
        rescale = jnp.exp(peak - new_peak)
        upper = weights.astype(jnp.bfloat16)
        lower = (weights - upper.astype(jnp.float32)).astype(jnp.bfloat16)
        update = jnp.einsum(
            "hqk,kd->qhd", upper, kv_block[:, 1], preferred_element_type=jnp.float32
        ) + jnp.einsum("hqk,kd->qhd", lower, kv_block[:, 1], preferred_element_type=jnp.float32)
        return (
            new_peak,
            total * rescale + jnp.sum(weights, axis=-1),
            weighted * rescale.T[:, :, None] + update,
        )

    start_state = (
        jnp.full((local_heads, group), NEGATIVE, jnp.float32),
        jnp.zeros((local_heads, group), jnp.float32),
        jnp.zeros((group, local_heads, HD), jnp.float32),
    )
    key_pack = (kv_heads, seg_ids.astype(jnp.bfloat16))
    peak, total, weighted = sweep(
        attend_block,
        start_state,
        (
            lax.all_gather(key_pack[0], "blk", axis=0, tiled=True),
            lax.all_gather(key_pack[1], "blk", axis=0, tiled=True),
        ),
        jnp.int32(0),
    )
    att_full = weighted / total.T[:, :, None]
    log_total = peak + jnp.log(total)
    att_out = att_full.astype(jnp.bfloat16).reshape(group, local_heads * HD)
    contract = (((1,), (1,)), ((), ()))
    mixed_term = lax.dot_general(
        att_out, wo_cols, contract, preferred_element_type=jnp.float32
    ) + lax.dot_general(ssm_out, wm_cols, contract, preferred_element_type=jnp.float32)
    middle = stream_in + reduce_rows(mixed_term)
    normed_two, norm_two_back = jax.vjp(rms_norm, middle, gain_two.astype(jnp.float32))
    rows_two = gather_rows(normed_two.astype(jnp.bfloat16))
    gate_up = jnp.einsum(
        "td,dgf->tgf", rows_two, gu_cols, preferred_element_type=jnp.float32
    ).astype(jnp.bfloat16)
    gate_val = gate_up[:, 0].astype(jnp.float32)
    up_val = gate_up[:, 1].astype(jnp.float32)
    sigma = jax.nn.sigmoid(gate_val)
    hidden = (gate_val * sigma * up_val).astype(jnp.bfloat16)
    result = middle + reduce_rows(
        lax.dot_general(hidden, down_cols, contract, preferred_element_type=jnp.float32)
    )
    layer_out = result.astype(jnp.bfloat16)
    grad_rows = gather_rows(cotangent)
    grad_hidden = (
        jnp.dot(grad_rows, down_cols, preferred_element_type=jnp.float32)
        .astype(jnp.bfloat16)
        .astype(jnp.float32)
    )
    grad_down = jnp.einsum("td,tf->df", grad_rows, hidden, preferred_element_type=jnp.float32)
    grad_gate = grad_hidden * up_val * (sigma * (1.0 + gate_val * (1.0 - sigma)))
    grad_up = grad_hidden * gate_val * sigma
    grad_gu = jnp.stack([grad_gate, grad_up], axis=1).astype(jnp.bfloat16)
    grad_gu_w = jnp.einsum("td,tgf->dgf", rows_two, grad_gu, preferred_element_type=jnp.float32)
    grad_normed_two = reduce_rows(
        jnp.einsum("tgf,dgf->td", grad_gu, gu_cols, preferred_element_type=jnp.float32)
    )
    grad_middle_part, grad_gain_two = norm_two_back(grad_normed_two)
    grad_middle = cotangent.astype(jnp.float32) + grad_middle_part
    grad_mixed_rows = gather_rows(grad_middle.astype(jnp.bfloat16))
    grad_att = jnp.einsum(
        "td,dc->tc", grad_mixed_rows, wo_cols, preferred_element_type=jnp.float32
    ).astype(jnp.bfloat16)
    grad_wo = jnp.einsum("td,tc->dc", grad_mixed_rows, att_out, preferred_element_type=jnp.float32)
    grad_ssm = jnp.einsum(
        "td,dc->tc", grad_mixed_rows, wm_cols, preferred_element_type=jnp.float32
    ).astype(jnp.bfloat16)
    grad_wm = jnp.einsum("td,tc->dc", grad_mixed_rows, ssm_out, preferred_element_type=jnp.float32)
    part_grads = output_back(grad_ssm.astype(jnp.float32))
    joined_in = ((in_label == last_label) | (in_label < 0)).astype(jnp.float32)
    back_start = (jnp.ones((local_ssm,), jnp.float32), empty_state)
    unused_factor, grad_held_out = carried_in(
        (joined_in * total_own, part_grads[8]), "blk", link_grads, back_start
    )
    grad_total = joined_in * jnp.sum(grad_held_out * in_held, axis=(1, 2))
    sum_grads = summary_back((grad_held_out, grad_total))
    ssm_grads = tuple((part_grads[index] + sum_grads[index] for index in range(8)))
    grad_zx = jnp.stack(
        [ssm_grads[1].reshape(group, -1), ssm_grads[0].reshape(group, -1)], axis=1
    ).astype(jnp.bfloat16)
    grad_bc = jnp.concatenate([ssm_grads[2], ssm_grads[3]], axis=1).astype(jnp.bfloat16)
    grad_dt = ssm_grads[4].astype(jnp.bfloat16)
    grad_att_heads = grad_att.reshape(group, local_heads, HD)
    delta = jnp.sum(grad_att_heads.astype(jnp.float32) * att_full, axis=-1).T

    def back_block(state, kv_block, key_seg, first):
        grad_query, grad_keys = state
        allowed = key_mask(key_seg, first)[None]
        scores = (
            jnp.einsum("qhd,kd->hqk", q_heads, kv_block[:, 0], preferred_element_type=jnp.float32)
            * scale
        )
        masked = jnp.where(allowed, scores, NEGATIVE)
        probs = jnp.where(allowed, jnp.exp(masked - log_total[:, :, None]), 0.0)
        grad_probs = jnp.einsum(
            "qhd,kd->hqk", grad_att_heads, kv_block[:, 1], preferred_element_type=jnp.float32
        )
        grad_scores = (probs * (grad_probs - delta[:, :, None])).astype(jnp.bfloat16)
        grad_query = (
            grad_query
            + jnp.einsum(
                "hqk,kd->qhd", grad_scores, kv_block[:, 0], preferred_element_type=jnp.float32
            )
            * scale
        )
        grad_key = (
            jnp.einsum("hqk,qhd->kd", grad_scores, q_heads, preferred_element_type=jnp.float32)
            * scale
        )
        upper = probs.astype(jnp.bfloat16)
        lower = (probs - upper.astype(jnp.float32)).astype(jnp.bfloat16)
        grad_value = jnp.einsum(
            "hqk,qhd->kd", upper, grad_att_heads, preferred_element_type=jnp.float32
        ) + jnp.einsum("hqk,qhd->kd", lower, grad_att_heads, preferred_element_type=jnp.float32)
        grad_keys = lax.dynamic_update_slice_in_dim(
            grad_keys, jnp.stack([grad_key, grad_value], axis=1), first, 0
        )
        return (grad_query, grad_keys)

    back_state = (
        jnp.zeros((group, local_heads, HD), jnp.float32),
        jnp.zeros((group * cycle_count, 2, HD), jnp.float32),
    )
    grad_query, grad_keys = sweep(
        back_block,
        back_state,
        (
            lax.all_gather(key_pack[0], "blk", axis=0, tiled=True),
            lax.all_gather(key_pack[1], "blk", axis=0, tiled=True),
        ),
        jnp.int32(0),
    )
    grad_kv_own = lax.psum_scatter(
        grad_keys.astype(jnp.bfloat16), "blk", scatter_dimension=0, tiled=True
    ).astype(jnp.float32)
    grad_q_proj = rope(grad_query, -group_pos).astype(jnp.bfloat16).reshape(group, local_heads * HD)
    grad_kv = jnp.stack(
        [rope(grad_kv_own[:, 0:1], -group_pos)[:, 0], grad_kv_own[:, 1]], axis=1
    ).astype(jnp.bfloat16)
    rows_one = gather_rows(normed)
    grad_in_term = jnp.einsum("tc,dc->td", grad_q_proj, q_cols, preferred_element_type=jnp.float32)
    grad_in_term = grad_in_term + jnp.einsum(
        "tgh,dgh->td", grad_kv, kv_sel, preferred_element_type=jnp.float32
    )
    grad_in_term = grad_in_term + jnp.einsum(
        "tgc,dgc->td", grad_zx, zx_cols, preferred_element_type=jnp.float32
    )
    grad_in_term = grad_in_term + jnp.einsum(
        "th,dh->td", grad_dt, dt_cols, preferred_element_type=jnp.float32
    )
    grad_in_term = grad_in_term + jnp.einsum(
        "tc,dc->td", grad_bc, bc_full, preferred_element_type=jnp.float32
    )
    grad_input_part, grad_gain_one = norm_one_back(reduce_rows(grad_in_term))
    input_grad = grad_middle + grad_input_part
    grad_q_w = jnp.einsum("td,tc->dc", rows_one, grad_q_proj, preferred_element_type=jnp.float32)
    grad_kv_sel = jnp.einsum("td,tgh->dgh", rows_one, grad_kv, preferred_element_type=jnp.float32)
    grad_kv_w = lax.dynamic_update_slice_in_dim(
        jnp.zeros(kv_full.shape, jnp.float32), grad_kv_sel, kv_group * HD, 2
    )
    grad_zx_w = jnp.einsum("td,tgc->dgc", rows_one, grad_zx, preferred_element_type=jnp.float32)
    grad_dt_w = jnp.einsum("td,th->dh", rows_one, grad_dt, preferred_element_type=jnp.float32)
    grad_bc_w = jnp.einsum("td,tc->dc", rows_one, grad_bc, preferred_element_type=jnp.float32)
    q_grad, zx_grad, dt_grad, wo_grad, wm_grad, gu_grad, down_grad = (
        lax.psum_scatter(
            grad_q_w.astype(jnp.bfloat16), "blk", scatter_dimension=0, tiled=True
        ).astype(jnp.float32),
        lax.psum_scatter(
            grad_zx_w.astype(jnp.bfloat16), "blk", scatter_dimension=0, tiled=True
        ).astype(jnp.float32),
        lax.psum_scatter(
            grad_dt_w.astype(jnp.bfloat16), "blk", scatter_dimension=0, tiled=True
        ).astype(jnp.float32),
        lax.psum_scatter(
            grad_wo.astype(jnp.bfloat16), "blk", scatter_dimension=0, tiled=True
        ).astype(jnp.float32),
        lax.psum_scatter(
            grad_wm.astype(jnp.bfloat16), "blk", scatter_dimension=0, tiled=True
        ).astype(jnp.float32),
        lax.psum_scatter(
            grad_gu_w.astype(jnp.bfloat16), "blk", scatter_dimension=0, tiled=True
        ).astype(jnp.float32),
        lax.psum_scatter(
            grad_down.astype(jnp.bfloat16), "blk", scatter_dimension=0, tiled=True
        ).astype(jnp.float32),
    )
    kv_grad, bc_grad, gain_mix_grad, gain_ff_grad = (
        lax.psum_scatter(grad_kv_w, ("blk", "head"), scatter_dimension=0, tiled=True),
        lax.psum_scatter(grad_bc_w, ("blk", "head"), scatter_dimension=0, tiled=True),
        lax.psum_scatter(grad_gain_one, ("blk", "head"), scatter_dimension=0, tiled=True),
        lax.psum_scatter(grad_gain_two, ("blk", "head"), scatter_dimension=0, tiled=True),
    )
    a_log_grad, dt_bias_grad, skip_grad = lax.psum(
        (ssm_grads[5], ssm_grads[6], ssm_grads[7]), "blk"
    )
    return (
        layer_out,
        input_grad,
        gain_mix_grad,
        q_grad,
        kv_grad,
        zx_grad,
        dt_grad,
        bc_grad,
        a_log_grad,
        dt_bias_grad,
        skip_grad,
        wo_grad,
        wm_grad,
        gain_ff_grad,
        gu_grad,
        down_grad,
    )


def solution(mesh):
    placed = (
        P(("blk", "head"), None),
        P("blk"),
        P(("blk", "head"), None),
        P(("blk", "head")),
        P("blk", "head"),
        P(("blk", "head"), None, None),
        P("blk", None, "head"),
        P("blk", "head"),
        P(("blk", "head"), None),
        P("head"),
        P("head"),
        P("head"),
        P("blk", "head"),
        P("blk", "head"),
        P(("blk", "head")),
        P("blk", None, "head"),
        P("blk", "head"),
    )
    return jax.shard_map(
        shards,
        mesh=mesh,
        in_specs=placed,
        out_specs=(
            P(("blk", "head"), None),
            P(("blk", "head"), None),
            P(("blk", "head")),
            P("blk", "head"),
            P(("blk", "head"), None, None),
            P("blk", None, "head"),
            P("blk", "head"),
            P(("blk", "head"), None),
            P("head"),
            P("head"),
            P("head"),
            P("blk", "head"),
            P("blk", "head"),
            P(("blk", "head")),
            P("blk", None, "head"),
            P("blk", "head"),
        ),
        check_vma=False,
    )
```

profile of v0, /device:TPU:0, one launch (start us, length us, event | category | flops | bytes accessed | tf_op | source)
XLA Modules:
  0.0 2387.1 jit_solution(2052880018247888739)
XLA Ops:
  11.5 101.1 %all-gather.34.cloned.1.call-done = bf16[2048,2,768]{2,0,1:T(8,128)(2,1)} async-done(((bf16[256,2,768]{2,0,1:T(8,128)(2,1)}), bf16[2048,2,768]{2,0,1:T(8,128)(2,1)}) %all-gather.34.cloned.1.call-update) | async-done | bytes 6291472 | tf_op jit(solution)/shard_map/all_gather | solution.py:189
  112.6 40.5 %all-gather.28.cloned.1.call-done = bf16[2048,256]{1,0:T(8,128)(2,1)} async-done(((bf16[256,256]{1,0:T(8,128)(2,1)}), bf16[2048,256]{1,0:T(8,128)(2,1)}) %all-gather.28.cloned.1.call-update) | async-done | bytes 1048592 | tf_op jit(solution)/shard_map/all_gather | solution.py:188
  153.7 38.5 %all-reduce.14 = (bf16[2048]{0:T(1024)(128)(2,1)S(1)}, bf16[2048]{0:T(1024)(128)(2,1)}) all-reduce(bf16[2048]{0:T(1024)(128)(2,1)S(1)} %dynamic-update-slice, bf16[2048]{0:T(1024)(128)(2,1)S(1)} %dynamic-update-slice.3), channel_id=1, replica_groups=mesh['blk'=8,'head'=4] {'blk','head'}, use_global_device_ids=true, to_apply=%add.4 | all-reduce | flops 4096 | bytes 16384
  192.2 30.6 %all_gather.97 = bf16[2048,12]{0,1:T(8,128)(2,1)S(1)} all-gather(bf16[256,12]{0,1:T(8,128)(2,1)S(1)} %copy-done.102), channel_id=1, replica_groups=mesh['blk'=8,'head'=4] {'blk'}, dimensions={0}, use_global_device_ids=true | all-gather | bytes 55296 | tf_op jit(solution)/shard_map/all_gather | solution.py:190
  222.7 6.8 all-gather.5
  257.8 14.2 all-gather.38.cloned.1.call-done
  274.0 152.6 %all-gather.36.cloned.1.call-done = bf16[2048,2,3072]{2,0,1:T(8,128)(2,1)} async-done(((bf16[2048,2,768]{2,0,1:T(8,128)(2,1)}), bf16[2048,2,3072]{2,0,1:T(8,128)(2,1)}) %all-gather.36.cloned.1.call-update) | async-done | bytes 25165840 | tf_op jit(solution)/shard_map/all_gather | solution.py:215
  426.6 32.8 %copy.379 = bf16[2048,2,3072]{0,2,1:T(8,128)(2,1)} copy(bf16[2048,2,3072]{2,0,1:T(8,128)(2,1)} %all-gather.36.cloned.1.call-done) | data formatting | bytes 50331648 | tf_op jit(solution)/shard_map/all_gather | solution.py:215
  463.7 13.2 fusion.205
  485.6 17.0 all-to-all-done.3
  511.7 11.5 while.152
  526.6 26.2 %all-gather.4 = bf16[8,1,512]{2,1,0:T(2,128)(2,1)S(1)} all-gather(bf16[1,1,512]{2,1,0:T(2,128)(2,1)S(1)} %reshape.1113), channel_id=1, replica_groups=mesh['blk'=8,'head'=4] {'blk'}, dimensions={0}, use_global_device_ids=true | all-gather | bytes 9216 | tf_op jit(solution)/shard_map/all_gather | solution.py:351
  564.0 20.6 all-reduce.15
  589.7 46.1 %while.149 = (s32[]{:T(128)}, f32[2,512]{1,0:T(2,128)S(1)}, f32[2,512]{1,0:T(2,128)S(1)}, f32[512,2,128]{2,0,1:T(8,128)S(1)}, s32[8]{0:T(128)S(1)}, /*index=5*/s...) while((s32[]{:T(128)}, f32[2,512]{1,0:T(2,128)S(1)}, ...), condition=%wide.region_6.7_spmd.clone, body=%wide.region_1.6_spmd.clone.sunk | while | flops 414846976 | bytes 13066635 | solution.py:315
  651.6 32.3 %while.150 = (s32[]{:T(128)}, f32[12,64,256]{2,1,0:T(8,128)S(1)}, f32[]{:T(128)}, bf16[2,256,768]{2,1,0:T(8,128)(2,1)}, f32[2,12,64,256]{3,2,1,0:T(8,128)}, /*in...) while((s32[]{:T(128)}, f32[12,64,256]{2,1,0:T(8,128)S(1)}, ...), condition=%wide.region_17.19_spmd.clone, body=%wide.region_14.18_spmd.clone.sunk | while | flops 946620992 | bytes 12430115 | solution.py:128
  689.9 11.6 all-gather.32.cloned.1.call-done
  709.2 59.3 %reduce-scatter.14.cloned.1.call-done = bf16[128,2048]{1,0:T(8,128)(2,1)} async-done(((bf16[512,2048]{1,0:T(8,128)(2,1)}), bf16[128,2048]{1,0:T(8,128)(2,1)}) %reduce-scatter.14.cloned.1.call-update) | async-done | bytes 524304 | tf_op jit(solution)/shard_map/reduce_scatter | solution.py:157
  773.1 123.2 %all-gather.44.cloned.1.call-done = bf16[2048,2,1024]{2,0,1:T(8,128)(2,1)} async-done(((bf16[256,2,1024]{2,0,1:T(8,128)(2,1)}), bf16[2048,2,1024]{2,0,1:T(8,128)(2,1)}) %all-gather.44.cloned.1.call-update) | async-done | bytes 8388624 | tf_op jit(solution)/shard_map/all_gather | solution.py:193
  896.3 23.0 all-gather.42.cloned.1.call-done
  919.4 10.0 fusion.202
  929.3 14.2 all-gather.48.cloned.1.call-done
  943.5 75.6 %all-gather.46.cloned.1.call-done = bf16[2048,1024]{1,0:T(8,128)(2,1)} async-done(((bf16[256,1024]{1,0:T(8,128)(2,1)}), bf16[2048,1024]{1,0:T(8,128)(2,1)}) %all-gather.46.cloned.1.call-update) | async-done | bytes 4194320 | tf_op jit(solution)/shard_map/all_gather | solution.py:194
  1026.8 9.1 bitcast_convert_fusion.1
  1035.9 29.8 %reduce-scatter.18.cloned.1.call-done = bf16[128,2048]{1,0:T(8,128)(2,1)} async-done(((bf16[512,2048]{1,0:T(8,128)(2,1)}), bf16[128,2048]{1,0:T(8,128)(2,1)}) %reduce-scatter.18.cloned.1.call-update) | async-done | bytes 524304 | tf_op jit(solution)/shard_map/reduce_scatter | solution.py:157
  1072.7 20.4 all-gather.50.cloned.1.call-done
  1102.8 66.0 %while.151 = (s32[]{:T(128)}, f32[512,2,128]{2,0,1:T(8,128)}, bf16[4096,2,128]{2,0,1:T(8,128)(2,1)}, s32[8]{0:T(128)S(1)}, s32[]{:T(128)}, /*index=5*/f32[8,512]...) while((s32[]{:T(128)}, f32[512,2,128]{2,0,1:T(8,128)}, ...), condition=%wide.region_27.29_spmd.clone, body=%wide.region_24.28_spmd.clone.sunk | while | flops 813040640 | bytes 18248156 | solution.py:315
  1109.2 14.9 conditional.7
  1175.7 80.0 %while.153 = (s32[]{:T(128)}, f32[12]{0:T(128)}, f32[12]{0:T(128)}, f32[12,64,256]{2,1,0:T(8,128)}, f32[2,256,12,64]{1,3,2,0:T(8,128)}, /*index=5*/bf16[2,256,12...) while((s32[]{:T(128)}, f32[12]{0:T(128)}, f32[12]{0:T(128)}, ...), condition=%wide.region_44.46_spmd.clone, body=%wide.region_29.45_spmd.clone.sunk | while | flops 2544652800 | bytes 106472128 | solution.py:128
  1257.7 6.8 convert_bitcast_fusion
  1270.3 93.0 %all-reduce.8 = bf16[96]{0:T(256)(128)(2,1)S(1)} all-reduce(bf16[96]{0:T(256)(128)(2,1)S(1)} %dynamic-update-slice.4), channel_id=5, replica_groups=mesh['blk'=8,'head'=4] {'blk'}, use_global_device_ids=true, to_apply=%add.8 | all-reduce | flops 96 | bytes 384
  1374.6 17.0 all-gather.56.cloned.1.call-done
  1391.6 8.8 while.148
  1405.2 34.3 %while.154 = (s32[]{:T(128)}, f32[12]{0:T(128)S(1)}, f32[12,64,256]{2,1,0:T(8,128)S(1)}, f32[2,256,12,64]{1,3,2,0:T(8,128)}, f32[2,256,256]{2,1,0:T(8,128)}, /*i...) while((s32[]{:T(128)}, f32[12]{0:T(128)S(1)}, ...), condition=%wide.region_56.58_spmd.clone, body=%wide.region_47.57_spmd.clone.sunk | while | flops 606204288 | bytes 20253456 | solution.py:128
  1449.6 8.6 copy_dynamic-update-slice_fusion
  1466.0 8.5 convolution_convert_fusion
  1498.0 6.8 convolution_convert_fusion.3
  1505.1 7.2 convolution_convert_fusion.1
  1519.7 29.7 %reduce-scatter.32.cloned.1.call-done = bf16[256,256]{1,0:T(8,128)(2,1)} async-done(((bf16[2048,256]{1,0:T(8,128)(2,1)}), bf16[256,256]{1,0:T(8,128)(2,1)}) %reduce-scatter.32.cloned.1.call-update) | async-done | bytes 131088 | tf_op jit(solution)/shard_map/reduce_scatter | solution.py:506
  1550.9 64.9 %reduce-scatter.24.cloned.1.call-done = bf16[256,256]{1,0:T(8,128)(2,1)} async-done(((bf16[2048,256]{1,0:T(8,128)(2,1)}), bf16[256,256]{1,0:T(8,128)(2,1)}) %reduce-scatter.24.cloned.1.call-update) | async-done | bytes 131088 | tf_op jit(solution)/shard_map/reduce_scatter | solution.py:497
  1617.5 20.0 all-reduce.13
  1637.4 34.4 %reduce-scatter.28.cloned.1.call-done = bf16[256,12]{0,1:T(8,128)(2,1)} async-done(((bf16[2048,12]{0,1:T(8,128)(2,1)}), bf16[256,12]{0,1:T(8,128)(2,1)}) %reduce-scatter.28.cloned.1.call-update) | async-done | bytes 6160 | tf_op jit(solution)/shard_map/reduce_scatter | solution.py:503
  1673.1 145.9 %all-reduce.18.cloned.1.call-done = f32[2048,2,256]{2,1,0:T(2,128)} async-done(((f32[2048,2,256]{2,1,0:T(2,128)}), f32[2048,2,256]{2,1,0:T(2,128)}) %all-reduce.18.cloned.1.call-update) | async-done | bytes 4194320
  1820.6 75.4 %reduce-scatter.34.cloned.1.call-done = bf16[256,768]{1,0:T(8,128)(2,1)} async-done(((bf16[2048,768]{1,0:T(8,128)(2,1)}), bf16[256,768]{1,0:T(8,128)(2,1)}) %reduce-scatter.34.cloned.1.call-update) | async-done | bytes 393232 | tf_op jit(solution)/shard_map/reduce_scatter | solution.py:509
  1898.0 150.3 %reduce-scatter.36.cloned.1.call-done = bf16[256,2,1024]{2,0,1:T(8,128)(2,1)} async-done(((bf16[2048,2,1024]{2,0,1:T(8,128)(2,1)}), bf16[256,2,1024]{2,0,1:T(8,128)(2,1)}) %reduce-scatter.36.cloned.1.call-update) | async-done | bytes 1048592 | tf_op jit(solution)/shard_map/reduce_scatter | solution.py:512
  2052.0 29.4 %reduce-scatter.22.cloned.1.call-done = bf16[128,2048]{1,0:T(8,128)(2,1)} async-done(((bf16[512,2048]{1,0:T(8,128)(2,1)}), bf16[128,2048]{1,0:T(8,128)(2,1)}) %reduce-scatter.22.cloned.1.call-update) | async-done | bytes 524304 | tf_op jit(solution)/shard_map/reduce_scatter | solution.py:157
  2083.0 39.5 %all-reduce.12 = (f32[2048]{0:T(1024)S(1)}, f32[2048]{0:T(1024)S(1)}) all-reduce(f32[2048]{0:T(1024)S(1)} %get-tuple-element.2245, f32[2048]{0:T(1024)S(1)} %copy-done.93), channel_id=11, replica_groups=mesh['blk'=8,'head'=4] {'blk','head'}, use_global_device_ids=true, to_apply=%region_61.63.clone | all-reduce | flops 4096 | bytes 32768
  2126.9 110.1 %reduce-scatter.26.cloned.1.call-done = bf16[256,2,768]{2,0,1:T(8,128)(2,1)} async-done(((bf16[2048,2,768]{2,0,1:T(8,128)(2,1)}), bf16[256,2,768]{2,0,1:T(8,128)(2,1)}) %reduce-scatter.26.cloned.1.call-update) | async-done | bytes 786448 | tf_op jit(solution)/shard_map/reduce_scatter | solution.py:500
  2240.1 140.0 %reduce-scatter.30.cloned.1.call-done = f32[64,512]{1,0:T(8,128)} async-done(((f32[2048,512]{1,0:T(8,128)}), f32[64,512]{1,0:T(8,128)}) %reduce-scatter.30.cloned.1.call-update) | async-done | bytes 131088 | tf_op jit(solution)/shard_map/reduce_scatter | solution.py:521
  (1026 shorter events, 442.0 us)
Async XLA Ops:
  7.2 105.4 %all-gather.34.cloned.1.call-start = ((), (), s32[]{:S(2)}) async-start(), calls=%async_computation.23 | async-start | bytes 7077888 | tf_op jit(solution)/shard_map/all_gather | solution.py:189
  9.4 143.8 %all-gather.28.cloned.1.call-start = ((), (), s32[]{:S(2)}) async-start(), calls=%async_computation.20 | async-start | bytes 1179648 | tf_op jit(solution)/shard_map/all_gather | solution.py:188
  10.1 225.2 %all-gather.24.cloned.1.call-start = ((), (), s32[]{:S(2)}) async-start(), calls=%async_computation.18 | async-start | bytes 2162688 | tf_op jit(solution)/shard_map/all_gather | solution.py:197
  10.8 261.1 %all-gather.38.cloned.1.call-start = ((), (), s32[]{:S(2)}) async-start(), calls=%async_computation.25 | async-start | bytes 2162688 | tf_op jit(solution)/shard_map/all_gather | solution.py:198
  11.4 415.2 %all-gather.36.cloned.1.call-start = ((), (), s32[]{:S(2)}) async-start(), calls=%async_computation.24 | async-start | bytes 31457280 | tf_op jit(solution)/shard_map/all_gather | solution.py:215
  112.6 442.8 %all-gather.30.cloned.1.call-start = ((), (), s32[]{:S(2)}) async-start(), calls=%async_computation.21 | async-start | bytes 5242880 | tf_op jit(solution)/shard_map/all_gather | solution.py:214
  230.5 233.2 %copy-start.24 = (bf16[128,2048]{1,0:T(8,128)(2,1)}, bf16[128,2048]{1,0:T(8,128)(2,1)S(1)}, u32[]{:S(2)}) copy-start(bf16[128,2048]{1,0:T(8,128)(2,1)S(1)} %fusion.213) | copy-start | bytes 1572868
  231.8 22.6 all-to-all-start.2
  254.4 205.0 %all-to-all-start = ((bf16[128,4,2,128]{0,3,2,1:T(8,128)(2,1)}), bf16[128,4,2,128]{0,3,2,1:T(8,128)(2,1)S(1)}, u32[]{:S(2)}, u32[]{:S(2)}) async-start(bf16[128,4,2,128]{0,3,2,1:T(8,128)(2,1)} %copy.369), calls=%async_computation | async-start | bytes 524288 | tf_op jit(solution)/shard_map/all_to_all | solution.py:245
  460.2 18.0 all-to-all-start.4
  479.0 23.6 all-to-all-start.3
  482.6 102.9 %all-gather.26.cloned.1.call-start = ((), (), s32[]{:S(2)}) async-start(), calls=%async_computation.19 | async-start | bytes 2359296 | tf_op jit(solution)/shard_map/all_gather | solution.py:350
  484.0 163.7 %all-gather.54.cloned.1.call-start = ((), (), s32[]{:S(2)}) async-start(), calls=%async_computation.46 | async-start | bytes 3538944 | tf_op jit(solution)/shard_map/all_gather | solution.py:25
  524.0 159.9 %all-gather.40.cloned.1.call-start = ((), (), s32[]{:S(2)}) async-start(), calls=%async_computation.26 | async-start | bytes 3538944 | tf_op jit(solution)/shard_map/all_gather | solution.py:192
  524.8 176.8 %all-gather.32.cloned.1.call-start = ((), (), s32[]{:S(2)}) async-start(), calls=%async_computation.22 | async-start | bytes 1179648 | tf_op jit(solution)/shard_map/all_gather | solution.py:191
  560.3 28.4 %all-to-all-start.1 = ((bf16[128,4,256]{0,2,1:T(8,128)(2,1)}), bf16[128,4,256]{0,2,1:T(8,128)(2,1)S(1)}, u32[]{:S(2)}, u32[]{:S(2)}) async-start(bf16[128,4,256]{0,2,1:T(8,128)(2,1)} %bitcast.42), calls=%async_computation.1 | async-start | bytes 524288 | tf_op jit(solution)/shard_map/all_to_all | solution.py:244
  563.7 204.9 %reduce-scatter.14.cloned.1.call-start = ((), (), s32[]{:S(2)}) async-start(), calls=%async_computation.27 | async-start | bytes 2621440 | tf_op jit(solution)/shard_map/reduce_scatter | solution.py:157
  706.2 190.2 %all-gather.44.cloned.1.call-start = ((), (), s32[]{:S(2)}) async-start(), calls=%async_computation.29 | async-start | bytes 9437184 | tf_op jit(solution)/shard_map/all_gather | solution.py:193
  708.8 210.6 %all-gather.42.cloned.1.call-start = ((), (), s32[]{:S(2)}) async-start(), calls=%async_computation.28 | async-start | bytes 2621440 | tf_op jit(solution)/shard_map/all_gather | solution.py:153
  709.2 358.6 %copy-start.74 = (f32[2048]{0:T(1024)}, f32[2048]{0:T(1024)S(1)}, u32[]{:S(2)}) copy-start(f32[2048]{0:T(1024)S(1)} %convert_element_type.375) | copy-start | bytes 24580
  769.9 298.0 %copy-start.100 = (f32[128]{0:T(128)}, f32[128]{0:T(128)S(1)}, u32[]{:S(2)}) copy-start(f32[128]{0:T(128)S(1)} %fusion.244) | copy-start | bytes 1540
  771.9 171.5 %all-gather.48.cloned.1.call-start = ((), (), s32[]{:S(2)}) async-start(), calls=%async_computation.32 | async-start | bytes 2621440 | tf_op jit(solution)/shard_map/all_gather | solution.py:153
  772.5 246.6 %all-gather.46.cloned.1.call-start = ((), (), s32[]{:S(2)}) async-start(), calls=%async_computation.30 | async-start | bytes 4718592 | tf_op jit(solution)/shard_map/all_gather | solution.py:194
  773.1 292.6 %reduce-scatter.18.cloned.1.call-start = ((), (), s32[]{:S(2)}) async-start(), calls=%async_computation.33 | async-start | bytes 2621440 | tf_op jit(solution)/shard_map/reduce_scatter | solution.py:157
  1035.9 57.2 %all-gather.50.cloned.1.call-start = ((), (), s32[]{:S(2)}) async-start(), calls=%async_computation.34 | async-start | bytes 2621440 | tf_op jit(solution)/shard_map/all_gather | solution.py:153
  1070.4 294.5 %all-gather.52.cloned.1.call-start = ((), (), s32[]{:S(2)}) async-start(), calls=%async_computation.37 | async-start | bytes 2621440 | tf_op jit(solution)/shard_map/all_gather | solution.py:153
  1070.9 297.4 %reduce-scatter.20.cloned.1.call-start = ((), (), s32[]{:S(2)}) async-start(), calls=%async_computation.35 | async-start | bytes 2359296 | tf_op jit(solution)/shard_map/reduce_scatter | solution.py:465
  1172.9 218.7 %all-gather.56.cloned.1.call-start = ((), (), s32[]{:S(2)}) async-start(), calls=%async_computation.47 | async-start | bytes 3538944 | tf_op jit(solution)/shard_map/all_gather | solution.py:49
  1257.7 259.8 %reduce-scatter.38.cloned.1.call-start = ((), (), s32[]{:S(2)}) async-start(), calls=%async_computation.45 | async-start | bytes 4718592 | tf_op jit(solution)/shard_map/reduce_scatter | solution.py:515
  1264.6 284.8 %reduce-scatter.32.cloned.1.call-start = ((), (), s32[]{:S(2)}) async-start(), calls=%async_computation.42 | async-start | bytes 1179648 | tf_op jit(solution)/shard_map/reduce_scatter | solution.py:506
  1268.8 347.0 %reduce-scatter.24.cloned.1.call-start = ((), (), s32[]{:S(2)}) async-start(), calls=%async_computation.38 | async-start | bytes 1179648 | tf_op jit(solution)/shard_map/reduce_scatter | solution.py:497
  1368.3 303.6 %reduce-scatter.28.cloned.1.call-start = ((), (), s32[]{:S(2)}) async-start(), calls=%async_computation.40 | async-start | bytes 73728 | tf_op jit(solution)/shard_map/reduce_scatter | solution.py:503
  1446.3 372.8 %all-reduce.18.cloned.1.call-start = ((), (), s32[]{:S(2)}) async-start(), calls=%async_computation.48 | async-start | bytes 8388608
  1458.2 437.8 %reduce-scatter.34.cloned.1.call-start = ((), (), s32[]{:S(2)}) async-start(), calls=%async_computation.43 | async-start | bytes 3538944 | tf_op jit(solution)/shard_map/reduce_scatter | solution.py:509
  1464.5 583.9 %reduce-scatter.36.cloned.1.call-start = ((), (), s32[]{:S(2)}) async-start(), calls=%async_computation.44 | async-start | bytes 9437184 | tf_op jit(solution)/shard_map/reduce_scatter | solution.py:512
  1474.5 606.8 %reduce-scatter.22.cloned.1.call-start = ((), (), s32[]{:S(2)}) async-start(), calls=%async_computation.36 | async-start | bytes 2621440 | tf_op jit(solution)/shard_map/reduce_scatter | solution.py:157
  1498.0 625.7 %reduce-scatter.16.cloned.1.call-start = ((), (), s32[]{:S(2)}) async-start(), calls=%async_computation.31 | async-start | bytes 2621440 | tf_op jit(solution)/shard_map/reduce_scatter | solution.py:157
  1504.9 732.1 %reduce-scatter.26.cloned.1.call-start = ((), (), s32[]{:S(2)}) async-start(), calls=%async_computation.39 | async-start | bytes 7077888 | tf_op jit(solution)/shard_map/reduce_scatter | solution.py:500
  1512.4 867.7 %reduce-scatter.30.cloned.1.call-start = ((), (), s32[]{:S(2)}) async-start(), calls=%async_computation.41 | async-start | bytes 4325376 | tf_op jit(solution)/shard_map/reduce_scatter | solution.py:521
  1820.6 260.7 %copy-start.19 = (bf16[128,2048]{1,0:T(8,128)(2,1)S(1)}, bf16[128,2048]{1,0:T(8,128)(2,1)}, u32[]{:S(2)}) copy-start(bf16[128,2048]{1,0:T(8,128)(2,1)} %param.40) | copy-start | bytes 1572868
  1820.6 260.7 %copy-start.84 = (f32[2048]{0:T(1024)S(1)}, f32[2048]{0:T(1024)}, u32[]{:S(2)}) copy-start(f32[2048]{0:T(1024)} %copy-done.83) | copy-start | bytes 24580
  1820.6 260.7 %copy-start.104 = (f32[128]{0:T(128)S(1)}, f32[128]{0:T(128)}, u32[]{:S(2)}) copy-start(f32[128]{0:T(128)} %copy-done.103) | copy-start | bytes 1540
  1898.0 225.7 %copy-start.28 = (bf16[128,2048]{1,0:T(8,128)(2,1)S(1)}, bf16[128,2048]{1,0:T(8,128)(2,1)}, u32[]{:S(2)}) copy-start(bf16[128,2048]{1,0:T(8,128)(2,1)} %reduce-scatter.14.cloned.1.call-done) | copy-start | bytes 1572868
  1898.0 225.7 %copy-start.35 = (bf16[128,2048]{1,0:T(8,128)(2,1)S(1)}, bf16[128,2048]{1,0:T(8,128)(2,1)}, u32[]{:S(2)}) copy-start(bf16[128,2048]{1,0:T(8,128)(2,1)} %param.42) | copy-start | bytes 1572868
  1898.0 225.7 %copy-start.36 = (bf16[128,2048]{1,0:T(8,128)(2,1)S(1)}, bf16[128,2048]{1,0:T(8,128)(2,1)}, u32[]{:S(2)}) copy-start(bf16[128,2048]{1,0:T(8,128)(2,1)} %reduce-scatter.18.cloned.1.call-done) | copy-start | bytes 1572868
  1898.0 225.7 %copy-start.75 = (f32[2048]{0:T(1024)S(1)}, f32[2048]{0:T(1024)}, u32[]{:S(2)}) copy-start(f32[2048]{0:T(1024)} %copy-done.74) | copy-start | bytes 24580
  1898.0 225.7 %copy-start.101 = (f32[128]{0:T(128)S(1)}, f32[128]{0:T(128)}, u32[]{:S(2)}) copy-start(f32[128]{0:T(128)} %copy-done.100) | copy-start | bytes 1540
  1898.0 225.7 %copy-start.111 = (f32[128]{0:T(128)S(1)}, f32[128]{0:T(128)}, u32[]{:S(2)}) copy-start(f32[128]{0:T(128)} %copy-done.110) | copy-start | bytes 1540
  (168 other events, 2052.5 us)
Sparse Core Ops, SparseCore 0:
  10.8 101.7 all-gather.33
  114.7 38.3 all-gather.27
  156.6 55.4 all-gather.23
  214.8 57.0 all-gather.37
  273.4 153.1 all-gather.35
  428.0 35.0 all-gather.29
  486.2 50.7 all-gather.25
  539.8 59.5 all-gather.53
  601.6 59.0 all-gather.39
  662.7 38.8 all-gather.31
  706.3 62.2 reduce-scatter.13
  771.4 124.8 all-gather.43
  898.5 20.7 all-gather.41
  920.8 22.5 all-gather.47
  945.7 73.3 all-gather.45
  1036.0 29.6 reduce-scatter.17
  1070.5 22.5 all-gather.49
  1094.5 22.5 all-gather.51
  1173.0 141.1 reduce-scatter.19
  1316.3 75.2 all-gather.55
  1395.2 87.0 reduce-scatter.37
  1486.0 63.2 reduce-scatter.31
  1553.3 62.4 reduce-scatter.23
  1619.1 52.6 reduce-scatter.27
  1678.3 140.7 all-reduce.17
  1822.9 73.0 reduce-scatter.33
  1900.0 148.3 reduce-scatter.35
  2050.9 30.4 reduce-scatter.21
  2084.0 31.4 reduce-scatter.15
  2119.0 117.9 reduce-scatter.25
  2239.8 140.1 reduce-scatter.29
where the time goes:
time: 2400 us; the launch traced here: 2390 us
  waiting for transfers between devices  1480 us (62%)
  blocking collectives  275 us (11%)
  local copies, waits for them, and re-layouts  225 us (9%)
  matrix products  206 us (9%)
  other arithmetic  83.7 us (3%)
  loops' own time  75.8 us (3%)
    unnamed x4, blocking collectives  192 us
    all_gather x1, waiting for transfers between devices, shards(): lax.all_gather(zx_cols, 'head', axis=2, tiled=True)  153 us
    reduce_scatter x1, waiting for transfers between devices, shards(): lax.psum_scatter(grad_gu_w.astype(jnp.bfloat16), 'blk', scatter_dimension...  150 us
    unnamed x32, waiting for transfers between devices  150 us
    reduce_scatter x1, waiting for transfers between devices, shards(): lax.psum_scatter(grad_bc_w, ('blk', 'head'), scatter_dimension=0, tiled=T...  140 us
    all_gather x1, waiting for transfers between devices, shards(): lax.all_gather(gu_w, 'blk', axis=0, tiled=True)  123 us
    reduce_scatter x4, waiting for transfers between devices, reduce_rows(): lax.psum_scatter(term.astype(jnp.bfloat16), 'head', scatter_dimension=0,...  119 us
    reduce_scatter x1, waiting for transfers between devices, shards(): lax.psum_scatter(grad_zx_w.astype(jnp.bfloat16), 'blk', scatter_dimension...  110 us
  transfers between devices with their start and end apart: 36, of which 23 were waited for; matrix products, arithmetic and copies ran while one was open for 20% of the time, Pallas kernels for 0%

commit v1 on v0

v1 whole, which is shorter than its diff:
```python
import functools
import math

import jax
import jax.numpy as jnp
from jax import lax
from jax.experimental import pallas as pl
from jax.experimental.pallas import tpu as pltpu
from jax.sharding import Mesh
from jax.sharding import PartitionSpec as P

QH = 8
KVH = 2
HD = 128
MP = 64
CHUNK = 256
KEYS = 512
EPS = 1e-05
THETA = 100000000000.0
NEGATIVE = -1e30
EXACT = lax.Precision.HIGHEST
F32 = jnp.float32
BF16 = jnp.bfloat16
VMEM_BYTES = 56 * 1024 * 1024
SWAP = [(0, 1), (1, 0)]


def mm(a, b, ca, cb, precision=None):
    return lax.dot_general(
        a, b, (((ca,), (cb,)), ((), ())), preferred_element_type=F32, precision=precision
    )


def swap(a, axis):
    return lax.ppermute(a, axis, SWAP)


def line_gather(pieces, put, out, up_only=False):
    count = lax.axis_size("z")
    place = lax.axis_index("z")
    ups, downs = [list(pieces)], [list(pieces)]
    for step in range(1, count):
        ups.append(
            [lax.ppermute(a, "z", [(i, i + 1) for i in range(step - 1, count - 1)]) for a in ups[-1]]
        )
        if not up_only:
            downs.append(
                [lax.ppermute(a, "z", [(i, i - 1) for i in range(count - step, 0, -1)]) for a in downs[-1]]
            )
    for number, piece in enumerate(pieces):
        out = put(out, place, number, piece)
    for step in range(1, count):
        for number in range(len(pieces)):
            value = ups[step][number]
            if not up_only:
                value = jnp.where(place >= step, value, downs[count - step][number])
            out = put(out, (place - step + count) % count, number, value)
    return out


def line_scatter(take, down_only=False):
    count = lax.axis_size("z")
    place = lax.axis_index("z")
    up = down = None
    for step in range(1, count):
        if not down_only:
            give = take(jnp.clip(count - step + place, 0, count - 1))
            give = give if up is None else give + up
            up = lax.ppermute(give, "z", [(i, i + 1) for i in range(step)])
        give = take(jnp.clip(place - (count - step), 0, count - 1))
        give = give if down is None else give + down
        down = lax.ppermute(give, "z", [(i, i - 1) for i in range(count - 1, count - 1 - step, -1)])
    total = take(place).astype(F32) + down.astype(F32)
    return total if down_only else total + up.astype(F32)


def spots(dx, dy, dc):
    x, y, c = (lax.axis_index(name) for name in "xyc")
    return ((x ^ dx) * 2 + (y ^ dy)) * 2 + (c ^ dc)


def cube_gather(a, axis):
    half = a.shape[0] // 2
    by_x, by_y = swap(a, "x"), swap(a, "y")
    far_low = swap(by_x[:half], "y")
    far_high = swap(by_y[half:], "x")
    far = jnp.concatenate([far_low, far_high], 0)
    out = jnp.zeros(a.shape[:axis] + (8,) + a.shape[axis:], a.dtype)
    other_far = jnp.concatenate([swap(far_low, "c"), swap(far_high, "c")], 0)
    for (dx, dy), near, other in (
        ((0, 0), a, swap(a, "c")),
        ((1, 0), by_x, swap(by_x, "c")),
        ((0, 1), by_y, swap(by_y, "c")),
        ((1, 1), far, other_far),
    ):
        out = lax.dynamic_update_index_in_dim(out, near, spots(dx, dy, 0), axis)
        out = lax.dynamic_update_index_in_dim(out, other, spots(dx, dy, 1), axis)
    return out


def cube_scatter(terms, axis):
    x, y, c = (lax.axis_index(name) for name in "xyc")
    pairs = terms.reshape(terms.shape[:axis] + (4, 2) + terms.shape[axis + 1 :])
    mine = lax.dynamic_index_in_dim(pairs, c, axis + 1, False)
    mine = mine + swap(lax.dynamic_index_in_dim(pairs, c ^ 1, axis + 1, False), "c")

    def share(dx, dy):
        return lax.dynamic_index_in_dim(mine, (x ^ dx) * 2 + (y ^ dy), axis, False)

    far, to_x, to_y = share(1, 1), share(1, 0), share(0, 1)
    half = far.shape[0] // 2
    from_x = swap(far[:half], "x")
    from_y = swap(far[half:], "y")
    to_x = jnp.concatenate([to_x[:half], to_x[half:] + from_y], 0)
    to_y = jnp.concatenate([to_y[:half] + from_x, to_y[half:]], 0)
    return share(0, 0).astype(F32) + swap(to_x, "x").astype(F32) + swap(to_y, "y").astype(F32)


def weight_gather(pack, after=None):
    if after is not None:
        pack, _ = lax.optimization_barrier((pack, after))
    x = lax.axis_index("x")
    own = lax.dynamic_index_in_dim(pack, x, 0, False)
    got = swap(lax.dynamic_index_in_dim(pack, x ^ 1, 0, False), "x")
    rows, cols = own.shape
    count = lax.axis_size("z")

    def put(out, group, number, value):
        return lax.dynamic_update_slice(out, value[None, None], (group, x ^ number, 0, 0))

    out = line_gather([own, got], put, jnp.zeros((count, 2, rows, cols), pack.dtype))
    return out.reshape(count * 2 * rows, cols)


def weight_scatter(grad):
    count = lax.axis_size("z")
    x = lax.axis_index("x")
    blocks = grad.reshape(count, 2, -1, grad.shape[1])

    def take(number):
        return lambda group: lax.dynamic_slice(
            blocks, (group, number, 0, 0), (1, 1) + blocks.shape[2:]
        )[0, 0]

    give = line_scatter(take(x ^ 1)).astype(BF16)
    got = swap(give, "x").astype(F32)
    own = line_scatter(take(x))
    return jnp.stack([jnp.where(x == 0, own, got), jnp.where(x == 0, got, own)], axis=1)


def lanes_of(cols, heads):
    rows = cols.shape[0]
    low = lax.broadcasted_iota(jnp.int32, (rows, 2 * MP), 1) < MP
    return jnp.concatenate(
        [
            jnp.where(low, cols[:, 2 * j : 2 * j + 1], cols[:, 2 * j + 1 : 2 * j + 2])
            for j in range(heads // 2)
        ],
        axis=1,
    )


def head_sums(values):
    wide = values.shape[1]
    lane = lax.broadcasted_iota(jnp.int32, (wide, 128), 0) // MP
    pick = (lane == lax.broadcasted_iota(jnp.int32, (wide, 128), 1)).astype(F32)
    return mm(values, pick, 1, 0, EXACT)


def softplus(v):
    return jnp.maximum(v, 0.0) + jnp.log1p(jnp.exp(-jnp.abs(v)))


def sigmoid(v):
    return 1.0 / (1.0 + jnp.exp(-v))


def chunk_common(rest_ref, dt_row_ref, par_ref, par_col_ref, seg_col_ref, seg_row_ref, wide):
    heads = wide // MP
    base = 2 * wide + HD
    states = (rest_ref.shape[1] - base - 128) // 2
    b_val = rest_ref[:, base : base + states]
    c_val = rest_ref[:, base + states : base + 2 * states]
    raw = rest_ref[:, base + 2 * states :].astype(F32) + par_ref[0:1, :]
    dt = softplus(raw)
    rate = par_ref[1:2, :]
    raw_row = dt_row_ref[...].astype(F32) + par_col_ref[:, 0:1]
    e_row = -softplus(raw_row) * par_col_ref[:, 1:2]
    first = lax.broadcasted_iota(jnp.int32, (CHUNK, CHUNK), 0)
    second = lax.broadcasted_iota(jnp.int32, (CHUNK, CHUNK), 1)
    lower = (first >= second).astype(F32)
    run = mm(lower, -dt * rate, 1, 0, EXACT)
    run_row = mm(e_row, lower, 1, 1, EXACT)
    bias = jnp.where((first >= second) & (seg_col_ref[...] == seg_row_ref[0]), 0.0, NEGATIVE)
    return heads, b_val, c_val, raw, dt, rate, run, run_row, bias, lower


def mamba_local_kernel(
    rest_ref, dt_row_ref, par_ref, par_col_ref, skip_ref, seg_col_ref, seg_row_ref, marks_ref,
    y_ref, run_ref, held_ref, total_ref, starts_ref, state, base_run,
):
    step = pl.program_id(0)
    wide = skip_ref.shape[1]
    heads, b_val, c_val, raw, dt, rate, run, run_row, bias, _ = chunk_common(
        rest_ref, dt_row_ref, par_ref, par_col_ref, seg_col_ref, seg_row_ref, wide
    )

    @pl.when(step == 0)
    def _():
        state[...] = jnp.zeros_like(state)
        base_run[...] = jnp.zeros_like(base_run)

    x_val = rest_ref[:, wide : 2 * wide].astype(F32)
    seg = seg_col_ref[...]
    label = marks_ref[step]
    final = marks_ref[step + 1]
    held = state[...]
    starts_ref[0] = held
    x_dt = x_val * lanes_of(dt, heads)
    x_dt_b = x_dt.astype(BF16)
    entry = jnp.where(seg == label, jnp.exp(run), 0.0)
    last = run[CHUNK - 1 : CHUNK, :]
    tail = jnp.where(seg == final, jnp.exp(last - run), 0.0)
    y_val = skip_ref[...] * x_val
    y_val = y_val + lanes_of(entry, heads) * mm(c_val, held.astype(BF16), 1, 0)
    gram = mm(c_val, b_val, 1, 1)
    low = lax.broadcasted_iota(jnp.int32, (CHUNK, 2 * MP), 1) < MP
    parts = []
    for pair in range(heads // 2):
        both = x_dt_b[:, pair * 2 * MP : (pair + 1) * 2 * MP]
        outs = []
        for h in (2 * pair, 2 * pair + 1):
            decay = jnp.exp(run[:, h : h + 1] - run_row[h : h + 1, :] + bias)
            outs.append(mm((decay * gram).astype(BF16), both, 1, 0))
        parts.append(jnp.where(low, outs[0], outs[1]))
    y_ref[...] = y_val + jnp.concatenate(parts, axis=1)
    fresh = mm(b_val, (x_dt * lanes_of(tail, heads)).astype(BF16), 0, 0)
    kept = jnp.where(label == final, jnp.exp(last), 0.0)
    new = lanes_of(jnp.broadcast_to(kept, (8, 128)), heads)[0:1] * held + fresh
    state[...] = new
    held_ref[...] = new
    run_all = run + base_run[0:1, :]
    run_ref[...] = run_all
    base_run[...] = jnp.broadcast_to(run_all[CHUNK - 1 : CHUNK, :], base_run.shape)
    total_ref[...] = jnp.exp(base_run[...])


def mamba_close_kernel(rest_ref, y_ref, run_ref, seg_col_ref, held_ref, marks_ref, out_ref, full_ref):
    wide = y_ref.shape[1]
    heads = wide // MP
    states = held_ref.shape[0]
    base = 2 * wide + HD + states
    c_val = rest_ref[:, base : base + states]
    entry = jnp.where(seg_col_ref[...] == marks_ref[0], jnp.exp(run_ref[...]), 0.0)
    y_val = y_ref[...] + lanes_of(entry, heads) * mm(c_val, held_ref[...].astype(BF16), 1, 0)
    full_ref[...] = y_val
    z_val = rest_ref[:, :wide].astype(F32)
    out_ref[...] = (y_val * z_val * sigmoid(z_val)).astype(BF16)


def mamba_grad_state_kernel(rest_ref, grad_ref, run_ref, seg_col_ref, marks_ref, out_ref):
    wide = grad_ref.shape[1]
    heads = wide // MP
    states = out_ref.shape[0]
    base = 2 * wide + HD + states
    c_val = rest_ref[:, base : base + states]
    z_val = rest_ref[:, :wide].astype(F32)
    entry = jnp.where(seg_col_ref[...] == marks_ref[0], jnp.exp(run_ref[...]), 0.0)
    grad_y = grad_ref[...].astype(F32) * z_val * sigmoid(z_val)

    @pl.when(pl.program_id(0) == 0)
    def _():
        out_ref[...] = jnp.zeros_like(out_ref)

    out_ref[...] += mm(c_val, (grad_y * lanes_of(entry, heads)).astype(BF16), 0, 0)


def mamba_grad_kernel(
    rest_ref, dt_row_ref, par_ref, par_col_ref, skip_ref, seg_col_ref, seg_row_ref, marks_ref,
    y_ref, run_ref, starts_ref, held_ref, grad_ref, deep_ref,
    zx_ref, bc_ref, dt_ref, sums_ref, skip_sum_ref, deep,
):
    step = pl.num_programs(0) - 1 - pl.program_id(0)
    wide = skip_ref.shape[1]
    heads, b_val, c_val, raw, dt, rate, run, run_row, bias, lower = chunk_common(
        rest_ref, dt_row_ref, par_ref, par_col_ref, seg_col_ref, seg_row_ref, wide
    )
    states = b_val.shape[1]

    @pl.when(pl.program_id(0) == 0)
    def _():
        deep[...] = deep_ref[...]
        sums_ref[...] = jnp.zeros_like(sums_ref)
        skip_sum_ref[...] = jnp.zeros_like(skip_sum_ref)

    z_val = rest_ref[:, :wide].astype(F32)
    x_val = rest_ref[:, wide : 2 * wide].astype(F32)
    seg = seg_col_ref[...]
    label = marks_ref[step]
    final = marks_ref[step + 1]
    last = run[CHUNK - 1 : CHUNK, :]
    before = run_ref[0:1, :] - run[0:1, :]
    carry = jnp.where(label == marks_ref[0], jnp.exp(before), 0.0)
    held = starts_ref[0] + lanes_of(jnp.broadcast_to(carry, (8, 128)), heads)[0:1] * held_ref[...]
    held_b = held.astype(BF16)
    after = deep[...]
    after_b = after.astype(BF16)
    grad = grad_ref[...].astype(F32)
    sig = sigmoid(z_val)
    grad_y = grad * z_val * sig
    grad_z = grad * y_ref[...] * (sig * (1.0 + z_val * (1.0 - sig)))
    dt_wide = lanes_of(dt, heads)
    x_dt = x_val * dt_wide
    entry = lanes_of(jnp.where(seg == label, jnp.exp(run), 0.0), heads)
    tail = lanes_of(jnp.where(seg == final, jnp.exp(last - run), 0.0), heads)
    grad_in = (entry * grad_y).astype(BF16)
    run_grad = head_sums(grad_y * entry * mm(c_val, held_b, 1, 0))
    grad_c = mm(grad_in, held_b, 1, 1)
    x_tail = x_dt * tail
    back = mm(b_val, after_b, 1, 0)
    grad_b = mm(x_tail.astype(BF16), after_b, 1, 1)
    tail_grad = head_sums(x_tail * back)
    run_grad = run_grad - tail_grad
    kept = jnp.where(label == final, jnp.exp(last), 0.0)
    kept_wide = lanes_of(jnp.broadcast_to(kept, (8, 128)), heads)[0:1]
    kept_grad = head_sums(
        jnp.broadcast_to(kept_wide * jnp.sum(after * held, axis=0, keepdims=True), (8, wide))
    )
    last_grad = jnp.sum(tail_grad, axis=0, keepdims=True) + kept_grad[0:1]
    deep[...] = kept_wide * after + mm(c_val, grad_in, 0, 0)
    gram = mm(c_val, b_val, 1, 1)
    low = lax.broadcasted_iota(jnp.int32, (CHUNK, 2 * MP), 1) < MP
    lane = lax.broadcasted_iota(jnp.int32, (CHUNK, 128), 1)
    x_dt_b = x_dt.astype(BF16)
    grad_y_b = grad_y.astype(BF16)
    none = jnp.zeros((CHUNK, 2 * MP), BF16)
    gram_grad = None
    parts, cols = [], []
    for pair in range(heads // 2):
        span = slice(pair * 2 * MP, (pair + 1) * 2 * MP)
        outs = []
        for h in (2 * pair, 2 * pair + 1):
            mask = low if h % 2 == 0 else ~low
            decay = jnp.exp(run[:, h : h + 1] - run_row[h : h + 1, :] + bias)
            mixing = (decay * gram).astype(BF16)
            outs.append(mm(mixing, grad_y_b[:, span], 0, 0))
            mixing_grad = mm(jnp.where(mask, grad_y_b[:, span], none), x_dt_b[:, span], 1, 1)
            weighted = mixing_grad * decay
            gram_grad = weighted if gram_grad is None else gram_grad + weighted
            weighted = weighted * gram
            run_grad = run_grad + jnp.where(
                lane == h, jnp.sum(weighted, axis=1, keepdims=True), 0.0
            )
            cols.append(jnp.sum(weighted, axis=0, keepdims=True))
        parts.append(jnp.where(low, outs[0], outs[1]))
    gram_grad_b = gram_grad.astype(BF16)
    grad_c = grad_c + mm(gram_grad_b, b_val, 1, 0)
    grad_b = grad_b + mm(gram_grad_b, c_val, 0, 0)
    x_dt_grad = jnp.concatenate(parts, axis=1) + tail * back
    zx_ref[:, :wide] = grad_z.astype(BF16)
    zx_ref[:, wide:] = (x_dt_grad * dt_wide + skip_ref[...] * grad_y).astype(BF16)
    bc_ref[:, :states] = grad_b.astype(BF16)
    bc_ref[:, states:] = grad_c.astype(BF16)
    col_grad = jnp.concatenate(cols + [jnp.zeros((128 - heads, CHUNK), F32)], axis=0)
    e_grad = mm(lower, run_grad, 0, 0, EXACT) - mm(lower, col_grad, 0, 1, EXACT) + last_grad
    dt_grad = head_sums(x_dt_grad * x_val) - rate * e_grad
    raw_grad = dt_grad * sigmoid(raw)
    dt_ref[...] = jnp.where(lane < heads, raw_grad, 0.0).astype(BF16)
    sums_ref[0:1, :] += jnp.sum(-rate * dt * e_grad, axis=0, keepdims=True)
    sums_ref[1:2, :] += jnp.sum(raw_grad, axis=0, keepdims=True)
    skip_sum_ref[0:1, :] += jnp.sum(grad_y * x_val, axis=0, keepdims=True)


def seen(kseg_ref, qseg, first_query, block):
    rows = qseg.shape[0]
    key_pos = block * KEYS + lax.broadcasted_iota(jnp.int32, (rows, KEYS), 1)
    query_pos = first_query + lax.broadcasted_iota(jnp.int32, (rows, KEYS), 0)
    return (key_pos <= query_pos) & (kseg_ref[pl.ds(block, 1), :] == qseg)


def attend_kernel(low_ref, high_ref, start_ref, q_ref, kv_ref, kseg_ref, qseg_ref, att_ref, log_ref):
    step = pl.program_id(0)
    rows = q_ref.shape[0]
    query = q_ref[...]
    qseg = qseg_ref[...]
    first_query = start_ref[0] + step * rows
    scale = HD**-0.5

    def visit(block, state):
        peak, total, acc = state
        span = pl.ds(pl.multiple_of(block * KEYS, KEYS), KEYS)
        scores = mm(query, kv_ref[span, :HD], 1, 1) * scale
        scores = jnp.where(seen(kseg_ref, qseg, first_query, block), scores, NEGATIVE)
        new_peak = jnp.maximum(peak, jnp.max(scores, axis=1, keepdims=True))
        weights = jnp.exp(scores - new_peak)
        rescale = jnp.exp(peak - new_peak)
        total = total * rescale + jnp.sum(weights, axis=1, keepdims=True)
        acc = acc * rescale + mm(weights.astype(BF16), kv_ref[span, HD:], 1, 0)
        return new_peak, total, acc

    peak, total, acc = lax.fori_loop(
        low_ref[step],
        high_ref[step],
        visit,
        (
            jnp.full((rows, 1), NEGATIVE, F32),
            jnp.zeros((rows, 1), F32),
            jnp.zeros((rows, HD), F32),
        ),
    )
    att_ref[...] = acc / total
    log_ref[...] = jnp.broadcast_to(peak + jnp.log(total), log_ref.shape)


def attend_grad_kernel(
    low_ref, high_ref, start_ref, q_ref, kv_ref, kseg_ref, qseg_ref, att_ref, log_ref, grad_ref,
    dq_ref, dkv_ref, sums,
):
    step = pl.program_id(0)
    rows = q_ref.shape[0]
    query = q_ref[...]
    grad = grad_ref[...]
    qseg = qseg_ref[...]
    log_total = log_ref[:, 0:1]
    first_query = start_ref[0] + step * rows
    scale = HD**-0.5
    delta = jnp.sum(grad.astype(F32) * att_ref[...], axis=1, keepdims=True)

    @pl.when(step == 0)
    def _():
        sums[...] = jnp.zeros_like(sums)

    def visit(block, acc):
        span = pl.ds(pl.multiple_of(block * KEYS, KEYS), KEYS)
        keys = kv_ref[span, :HD]
        scores = mm(query, keys, 1, 1) * scale - log_total
        scores = jnp.where(seen(kseg_ref, qseg, first_query, block), scores, NEGATIVE)
        probs = jnp.exp(scores)
        probs_grad = mm(grad, kv_ref[span, HD:], 1, 1)
        scores_grad = (probs * (probs_grad - delta)).astype(BF16)
        sums[span, :HD] += mm(scores_grad, query, 0, 0)
        sums[span, HD:] += mm(probs.astype(BF16), grad, 0, 0)
        return acc + mm(scores_grad, keys, 1, 0)

    acc = lax.fori_loop(low_ref[step], high_ref[step], visit, jnp.zeros((rows, HD), F32))
    dq_ref[...] = acc * scale

    @pl.when(step == pl.num_programs(0) - 1)
    def _():
        dkv_ref[:, :HD] = (sums[:, :HD] * scale).astype(BF16)
        dkv_ref[:, HD:] = sums[:, HD:].astype(BF16)


def call(kernel, out_shape, grid, in_specs, out_specs, scratch=(), prefetch=0, cost=None):
    return pl.pallas_call(
        kernel,
        out_shape=out_shape,
        grid_spec=pltpu.PrefetchScalarGridSpec(
            num_scalar_prefetch=prefetch,
            grid=grid,
            in_specs=in_specs,
            out_specs=out_specs,
            scratch_shapes=list(scratch),
        ),
        compiler_params=pltpu.CompilerParams(
            vmem_limit_bytes=VMEM_BYTES, dimension_semantics=("arbitrary",) * len(grid)
        ),
        cost_estimate=cost,
    )


def shape(dims, dtype=F32):
    return jax.ShapeDtypeStruct(dims, dtype)


def rope_tables(positions):
    half = HD // 2
    frequency = jnp.exp(jnp.arange(half, dtype=F32) * (-2.0 * math.log(THETA) / HD))
    angle = positions.astype(F32)[:, None] * frequency[None, :]
    cosine, sine = jnp.cos(angle), jnp.sin(angle)
    return jnp.concatenate([cosine, cosine], 1), jnp.concatenate([-sine, sine], 1)


def rope(values, tables):
    cosine, sine = tables
    return values * cosine + jnp.concatenate([values[:, HD // 2 :], values[:, : HD // 2]], 1) * sine


def rope_back(values, tables):
    cosine, sine = tables
    return values * cosine - jnp.concatenate([values[:, HD // 2 :], values[:, : HD // 2]], 1) * sine


def unit(values):
    return values * lax.rsqrt(jnp.mean(values * values, axis=-1, keepdims=True) + EPS)


def norm_back(values, gain, grad):
    scale = lax.rsqrt(jnp.mean(values * values, axis=-1, keepdims=True) + EPS)
    u = values * scale
    inner = jnp.mean(grad * gain * u, axis=-1, keepdims=True)
    return scale * (grad * gain - u * inner), jnp.sum(grad * u, axis=0)


def shards(
    tokens, seg_ids, cotangent, gain_mix, q_w, kv_w, zx_w, dt_w, bc_w,
    a_log, dt_bias, skip, wo_w, wm_w, gain_ff, gu_w, down_w,
):
    groups = lax.axis_size("z")
    z, x, y, c = (lax.axis_index(name) for name in "zxyc")
    own_rows, width = tokens.shape
    group = 8 * own_rows
    rows_w = q_w.shape[0]
    part = kv_w.shape[0]
    ratio = rows_w // part
    heads = dt_w.shape[1] // 2
    wide = heads * MP
    states = bc_w.shape[1] // 2
    ff = gu_w.shape[2] // 2
    inner = q_w.shape[1] // 2
    steps = group // CHUNK

    pack_one = jnp.concatenate(
        [
            q_w.reshape(rows_w, 2, inner).transpose(1, 0, 2),
            zx_w.reshape(rows_w, 2, 2, wide).transpose(2, 0, 1, 3).reshape(2, rows_w, 2 * wide),
        ],
        axis=2,
    )
    pack_out = jnp.concatenate(
        [
            wo_w.reshape(rows_w, 2, inner).transpose(1, 0, 2),
            wm_w.reshape(rows_w, 2, wide).transpose(1, 0, 2),
        ],
        axis=2,
    )
    pack_gu = gu_w.reshape(rows_w, 2, 2, ff).transpose(2, 0, 1, 3).reshape(2, rows_w, 2 * ff)
    pack_down = down_w.reshape(rows_w, 2, ff).transpose(1, 0, 2)
    kv_cols = kv_w.shape[1] * kv_w.shape[2]
    bc_cols = bc_w.shape[1]
    lead = kv_cols + bc_cols
    dt_cols = dt_w.shape[1]
    dt_part = dt_w.reshape(ratio, part, dt_cols).transpose(1, 0, 2).reshape(part, ratio * dt_cols)
    pack_two = jnp.concatenate(
        [kv_w.reshape(part, kv_cols), bc_w, gain_mix[:, None], gain_ff[:, None], dt_part], axis=1
    )
    used = pack_two.shape[1]
    total_cols = -(-used // 128) * 128
    pack_two = jnp.pad(pack_two, ((0, 0), (0, total_cols - used)))

    def put_two(out, at, number, value):
        return lax.dynamic_update_slice(out, value[None], (at, 0, 0))

    rows_all = cube_gather(tokens, 0).reshape(group, width)
    two = line_gather([pack_two], put_two, jnp.zeros((groups,) + pack_two.shape, BF16))
    two = cube_gather(two, 1).reshape(width, total_cols)
    w_one = weight_gather(pack_one)
    w_out = weight_gather(pack_out, w_one[0, 0])
    w_gu = weight_gather(pack_gu, w_out[0, 0])
    w_down = weight_gather(pack_down, w_gu[0, 0])
    grad_rows = cube_gather(cotangent, 0).reshape(group, width)

    seg_pair = jnp.zeros((2, seg_ids.shape[0]), jnp.int32)
    seg_pair = lax.dynamic_update_index_in_dim(seg_pair, seg_ids, x, 0)
    seg_pair = lax.dynamic_update_index_in_dim(seg_pair, swap(seg_ids, "x"), x ^ 1, 0)
    seg_own = seg_pair.reshape(1, group)
    seg_all = line_gather(
        [seg_own],
        lambda out, at, number, value: lax.dynamic_update_slice(out, value, (at, 0)),
        jnp.zeros((groups, group), jnp.int32),
        up_only=True,
    )
    segment = seg_own.astype(F32)
    seg_col = segment.reshape(group, 1)
    seg_row = segment.reshape(steps, 1, CHUNK)
    previous = lax.dynamic_index_in_dim(seg_all, jnp.maximum(z - 1, 0), 0, False)[group - 1]
    in_label = jnp.where(z > 0, previous, -1).astype(F32)
    marks = jnp.concatenate([in_label[None], segment[0, CHUNK - 1 :: CHUNK]])

    gain_one = two[:, lead].astype(F32)
    gain_two = two[:, lead + 1].astype(F32)
    dt_all = two[:, lead + 2 : lead + 2 + ratio * dt_cols].reshape(
        groups, 2, 4, part, ratio, 2, heads
    )
    dt_own = lax.dynamic_index_in_dim(dt_all, y * 2 + c, 2, False)
    dt_own = lax.dynamic_index_in_dim(dt_own, x, 4, False)
    w_dt = dt_own.transpose(0, 1, 3, 2, 4).reshape(width, heads)
    kv_head = ((y * 2 + c) * 2 + x) * (inner // HD) // (QH // KVH)
    w_k = lax.dynamic_slice_in_dim(two, kv_head * HD, HD, 1)
    w_v = lax.dynamic_slice_in_dim(two, kv_cols // 2 + kv_head * HD, HD, 1)
    w_rest = jnp.concatenate(
        [
            w_one[:, inner:],
            w_v,
            two[:, kv_cols:lead],
            jnp.pad(w_dt, ((0, 0), (0, 128 - heads))),
        ],
        axis=1,
    )
    w_qk = jnp.concatenate([w_one[:, :inner], w_k], axis=1)

    stream = rows_all.astype(F32)
    normed = (unit(stream) * gain_one).astype(BF16)
    positions = z * group + jnp.arange(group, dtype=jnp.int32)
    tables = rope_tables(positions)
    qk = mm(normed, w_qk, 1, 0)
    rest = mm(normed, w_rest, 1, 0).astype(BF16)
    query = rope(qk[:, :HD], tables).astype(BF16)
    kv_own = jnp.concatenate(
        [rope(qk[:, HD:], tables).astype(BF16), rest[:, 2 * wide : 2 * wide + HD]], axis=1
    )
    half = group // 2
    kv_half = lax.dynamic_slice_in_dim(kv_own, c * half, half, 0)
    kv_got = line_gather(
        [kv_half], put_two, jnp.zeros((groups, half, 2 * HD), BF16), up_only=True
    )
    kv_other = swap(kv_got, "c")
    kv_all = jnp.zeros((groups, 2, half, 2 * HD), BF16)
    kv_all = lax.dynamic_update_index_in_dim(kv_all, kv_got, c, 1)
    kv_all = lax.dynamic_update_index_in_dim(kv_all, kv_other, c ^ 1, 1)
    kv_all = kv_all.reshape(groups * group, 2 * HD)

    dt_row = jnp.pad(rest[:, -128 : -128 + 8].T, ((0, 8), (0, 0)))
    pad = ((0, 128 - heads),)

    def pick(values):
        return lax.dynamic_slice_in_dim(values, x * heads, heads, 0)

    rates = jnp.exp(pick(a_log))
    params = jnp.stack([jnp.pad(pick(dt_bias), pad), jnp.pad(rates, pad)])
    params = jnp.pad(params, ((0, 6), (0, 0)))
    params_col = jnp.pad(
        jnp.stack([pick(dt_bias), rates], axis=1), ((0, 16 - heads), (0, 126))
    )
    skip_wide = jnp.repeat(pick(skip), MP)[None, :]
    rest_cols = rest.shape[1]

    def flow(cols, back=False):
        at = (lambda i: (steps - 1 - i, 0)) if back else (lambda i: (i, 0))
        return pl.BlockSpec((CHUNK, cols), at)

    def chunk_specs(back=False):
        def turn(i):
            return steps - 1 - i if back else i

        return [
            flow(rest_cols, back),
            pl.BlockSpec((16, CHUNK), lambda i: (0, turn(i))),
            pl.BlockSpec((8, 128), lambda i: (0, 0)),
            pl.BlockSpec((16, 128), lambda i: (0, 0)),
            pl.BlockSpec((1, wide), lambda i: (0, 0)),
            flow(1, back),
            pl.BlockSpec((1, 1, CHUNK), lambda i: (turn(i), 0, 0)),
            pl.BlockSpec(memory_space=pltpu.SMEM),
        ]

    whole = pl.BlockSpec((states, wide), lambda i: (0, 0))
    smem = pl.BlockSpec(memory_space=pltpu.SMEM)
    chunk_args = (rest, dt_row, params, params_col, skip_wide, seg_col, seg_row, marks)
    y_local, run, held_own, total, starts = call(
        mamba_local_kernel,
        (
            shape((group, wide)),
            shape((group, 128)),
            shape((states, wide)),
            shape((8, 128)),
            shape((steps, states, wide)),
        ),
        (steps,),
        chunk_specs(),
        (
            flow(wide),
            flow(128),
            whole,
            pl.BlockSpec((8, 128), lambda i: (0, 0)),
            pl.BlockSpec((1, states, wide), lambda i: (i, 0, 0)),
        ),
        [pltpu.VMEM((states, wide), F32), pltpu.VMEM((8, 128), F32)],
    )(*chunk_args)
    joined = jnp.where(in_label == segment[0, group - 1], 1.0, 0.0)
    factor = jnp.repeat(total[0, :heads] * joined, MP)[None, :]
    up_line = [(i, i + 1) for i in range(groups - 1)]
    down_line = [(i + 1, i) for i in range(groups - 1)]
    entering = jnp.zeros((states, wide), BF16)
    for step in range(groups - 1):
        leaving = held_own if step == 0 else held_own + factor * entering.astype(F32)
        entering = lax.ppermute(leaving.astype(BF16), "z", up_line)
    in_held = entering

    q_rows = CHUNK
    blocks = group // q_rows
    first_rows = z * group + q_rows * jnp.arange(blocks, dtype=jnp.int32)
    first_seg = seg_own[0, ::q_rows]
    reached = jnp.arange(groups * group, dtype=jnp.int32)[None, :] < (z + 1) * group
    earlier = (seg_all.reshape(1, -1) < first_seg[:, None]) & reached
    low = jnp.sum(earlier, axis=1, dtype=jnp.int32) // KEYS
    high = (first_rows + q_rows - 1) // KEYS + 1
    start = (z * group)[None].astype(jnp.int32)
    key_seg = seg_all.astype(F32).reshape(groups * group // KEYS, KEYS)

    def rows_spec(cols):
        return pl.BlockSpec((q_rows, cols), lambda i, *_: (i, 0))

    def full_spec(a):
        return pl.BlockSpec(a.shape, lambda i, *_: (0, 0))

    att_full, log_total = call(
        attend_kernel,
        (shape((group, HD)), shape((group, 128))),
        (blocks,),
        [rows_spec(HD), full_spec(kv_all), full_spec(key_seg), rows_spec(1)],
        (rows_spec(HD), rows_spec(128)),
        prefetch=3,
    )(low, high, start, query, kv_all, key_seg, seg_col)

    ssm_out, y_full = call(
        mamba_close_kernel,
        (shape((group, wide), BF16), shape((group, wide))),
        (steps,),
        [flow(rest_cols), flow(wide), flow(128), flow(1), whole, smem],
        (flow(wide), flow(wide)),
    )(rest, y_local, run, seg_col, in_held, marks)
    mixer_out = jnp.concatenate([att_full.astype(BF16), ssm_out], axis=1)

    def to_rows(term):
        return cube_scatter(term.astype(BF16).reshape(8, own_rows, width), 0)

    stream_own = tokens.astype(F32)
    middle = stream_own + to_rows(mm(mixer_out, w_out, 1, 1))
    normed_two = (unit(middle) * gain_two).astype(BF16)
    rows_two = cube_gather(normed_two, 0).reshape(group, width)
    gate_up = mm(rows_two, w_gu, 1, 0).astype(BF16)
    gate = gate_up[:, :ff].astype(F32)
    up = gate_up[:, ff:].astype(F32)
    sig = jax.nn.sigmoid(gate)
    hidden = (gate * sig * up).astype(BF16)
    grad_hidden = mm(grad_rows, w_down, 1, 0).astype(BF16).astype(F32)
    grad_gate = grad_hidden * up * (sig * (1.0 + gate * (1.0 - sig)))
    grad_gu = jnp.concatenate([grad_gate, grad_hidden * gate * sig], axis=1).astype(BF16)
    grad_normed_two = to_rows(mm(grad_gu, w_gu, 1, 1))
    layer_out = (middle + to_rows(mm(hidden, w_down, 1, 1))).astype(BF16)
    down_part = weight_scatter(mm(grad_rows, hidden, 0, 0).astype(BF16))
    gu_part = weight_scatter(mm(rows_two, grad_gu, 0, 0).astype(BF16))
    middle_part, gain_two_part = norm_back(middle, gain_two, grad_normed_two)
    grad_middle = cotangent.astype(F32) + middle_part
    mixed_rows = cube_gather(grad_middle.astype(BF16), 0).reshape(group, width)
    grad_mixer = mm(mixed_rows, w_out, 1, 0).astype(BF16)
    out_part = weight_scatter(mm(mixed_rows, mixer_out, 0, 0).astype(BF16))

    grad_att = grad_mixer[:, :inner]
    grad_ssm = grad_mixer[:, inner:]
    state_grad = call(
        mamba_grad_state_kernel,
        shape((states, wide)),
        (steps,),
        [flow(rest_cols), flow(wide), flow(128), flow(1), smem],
        whole,
    )(rest, grad_ssm, run, seg_col, marks)
    deep = jnp.zeros((states, wide), BF16)
    for step in range(groups - 1):
        leaving = state_grad if step == 0 else state_grad + factor * deep.astype(F32)
        deep = lax.ppermute(leaving.astype(BF16), "z", down_line)
    deep = deep.astype(F32)
    grad_query, grad_kv_all = call(
        attend_grad_kernel,
        (shape((group, HD)), shape((groups * group, 2 * HD), BF16)),
        (blocks,),
        [
            rows_spec(HD), full_spec(kv_all), full_spec(key_seg), rows_spec(1),
            rows_spec(HD), rows_spec(128), rows_spec(HD),
        ],
        (rows_spec(HD), full_spec(kv_all)),
        [pltpu.VMEM((groups * group, 2 * HD), F32)],
        prefetch=3,
    )(low, high, start, query, kv_all, key_seg, seg_col, att_full, log_total, grad_att)
    kv_terms = grad_kv_all.reshape(groups, 2, half, 2 * HD)
    kv_terms = lax.dynamic_index_in_dim(kv_terms, c, 1, False) + swap(
        lax.dynamic_index_in_dim(kv_terms, c ^ 1, 1, False), "c"
    )
    grad_kv_half = line_scatter(
        lambda at: lax.dynamic_index_in_dim(kv_terms, at, 0, False), down_only=True
    )
    half_tables = tuple(lax.dynamic_slice_in_dim(table, c * half, half, 0) for table in tables)
    grad_kv_half = jnp.concatenate(
        [rope_back(grad_kv_half[:, :HD], half_tables), grad_kv_half[:, HD:]], axis=1
    ).astype(BF16)
    grad_kv = lax.dynamic_update_slice(
        jnp.zeros((group, 2 * HD), BF16), grad_kv_half, (c * half, 0)
    )
    grad_q = rope_back(grad_query, tables).astype(BF16)
    grad_zx, grad_bc, grad_dt, sums, skip_sums = call(
        mamba_grad_kernel,
        (
            shape((group, 2 * wide), BF16),
            shape((group, 2 * states), BF16),
            shape((group, 128), BF16),
            shape((8, 128)),
            shape((8, wide)),
        ),
        (steps,),
        chunk_specs(True)
        + [
            flow(wide, True),
            flow(128, True),
            pl.BlockSpec((1, states, wide), lambda i: (steps - 1 - i, 0, 0)),
            whole,
            flow(wide, True),
            whole,
        ],
        (
            flow(2 * wide, True),
            flow(2 * states, True),
            flow(128, True),
            pl.BlockSpec((8, 128), lambda i: (0, 0)),
            pl.BlockSpec((8, wide), lambda i: (0, 0)),
        ),
        [pltpu.VMEM((states, wide), F32)],
    )(*chunk_args, y_full, run, starts, in_held, grad_ssm, deep)

    grad_rest = jnp.concatenate([grad_zx, grad_kv[:, HD:], grad_bc, grad_dt], axis=1)
    grad_qk = jnp.concatenate([grad_q, grad_kv[:, :HD]], axis=1)
    in_term = (mm(grad_rest, w_rest, 1, 1) + mm(grad_qk, w_qk, 1, 1)).astype(BF16)
    gain_one_part = jnp.sum(in_term.astype(F32) * unit(stream), axis=0)
    rest_w = mm(normed, grad_rest, 0, 0).astype(BF16)
    qk_w = mm(normed, grad_qk, 0, 0).astype(BF16)
    one_part = weight_scatter(jnp.concatenate([qk_w[:, :inner], rest_w[:, : 2 * wide]], axis=1))
    input_part, _ = norm_back(stream_own, gain_one, to_rows(in_term))
    input_grad = grad_middle + input_part
    kv_grads = jnp.zeros((width, kv_cols), BF16)
    kv_grads = lax.dynamic_update_slice_in_dim(kv_grads, qk_w[:, inner:], kv_head * HD, 1)
    kv_grads = lax.dynamic_update_slice_in_dim(
        kv_grads, rest_w[:, 2 * wide : 2 * wide + HD], kv_cols // 2 + kv_head * HD, 1
    )
    dt_full = rest_w[:, -128 : -128 + heads].reshape(groups, 2, ratio, part, heads)
    dt_full = dt_full.transpose(0, 1, 3, 2, 4)[:, :, :, :, None, :]
    dt_full = jnp.where(jnp.arange(2)[:, None] == x, dt_full, 0).reshape(
        groups, 2, 1, part, ratio * dt_cols
    )
    dt_full = jnp.where(
        jnp.arange(4)[:, None, None] == y * 2 + c, dt_full, 0
    ).reshape(width, ratio * dt_cols)
    two_grads = jnp.concatenate(
        [
            kv_grads,
            rest_w[:, 2 * wide + HD : 2 * wide + HD + bc_cols],
            gain_one_part.astype(BF16)[:, None],
            gain_two_part.astype(BF16)[:, None],
            dt_full,
            jnp.zeros((width, total_cols - used), BF16),
        ],
        axis=1,
    )
    two_part = cube_scatter(two_grads.reshape(groups, 8, part, total_cols), 1).astype(BF16)
    two_part = line_scatter(lambda at: lax.dynamic_index_in_dim(two_part, at, 0, False))
    kv_grad = two_part[:, :kv_cols].reshape(kv_w.shape)
    bc_grad = two_part[:, kv_cols:lead]
    dt_grad = two_part[:, lead + 2 : used].reshape(part, ratio, dt_cols)
    dt_grad = dt_grad.transpose(1, 0, 2).reshape(rows_w, dt_cols)
    small = jnp.stack(
        [sums[0, :heads], sums[1, :heads], jnp.sum(skip_sums[0].reshape(heads, MP), axis=1)]
    )
    small_pair = jnp.zeros((2, 3, heads), F32)
    small_pair = lax.dynamic_update_index_in_dim(small_pair, small, x, 0)
    small_pair = lax.dynamic_update_index_in_dim(small_pair, swap(small, "x"), x ^ 1, 0)
    small_line = line_gather(
        [small_pair],
        lambda out, at, number, value: lax.dynamic_update_slice(out, value[None], (at, 0, 0, 0)),
        jnp.zeros((groups, 2, 3, heads), F32),
    )
    small_sum = jnp.sum(small_line, axis=0).transpose(1, 0, 2).reshape(3, 2 * heads)
    return (
        layer_out,
        input_grad,
        two_part[:, lead],
        one_part[:, :, :inner].reshape(rows_w, 2 * inner),
        kv_grad,
        one_part[:, :, inner:].reshape(rows_w, 2, 2, wide).transpose(0, 2, 1, 3).reshape(zx_w.shape),
        dt_grad,
        bc_grad,
        small_sum[0],
        small_sum[1],
        small_sum[2],
        out_part[:, :, :inner].reshape(wo_w.shape),
        out_part[:, :, inner:].reshape(wm_w.shape),
        two_part[:, lead + 1],
        gu_part.reshape(rows_w, 2, 2, ff).transpose(0, 2, 1, 3).reshape(gu_w.shape),
        down_part.reshape(down_w.shape),
    )


def solution(mesh):
    groups = mesh.shape["blk"] // 2
    fine = Mesh(mesh.devices.reshape(groups, 2, 2, mesh.shape["head"] // 2), ("z", "x", "y", "c"))
    blk, head = ("z", "x"), ("y", "c")
    every = blk + head
    rows = P(every, None)
    return jax.shard_map(
        shards,
        mesh=fine,
        in_specs=(
            rows,
            P(blk),
            rows,
            P(every),
            P(blk, head),
            P(every, None, None),
            P(blk, None, head),
            P(blk, head),
            rows,
            P(head),
            P(head),
            P(head),
            P(blk, head),
            P(blk, head),
            P(every),
            P(blk, None, head),
            P(blk, head),
        ),
        out_specs=(
            rows,
            rows,
            P(every),
            P(blk, head),
            P(every, None, None),
            P(blk, None, head),
            P(blk, head),
            rows,
            P(head),
            P(head),
            P(head),
            P(blk, head),
            P(blk, head),
            P(every),
            P(blk, None, head),
            P(blk, head),
        ),
        check_vma=False,
    )
```

time: 2400 us -> 1080 us (0.45)
  waiting for transfers between devices: 1480 us -> 297 us
  starting transfers between devices: 19.7 us -> 401 us
  blocking collectives: 275 us -> 0 us
  matrix products: 206 us -> 73.9 us
  local copies, waits for them, and re-layouts: 225 us -> 142 us
  loops' own time: 75.8 us -> 0 us
  Pallas kernels: 0 us -> 60 us
    reduce_scatter x13 -> x0, waiting for transfers between devices: 723 us -> none  [the longest x1 150 us: shards(): lax.psum_scatter(grad_gu_w.astype(jnp.bfloat16), 'blk', scatter_dimension...]
    all_gather x17 -> x0, waiting for transfers between devices: 593 us -> none  [the longest x1 153 us: shards(): lax.all_gather(zx_cols, 'head', axis=2, tiled=True)]
    ppermute x0 -> x211, starting transfers between devices: none -> 401 us  [the longest x27 138 us: line_scatter(): up = lax.ppermute(give, 'z', [(i, i + 1) for i in range(step)])]
    ppermute x0 -> x211, waiting for transfers between devices: none -> 297 us  [the longest x30 134 us: line_gather(): lax.ppermute(a, 'z', [(i, i - 1) for i in range(count - step, 0, -1)])]
    unnamed x4 -> x0, blocking collectives: 192 us -> none
    unnamed x32 -> x0, waiting for transfers between devices: 150 us -> none
    dot_general x71 -> x15, matrix products: 202 us -> 73.9 us  [mm(): lax.dot_general(a, b, (((ca,), (cb,)), ((), ())), preferred_element_type=...]
    another operation x24 -> x0, loops' own time: 75.8 us -> none  [the longest x2 60.6 us: sweep(): carry, unused = lax.scan(visit, carry, items)]
  transfers between devices with their start and end apart: 36 -> 211, of which waited for: 23 -> 60; matrix products, arithmetic and copies ran while one was open for 20% -> 22% of each run, Pallas kernels for 0% -> 6%
where the time goes in v1:
time: 1080 us; the launch traced here: 1070 us
  starting transfers between devices  401 us (37%)
  waiting for transfers between devices  297 us (28%)
  local copies, waits for them, and re-layouts  142 us (13%)
  other arithmetic  89.4 us (8%)
  matrix products  73.9 us (7%)
  Pallas kernels  60 us (6%)
    ppermute x27, starting transfers between devices, line_scatter(): up = lax.ppermute(give, 'z', [(i, i + 1) for i in range(step)])  138 us
    ppermute x30, waiting for transfers between devices, line_gather(): lax.ppermute(a, 'z', [(i, i - 1) for i in range(count - step, 0, -1)])  134 us
    ppermute x36, starting transfers between devices, line_gather(): lax.ppermute(a, 'z', [(i, i + 1) for i in range(step - 1, count - 1)])  94.6 us
    ppermute x82, waiting for transfers between devices, swap(): return lax.ppermute(a, axis, SWAP)  80.4 us
    dot_general x15, matrix products, mm(): lax.dot_general(a, b, (((ca,), (cb,)), ((), ())), preferred_element_type=...  73.9 us
    ppermute x82, starting transfers between devices, swap(): return lax.ppermute(a, axis, SWAP)  60.7 us
    ppermute x30, starting transfers between devices, line_gather(): lax.ppermute(a, 'z', [(i, i - 1) for i in range(count - step, 0, -1)])  39.6 us
    ppermute x3, starting transfers between devices, shards(): entering = lax.ppermute(leaving.astype(BF16), 'z', up_line)  32.7 us
  transfers between devices with their start and end apart: 211, of which 60 were waited for; matrix products, arithmetic and copies ran while one was open for 22% of the time, Pallas kernels for 6%

profile of v1, /device:TPU:0, one launch (start us, length us, event | category | flops | bytes accessed | tf_op | source)
XLA Modules:
  0.0 1069.8 jit_solution(10357802647652238092)
XLA Ops:
  6.9 6.2 collective-permute-start.13
  65.6 5.8 collective-permute-done.15
  73.4 6.2 collective-permute-done.16
  83.8 7.5 collective-permute-done.28
  98.3 6.4 collective-permute-done.50
  109.6 8.2 collective-permute-start.49
  141.7 9.9 collective-permute-done.20
  157.6 6.3 collective-permute-start.29
  167.2 16.7 %collective-permute-done.55 = bf16[256,512]{1,0:T(8,128)(2,1)S(1)} collective-permute-done((bf16[256,512]{1,0:T(8,128)(2,1)S(1)}, bf16[256,512]{1,0:T(8,128)(2,1)S(1)}, u32[]{:S(2)}, u32[]{:S(2)}) %collective-permute-start.55) | collective-permute-done | bytes 262176 | tf_op jit(solution)/shard_map/ppermute | solution.py:48
  201.8 6.2 collective-permute-done.32
  209.6 17.3 %collective-permute-done.34 = bf16[256,896]{1,0:T(8,128)(2,1)S(1)} collective-permute-done((bf16[256,896]{1,0:T(8,128)(2,1)S(1)}, bf16[256,896]{1,0:T(8,128)(2,1)S(1)}, u32[]{:S(2)}, u32[]{:S(2)}) %collective-permute-start.34) | collective-permute-done | bytes 458784 | tf_op jit(solution)/shard_map/ppermute | solution.py:48
  260.6 12.9 %collective-permute-start.76 = (bf16[256,1024]{1,0:T(8,128)(2,1)}, bf16[256,1024]{1,0:T(8,128)(2,1)}, u32[]{:S(2)}, u32[]{:S(2)}) collective-permute-start(bf16[256,1024]{1,0:T(8,128)(2,1)} %bitcast.114), channel_id=1, source_target_pairs={{0,8},{8,16},{16,24},{1,9},{9,17},{17,25},{2,10},{10,18},{18,26},{... | collective-permute-start | bytes 1572872 | tf_op jit(solution)/shard_map/ppermute | solution.py:44
  279.8 7.6 convolution_convert_fusion.1.rest_ref
  289.3 7.4 collective-permute-start.41
  302.6 10.5 shard_map.289
  316.8 20.2 %collective-permute-start.45 = (bf16[256,384]{1,0:T(8,128)(2,1)S(1)}, bf16[256,384]{1,0:T(8,128)(2,1)S(1)}, u32[]{:S(2)}, u32[]{:S(2)}) collective-permute-start(bf16[256,384]{1,0:T(8,128)(2,1)S(1)} %convert_element_type.465), channel_id=1, source_target_pairs={{0,8},{8,16},{16,24},{1,9},{9,17},{17,25},{2,10},{10,18},{18,26},{... | collective-permute-start | bytes 589832 | tf_op jit(solution)/shard_map/ppermute | solution.py:687
  341.2 7.5 collective-permute-start.46
  368.4 5.4 shard_map.290
  377.0 7.2 shard_map.288
  402.0 11.3 %collective-permute-done.96 = bf16[256,512]{1,0:T(8,128)(2,1)S(1)} collective-permute-done((bf16[256,512]{1,0:T(8,128)(2,1)S(1)}, bf16[256,512]{1,0:T(8,128)(2,1)S(1)}, u32[]{:S(2)}, u32[]{:S(2)}) %collective-permute-start.96) | collective-permute-done | bytes 262176 | tf_op jit(solution)/shard_map/ppermute | solution.py:48
  413.4 9.9 collective-permute-start.80
  424.1 10.4 collective-permute-done.78
  440.1 27.2 %collective-permute-done.82 = bf16[256,1024]{1,0:T(8,128)(2,1)S(1)} collective-permute-done((bf16[256,1024]{1,0:T(8,128)(2,1)S(1)}, bf16[256,1024]{1,0:T(8,128)(2,1)S(1)}, u32[]{:S(2)}, u32[]{:S(2)}) %collective-permute-start.82) | collective-permute-done | bytes 524320 | tf_op jit(solution)/shard_map/ppermute | solution.py:48
  472.2 6.6 collective-permute-done.83
  481.9 7.3 collective-permute-done.63
  495.0 9.9 collective-permute-done.67
  515.7 5.2 convolution_convert_fusion.9
  529.9 6.9 collective-permute-start.201
  538.8 5.9 convolution_convert_fusion.4
  550.7 9.4 collective-permute-start.202
  566.4 15.3 %collective-permute-start.194 = (bf16[256,1024]{1,0:T(8,128)(2,1)S(1)}, bf16[256,1024]{1,0:T(8,128)(2,1)S(1)}, u32[]{:S(2)}, u32[]{:S(2)}) collective-permute-start(bf16[256,1024]{1,0:T(8,128)(2,1)S(1)} %get-tuple-element.76), channel_id=1, source_target_pairs={{0,8},{1,9},{2,10},{3,11},{4,12},{5,13},{6,14},{7,15}} | collective-permute-start | bytes 1572872 | tf_op jit(solution)/shard_map/ppermute | solution.py:69
  585.2 12.4 %collective-permute-done.208 = bf16[256,512]{1,0:T(8,128)(2,1)S(1)} collective-permute-done((bf16[256,512]{1,0:T(8,128)(2,1)S(1)}, bf16[256,512]{1,0:T(8,128)(2,1)S(1)}, u32[]{:S(2)}, u32[]{:S(2)}) %collective-permute-start.208) | collective-permute-done | bytes 262176 | tf_op jit(solution)/shard_map/ppermute | solution.py:69
  611.4 5.3 collective-permute-start.195
  623.9 5.2 collective-permute-start.203
  674.1 5.3 collective-permute-start.190
  742.1 5.7 shard_map.291
  750.2 10.3 shard_map.293
  765.9 14.5 %collective-permute-done.130 = bf16[256,384]{1,0:T(8,128)(2,1)S(1)} collective-permute-done((bf16[256,384]{1,0:T(8,128)(2,1)S(1)}, bf16[256,384]{1,0:T(8,128)(2,1)S(1)}, u32[]{:S(2)}, u32[]{:S(2)}) %collective-permute-start.130) | collective-permute-done | bytes 196640 | tf_op jit(solution)/shard_map/ppermute | solution.py:762
  783.9 12.8 %collective-permute-start.176 = (bf16[256,512]{1,0:T(8,128)(2,1)}, bf16[256,512]{1,0:T(8,128)(2,1)}, u32[]{:S(2)}, u32[]{:S(2)}) collective-permute-start(bf16[256,512]{1,0:T(8,128)(2,1)} %get-tuple-element.121), channel_id=1, source_target_pairs={{0,8},{8,16},{1,9},{9,17},{2,10},{10,18},{3,11},{11,19},{4,12},{12... | collective-permute-start | bytes 786440 | tf_op jit(solution)/shard_map/ppermute | solution.py:69
  798.9 20.9 %shard_map.292 = (bf16[1024,768]{1,0:T(8,128)(2,1)}, bf16[1024,512]{1,0:T(8,128)(2,1)}, bf16[1024,128]{1,0:T(8,128)(2,1)}, f32[8,128]{1,0:T(8,128)}, f32[8,384]{1,0:T(8,128)}) custom-call(bf16[1024,1536]{1,0:T(8,128)(2,1)} %copy-done, bf16[16,1024]{1,0:T(8,128)(2,1)} %pad.29.clone.dt_row_ref, f32[8,128]{1,0:T(8,128)} %select_maximum_fusion.par_ref, ...), custom_call_target="tpu_custom_call" | custom-call | tf_op jit(solution)/shard_map/pallas_call | solution.py:791
  840.1 5.3 collective-permute-start.182
  852.9 13.3 %collective-permute-done.135 = bf16[512,256]{1,0:T(8,128)(2,1)S(1)} collective-permute-done((bf16[512,256]{1,0:T(8,128)(2,1)S(1)}, bf16[512,256]{1,0:T(8,128)(2,1)S(1)}, u32[]{:S(2)}, u32[]{:S(2)}) %collective-permute-start.135) | collective-permute-done | bytes 262176 | tf_op jit(solution)/shard_map/ppermute | solution.py:72
  866.9 8.1 convolution_convert_fusion
  900.4 13.1 %multiply_reduce_fusion = (bf16[2048]{0:T(1024)(128)(2,1)S(1)}, bf16[1024,2048]{1,0:T(8,128)(2,1)}) fusion(bf16[8,128,2048]{2,1,0:T(8,128)(2,1)} %copy-done.3, f32[1024]{0:T(1024)S(1)} %copy-done.108, f32[1024,2048]{1,0:T(8,128)} %fusion.37, bf16[2048,6]{1,0:T(8,128)(2,1)S(1)} %bitcast.743, bf16[2048,512]{1,0:T(8,128)(2,1)} %slice.513, ...), kind=kOutput, calls=%fused_computation.3 | convolution fusion | flops 6501169152 | bytes 25722880 | tf_op jit(solution)/shard_map/dot_general | solution.py:29
  923.8 8.7 concatenate.166
  962.0 5.5 collective-permute-start.177
  1027.6 9.9 collective-permute-done.143
  1049.5 7.3 collective-permute-start.150
  (992 shorter events, 598.7 us)
Async XLA Ops:
  5.6 54.3 %collective-permute-start.14 = (bf16[64,1152]{1,0:T(8,128)(2,1)}, bf16[64,1152]{1,0:T(8,128)(2,1)}, u32[]{:S(2)}, u32[]{:S(2)}) collective-permute-start(bf16[64,1152]{1,0:T(8,128)(2,1)} %pad.27), channel_id=1, source_target_pairs={{24,16},{16,8},{8,0},{25,17},{17,9},{9,1},{26,18},{18,10},{10,2},{... | collective-permute-start | bytes 442376 | tf_op jit(solution)/shard_map/ppermute | solution.py:48
  6.9 56.5 %collective-permute-start.13 = (bf16[64,1152]{1,0:T(8,128)(2,1)}, bf16[64,1152]{1,0:T(8,128)(2,1)}, u32[]{:S(2)}, u32[]{:S(2)}) collective-permute-start(bf16[64,1152]{1,0:T(8,128)(2,1)} %pad.27), channel_id=1, source_target_pairs={{0,8},{8,16},{16,24},{1,9},{9,17},{17,25},{2,10},{10,18},{18,26},{... | collective-permute-start | bytes 442376 | tf_op jit(solution)/shard_map/ppermute | solution.py:44
  13.1 80.5 %collective-permute-start.4 = (bf16[128,2048]{1,0:T(8,128)(2,1)}, bf16[128,2048]{1,0:T(8,128)(2,1)}, u32[]{:S(2)}, u32[]{:S(2)}) collective-permute-start(bf16[128,2048]{1,0:T(8,128)(2,1)} %param.17), channel_id=1, source_target_pairs={{0,1},{1,0},{2,3},{3,2},{4,5},{5,4},{6,7},{7,6},{8,9},{9,8},{10,11... | collective-permute-start | bytes 1572872 | tf_op jit(solution)/shard_map/ppermute | solution.py:35
  18.2 42.3 %collective-permute-start.48 = (bf16[256,512]{1,0:T(8,128)(2,1)}, bf16[256,512]{1,0:T(8,128)(2,1)}, u32[]{:S(2)}, u32[]{:S(2)}) collective-permute-start(bf16[256,512]{1,0:T(8,128)(2,1)} %bitcast.79), channel_id=1, source_target_pairs={{0,4},{4,0},{1,5},{5,1},{2,6},{6,2},{3,7},{7,3},{8,12},{12,8},{9,1... | collective-permute-start | bytes 786440 | tf_op jit(solution)/shard_map/ppermute | solution.py:35
  59.9 48.4 %collective-permute-start.5 = (bf16[128,2048]{1,0:T(8,128)(2,1)S(1)}, bf16[128,2048]{1,0:T(8,128)(2,1)S(1)}, u32[]{:S(2)}, u32[]{:S(2)}) collective-permute-start(bf16[128,2048]{1,0:T(8,128)(2,1)S(1)} %copy-done.14), channel_id=1, source_target_pairs={{0,4},{4,0},{1,5},{5,1},{2,6},{6,2},{3,7},{7,3},{8,12},{12,8},{9,1... | collective-permute-start | bytes 1572872 | tf_op jit(solution)/shard_map/ppermute | solution.py:35
  63.4 46.2 %collective-permute-start.7 = (bf16[128,2048]{1,0:T(8,128)(2,1)S(1)}, bf16[128,2048]{1,0:T(8,128)(2,1)S(1)}, u32[]{:S(2)}, u32[]{:S(2)}) collective-permute-start(bf16[128,2048]{1,0:T(8,128)(2,1)S(1)} %copy-done.14), channel_id=1, source_target_pairs={{0,2},{2,0},{1,3},{3,1},{4,6},{6,4},{5,7},{7,5},{8,10},{10,8},{9,1... | collective-permute-start | bytes 1572872 | tf_op jit(solution)/shard_map/ppermute | solution.py:35
  91.2 30.3 %collective-permute-start.107 = (bf16[128,2048]{1,0:T(8,128)(2,1)S(1)}, bf16[128,2048]{1,0:T(8,128)(2,1)S(1)}, u32[]{:S(2)}, u32[]{:S(2)}) collective-permute-start(bf16[128,2048]{1,0:T(8,128)(2,1)S(1)} %copy-done.46), channel_id=1, source_target_pairs={{0,4},{4,0},{1,5},{5,1},{2,6},{6,2},{3,7},{7,3},{8,12},{12,8},{9,1... | collective-permute-start | bytes 1572872 | tf_op jit(solution)/shard_map/ppermute | solution.py:35
  135.1 28.7 %collective-permute-start.54 = (bf16[256,512]{1,0:T(8,128)(2,1)}, bf16[256,512]{1,0:T(8,128)(2,1)S(1)}, u32[]{:S(2)}, u32[]{:S(2)}) collective-permute-start(bf16[256,512]{1,0:T(8,128)(2,1)} %collective-permute-done.48), channel_id=1, source_target_pairs={{24,16},{16,8},{8,0},{25,17},{17,9},{9,1},{26,18},{18,10},{10,2},{... | collective-permute-start | bytes 786440 | tf_op jit(solution)/shard_map/ppermute | solution.py:48
  157.6 42.6 %collective-permute-start.29 = (bf16[256,896]{1,0:T(8,128)(2,1)S(1)}, bf16[256,896]{1,0:T(8,128)(2,1)}, u32[]{:S(2)}, u32[]{:S(2)}) collective-permute-start(bf16[256,896]{1,0:T(8,128)(2,1)S(1)} %bitcast.732), channel_id=1, source_target_pairs={{0,8},{8,16},{16,24},{1,9},{9,17},{17,25},{2,10},{10,18},{18,26},{... | collective-permute-start | bytes 1376264 | tf_op jit(solution)/shard_map/ppermute | solution.py:44
  192.2 197.5 %collective-permute-start.77 = (bf16[256,1024]{1,0:T(8,128)(2,1)}, bf16[256,1024]{1,0:T(8,128)(2,1)}, u32[]{:S(2)}, u32[]{:S(2)}) collective-permute-start(bf16[256,1024]{1,0:T(8,128)(2,1)} %bitcast.114), channel_id=1, source_target_pairs={{24,16},{16,8},{8,0},{25,17},{17,9},{9,1},{26,18},{18,10},{10,2},{... | collective-permute-start | bytes 1572872 | tf_op jit(solution)/shard_map/ppermute | solution.py:48
  198.1 28.8 %collective-permute-start.34 = (bf16[256,896]{1,0:T(8,128)(2,1)S(1)}, bf16[256,896]{1,0:T(8,128)(2,1)S(1)}, u32[]{:S(2)}, u32[]{:S(2)}) collective-permute-start(bf16[256,896]{1,0:T(8,128)(2,1)S(1)} %collective-permute-done.28), channel_id=1, source_target_pairs={{24,16},{16,8},{8,0},{25,17},{17,9},{9,1},{26,18},{18,10},{10,2},{... | collective-permute-start | bytes 1376264 | tf_op jit(solution)/shard_map/ppermute | solution.py:48
  200.2 29.0 %collective-permute-start.24 = (bf16[2,64,1152]{2,1,0:T(8,128)(2,1)S(1)}, bf16[2,64,1152]{2,1,0:T(8,128)(2,1)S(1)}, u32[]{:S(2)}, u32[]{:S(2)}) collective-permute-start(bf16[2,64,1152]{2,1,0:T(8,128)(2,1)S(1)} %slice.502), channel_id=1, source_target_pairs={{0,2},{2,0},{1,3},{3,1},{4,6},{6,4},{5,7},{7,5},{8,10},{10,8},{9,1... | collective-permute-start | bytes 884744 | tf_op jit(solution)/shard_map/ppermute | solution.py:35
  260.6 130.0 %collective-permute-start.76 = (bf16[256,1024]{1,0:T(8,128)(2,1)}, bf16[256,1024]{1,0:T(8,128)(2,1)}, u32[]{:S(2)}, u32[]{:S(2)}) collective-permute-start(bf16[256,1024]{1,0:T(8,128)(2,1)} %bitcast.114), channel_id=1, source_target_pairs={{0,8},{8,16},{16,24},{1,9},{9,17},{17,25},{2,10},{10,18},{18,26},{... | collective-permute-start | bytes 1572872 | tf_op jit(solution)/shard_map/ppermute | solution.py:44
  273.4 67.8 %collective-permute-start.59 = (bf16[256,512]{1,0:T(8,128)(2,1)}, bf16[256,512]{1,0:T(8,128)(2,1)}, u32[]{:S(2)}, u32[]{:S(2)}) collective-permute-start(bf16[256,512]{1,0:T(8,128)(2,1)} %collective-permute-done.57), channel_id=1, source_target_pairs={{16,24},{17,25},{18,26},{19,27},{20,28},{21,29},{22,30},{23,31}} | collective-permute-start | bytes 786440 | tf_op jit(solution)/shard_map/ppermute | solution.py:44
  274.8 80.1 %collective-permute-start.60 = (bf16[256,512]{1,0:T(8,128)(2,1)}, bf16[256,512]{1,0:T(8,128)(2,1)}, u32[]{:S(2)}, u32[]{:S(2)}) collective-permute-start(bf16[256,512]{1,0:T(8,128)(2,1)} %collective-permute-done.58), channel_id=1, source_target_pairs={{16,24},{17,25},{18,26},{19,27},{20,28},{21,29},{22,30},{23,31}} | collective-permute-start | bytes 786440 | tf_op jit(solution)/shard_map/ppermute | solution.py:44
  340.2 33.9 %collective-permute-start.44 = (bf16[4,512,256]{2,1,0:T(8,128)(2,1)S(1)}, bf16[4,512,256]{2,1,0:T(8,128)(2,1)S(1)}, u32[]{:S(2)}, u32[]{:S(2)}) collective-permute-start(bf16[4,512,256]{2,1,0:T(8,128)(2,1)S(1)} %bitcast_dynamic-update-slice_fusion.64), channel_id=1, source_target_pairs={{0,1},{1,0},{2,3},{3,2},{4,5},{5,4},{6,7},{7,6},{8,9},{9,8},{10,11... | collective-permute-start | bytes 3145736 | tf_op jit(solution)/shard_map/ppermute | solution.py:35
  364.0 28.2 %collective-permute-start.93 = (bf16[256,512]{1,0:T(8,128)(2,1)}, bf16[256,512]{1,0:T(8,128)(2,1)S(1)}, u32[]{:S(2)}, u32[]{:S(2)}) collective-permute-start(bf16[256,512]{1,0:T(8,128)(2,1)} %copy-done.84), channel_id=1, source_target_pairs={{0,8},{8,16},{16,24},{1,9},{9,17},{17,25},{2,10},{10,18},{18,26},{... | collective-permute-start | bytes 786440 | tf_op jit(solution)/shard_map/ppermute | solution.py:44
  374.0 27.3 %collective-permute-start.110 = (bf16[128,2048]{1,0:T(8,128)(2,1)S(1)}, bf16[128,2048]{1,0:T(8,128)(2,1)S(1)}, u32[]{:S(2)}, u32[]{:S(2)}) collective-permute-start(bf16[128,2048]{1,0:T(8,128)(2,1)S(1)} %copy-done.56), channel_id=1, source_target_pairs={{0,1},{1,0},{2,3},{3,2},{4,5},{5,4},{6,7},{7,6},{8,9},{9,8},{10,11... | collective-permute-start | bytes 1572872 | tf_op jit(solution)/shard_map/ppermute | solution.py:35
  394.3 40.2 %collective-permute-start.81 = (bf16[256,1024]{1,0:T(8,128)(2,1)S(1)}, bf16[256,1024]{1,0:T(8,128)(2,1)S(1)}, u32[]{:S(2)}, u32[]{:S(2)}) collective-permute-start(bf16[256,1024]{1,0:T(8,128)(2,1)S(1)} %copy-done.67), channel_id=1, source_target_pairs={{24,16},{16,8},{8,0},{25,17},{17,9},{9,1},{26,18},{18,10},{10,2},{... | collective-permute-start | bytes 1572872 | tf_op jit(solution)/shard_map/ppermute | solution.py:48
  399.3 35.2 %collective-permute-start.78 = (bf16[256,1024]{1,0:T(8,128)(2,1)}, bf16[256,1024]{1,0:T(8,128)(2,1)S(1)}, u32[]{:S(2)}, u32[]{:S(2)}) collective-permute-start(bf16[256,1024]{1,0:T(8,128)(2,1)} %collective-permute-done.77), channel_id=1, source_target_pairs={{16,8},{8,0},{17,9},{9,1},{18,10},{10,2},{19,11},{11,3},{20,12},{1... | collective-permute-start | bytes 1572872 | tf_op jit(solution)/shard_map/ppermute | solution.py:48
  413.3 56.3 %collective-permute-start.61 = (bf16[4,128,2048]{2,1,0:T(8,128)(2,1)S(1)}, bf16[4,128,2048]{2,1,0:T(8,128)(2,1)S(1)}, u32[]{:S(2)}, u32[]{:S(2)}) collective-permute-start(bf16[4,128,2048]{2,1,0:T(8,128)(2,1)S(1)} %dynamic-slice_bitcast_fusion.3), channel_id=1, source_target_pairs={{0,1},{1,0},{2,3},{3,2},{4,5},{5,4},{6,7},{7,6},{8,9},{9,8},{10,11... | collective-permute-start | bytes 6291464 | tf_op jit(solution)/shard_map/ppermute | solution.py:35
  435.9 33.5 %collective-permute-start.79 = (bf16[256,1024]{1,0:T(8,128)(2,1)S(1)}, bf16[256,1024]{1,0:T(8,128)(2,1)S(1)}, u32[]{:S(2)}, u32[]{:S(2)}) collective-permute-start(bf16[256,1024]{1,0:T(8,128)(2,1)S(1)} %collective-permute-done.78), channel_id=1, source_target_pairs={{8,0},{9,1},{10,2},{11,3},{12,4},{13,5},{14,6},{15,7}} | collective-permute-start | bytes 1572872 | tf_op jit(solution)/shard_map/ppermute | solution.py:48
  437.2 30.2 %collective-permute-start.82 = (bf16[256,1024]{1,0:T(8,128)(2,1)S(1)}, bf16[256,1024]{1,0:T(8,128)(2,1)S(1)}, u32[]{:S(2)}, u32[]{:S(2)}) collective-permute-start(bf16[256,1024]{1,0:T(8,128)(2,1)S(1)} %collective-permute-done.81), channel_id=1, source_target_pairs={{16,8},{8,0},{17,9},{9,1},{18,10},{10,2},{19,11},{11,3},{20,12},{1... | collective-permute-start | bytes 1572872 | tf_op jit(solution)/shard_map/ppermute | solution.py:48
  438.5 30.1 %collective-permute-start.85 = (bf16[256,1024]{1,0:T(8,128)(2,1)S(1)}, bf16[256,1024]{1,0:T(8,128)(2,1)S(1)}, u32[]{:S(2)}, u32[]{:S(2)}) collective-permute-start(bf16[256,1024]{1,0:T(8,128)(2,1)S(1)} %collective-permute-done.80), channel_id=1, source_target_pairs={{8,16},{16,24},{9,17},{17,25},{10,18},{18,26},{11,19},{19,27},{12,... | collective-permute-start | bytes 1572872 | tf_op jit(solution)/shard_map/ppermute | solution.py:44
  439.4 54.2 %collective-permute-start.86 = (bf16[256,1024]{1,0:T(8,128)(2,1)S(1)}, bf16[256,1024]{1,0:T(8,128)(2,1)S(1)}, u32[]{:S(2)}, u32[]{:S(2)}) collective-permute-start(bf16[256,1024]{1,0:T(8,128)(2,1)S(1)} %collective-permute-done.84), channel_id=1, source_target_pairs={{16,24},{17,25},{18,26},{19,27},{20,28},{21,29},{22,30},{23,31}} | collective-permute-start | bytes 1572872 | tf_op jit(solution)/shard_map/ppermute | solution.py:44
  549.7 86.9 %collective-permute-start.101 = (bf16[4,128,2048]{2,1,0:T(8,128)(2,1)}, bf16[4,128,2048]{2,1,0:T(8,128)(2,1)}, u32[]{:S(2)}, u32[]{:S(2)}) collective-permute-start(bf16[4,128,2048]{2,1,0:T(8,128)(2,1)} %dynamic-slice_bitcast_fusion.2), channel_id=1, source_target_pairs={{0,1},{1,0},{2,3},{3,2},{4,5},{5,4},{6,7},{7,6},{8,9},{9,8},{10,11... | collective-permute-start | bytes 6291464 | tf_op jit(solution)/shard_map/ppermute | solution.py:35
  550.7 31.0 %collective-permute-start.202 = (bf16[256,512]{1,0:T(8,128)(2,1)S(1)}, bf16[256,512]{1,0:T(8,128)(2,1)S(1)}, u32[]{:S(2)}, u32[]{:S(2)}) collective-permute-start(bf16[256,512]{1,0:T(8,128)(2,1)S(1)} %get-tuple-element.110), channel_id=1, source_target_pairs={{0,8},{8,16},{1,9},{9,17},{2,10},{10,18},{3,11},{11,19},{4,12},{12... | collective-permute-start | bytes 786440 | tf_op jit(solution)/shard_map/ppermute | solution.py:69
  565.6 32.8 %collective-permute-start.191 = (bf16[256,1024]{1,0:T(8,128)(2,1)S(1)}, bf16[256,1024]{1,0:T(8,128)(2,1)S(1)}, u32[]{:S(2)}, u32[]{:S(2)}) collective-permute-start(bf16[256,1024]{1,0:T(8,128)(2,1)S(1)} %get-tuple-element.77), channel_id=1, source_target_pairs={{24,16},{25,17},{26,18},{27,19},{28,20},{29,21},{30,22},{31,23}} | collective-permute-start | bytes 1572872 | tf_op jit(solution)/shard_map/ppermute | solution.py:72
  566.4 33.3 %collective-permute-start.194 = (bf16[256,1024]{1,0:T(8,128)(2,1)S(1)}, bf16[256,1024]{1,0:T(8,128)(2,1)S(1)}, u32[]{:S(2)}, u32[]{:S(2)}) collective-permute-start(bf16[256,1024]{1,0:T(8,128)(2,1)S(1)} %get-tuple-element.76), channel_id=1, source_target_pairs={{0,8},{1,9},{2,10},{3,11},{4,12},{5,13},{6,14},{7,15}} | collective-permute-start | bytes 1572872 | tf_op jit(solution)/shard_map/ppermute | solution.py:69
  597.6 42.7 %collective-permute-start.115 = (bf16[4,128,2048]{2,1,0:T(8,128)(2,1)}, bf16[4,128,2048]{2,1,0:T(8,128)(2,1)}, u32[]{:S(2)}, u32[]{:S(2)}) collective-permute-start(bf16[4,128,2048]{2,1,0:T(8,128)(2,1)} %dynamic-slice_bitcast_fusion.1), channel_id=1, source_target_pairs={{0,1},{1,0},{2,3},{3,2},{4,5},{5,4},{6,7},{7,6},{8,9},{9,8},{10,11... | collective-permute-start | bytes 6291464 | tf_op jit(solution)/shard_map/ppermute | solution.py:35
  622.6 36.5 %collective-permute-start.200 = (bf16[256,512]{1,0:T(8,128)(2,1)}, bf16[256,512]{1,0:T(8,128)(2,1)S(1)}, u32[]{:S(2)}, u32[]{:S(2)}) collective-permute-start(bf16[256,512]{1,0:T(8,128)(2,1)} %get-tuple-element.107), channel_id=1, source_target_pairs={{24,16},{16,8},{8,0},{25,17},{17,9},{9,1},{26,18},{18,10},{10,2},{... | collective-permute-start | bytes 786440 | tf_op jit(solution)/shard_map/ppermute | solution.py:72
  623.9 36.3 %collective-permute-start.203 = (bf16[256,512]{1,0:T(8,128)(2,1)}, bf16[256,512]{1,0:T(8,128)(2,1)S(1)}, u32[]{:S(2)}, u32[]{:S(2)}) collective-permute-start(bf16[256,512]{1,0:T(8,128)(2,1)} %get-tuple-element.115), channel_id=1, source_target_pairs={{0,8},{8,16},{16,24},{1,9},{9,17},{17,25},{2,10},{10,18},{18,26},{... | collective-permute-start | bytes 786440 | tf_op jit(solution)/shard_map/ppermute | solution.py:69
  633.8 27.5 %collective-permute-start.210 = (bf16[256,512]{1,0:T(8,128)(2,1)S(1)}, bf16[256,512]{1,0:T(8,128)(2,1)S(1)}, u32[]{:S(2)}, u32[]{:S(2)}) collective-permute-start(bf16[256,512]{1,0:T(8,128)(2,1)S(1)} %fusion.60), channel_id=1, source_target_pairs={{0,4},{4,0},{1,5},{5,1},{2,6},{6,2},{3,7},{7,3},{8,12},{12,8},{9,1... | collective-permute-start | bytes 786440 | tf_op jit(solution)/shard_map/ppermute | solution.py:35
  734.6 29.9 %collective-permute-start.172 = (bf16[256,512]{1,0:T(8,128)(2,1)S(1)}, bf16[256,512]{1,0:T(8,128)(2,1)S(1)}, u32[]{:S(2)}, u32[]{:S(2)}) collective-permute-start(bf16[256,512]{1,0:T(8,128)(2,1)S(1)} %get-tuple-element.122), channel_id=1, source_target_pairs={{24,16},{25,17},{26,18},{27,19},{28,20},{29,21},{30,22},{31,23}} | collective-permute-start | bytes 786440 | tf_op jit(solution)/shard_map/ppermute | solution.py:72
  735.3 46.3 %collective-permute-start.175 = (bf16[256,512]{1,0:T(8,128)(2,1)S(1)}, bf16[256,512]{1,0:T(8,128)(2,1)S(1)}, u32[]{:S(2)}, u32[]{:S(2)}) collective-permute-start(bf16[256,512]{1,0:T(8,128)(2,1)S(1)} %get-tuple-element.125), channel_id=1, source_target_pairs={{0,8},{1,9},{2,10},{3,11},{4,12},{5,13},{6,14},{7,15}} | collective-permute-start | bytes 786440 | tf_op jit(solution)/shard_map/ppermute | solution.py:69
  740.1 42.8 %collective-permute-start.178 = (bf16[256,512]{1,0:T(8,128)(2,1)S(1)}, bf16[256,512]{1,0:T(8,128)(2,1)S(1)}, u32[]{:S(2)}, u32[]{:S(2)}) collective-permute-start(bf16[256,512]{1,0:T(8,128)(2,1)S(1)} %get-tuple-element.124), channel_id=1, source_target_pairs={{24,16},{25,17},{26,18},{27,19},{28,20},{29,21},{30,22},{31,23}} | collective-permute-start | bytes 786440 | tf_op jit(solution)/shard_map/ppermute | solution.py:72
  740.8 42.1 %collective-permute-start.181 = (bf16[256,512]{1,0:T(8,128)(2,1)S(1)}, bf16[256,512]{1,0:T(8,128)(2,1)S(1)}, u32[]{:S(2)}, u32[]{:S(2)}) collective-permute-start(bf16[256,512]{1,0:T(8,128)(2,1)S(1)} %get-tuple-element.123), channel_id=1, source_target_pairs={{0,8},{1,9},{2,10},{3,11},{4,12},{5,13},{6,14},{7,15}} | collective-permute-start | bytes 786440 | tf_op jit(solution)/shard_map/ppermute | solution.py:69
  764.3 66.6 %collective-permute-start.132 = (bf16[4,512,256]{2,1,0:T(8,128)(2,1)}, bf16[4,512,256]{2,1,0:T(8,128)(2,1)}, u32[]{:S(2)}, u32[]{:S(2)}) collective-permute-start(bf16[4,512,256]{2,1,0:T(8,128)(2,1)} %dynamic-slice_bitcast_fusion.4), channel_id=1, source_target_pairs={{0,1},{1,0},{2,3},{3,2},{4,5},{5,4},{6,7},{7,6},{8,9},{9,8},{10,11... | collective-permute-start | bytes 3145736 | tf_op jit(solution)/shard_map/ppermute | solution.py:35
  783.9 66.7 %collective-permute-start.176 = (bf16[256,512]{1,0:T(8,128)(2,1)}, bf16[256,512]{1,0:T(8,128)(2,1)}, u32[]{:S(2)}, u32[]{:S(2)}) collective-permute-start(bf16[256,512]{1,0:T(8,128)(2,1)} %get-tuple-element.121), channel_id=1, source_target_pairs={{0,8},{8,16},{1,9},{9,17},{2,10},{10,18},{3,11},{11,19},{4,12},{12... | collective-permute-start | bytes 786440 | tf_op jit(solution)/shard_map/ppermute | solution.py:69
  796.7 53.8 %collective-permute-start.179 = (bf16[256,512]{1,0:T(8,128)(2,1)S(1)}, bf16[256,512]{1,0:T(8,128)(2,1)}, u32[]{:S(2)}, u32[]{:S(2)}) collective-permute-start(bf16[256,512]{1,0:T(8,128)(2,1)S(1)} %get-tuple-element.120), channel_id=1, source_target_pairs={{24,16},{16,8},{25,17},{17,9},{26,18},{18,10},{27,19},{19,11},{28,... | collective-permute-start | bytes 786440 | tf_op jit(solution)/shard_map/ppermute | solution.py:72
  889.7 27.8 %collective-permute-start.152 = (bf16[256,896]{1,0:T(8,128)(2,1)}, bf16[256,896]{1,0:T(8,128)(2,1)}, u32[]{:S(2)}, u32[]{:S(2)}) collective-permute-start(bf16[256,896]{1,0:T(8,128)(2,1)} %get-tuple-element.86), channel_id=1, source_target_pairs={{24,16},{25,17},{26,18},{27,19},{28,20},{29,21},{30,22},{31,23}} | collective-permute-start | bytes 1376264 | tf_op jit(solution)/shard_map/ppermute | solution.py:72
  891.2 47.1 %collective-permute-start.155 = (bf16[256,896]{1,0:T(8,128)(2,1)}, bf16[256,896]{1,0:T(8,128)(2,1)}, u32[]{:S(2)}, u32[]{:S(2)}) collective-permute-start(bf16[256,896]{1,0:T(8,128)(2,1)} %get-tuple-element.89), channel_id=1, source_target_pairs={{0,8},{1,9},{2,10},{3,11},{4,12},{5,13},{6,14},{7,15}} | collective-permute-start | bytes 1376264 | tf_op jit(solution)/shard_map/ppermute | solution.py:69
  896.2 43.6 %collective-permute-start.158 = (bf16[256,896]{1,0:T(8,128)(2,1)}, bf16[256,896]{1,0:T(8,128)(2,1)}, u32[]{:S(2)}, u32[]{:S(2)}) collective-permute-start(bf16[256,896]{1,0:T(8,128)(2,1)} %get-tuple-element.88), channel_id=1, source_target_pairs={{24,16},{25,17},{26,18},{27,19},{28,20},{29,21},{30,22},{31,23}} | collective-permute-start | bytes 1376264 | tf_op jit(solution)/shard_map/ppermute | solution.py:72
  897.6 46.9 %collective-permute-start.161 = (bf16[256,896]{1,0:T(8,128)(2,1)}, bf16[256,896]{1,0:T(8,128)(2,1)}, u32[]{:S(2)}, u32[]{:S(2)}) collective-permute-start(bf16[256,896]{1,0:T(8,128)(2,1)} %get-tuple-element.87), channel_id=1, source_target_pairs={{0,8},{1,9},{2,10},{3,11},{4,12},{5,13},{6,14},{7,15}} | collective-permute-start | bytes 1376264 | tf_op jit(solution)/shard_map/ppermute | solution.py:69
  916.6 76.3 %collective-permute-start.136 = (bf16[4,128,2048]{2,1,0:T(8,128)(2,1)}, bf16[4,128,2048]{2,1,0:T(8,128)(2,1)}, u32[]{:S(2)}, u32[]{:S(2)}) collective-permute-start(bf16[4,128,2048]{2,1,0:T(8,128)(2,1)} %dynamic-slice_bitcast_fusion), channel_id=1, source_target_pairs={{0,1},{1,0},{2,3},{3,2},{4,5},{5,4},{6,7},{7,6},{8,9},{9,8},{10,11... | collective-permute-start | bytes 6291464 | tf_op jit(solution)/shard_map/ppermute | solution.py:35
  944.6 52.9 %collective-permute-start.141 = (bf16[4,4,64,1152]{3,2,0,1:T(8,128)(2,1)}, bf16[4,4,64,1152]{3,2,0,1:T(8,128)(2,1)}, u32[]{:S(2)}, u32[]{:S(2)}) collective-permute-start(bf16[4,4,64,1152]{3,2,0,1:T(8,128)(2,1)} %bitcast.657), channel_id=1, source_target_pairs={{0,1},{1,0},{2,3},{3,2},{4,5},{5,4},{6,7},{7,6},{8,9},{9,8},{10,11... | collective-permute-start | bytes 7077896 | tf_op jit(solution)/shard_map/ppermute | solution.py:35
  995.7 29.2 %collective-permute-start.137 = (bf16[64,2048]{1,0:T(8,128)(2,1)}, bf16[64,2048]{1,0:T(8,128)(2,1)}, u32[]{:S(2)}, u32[]{:S(2)}) collective-permute-start(bf16[64,2048]{1,0:T(8,128)(2,1)} %get-tuple-element.130), channel_id=1, source_target_pairs={{0,2},{2,0},{1,3},{3,1},{4,6},{6,4},{5,7},{7,5},{8,10},{10,8},{9,1... | collective-permute-start | bytes 786440 | tf_op jit(solution)/shard_map/ppermute | solution.py:35
  997.5 27.4 %collective-permute-start.139 = (bf16[64,2048]{1,0:T(8,128)(2,1)}, bf16[64,2048]{1,0:T(8,128)(2,1)}, u32[]{:S(2)}, u32[]{:S(2)}) collective-permute-start(bf16[64,2048]{1,0:T(8,128)(2,1)} %get-tuple-element.132), channel_id=1, source_target_pairs={{0,4},{4,0},{1,5},{5,1},{2,6},{6,2},{3,7},{7,3},{8,12},{12,8},{9,1... | collective-permute-start | bytes 786440 | tf_op jit(solution)/shard_map/ppermute | solution.py:35
  (284 other events, 4307.9 us)

commit v2 on v1

--- a/solution.py
+++ b/solution.py
@@ -35,43 +35,53 @@
     return lax.ppermute(a, axis, SWAP)
 
 
-def line_gather(pieces, put, out, up_only=False):
-    count = lax.axis_size("z")
-    place = lax.axis_index("z")
-    ups, downs = [list(pieces)], [list(pieces)]
-    for step in range(1, count):
-        ups.append(
-            [lax.ppermute(a, "z", [(i, i + 1) for i in range(step - 1, count - 1)]) for a in ups[-1]]
-        )
-        if not up_only:
-            downs.append(
-                [lax.ppermute(a, "z", [(i, i - 1) for i in range(count - step, 0, -1)]) for a in downs[-1]]
-            )
-    for number, piece in enumerate(pieces):
-        out = put(out, place, number, piece)
-    for step in range(1, count):
-        for number in range(len(pieces)):
-            value = ups[step][number]
-            if not up_only:
-                value = jnp.where(place >= step, value, downs[count - step][number])
-            out = put(out, (place - step + count) % count, number, value)
-    return out
-
-
-def line_scatter(take, down_only=False):
-    count = lax.axis_size("z")
-    place = lax.axis_index("z")
-    up = down = None
-    for step in range(1, count):
-        if not down_only:
-            give = take(jnp.clip(count - step + place, 0, count - 1))
-            give = give if up is None else give + up
-            up = lax.ppermute(give, "z", [(i, i + 1) for i in range(step)])
-        give = take(jnp.clip(place - (count - step), 0, count - 1))
-        give = give if down is None else give + down
-        down = lax.ppermute(give, "z", [(i, i - 1) for i in range(count - 1, count - 1 - step, -1)])
-    total = take(place).astype(F32) + down.astype(F32)
-    return total if down_only else total + up.astype(F32)
+class Order:
+    def __init__(self):
+        self.done = ()
+
+    def begin(self, *values):
+        out = lax.optimization_barrier(tuple(values) + self.done)
+        return out[0] if len(values) == 1 else out[: len(values)]
+
+    def finish(self, *values):
+        self.done = tuple(values)
+
+
+def after(value, *earlier):
+    return lax.optimization_barrier((value,) + earlier)[0]
+
+
+def up_pairs(step):
+    return [(i, i + 1) for i in range(step - 1, lax.axis_size("z") - 1)]
+
+
+def down_pairs(step):
+    return [(i, i - 1) for i in range(lax.axis_size("z") - step, 0, -1)]
+
+
+class Line:
+    def __init__(self, piece, both=True):
+        self.ups, self.downs, self.both = [piece], [piece], both
+
+    def moving(self):
+        return (self.ups[-1], self.downs[-1]) if self.both else (self.ups[-1],)
+
+    def step(self, moving):
+        number = len(self.ups)
+        self.ups.append(lax.ppermute(moving[0], "z", up_pairs(number)))
+        if self.both:
+            self.downs.append(lax.ppermute(moving[1], "z", down_pairs(number)))
+
+    def place(self, out, put):
+        count = lax.axis_size("z")
+        here = lax.axis_index("z")
+        out = put(out, here, self.ups[0])
+        for step in range(1, count):
+            value = self.ups[step]
+            if self.both:
+                value = jnp.where(here >= step, value, self.downs[count - step])
+            out = put(out, (here - step + count) % count, value)
+        return out
 
 
 def spots(dx, dy, dc):
@@ -79,73 +89,185 @@
     return ((x ^ dx) * 2 + (y ^ dy)) * 2 + (c ^ dc)
 
 
-def cube_gather(a, axis):
-    half = a.shape[0] // 2
-    by_x, by_y = swap(a, "x"), swap(a, "y")
-    far_low = swap(by_x[:half], "y")
-    far_high = swap(by_y[half:], "x")
-    far = jnp.concatenate([far_low, far_high], 0)
-    out = jnp.zeros(a.shape[:axis] + (8,) + a.shape[axis:], a.dtype)
-    other_far = jnp.concatenate([swap(far_low, "c"), swap(far_high, "c")], 0)
-    for (dx, dy), near, other in (
-        ((0, 0), a, swap(a, "c")),
-        ((1, 0), by_x, swap(by_x, "c")),
-        ((0, 1), by_y, swap(by_y, "c")),
-        ((1, 1), far, other_far),
-    ):
-        out = lax.dynamic_update_index_in_dim(out, near, spots(dx, dy, 0), axis)
-        out = lax.dynamic_update_index_in_dim(out, other, spots(dx, dy, 1), axis)
-    return out
-
-
-def cube_scatter(terms, axis):
+def cube_gather(piece):
+    half = piece.shape[0] // 2
+    by_x, by_y = swap(piece, "x"), swap(piece, "y")
+    low, high = swap(by_x[:half], "y"), swap(by_y[half:], "x")
+    own = jnp.concatenate([piece, by_y, by_x, low, high], axis=0)
+    return own, swap(own, "c")
+
+
+def cube_scatter(mine, other):
+    mine = mine + swap(other, "c")
+    here, to_y, to_x, far = mine[0], mine[1], mine[2], mine[3]
+    half = far.shape[0] // 2
+    from_x, from_y = swap(far[:half], "x"), swap(far[half:], "y")
+    x_low, y_high = swap(to_x[:half], "x"), swap(to_y[half:], "y")
+    x_high = swap(to_x[half:] + from_y, "x")
+    y_low = swap(to_y[:half] + from_x, "y")
+    by_x = jnp.concatenate([x_low, x_high], 0).astype(F32)
+    by_y = jnp.concatenate([y_low, y_high], 0).astype(F32)
+    return here.astype(F32) + by_x + by_y
+
+
+def place_ref():
     x, y, c = (lax.axis_index(name) for name in "xyc")
-    pairs = terms.reshape(terms.shape[:axis] + (4, 2) + terms.shape[axis + 1 :])
-    mine = lax.dynamic_index_in_dim(pairs, c, axis + 1, False)
-    mine = mine + swap(lax.dynamic_index_in_dim(pairs, c ^ 1, axis + 1, False), "c")
-
-    def share(dx, dy):
-        return lax.dynamic_index_in_dim(mine, (x ^ dx) * 2 + (y ^ dy), axis, False)
-
-    far, to_x, to_y = share(1, 1), share(1, 0), share(0, 1)
-    half = far.shape[0] // 2
-    from_x = swap(far[:half], "x")
-    from_y = swap(far[half:], "y")
-    to_x = jnp.concatenate([to_x[:half], to_x[half:] + from_y], 0)
-    to_y = jnp.concatenate([to_y[:half] + from_x, to_y[half:]], 0)
-    return share(0, 0).astype(F32) + swap(to_x, "x").astype(F32) + swap(to_y, "y").astype(F32)
-
-
-def weight_gather(pack, after=None):
-    if after is not None:
-        pack, _ = lax.optimization_barrier((pack, after))
+    return jnp.stack([x * 2 + y, c]).astype(jnp.int32)
+
+
+def settle_kernel(place, own_ref, other_ref, out_ref):
+    near = (pl.program_id(0) & 1) == place[1]
+    out_ref[...] = jnp.where(near, own_ref[...], other_ref[...]).reshape(out_ref.shape)
+
+
+def settle(own, other, rows):
+    cols = own.shape[1]
+    spec = pl.BlockSpec((rows, cols), lambda i, place: ((i // 2) ^ place[0], 0))
+    return call(
+        settle_kernel,
+        shape((8 * rows, cols), own.dtype),
+        (8,),
+        [spec, spec],
+        pl.BlockSpec((rows, cols), lambda i, place: (i, 0)),
+        prefetch=1,
+    )(place_ref(), own, other)
+
+
+def settle_groups_kernel(place, own_ref, other_ref, main_ref, misc_ref):
+    near = (pl.program_id(0) & 1) == place[1]
+    values = jnp.where(near, own_ref[...], other_ref[...])
+    main = main_ref.shape[-1]
+    main_ref[:, 0] = values[:, :, :main]
+    misc_ref[:, 0] = values[:, :, main:]
+
+
+def settle_groups(own, other, groups, main):
+    rows, cols = own.shape[1:]
+    spec = pl.BlockSpec((groups, rows, cols), lambda i, place: ((i // 2) ^ place[0], 0, 0))
+    outs = call(
+        settle_groups_kernel,
+        tuple(shape((groups, 8, rows, n), own.dtype) for n in (main, cols - main)),
+        (8,),
+        [spec, spec],
+        tuple(
+            pl.BlockSpec((groups, 1, rows, n), lambda i, place: (0, i, 0, 0))
+            for n in (main, cols - main)
+        ),
+        prefetch=1,
+    )(place_ref(), own, other)
+    return tuple(out.reshape(groups * 8 * rows, -1) for out in outs)
+
+
+def settle_norm_kernel(place, own_ref, other_ref, gain_ref, out_ref):
+    near = (pl.program_id(0) & 1) == place[1]
+    values = jnp.where(near, own_ref[...], other_ref[...]).astype(F32)
+    scale = lax.rsqrt(jnp.mean(values * values, axis=1, keepdims=True) + EPS)
+    out_ref[...] = (values * scale * gain_ref[...]).astype(BF16)
+
+
+def settle_norm(own, other, gain, rows):
+    cols = own.shape[1]
+    spec = pl.BlockSpec((rows, cols), lambda i, place: ((i // 2) ^ place[0], 0))
+    return call(
+        settle_norm_kernel,
+        shape((8 * rows, cols), BF16),
+        (8,),
+        [spec, spec, pl.BlockSpec((1, cols), lambda i, place: (0, 0))],
+        pl.BlockSpec((rows, cols), lambda i, place: (i, 0)),
+        prefetch=1,
+    )(place_ref(), own, other, gain)
+
+
+def unsettle_kernel(place, in_ref, out_ref):
+    out_ref[...] = in_ref[...]
+
+
+def unsettle(values, rows):
+    cols = values.shape[1]
+
+    def source(i, place):
+        return (((i % 4) ^ place[0]) * 2 + ((i // 4) ^ place[1]), 0)
+
+    out = call(
+        unsettle_kernel,
+        shape(values.shape, values.dtype),
+        (8,),
+        [pl.BlockSpec((rows, cols), source)],
+        pl.BlockSpec((rows, cols), lambda i, place: (i, 0)),
+        prefetch=1,
+    )(place_ref(), values)
+    return out[: 4 * rows], out[4 * rows :]
+
+
+def assemble_kernel(
+    place, q_ref, x_ref, kv_ref, bc_ref, dt_ref, z_ref, all_ref, two_ref
+):
+    head = place[2]
+    zero = jnp.zeros((kv_ref.shape[0], HD), BF16)
+    parts = []
+    for part in (kv_ref[:, :HD], kv_ref[:, HD:]):
+        parts += [jnp.where(head == i, part, zero) for i in range(KVH)]
+    two = jnp.concatenate(parts + [bc_ref[...]], axis=1)
+    two_ref[...] = two
+    all_ref[...] = jnp.concatenate(
+        [q_ref[...], x_ref[...], two, dt_ref[...], z_ref[...]], axis=1
+    )
+
+
+def assemble(kv_head, rows, *parts):
+    total = parts[0].shape[0]
+
+    def source(i, place):
+        return (((i % 4) ^ place[0]) * 2 + ((i // 4) ^ place[1]), 0)
+
+    two = 2 * KVH * HD + parts[3].shape[1]
+    wide = sum(a.shape[1] for a in parts) - parts[2].shape[1] - parts[3].shape[1] + two
+    return call(
+        assemble_kernel,
+        (shape((total, wide), BF16), shape((total, two), BF16)),
+        (8,),
+        [pl.BlockSpec((rows, a.shape[1]), source) for a in parts],
+        (
+            pl.BlockSpec((rows, wide), lambda i, place: (i, 0)),
+            pl.BlockSpec((rows, two), source),
+        ),
+        prefetch=1,
+    )(jnp.concatenate([place_ref(), kv_head[None].astype(jnp.int32)]), *parts)
+
+
+def halves(pack):
     x = lax.axis_index("x")
     own = lax.dynamic_index_in_dim(pack, x, 0, False)
-    got = swap(lax.dynamic_index_in_dim(pack, x ^ 1, 0, False), "x")
-    rows, cols = own.shape
+    return own, lax.dynamic_index_in_dim(pack, x ^ 1, 0, False)
+
+
+def weight_gather(own, got):
+    x = lax.axis_index("x")
+    both = jnp.concatenate([jnp.where(x == 0, own, got), jnp.where(x == 0, got, own)], axis=0)
+    return lax.all_gather(both, "z", axis=0, tiled=True)
+
+
+def both_halves(own, got):
+    x = lax.axis_index("x")
+    return jnp.stack([jnp.where(x == 0, own, got), jnp.where(x == 0, got, own)], axis=1)
+
+
+def weight_scatter(grad):
+    x = lax.axis_index("x")
+    part = lax.psum_scatter(grad, "z", scatter_dimension=0, tiled=True)
+    part = part.reshape(2, -1, grad.shape[1])
+    got = swap(lax.dynamic_index_in_dim(part, x ^ 1, 0, False), "x")
+    return both_halves(lax.dynamic_index_in_dim(part, x, 0, False), got).astype(F32)
+
+
+def line_sum(value):
     count = lax.axis_size("z")
-
-    def put(out, group, number, value):
-        return lax.dynamic_update_slice(out, value[None, None], (group, x ^ number, 0, 0))
-
-    out = line_gather([own, got], put, jnp.zeros((count, 2, rows, cols), pack.dtype))
-    return out.reshape(count * 2 * rows, cols)
-
-
-def weight_scatter(grad):
-    count = lax.axis_size("z")
-    x = lax.axis_index("x")
-    blocks = grad.reshape(count, 2, -1, grad.shape[1])
-
-    def take(number):
-        return lambda group: lax.dynamic_slice(
-            blocks, (group, number, 0, 0), (1, 1) + blocks.shape[2:]
-        )[0, 0]
-
-    give = line_scatter(take(x ^ 1)).astype(BF16)
-    got = swap(give, "x").astype(F32)
-    own = line_scatter(take(x))
-    return jnp.stack([jnp.where(x == 0, own, got), jnp.where(x == 0, got, own)], axis=1)
+    ring = [(i, (i + 1) % count) for i in range(count)]
+    total, moving = value, value
+    for _ in range(count - 1):
+        moving = lax.ppermute(moving, "z", ring)
+        total = total + moving
+    return total
 
 
 def lanes_of(cols, heads):
@@ -175,13 +297,12 @@
     return 1.0 / (1.0 + jnp.exp(-v))
 
 
-def chunk_common(rest_ref, dt_row_ref, par_ref, par_col_ref, seg_col_ref, seg_row_ref, wide):
+def chunk_common(bc_ref, dt_in_ref, dt_row_ref, par_ref, par_col_ref, seg_col_ref, seg_row_ref, wide):
     heads = wide // MP
-    base = 2 * wide + HD
-    states = (rest_ref.shape[1] - base - 128) // 2
-    b_val = rest_ref[:, base : base + states]
-    c_val = rest_ref[:, base + states : base + 2 * states]
-    raw = rest_ref[:, base + 2 * states :].astype(F32) + par_ref[0:1, :]
+    states = bc_ref.shape[1] // 2
+    b_val = bc_ref[:, :states]
+    c_val = bc_ref[:, states:]
+    raw = dt_in_ref[...].astype(F32) + par_ref[0:1, :]
     dt = softplus(raw)
     rate = par_ref[1:2, :]
     raw_row = dt_row_ref[...].astype(F32) + par_col_ref[:, 0:1]
@@ -196,13 +317,13 @@
 
 
 def mamba_local_kernel(
-    rest_ref, dt_row_ref, par_ref, par_col_ref, skip_ref, seg_col_ref, seg_row_ref, marks_ref,
+    x_in_ref, bc_in_ref, dt_in_ref, dt_row_ref, par_ref, par_col_ref, skip_ref, seg_col_ref, seg_row_ref, marks_ref,
     y_ref, run_ref, held_ref, total_ref, starts_ref, state, base_run,
 ):
     step = pl.program_id(0)
     wide = skip_ref.shape[1]
     heads, b_val, c_val, raw, dt, rate, run, run_row, bias, _ = chunk_common(
-        rest_ref, dt_row_ref, par_ref, par_col_ref, seg_col_ref, seg_row_ref, wide
+        bc_in_ref, dt_in_ref, dt_row_ref, par_ref, par_col_ref, seg_col_ref, seg_row_ref, wide
     )
 
     @pl.when(step == 0)
@@ -210,7 +331,7 @@
         state[...] = jnp.zeros_like(state)
         base_run[...] = jnp.zeros_like(base_run)
 
-    x_val = rest_ref[:, wide : 2 * wide].astype(F32)
+    x_val = x_in_ref[...].astype(F32)
     seg = seg_col_ref[...]
     label = marks_ref[step]
     final = marks_ref[step + 1]
@@ -245,28 +366,31 @@
     total_ref[...] = jnp.exp(base_run[...])
 
 
-def mamba_close_kernel(rest_ref, y_ref, run_ref, seg_col_ref, held_ref, marks_ref, out_ref, full_ref):
+def mamba_close_kernel(bc_in_ref, gate_ref, y_ref, run_ref, seg_col_ref, held_ref, marks_ref, out_ref, full_ref):
     wide = y_ref.shape[1]
     heads = wide // MP
     states = held_ref.shape[0]
-    base = 2 * wide + HD + states
-    c_val = rest_ref[:, base : base + states]
+    c_val = bc_in_ref[:, states:]
     entry = jnp.where(seg_col_ref[...] == marks_ref[0], jnp.exp(run_ref[...]), 0.0)
     y_val = y_ref[...] + lanes_of(entry, heads) * mm(c_val, held_ref[...].astype(BF16), 1, 0)
     full_ref[...] = y_val
-    z_val = rest_ref[:, :wide].astype(F32)
+    z_val = gate_ref[...].astype(F32)
     out_ref[...] = (y_val * z_val * sigmoid(z_val)).astype(BF16)
 
 
-def mamba_grad_state_kernel(rest_ref, grad_ref, run_ref, seg_col_ref, marks_ref, out_ref):
+def mamba_grad_state_kernel(
+    bc_in_ref, gate_ref, y_ref, grad_ref, run_ref, seg_col_ref, marks_ref, out_ref, gate_grad_ref
+):
     wide = grad_ref.shape[1]
     heads = wide // MP
     states = out_ref.shape[0]
-    base = 2 * wide + HD + states
-    c_val = rest_ref[:, base : base + states]
-    z_val = rest_ref[:, :wide].astype(F32)
+    c_val = bc_in_ref[:, states:]
+    z_val = gate_ref[...].astype(F32)
     entry = jnp.where(seg_col_ref[...] == marks_ref[0], jnp.exp(run_ref[...]), 0.0)
-    grad_y = grad_ref[...].astype(F32) * z_val * sigmoid(z_val)
+    grad = grad_ref[...].astype(F32)
+    sig = sigmoid(z_val)
+    grad_y = grad * z_val * sig
+    gate_grad_ref[...] = (grad * y_ref[...] * (sig * (1.0 + z_val * (1.0 - sig)))).astype(BF16)
 
     @pl.when(pl.program_id(0) == 0)
     def _():
@@ -276,14 +400,14 @@
 
 
 def mamba_grad_kernel(
-    rest_ref, dt_row_ref, par_ref, par_col_ref, skip_ref, seg_col_ref, seg_row_ref, marks_ref,
-    y_ref, run_ref, starts_ref, held_ref, grad_ref, deep_ref,
-    zx_ref, bc_ref, dt_ref, sums_ref, skip_sum_ref, deep,
+    x_in_ref, bc_in_ref, dt_in_ref, dt_row_ref, par_ref, par_col_ref, skip_ref, seg_col_ref, seg_row_ref, marks_ref,
+    gate_ref, run_ref, starts_ref, held_ref, grad_ref, deep_ref,
+    x_ref, bc_ref, dt_ref, sums_ref, skip_sum_ref, deep,
 ):
     step = pl.num_programs(0) - 1 - pl.program_id(0)
     wide = skip_ref.shape[1]
     heads, b_val, c_val, raw, dt, rate, run, run_row, bias, lower = chunk_common(
-        rest_ref, dt_row_ref, par_ref, par_col_ref, seg_col_ref, seg_row_ref, wide
+        bc_in_ref, dt_in_ref, dt_row_ref, par_ref, par_col_ref, seg_col_ref, seg_row_ref, wide
     )
     states = b_val.shape[1]
 
@@ -293,8 +417,8 @@
         sums_ref[...] = jnp.zeros_like(sums_ref)
         skip_sum_ref[...] = jnp.zeros_like(skip_sum_ref)
 
-    z_val = rest_ref[:, :wide].astype(F32)
-    x_val = rest_ref[:, wide : 2 * wide].astype(F32)
+    z_val = gate_ref[...].astype(F32)
+    x_val = x_in_ref[...].astype(F32)
     seg = seg_col_ref[...]
     label = marks_ref[step]
     final = marks_ref[step + 1]
@@ -308,7 +432,6 @@
     grad = grad_ref[...].astype(F32)
     sig = sigmoid(z_val)
     grad_y = grad * z_val * sig
-    grad_z = grad * y_ref[...] * (sig * (1.0 + z_val * (1.0 - sig)))
     dt_wide = lanes_of(dt, heads)
     x_dt = x_val * dt_wide
     entry = lanes_of(jnp.where(seg == label, jnp.exp(run), 0.0), heads)
@@ -357,8 +480,7 @@
     grad_c = grad_c + mm(gram_grad_b, b_val, 1, 0)
     grad_b = grad_b + mm(gram_grad_b, c_val, 0, 0)
     x_dt_grad = jnp.concatenate(parts, axis=1) + tail * back
-    zx_ref[:, :wide] = grad_z.astype(BF16)
-    zx_ref[:, wide:] = (x_dt_grad * dt_wide + skip_ref[...] * grad_y).astype(BF16)
+    x_ref[...] = (x_dt_grad * dt_wide + skip_ref[...] * grad_y).astype(BF16)
     bc_ref[:, :states] = grad_b.astype(BF16)
     bc_ref[:, states:] = grad_c.astype(BF16)
     col_grad = jnp.concatenate(cols + [jnp.zeros((128 - heads, CHUNK), F32)], axis=0)
@@ -466,6 +588,7 @@
             vmem_limit_bytes=VMEM_BYTES, dimension_semantics=("arbitrary",) * len(grid)
         ),
         cost_estimate=cost,
+        name=kernel.__name__,
     )
 
 
@@ -520,13 +643,9 @@
     inner = q_w.shape[1] // 2
     steps = group // CHUNK
 
-    pack_one = jnp.concatenate(
-        [
-            q_w.reshape(rows_w, 2, inner).transpose(1, 0, 2),
-            zx_w.reshape(rows_w, 2, 2, wide).transpose(2, 0, 1, 3).reshape(2, rows_w, 2 * wide),
-        ],
-        axis=2,
-    )
+    zx_cut = zx_w.reshape(rows_w, 2, 2, wide).transpose(1, 2, 0, 3)
+    pack_z = zx_cut[0]
+    pack_one = jnp.concatenate([q_w.reshape(rows_w, 2, inner).transpose(1, 0, 2), zx_cut[1]], axis=2)
     pack_out = jnp.concatenate(
         [
             wo_w.reshape(rows_w, 2, inner).transpose(1, 0, 2),
@@ -551,24 +670,37 @@
     def put_two(out, at, number, value):
         return lax.dynamic_update_slice(out, value[None], (at, 0, 0))
 
-    rows_all = cube_gather(tokens, 0).reshape(group, width)
-    two = line_gather([pack_two], put_two, jnp.zeros((groups,) + pack_two.shape, BF16))
-    two = cube_gather(two, 1).reshape(width, total_cols)
-    w_one = weight_gather(pack_one)
-    w_out = weight_gather(pack_out, w_one[0, 0])
-    w_gu = weight_gather(pack_gu, w_out[0, 0])
-    w_down = weight_gather(pack_down, w_gu[0, 0])
-    grad_rows = cube_gather(cotangent, 0).reshape(group, width)
+    own_one, give_one = halves(pack_one)
+    own_z, give_z = halves(pack_z)
+    own_out, give_out = halves(pack_out)
+    own_gu, give_gu = halves(pack_gu)
+    own_down, give_down = halves(pack_down)
+    w_one = weight_gather(own_one, swap(give_one, "x"))
+    line_two = Line(pack_two)
+    for step in range(1, groups):
+        line_two.step(line_two.moving())
+    two = line_two.place(
+        jnp.zeros((groups,) + pack_two.shape, BF16),
+        lambda out, at, value: lax.dynamic_update_slice(out, value[None], (at, 0, 0)),
+    )
+    rows_own, rows_other = cube_gather(tokens)
+    w_two, misc = settle_groups(*cube_gather(two), groups, lead)
+    got_z, got_out = swap(after(give_z, rows_own), "x"), swap(after(give_out, rows_own), "x")
+    w_z = weight_gather(own_z, got_z)
+    w_out = weight_gather(own_out, got_out)
+    w_gu = weight_gather(own_gu, swap(after(give_gu, got_out), "x"))
+    w_down = weight_gather(own_down, swap(after(give_down, got_out), "x"))
 
     seg_pair = jnp.zeros((2, seg_ids.shape[0]), jnp.int32)
     seg_pair = lax.dynamic_update_index_in_dim(seg_pair, seg_ids, x, 0)
     seg_pair = lax.dynamic_update_index_in_dim(seg_pair, swap(seg_ids, "x"), x ^ 1, 0)
     seg_own = seg_pair.reshape(1, group)
-    seg_all = line_gather(
-        [seg_own],
-        lambda out, at, number, value: lax.dynamic_update_slice(out, value, (at, 0)),
+    seg_line = Line(seg_own, both=False)
+    for step in range(1, groups):
+        seg_line.step(seg_line.moving())
+    seg_all = seg_line.place(
         jnp.zeros((groups, group), jnp.int32),
-        up_only=True,
+        lambda out, at, value: lax.dynamic_update_slice(out, value, (at, 0)),
     )
     segment = seg_own.astype(F32)
     seg_col = segment.reshape(group, 1)
@@ -577,50 +709,34 @@
     in_label = jnp.where(z > 0, previous, -1).astype(F32)
     marks = jnp.concatenate([in_label[None], segment[0, CHUNK - 1 :: CHUNK]])
 
-    gain_one = two[:, lead].astype(F32)
-    gain_two = two[:, lead + 1].astype(F32)
-    dt_all = two[:, lead + 2 : lead + 2 + ratio * dt_cols].reshape(
+    gain_one = misc[:, 0].astype(F32)
+    gain_two = misc[:, 1].astype(F32)
+    dt_all = misc[:, 2 : 2 + ratio * dt_cols].reshape(
         groups, 2, 4, part, ratio, 2, heads
     )
     dt_own = lax.dynamic_index_in_dim(dt_all, y * 2 + c, 2, False)
     dt_own = lax.dynamic_index_in_dim(dt_own, x, 4, False)
     w_dt = dt_own.transpose(0, 1, 3, 2, 4).reshape(width, heads)
     kv_head = ((y * 2 + c) * 2 + x) * (inner // HD) // (QH // KVH)
-    w_k = lax.dynamic_slice_in_dim(two, kv_head * HD, HD, 1)
-    w_v = lax.dynamic_slice_in_dim(two, kv_cols // 2 + kv_head * HD, HD, 1)
-    w_rest = jnp.concatenate(
-        [
-            w_one[:, inner:],
-            w_v,
-            two[:, kv_cols:lead],
-            jnp.pad(w_dt, ((0, 0), (0, 128 - heads))),
-        ],
-        axis=1,
-    )
-    w_qk = jnp.concatenate([w_one[:, :inner], w_k], axis=1)
-
-    stream = rows_all.astype(F32)
-    normed = (unit(stream) * gain_one).astype(BF16)
+    w_dt = jnp.pad(w_dt, ((0, 0), (0, 128 - heads)))
+
+    normed = settle_norm(rows_own, rows_other, gain_one[None, :], own_rows)
     positions = z * group + jnp.arange(group, dtype=jnp.int32)
     tables = rope_tables(positions)
-    qk = mm(normed, w_qk, 1, 0)
-    rest = mm(normed, w_rest, 1, 0).astype(BF16)
-    query = rope(qk[:, :HD], tables).astype(BF16)
-    kv_own = jnp.concatenate(
-        [rope(qk[:, HD:], tables).astype(BF16), rest[:, 2 * wide : 2 * wide + HD]], axis=1
-    )
-    half = group // 2
-    kv_half = lax.dynamic_slice_in_dim(kv_own, c * half, half, 0)
-    kv_got = line_gather(
-        [kv_half], put_two, jnp.zeros((groups, half, 2 * HD), BF16), up_only=True
-    )
-    kv_other = swap(kv_got, "c")
-    kv_all = jnp.zeros((groups, 2, half, 2 * HD), BF16)
-    kv_all = lax.dynamic_update_index_in_dim(kv_all, kv_got, c, 1)
-    kv_all = lax.dynamic_update_index_in_dim(kv_all, kv_other, c ^ 1, 1)
-    kv_all = kv_all.reshape(groups * group, 2 * HD)
-
-    dt_row = jnp.pad(rest[:, -128 : -128 + 8].T, ((0, 8), (0, 0)))
+    one = mm(normed, w_one, 1, 0)
+    other = mm(normed, w_two, 1, 0).astype(BF16)
+    dt_in = mm(normed, w_dt, 1, 0).astype(BF16)
+    query = rope(one[:, :inner], tables).astype(BF16)
+    x_in = one[:, inner:].astype(BF16)
+    bc_in = other[:, kv_cols:lead]
+    key = lax.dynamic_slice_in_dim(other, kv_head * HD, HD, 1).astype(F32)
+    value = lax.dynamic_slice_in_dim(other, kv_cols // 2 + kv_head * HD, HD, 1)
+    kv_own = jnp.concatenate([rope(key, tables).astype(BF16), value], axis=1)
+    x_in, w_z = lax.optimization_barrier((x_in, w_z))
+    cotangent_now = after(cotangent, normed)
+    gate_in = mm(normed, w_z, 1, 0).astype(BF16)
+
+    dt_row = jnp.pad(dt_in[:, :8].T, ((0, 8), (0, 0)))
     pad = ((0, 128 - heads),)
 
     def pick(values):
@@ -633,7 +749,6 @@
         jnp.stack([pick(dt_bias), rates], axis=1), ((0, 16 - heads), (0, 126))
     )
     skip_wide = jnp.repeat(pick(skip), MP)[None, :]
-    rest_cols = rest.shape[1]
 
     def flow(cols, back=False):
         at = (lambda i: (steps - 1 - i, 0)) if back else (lambda i: (i, 0))
@@ -644,7 +759,9 @@
             return steps - 1 - i if back else i
 
         return [
-            flow(rest_cols, back),
+            flow(wide, back),
+            flow(2 * states, back),
+            flow(128, back),
             pl.BlockSpec((16, CHUNK), lambda i: (0, turn(i))),
             pl.BlockSpec((8, 128), lambda i: (0, 0)),
             pl.BlockSpec((16, 128), lambda i: (0, 0)),
@@ -656,7 +773,7 @@
 
     whole = pl.BlockSpec((states, wide), lambda i: (0, 0))
     smem = pl.BlockSpec(memory_space=pltpu.SMEM)
-    chunk_args = (rest, dt_row, params, params_col, skip_wide, seg_col, seg_row, marks)
+    chunk_args = (x_in, bc_in, dt_in, dt_row, params, params_col, skip_wide, seg_col, seg_row, marks)
     y_local, run, held_own, total, starts = call(
         mamba_local_kernel,
         (
@@ -679,13 +796,34 @@
     )(*chunk_args)
     joined = jnp.where(in_label == segment[0, group - 1], 1.0, 0.0)
     factor = jnp.repeat(total[0, :heads] * joined, MP)[None, :]
-    up_line = [(i, i + 1) for i in range(groups - 1)]
-    down_line = [(i + 1, i) for i in range(groups - 1)]
+    half = group // 2
+    kv_line = Line(lax.dynamic_slice_in_dim(kv_own, c * half, half, 0), both=False)
+    order = Order()
     entering = jnp.zeros((states, wide), BF16)
-    for step in range(groups - 1):
-        leaving = held_own if step == 0 else held_own + factor * entering.astype(F32)
-        entering = lax.ppermute(leaving.astype(BF16), "z", up_line)
+    for step in range(1, groups + 1):
+        if step == 1:
+            kv_line.step((order.begin(*kv_line.moving()),))
+            order.finish(*kv_line.moving())
+            continue
+        leaving = held_own if step == 2 else held_own + factor * entering.astype(F32)
+        leaving = leaving.astype(BF16)
+        if step < groups:
+            moving, leaving = order.begin(*kv_line.moving(), leaving)
+            kv_line.step((moving,))
+        entering = lax.ppermute(leaving, "z", up_pairs(1))
+        order.finish(*kv_line.moving(), entering)
     in_held = entering
+    kv_got = kv_line.place(
+        jnp.zeros((groups, half, 2 * HD), BF16),
+        lambda out, at, value: lax.dynamic_update_slice(out, value[None], (at, 0, 0)),
+    )
+    kv_all = jnp.zeros((groups, 2, half, 2 * HD), BF16)
+    kv_all = lax.dynamic_update_index_in_dim(kv_all, kv_got, c, 1)
+    kv_all = lax.dynamic_update_index_in_dim(kv_all, swap(kv_got, "c"), c ^ 1, 1)
+    kv_all = kv_all.reshape(groups * group, 2 * HD)
+    cot_own, cot_other = cube_gather(cotangent_now)
+    query, cot_own, cot_other, w_out = lax.optimization_barrier((query, cot_own, cot_other, w_out))
+    w_all = jnp.concatenate([w_one, w_two, w_dt, w_z], axis=1)
 
     q_rows = CHUNK
     blocks = group // q_rows
@@ -717,50 +855,77 @@
         mamba_close_kernel,
         (shape((group, wide), BF16), shape((group, wide))),
         (steps,),
-        [flow(rest_cols), flow(wide), flow(128), flow(1), whole, smem],
+        [flow(2 * states), flow(wide), flow(wide), flow(128), flow(1), whole, smem],
         (flow(wide), flow(wide)),
-    )(rest, y_local, run, seg_col, in_held, marks)
+    )(bc_in, gate_in, y_local, run, seg_col, in_held, marks)
     mixer_out = jnp.concatenate([att_full.astype(BF16), ssm_out], axis=1)
 
-    def to_rows(term):
-        return cube_scatter(term.astype(BF16).reshape(8, own_rows, width), 0)
+    def to_rows(mine, other):
+        def term(products):
+            total = None
+            for a, w in products:
+                value = mm(a, w, 1, 1)
+                total = value if total is None else total + value
+            return total.astype(BF16).reshape(4, own_rows, width)
+
+        return cube_scatter(term(mine), term(other))
+
+    def weight_grad(pairs):
+        total = None
+        for a, g in pairs:
+            value = mm(a, g, 0, 0)
+            total = value if total is None else total + value
+        return weight_scatter(total.astype(BF16))
 
     stream_own = tokens.astype(F32)
-    middle = stream_own + to_rows(mm(mixer_out, w_out, 1, 1))
+    mixer_own, mixer_other = unsettle(mixer_out, own_rows)
+    middle = stream_own + to_rows([(mixer_own, w_out)], [(mixer_other, w_out)])
     normed_two = (unit(middle) * gain_two).astype(BF16)
-    rows_two = cube_gather(normed_two, 0).reshape(group, width)
-    gate_up = mm(rows_two, w_gu, 1, 0).astype(BF16)
-    gate = gate_up[:, :ff].astype(F32)
-    up = gate_up[:, ff:].astype(F32)
-    sig = jax.nn.sigmoid(gate)
-    hidden = (gate * sig * up).astype(BF16)
-    grad_hidden = mm(grad_rows, w_down, 1, 0).astype(BF16).astype(F32)
-    grad_gate = grad_hidden * up * (sig * (1.0 + gate * (1.0 - sig)))
-    grad_gu = jnp.concatenate([grad_gate, grad_hidden * gate * sig], axis=1).astype(BF16)
-    grad_normed_two = to_rows(mm(grad_gu, w_gu, 1, 1))
-    layer_out = (middle + to_rows(mm(hidden, w_down, 1, 1))).astype(BF16)
-    down_part = weight_scatter(mm(grad_rows, hidden, 0, 0).astype(BF16))
-    gu_part = weight_scatter(mm(rows_two, grad_gu, 0, 0).astype(BF16))
+    normed_two, w_gu = lax.optimization_barrier((normed_two, w_gu))
+    two_rows = cube_gather(normed_two)
+
+    def forward(rows):
+        gate_up = mm(rows, w_gu, 1, 0).astype(BF16)
+        gate = gate_up[:, :ff].astype(F32)
+        up = gate_up[:, ff:].astype(F32)
+        sig = jax.nn.sigmoid(gate)
+        return gate, up, sig, (gate * sig * up).astype(BF16)
+
+    def backward(rows, gate, up, sig):
+        grad_hidden = mm(rows, w_down, 1, 0).astype(BF16).astype(F32)
+        grad_gate = grad_hidden * up * (sig * (1.0 + gate * (1.0 - sig)))
+        return jnp.concatenate([grad_gate, grad_hidden * gate * sig], axis=1).astype(BF16)
+
+    *kept_own, hidden_own = forward(two_rows[0])
+    *kept_other, hidden_other = forward(two_rows[1])
+    gu_other = backward(cot_other, *kept_other)
+    gu_own = backward(cot_own, *kept_own)
+    grad_normed_two = to_rows([(gu_own, w_gu)], [(gu_other, w_gu)])
+    down_part = weight_grad([(cot_own, hidden_own), (cot_other, hidden_other)])
+    gu_part = weight_grad([(two_rows[0], gu_own), (two_rows[1], gu_other)])
     middle_part, gain_two_part = norm_back(middle, gain_two, grad_normed_two)
     grad_middle = cotangent.astype(F32) + middle_part
-    mixed_rows = cube_gather(grad_middle.astype(BF16), 0).reshape(group, width)
-    grad_mixer = mm(mixed_rows, w_out, 1, 0).astype(BF16)
-    out_part = weight_scatter(mm(mixed_rows, mixer_out, 0, 0).astype(BF16))
+    mixed_own, mixed_other = cube_gather(grad_middle.astype(BF16))
+    hidden_own, hidden_other = after(hidden_own, mixed_own), after(hidden_other, mixed_own)
+    layer_out = middle + to_rows([(hidden_own, w_down)], [(hidden_other, w_down)])
+    layer_out = layer_out.astype(BF16)
+    grad_mixer = settle(
+        mm(mixed_own, w_out, 1, 0).astype(BF16), mm(mixed_other, w_out, 1, 0).astype(BF16), own_rows
+    )
+    out_part = weight_grad([(mixed_own, mixer_own), (mixed_other, mixer_other)])
 
     grad_att = grad_mixer[:, :inner]
     grad_ssm = grad_mixer[:, inner:]
-    state_grad = call(
+    state_grad, grad_z = call(
         mamba_grad_state_kernel,
-        shape((states, wide)),
+        (shape((states, wide)), shape((group, wide), BF16)),
         (steps,),
-        [flow(rest_cols), flow(wide), flow(128), flow(1), smem],
-        whole,
-    )(rest, grad_ssm, run, seg_col, marks)
-    deep = jnp.zeros((states, wide), BF16)
-    for step in range(groups - 1):
-        leaving = state_grad if step == 0 else state_grad + factor * deep.astype(F32)
-        deep = lax.ppermute(leaving.astype(BF16), "z", down_line)
-    deep = deep.astype(F32)
+        [flow(2 * states), flow(wide), flow(wide), flow(wide), flow(128), flow(1), smem],
+        (whole, flow(wide)),
+    )(bc_in, gate_in, y_full, grad_ssm, run, seg_col, marks)
+    order = Order()
+    grad_att, down_part = lax.optimization_barrier((after(grad_att, state_grad), down_part))
+    deep = lax.ppermute(state_grad.astype(BF16), "z", down_pairs(1))
     grad_query, grad_kv_all = call(
         attend_grad_kernel,
         (shape((group, HD)), shape((groups * group, 2 * HD), BF16)),
@@ -777,9 +942,24 @@
     kv_terms = lax.dynamic_index_in_dim(kv_terms, c, 1, False) + swap(
         lax.dynamic_index_in_dim(kv_terms, c ^ 1, 1, False), "c"
     )
-    grad_kv_half = line_scatter(
-        lambda at: lax.dynamic_index_in_dim(kv_terms, at, 0, False), down_only=True
-    )
+    def kv_term(at):
+        at = jnp.clip(at, 0, groups - 1)
+        return lax.dynamic_index_in_dim(kv_terms, at, 0, False)
+
+    moved = None
+    for step in range(1, groups):
+        give = kv_term(z - (groups - step))
+        give = give if moved is None else give + moved
+        order.finish(deep)
+        leaving = (state_grad + factor * deep.astype(F32)).astype(BF16)
+        if step < groups - 1:
+            give, leaving = order.begin(give, leaving)
+            deep = lax.ppermute(leaving, "z", down_pairs(1))
+        last_ones = [(i, i - 1) for i in range(groups - 1, groups - 1 - step, -1)]
+        moved = lax.ppermute(give, "z", last_ones)
+        order.finish(deep, moved)
+    deep, gu_part = lax.optimization_barrier((deep.astype(F32), gu_part))
+    grad_kv_half = kv_term(z).astype(F32) + moved.astype(F32)
     half_tables = tuple(lax.dynamic_slice_in_dim(table, c * half, half, 0) for table in tables)
     grad_kv_half = jnp.concatenate(
         [rope_back(grad_kv_half[:, :HD], half_tables), grad_kv_half[:, HD:]], axis=1
@@ -788,10 +968,13 @@
         jnp.zeros((group, 2 * HD), BF16), grad_kv_half, (c * half, 0)
     )
     grad_q = rope_back(grad_query, tables).astype(BF16)
-    grad_zx, grad_bc, grad_dt, sums, skip_sums = call(
+    grad_qz = jnp.concatenate([grad_q, grad_z], axis=1)
+    qz_w = mm(normed, grad_qz, 0, 0)
+    qz_part = weight_scatter(qz_w.astype(BF16))
+    grad_x, grad_bc, grad_dt, sums, skip_sums = call(
         mamba_grad_kernel,
         (
-            shape((group, 2 * wide), BF16),
+            shape((group, wide), BF16),
             shape((group, 2 * states), BF16),
             shape((group, 128), BF16),
             shape((8, 128)),
@@ -808,73 +991,74 @@
             whole,
         ],
         (
-            flow(2 * wide, True),
+            flow(wide, True),
             flow(2 * states, True),
             flow(128, True),
             pl.BlockSpec((8, 128), lambda i: (0, 0)),
             pl.BlockSpec((8, wide), lambda i: (0, 0)),
         ),
         [pltpu.VMEM((states, wide), F32)],
-    )(*chunk_args, y_full, run, starts, in_held, grad_ssm, deep)
-
-    grad_rest = jnp.concatenate([grad_zx, grad_kv[:, HD:], grad_bc, grad_dt], axis=1)
-    grad_qk = jnp.concatenate([grad_q, grad_kv[:, :HD]], axis=1)
-    in_term = (mm(grad_rest, w_rest, 1, 1) + mm(grad_qk, w_qk, 1, 1)).astype(BF16)
-    gain_one_part = jnp.sum(in_term.astype(F32) * unit(stream), axis=0)
-    rest_w = mm(normed, grad_rest, 0, 0).astype(BF16)
-    qk_w = mm(normed, grad_qk, 0, 0).astype(BF16)
-    one_part = weight_scatter(jnp.concatenate([qk_w[:, :inner], rest_w[:, : 2 * wide]], axis=1))
-    input_part, _ = norm_back(stream_own, gain_one, to_rows(in_term))
+    )(*chunk_args, gate_in, run, starts, in_held, grad_ssm, deep)
+
+    grad_x, out_part = lax.optimization_barrier((grad_x, out_part))
+    x_w = mm(normed, grad_x, 0, 0)
+    x_part = weight_scatter(x_w.astype(BF16))
+    grad_all, grad_two = assemble(
+        kv_head, own_rows, grad_q, grad_x, grad_kv, grad_bc, grad_dt, grad_z
+    )
+    cut = group // 2
+    in_grad = to_rows([(grad_all[:cut], w_all)], [(grad_all[cut:], w_all)])
+    input_part, _ = norm_back(stream_own, gain_one, in_grad)
     input_grad = grad_middle + input_part
-    kv_grads = jnp.zeros((width, kv_cols), BF16)
-    kv_grads = lax.dynamic_update_slice_in_dim(kv_grads, qk_w[:, inner:], kv_head * HD, 1)
-    kv_grads = lax.dynamic_update_slice_in_dim(
-        kv_grads, rest_w[:, 2 * wide : 2 * wide + HD], kv_cols // 2 + kv_head * HD, 1
-    )
-    dt_full = rest_w[:, -128 : -128 + heads].reshape(groups, 2, ratio, part, heads)
-    dt_full = dt_full.transpose(0, 1, 3, 2, 4)[:, :, :, :, None, :]
-    dt_full = jnp.where(jnp.arange(2)[:, None] == x, dt_full, 0).reshape(
-        groups, 2, 1, part, ratio * dt_cols
-    )
-    dt_full = jnp.where(
-        jnp.arange(4)[:, None, None] == y * 2 + c, dt_full, 0
-    ).reshape(width, ratio * dt_cols)
-    two_grads = jnp.concatenate(
-        [
-            kv_grads,
-            rest_w[:, 2 * wide + HD : 2 * wide + HD + bc_cols],
-            gain_one_part.astype(BF16)[:, None],
-            gain_two_part.astype(BF16)[:, None],
-            dt_full,
-            jnp.zeros((width, total_cols - used), BF16),
-        ],
-        axis=1,
-    )
-    two_part = cube_scatter(two_grads.reshape(groups, 8, part, total_cols), 1).astype(BF16)
-    two_part = line_scatter(lambda at: lax.dynamic_index_in_dim(two_part, at, 0, False))
+    two_w = mm(normed, grad_two, 0, 0)
+    dt_w_grad = mm(normed, grad_dt, 0, 0)
+    two_cut = two_w.astype(BF16).reshape(groups, 8, part, lead)
+
+    def two_terms(core):
+        spot = [((x ^ dx) * 2 + (y ^ dy)) * 2 + core for dx, dy in ((0, 0), (0, 1), (1, 0), (1, 1))]
+        return jnp.stack([lax.dynamic_index_in_dim(two_cut, at, 1, False) for at in spot])
+
+    two_part = cube_scatter(two_terms(c), two_terms(c ^ 1)).astype(BF16)
+    two_part = lax.psum_scatter(two_part, "z", scatter_dimension=0).astype(F32)
     kv_grad = two_part[:, :kv_cols].reshape(kv_w.shape)
     bc_grad = two_part[:, kv_cols:lead]
-    dt_grad = two_part[:, lead + 2 : used].reshape(part, ratio, dt_cols)
-    dt_grad = dt_grad.transpose(1, 0, 2).reshape(rows_w, dt_cols)
-    small = jnp.stack(
+    gain_one_part = jnp.sum(two_w * w_two.astype(F32), axis=1)
+    gain_one_part += jnp.sum(dt_w_grad * w_dt.astype(F32), axis=1)
+    gain_one_part += jnp.sum(x_w * w_one[:, inner:].astype(F32), axis=1)
+    gain_one_part += jnp.sum(qz_w[:, :inner] * w_one[:, :inner].astype(F32), axis=1)
+    gain_one_part += jnp.sum(qz_w[:, inner:] * w_z.astype(F32), axis=1)
+    gain_one_part = gain_one_part / gain_one
+    small = jnp.concatenate(
         [sums[0, :heads], sums[1, :heads], jnp.sum(skip_sums[0].reshape(heads, MP), axis=1)]
     )
-    small_pair = jnp.zeros((2, 3, heads), F32)
-    small_pair = lax.dynamic_update_index_in_dim(small_pair, small, x, 0)
-    small_pair = lax.dynamic_update_index_in_dim(small_pair, swap(small, "x"), x ^ 1, 0)
-    small_line = line_gather(
-        [small_pair],
-        lambda out, at, number, value: lax.dynamic_update_slice(out, value[None], (at, 0, 0, 0)),
-        jnp.zeros((groups, 2, 3, heads), F32),
-    )
-    small_sum = jnp.sum(small_line, axis=0).transpose(1, 0, 2).reshape(3, 2 * heads)
+    small = jnp.pad(small, (0, width - small.shape[0]))
+    tiny = jnp.concatenate(
+        [dt_w_grad[:, :heads].T, jnp.stack([small, gain_one_part, gain_two_part])], axis=0
+    )
+    tiny = line_sum(tiny)
+    gains = tiny[heads + 1 :]
+    gains = gains + swap(gains, "c")
+    gains = gains + swap(gains, "y")
+    tiny_other = swap(jnp.concatenate([tiny[: heads + 1], gains], axis=0), "x")
+    gains = gains + tiny_other[heads + 1 :]
+    spot = spots(0, 0, 0) + z * 8
+    gain_grads = lax.dynamic_slice_in_dim(gains, spot * part, part, 1)
+    dt_grad = both_halves(
+        *(
+            lax.dynamic_slice_in_dim(a[:heads], (z * 2 + x) * rows_w, rows_w, 1).T
+            for a in (tiny, tiny_other)
+        )
+    ).reshape(rows_w, dt_cols)
+    small_sum = both_halves(
+        *(a[heads, : 3 * heads].reshape(3, heads) for a in (tiny, tiny_other))
+    ).reshape(3, dt_cols)
     return (
         layer_out,
         input_grad,
-        two_part[:, lead],
-        one_part[:, :, :inner].reshape(rows_w, 2 * inner),
+        gain_grads[0],
+        qz_part[:, :, :inner].reshape(rows_w, 2 * inner),
         kv_grad,
-        one_part[:, :, inner:].reshape(rows_w, 2, 2, wide).transpose(0, 2, 1, 3).reshape(zx_w.shape),
+        jnp.stack([qz_part[:, :, inner:], x_part], axis=1).reshape(zx_w.shape),
         dt_grad,
         bc_grad,
         small_sum[0],
@@ -882,7 +1066,7 @@
         small_sum[2],
         out_part[:, :, :inner].reshape(wo_w.shape),
         out_part[:, :, inner:].reshape(wm_w.shape),
-        two_part[:, lead + 1],
+        gain_grads[1],
         gu_part.reshape(rows_w, 2, 2, ff).transpose(0, 2, 1, 3).reshape(gu_w.shape),
         down_part.reshape(down_w.shape),
     )

time: 1080 us -> 830 us (0.77)
  starting transfers between devices: 401 us -> 146 us
  waiting for transfers between devices: 297 us -> 228 us
  matrix products: 73.9 us -> 125 us
  Pallas kernels: 60 us -> 96.8 us
  local copies, waits for them, and re-layouts: 142 us -> 125 us
  between operations: 6.72 us -> 17.6 us
    ppermute x129 -> x24, starting transfers between devices: 340 us -> 76.7 us  [the longest x3 39.6 us: shards(): entering = lax.ppermute(leaving, 'z', up_pairs(1))]
    ppermute x129 -> x24, waiting for transfers between devices: 216 us -> 75.7 us  [the longest x3 27.2 us: step(): self.downs.append(lax.ppermute(moving[1], 'z', down_pairs(number)))]
    dot_general x15 -> x28, matrix products: 73.9 us -> 125 us  [mm(): lax.dot_general(a, b, (((ca,), (cb,)), ((), ())), preferred_element_type=...]
    ppermute x82 -> x76, waiting for transfers between devices: 80.4 us -> 124 us  [swap(): return lax.ppermute(a, axis, SWAP)]
    pallas_call x2 -> x7, Pallas kernels: 26.6 us -> 63.7 us  [the longest x1 20.3 us: shards(): call(mamba_grad_kernel, (shape((group, wide), BF16), shape((group, 2 * st...]
    unnamed x250 -> x221, local copies, waits for them, and re-layouts: 22.8 us -> 53.7 us
    dynamic_update_slice x45 -> x5, local copies, waits for them, and re-layouts: 21 us -> 0.18 us  [the longest x4 0.1 us: shards(): lax.dynamic_update_slice(out, value[None], (at, 0, 0))]
    all_gather x0 -> x5, waiting for transfers between devices: none -> 18.1 us  [weight_gather(): return lax.all_gather(both, 'z', axis=0, tiled=True)]
  transfers between devices with their start and end apart: 211 -> 111, of which waited for: 60 -> 51; matrix products, arithmetic and copies ran while one was open for 22% -> 36% of each run, Pallas kernels for 6% -> 12%
where the time goes in v2:
time: 830 us; the launch traced here: 818 us
  waiting for transfers between devices  228 us (27%)
  starting transfers between devices  146 us (18%)
  local copies, waits for them, and re-layouts  125 us (15%)
  matrix products  125 us (15%)
  Pallas kernels  96.8 us (12%)
  other arithmetic  78.8 us (9%)
  between operations  17.6 us (2%)
    dot_general x28, matrix products, mm(): lax.dot_general(a, b, (((ca,), (cb,)), ((), ())), preferred_element_type=...  125 us
    ppermute x76, waiting for transfers between devices, swap(): return lax.ppermute(a, axis, SWAP)  124 us
    ppermute x76, starting transfers between devices, swap(): return lax.ppermute(a, axis, SWAP)  67.4 us
    unnamed x221, local copies, waits for them, and re-layouts  53.7 us
    ppermute x3, starting transfers between devices, shards(): entering = lax.ppermute(leaving, 'z', up_pairs(1))  39.6 us
    ppermute x3, waiting for transfers between devices, step(): self.downs.append(lax.ppermute(moving[1], 'z', down_pairs(number)))  27.2 us
    ppermute x2, waiting for transfers between devices, shards(): deep = lax.ppermute(leaving, 'z', down_pairs(1))  25.1 us
    pallas_call x1, Pallas kernels, shards(): call(mamba_grad_kernel, (shape((group, wide), BF16), shape((group, 2 * st...  20.3 us
  transfers between devices with their start and end apart: 111, of which 51 were waited for; matrix products, arithmetic and copies ran while one was open for 36% of the time, Pallas kernels for 12%

profile of v2, /device:TPU:0, one launch (start us, length us, event | category | flops | bytes accessed | tf_op | source)
XLA Modules:
  0.0 818.4 jit_solution(15957260134601265239)
XLA Ops:
  13.5 6.3 collective-permute-done.20
  32.4 10.4 %collective-permute-done.10 = bf16[64,1152]{1,0:T(8,128)(2,1)} collective-permute-done((bf16[64,1152]{1,0:T(8,128)(2,1)S(1)}, bf16[64,1152]{1,0:T(8,128)(2,1)}, u32[]{:S(2)}, u32[]{:S(2)}) %collective-permute-start.10) | collective-permute-done | bytes 147488 | tf_op jit(solution)/shard_map/ppermute | solution.py:73
  47.3 4.6 collective-permute-done.6
  60.1 14.5 %collective-permute-done.12 = bf16[64,1152]{1,0:T(8,128)(2,1)S(1)} collective-permute-done((bf16[64,1152]{1,0:T(8,128)(2,1)}, bf16[64,1152]{1,0:T(8,128)(2,1)S(1)}, u32[]{:S(2)}, u32[]{:S(2)}) %collective-permute-start.12) | collective-permute-done | bytes 147488 | tf_op jit(solution)/shard_map/ppermute | solution.py:73
  81.8 12.3 %collective-permute-done.26 = bf16[256,512]{1,0:T(8,128)(2,1)} collective-permute-done((bf16[256,512]{1,0:T(8,128)(2,1)}, bf16[256,512]{1,0:T(8,128)(2,1)}, u32[]{:S(2)}, u32[]{:S(2)}) %collective-permute-start.26) | collective-permute-done | bytes 262176 | tf_op jit(solution)/shard_map/ppermute | solution.py:35
  129.4 5.6 collective-permute-done.42
  137.8 8.3 %settle_groups_kernel.1 = (bf16[4,8,64,1024]{3,2,1,0:T(8,128)(2,1)}, bf16[4,8,64,128]{3,2,1,0:T(8,128)(2,1)}) custom-call(s32[2]{0:T(128)} %pad_add_fusion.place, bf16[16,64,1152]{2,1,0:T(8,128)(2,1)} %constant_dynamic-update-slice_fusion.5.own_ref, bf16[16,64,1152]{2,1,0:T(8,128)(2,1)} %collective-permute-done.19.other_ref), custom_call_target="tpu_custom_call" | custom-call | tf_op jit(solution)/shard_map/settle_groups_kernel/pallas_call | solution.py:147
  149.5 8.8 %settle_norm_kernel.1 = bf16[1024,2048]{1,0:T(8,128)(2,1)} custom-call(s32[2]{0:T(128)} %pad_add_fusion.place, bf16[512,2048]{1,0:T(8,128)(2,1)} %constant_dynamic-update-slice_fusion.own_ref, bf16[512,2048]{1,0:T(8,128)(2,1)} %collective-permute-done.8.other_ref, f32[1,2048]{1,0:T(1,128)} %bitcast.496), custom_call_target="tpu_custom_call" | custom-call | tf_op jit(solution)/shard_map/settle_norm_kernel/pallas_call | solution.py:171
  160.4 5.2 fusion.115
  177.2 8.0 convolution_convert_fusion.8
  191.6 5.8 collective-permute-start.27
  197.5 10.5 %mamba_local_kernel.1 = (f32[1024,384]{1,0:T(8,128)}, f32[1024,128]{1,0:T(8,128)}, f32[256,384]{1,0:T(8,128)}, f32[8,128]{1,0:T(8,128)}, f32[4,256,384]{2,1,0:T(8,128)}) custom-call(bf16[1024,384]{1,0:T(8,128)(2,1)} %slice.807.x_in_ref, bf16[1024,512]{1,0:T(8,128)(2,1)} %slice.610.bc_in_ref, bf16[1024,128]{1,0:T(8,128)(2,1)} %copy.252.dt_in_ref, ...), custom_call_target="tpu_custom_call" | custom-call | tf_op jit(solution)/shard_map/mamba_local_kernel/pallas_call | solution.py:777
  211.5 13.7 %collective-permute-start.30 = (bf16[256,384]{1,0:T(8,128)(2,1)S(1)}, bf16[256,384]{1,0:T(8,128)(2,1)S(1)}, u32[]{:S(2)}, u32[]{:S(2)}) collective-permute-start(bf16[256,384]{1,0:T(8,128)(2,1)S(1)} %convert_element_type.391), channel_id=1, source_target_pairs={{0,8},{8,16},{16,24},{1,9},{9,17},{17,25},{2,10},{10,18},{18,26},{... | collective-permute-start | bytes 589832 | tf_op jit(solution)/shard_map/ppermute | solution.py:813
  236.9 17.2 %collective-permute-start.33 = (bf16[256,384]{1,0:T(8,128)(2,1)S(1)}, bf16[256,384]{1,0:T(8,128)(2,1)S(1)}, u32[]{:S(2)}, u32[]{:S(2)}) collective-permute-start(bf16[256,384]{1,0:T(8,128)(2,1)S(1)} %add_convert_fusion.6), channel_id=1, source_target_pairs={{0,8},{8,16},{16,24},{1,9},{9,17},{17,25},{2,10},{10,18},{18,26},{... | collective-permute-start | bytes 589832 | tf_op jit(solution)/shard_map/ppermute | solution.py:813
  257.5 8.7 %collective-permute-start.34 = (bf16[256,384]{1,0:T(8,128)(2,1)S(1)}, bf16[256,384]{1,0:T(8,128)(2,1)S(1)}, u32[]{:S(2)}, u32[]{:S(2)}) collective-permute-start(bf16[256,384]{1,0:T(8,128)(2,1)S(1)} %add_convert_fusion.5), channel_id=1, source_target_pairs={{0,8},{8,16},{16,24},{1,9},{9,17},{17,25},{2,10},{10,18},{18,26},{... | collective-permute-start | bytes 589832 | tf_op jit(solution)/shard_map/ppermute | solution.py:813
  266.5 4.5 collective-permute-done.34.held_ref
  271.7 5.2 mamba_close_kernel.1
  278.3 7.2 attend_kernel.1
  287.7 5.9 unsettle_kernel.1
  306.1 5.1 collective-permute-done.37
  317.1 4.5 collective-permute-done.40
  326.6 10.3 %collective-permute-done.44 = bf16[128,2048]{1,0:T(8,128)(2,1)S(1)} collective-permute-done((bf16[128,2048]{1,0:T(8,128)(2,1)S(1)}, bf16[128,2048]{1,0:T(8,128)(2,1)S(1)}, u32[]{:S(2)}, u32[]{:S(2)}) %collective-permute-start.44) | collective-permute-done | bytes 524320 | tf_op jit(solution)/shard_map/ppermute | solution.py:35
  349.5 18.1 %all-gather.14.cloned.1.call-done = bf16[2048,512]{1,0:T(8,128)(2,1)} async-done(((bf16[512,512]{1,0:T(8,128)(2,1)}), bf16[2048,512]{1,0:T(8,128)(2,1)}) %all-gather.14.cloned.1.call-update) | async-done | bytes 2097168 | tf_op jit(solution)/shard_map/all_gather | solution.py:247
  367.6 5.0 fusion.10
  384.2 4.4 add_convert_fusion.2
  389.8 6.1 convolution_convert_fusion
  400.0 6.3 add_convert_fusion
  406.9 4.9 convolution_convert_fusion.1
  416.9 5.1 collective-permute-done.51
  437.9 11.1 %collective-permute-done.57 = bf16[128,2048]{1,0:T(8,128)(2,1)S(1)} collective-permute-done((bf16[128,2048]{1,0:T(8,128)(2,1)S(1)}, bf16[128,2048]{1,0:T(8,128)(2,1)S(1)}, u32[]{:S(2)}, u32[]{:S(2)}) %collective-permute-start.57) | collective-permute-done | bytes 524320 | tf_op jit(solution)/shard_map/ppermute | solution.py:35
  451.4 4.5 collective-permute-done.58
  461.2 4.4 convolution_convert_fusion.4
  489.8 5.7 settle_kernel.1
  505.5 6.3 mamba_grad_state_kernel.1
  513.6 10.1 %attend_grad_kernel.1 = (f32[1024,128]{1,0:T(8,128)}, bf16[4096,256]{1,0:T(8,128)(2,1)}) custom-call(s32[4]{0:T(128)} %and_select_fusion.1.low_ref, s32[4]{0:T(128)} %fusion.95.high_ref, s32[1]{0:T(128)} %bitcast.5.start_ref, bf16[1024,128]{1,0:T(8,128)(2,1)} %get-tuple-element.71.q_ref, bf16[4096,256]{1,0:T(8,128)(2,1)} %bitcast.460, ...), custom_call_target="tpu_custom_call" | custom-call | tf_op jit(solution)/shard_map/attend_grad_kernel/pallas_call | solution.py:929
  541.4 7.0 collective-permute-done.70
  588.9 22.6 %collective-permute-done.73 = bf16[256,384]{1,0:T(8,128)(2,1)S(1)} collective-permute-done((bf16[256,384]{1,0:T(8,128)(2,1)}, bf16[256,384]{1,0:T(8,128)(2,1)S(1)}, u32[]{:S(2)}, u32[]{:S(2)}) %collective-permute-start.73) | collective-permute-done | bytes 196640 | tf_op jit(solution)/shard_map/ppermute | solution.py:957
  612.2 6.3 collective-permute-done.77
  624.2 11.9 %collective-permute-done.74 = bf16[256,1024]{0,1:T(8,128)(2,1)} collective-permute-done((bf16[256,1024]{0,1:T(8,128)(2,1)}, bf16[256,1024]{0,1:T(8,128)(2,1)}, u32[]{:S(2)}, u32[]{:S(2)}) %collective-permute-start.74) | collective-permute-done | bytes 524320 | tf_op jit(solution)/shard_map/ppermute | solution.py:35
  637.5 20.3 %mamba_grad_kernel.1 = (bf16[1024,384]{1,0:T(8,128)(2,1)}, bf16[1024,512]{1,0:T(8,128)(2,1)}, bf16[1024,128]{1,0:T(8,128)(2,1)}, f32[8,128]{1,0:T(8,128)}, f32[8,384]{1,0:T(8,128)}) custom-call(bf16[1024,384]{1,0:T(8,128)(2,1)} %slice.807.x_in_ref, bf16[1024,512]{1,0:T(8,128)(2,1)} %slice.610.bc_in_ref, bf16[1024,128]{1,0:T(8,128)(2,1)} %copy.252.dt_in_ref, ...), custom_call_target="tpu_custom_call" | custom-call | tf_op jit(solution)/shard_map/mamba_grad_kernel/pallas_call | solution.py:974
  673.4 6.3 fusion.114
  679.7 8.4 %assemble_kernel.1 = (bf16[1024,2048]{1,0:T(8,128)(2,1)}, bf16[1024,1024]{1,0:T(8,128)(2,1)}) custom-call(s32[3]{0:T(128)} %pad_add_fusion.1.place, bf16[1024,128]{1,0:T(8,128)(2,1)} %copy-done.48, bf16[1024,384]{1,0:T(8,128)(2,1)} %get-tuple-element.108.x_ref, bf16[1024,256]{1,0:T(8,128)(2,1)} %copy-done.36, bf16[1024,512]{1,0:T(8,128)(2,1)} %get-tuple-element.110.bc_ref, ...), custom_call_target="tpu_custom_call" | custom-call | tf_op jit(solution)/shard_map/assemble_kernel/pallas_call | solution.py:225
  688.2 8.0 convolution_convert_fusion.2
  699.0 9.1 %fusion.105 = (bf16[2048,1024]{1,0:T(8,128)(2,1)S(1)}, f32[2048]{0:T(1024)S(1)}) fusion(bf16[4,8,64,1024]{3,2,1,0:T(8,128)(2,1)} %get-tuple-element.72, bf16[1024,2048]{1,0:T(8,128)(2,1)} %settle_norm_kernel.1, bf16[1024,1024]{1,0:T(8,128)(2,1)} %get-tuple-element.116), kind=kOutput, calls=%fused_computation.390 | convolution fusion | flops 4303353856 | bytes 14688256 | tf_op jit(solution)/shard_map/dot_general | solution.py:29
  708.8 5.1 collective-permute-start.85
  725.0 5.8 convolution_convert_fusion.3
  764.9 4.5 collective-permute-done.96
  799.3 10.0 %reduce-scatter.15.cloned.1.call-done = bf16[1,64,1024]{2,1,0:T(8,128)(2,1)} async-done(((bf16[4,64,1024]{2,1,0:T(8,128)(2,1)}), bf16[1,64,1024]{2,1,0:T(8,128)(2,1)}) %reduce-scatter.15.cloned.1.call-update) | async-done | bytes 131088 | tf_op jit(solution)/shard_map/reduce_scatter | solution.py:1022
  (686 shorter events, 400.9 us)
Async XLA Ops:
  7.2 153.2 %all-gather.6.cloned.1.call-start = ((), (), s32[]{:S(2)}) async-start(), calls=%async_computation.6 | async-start | bytes 2621440 | tf_op jit(solution)/shard_map/all_gather | solution.py:247
  20.8 167.3 %all-gather.10.cloned.1.call-start = ((), (), s32[]{:S(2)}) async-start(), calls=%async_computation.8 | async-start | bytes 1966080 | tf_op jit(solution)/shard_map/all_gather | solution.py:247
  20.9 24.6 %collective-permute-start.4 = (bf16[128,2048]{1,0:T(8,128)(2,1)S(1)}, bf16[128,2048]{1,0:T(8,128)(2,1)S(1)}, u32[]{:S(2)}, u32[]{:S(2)}) collective-permute-start(bf16[128,2048]{1,0:T(8,128)(2,1)S(1)} %copy-done.5), channel_id=1, source_target_pairs={{0,2},{2,0},{1,3},{3,1},{4,6},{6,4},{5,7},{7,5},{8,10},{10,8},{9,1... | collective-permute-start | bytes 1572872 | tf_op jit(solution)/shard_map/ppermute | solution.py:35
  22.7 22.7 %collective-permute-start.5 = (bf16[128,2048]{1,0:T(8,128)(2,1)S(1)}, bf16[128,2048]{1,0:T(8,128)(2,1)S(1)}, u32[]{:S(2)}, u32[]{:S(2)}) collective-permute-start(bf16[128,2048]{1,0:T(8,128)(2,1)S(1)} %copy-done.5), channel_id=1, source_target_pairs={{0,4},{4,0},{1,5},{5,1},{2,6},{6,2},{3,7},{7,3},{8,12},{12,8},{9,1... | collective-permute-start | bytes 1572872 | tf_op jit(solution)/shard_map/ppermute | solution.py:35
  24.8 19.3 %collective-permute-start.9 = (bf16[64,1152]{1,0:T(8,128)(2,1)S(1)}, bf16[64,1152]{1,0:T(8,128)(2,1)}, u32[]{:S(2)}, u32[]{:S(2)}) collective-permute-start(bf16[64,1152]{1,0:T(8,128)(2,1)S(1)} %pad.31), channel_id=1, source_target_pairs={{0,8},{8,16},{16,24},{1,9},{9,17},{17,25},{2,10},{10,18},{18,26},{... | collective-permute-start | bytes 442376 | tf_op jit(solution)/shard_map/ppermute | solution.py:71
  30.2 84.6 %collective-permute-start = (s32[512]{0:T(512)S(1)}, s32[512]{0:T(512)S(1)}, u32[]{:S(2)}, u32[]{:S(2)}) collective-permute-start(s32[512]{0:T(512)S(1)} %copy-done.71), channel_id=1, source_target_pairs={{0,4},{4,0},{1,5},{5,1},{2,6},{6,2},{3,7},{7,3},{8,12},{12,8},{9,1... | collective-permute-start | bytes 6152 | tf_op jit(solution)/shard_map/ppermute | solution.py:35
  57.0 17.6 %collective-permute-start.12 = (bf16[64,1152]{1,0:T(8,128)(2,1)}, bf16[64,1152]{1,0:T(8,128)(2,1)S(1)}, u32[]{:S(2)}, u32[]{:S(2)}) collective-permute-start(bf16[64,1152]{1,0:T(8,128)(2,1)} %collective-permute-done.11), channel_id=1, source_target_pairs={{8,0},{9,1},{10,2},{11,3},{12,4},{13,5},{14,6},{15,7}} | collective-permute-start | bytes 442376 | tf_op jit(solution)/shard_map/ppermute | solution.py:73
  58.3 17.3 %collective-permute-start.14 = (bf16[64,1152]{1,0:T(8,128)(2,1)}, bf16[64,1152]{1,0:T(8,128)(2,1)S(1)}, u32[]{:S(2)}, u32[]{:S(2)}) collective-permute-start(bf16[64,1152]{1,0:T(8,128)(2,1)} %collective-permute-done.13), channel_id=1, source_target_pairs={{16,24},{17,25},{18,26},{19,27},{20,28},{21,29},{22,30},{23,31}} | collective-permute-start | bytes 442376 | tf_op jit(solution)/shard_map/ppermute | solution.py:71
  60.1 217.0 %all-gather.8.cloned.1.call-start = ((), (), s32[]{:S(2)}) async-start(), calls=%async_computation.7 | async-start | bytes 2621440 | tf_op jit(solution)/shard_map/all_gather | solution.py:247
  76.6 21.3 %collective-permute-start.15 = (bf16[4,64,1152]{2,1,0:T(8,128)(2,1)S(1)}, bf16[4,64,1152]{2,1,0:T(8,128)(2,1)S(1)}, u32[]{:S(2)}, u32[]{:S(2)}) collective-permute-start(bf16[4,64,1152]{2,1,0:T(8,128)(2,1)S(1)} %bitcast_dynamic-update-slice_fusion.6), channel_id=1, source_target_pairs={{0,2},{2,0},{1,3},{3,1},{4,6},{6,4},{5,7},{7,5},{8,10},{10,8},{9,1... | collective-permute-start | bytes 1769480 | tf_op jit(solution)/shard_map/ppermute | solution.py:35
  77.8 19.0 %collective-permute-start.16 = (bf16[4,64,1152]{2,1,0:T(8,128)(2,1)S(1)}, bf16[4,64,1152]{2,1,0:T(8,128)(2,1)S(1)}, u32[]{:S(2)}, u32[]{:S(2)}) collective-permute-start(bf16[4,64,1152]{2,1,0:T(8,128)(2,1)S(1)} %bitcast_dynamic-update-slice_fusion.6), channel_id=1, source_target_pairs={{0,4},{4,0},{1,5},{5,1},{2,6},{6,2},{3,7},{7,3},{8,12},{12,8},{9,1... | collective-permute-start | bytes 1769480 | tf_op jit(solution)/shard_map/ppermute | solution.py:35
  78.9 15.3 %collective-permute-start.26 = (bf16[256,512]{1,0:T(8,128)(2,1)}, bf16[256,512]{1,0:T(8,128)(2,1)}, u32[]{:S(2)}, u32[]{:S(2)}) collective-permute-start(bf16[256,512]{1,0:T(8,128)(2,1)} %fusion.66), channel_id=1, source_target_pairs={{0,4},{4,0},{1,5},{5,1},{2,6},{6,2},{3,7},{7,3},{8,12},{12,8},{9,1... | collective-permute-start | bytes 786440 | tf_op jit(solution)/shard_map/ppermute | solution.py:35
  103.7 219.9 %all-gather.12.cloned.1.call-start = ((), (), s32[]{:S(2)}) async-start(), calls=%async_computation.9 | async-start | bytes 5242880 | tf_op jit(solution)/shard_map/all_gather | solution.py:247
  108.0 29.8 %collective-permute-start.19 = (bf16[16,64,1152]{2,1,0:T(8,128)(2,1)}, bf16[16,64,1152]{2,1,0:T(8,128)(2,1)}, u32[]{:S(2)}, u32[]{:S(2)}) collective-permute-start(bf16[16,64,1152]{2,1,0:T(8,128)(2,1)} %constant_dynamic-update-slice_fusion.5.own_ref), channel_id=1, source_target_pairs={{0,1},{1,0},{2,3},{3,2},{4,5},{5,4},{6,7},{7,6},{8,9},{9,8},{10,11... | collective-permute-start | bytes 7077896 | tf_op jit(solution)/shard_map/ppermute | solution.py:35
  110.6 38.8 %collective-permute-start.8 = (bf16[512,2048]{1,0:T(8,128)(2,1)}, bf16[512,2048]{1,0:T(8,128)(2,1)}, u32[]{:S(2)}, u32[]{:S(2)}) collective-permute-start(bf16[512,2048]{1,0:T(8,128)(2,1)} %constant_dynamic-update-slice_fusion.own_ref), channel_id=1, source_target_pairs={{0,1},{1,0},{2,3},{3,2},{4,5},{5,4},{6,7},{7,6},{8,9},{9,8},{10,11... | collective-permute-start | bytes 6291464 | tf_op jit(solution)/shard_map/ppermute | solution.py:35
  137.2 230.3 %all-gather.14.cloned.1.call-start = ((), (), s32[]{:S(2)}) async-start(), calls=%async_computation.10 | async-start | bytes 2621440 | tf_op jit(solution)/shard_map/all_gather | solution.py:247
  158.3 69.4 %collective-permute-start.21 = (bf16[128,2048]{1,0:T(8,128)(2,1)S(1)}, bf16[128,2048]{1,0:T(8,128)(2,1)}, u32[]{:S(2)}, u32[]{:S(2)}) collective-permute-start(bf16[128,2048]{1,0:T(8,128)(2,1)S(1)} %copy-done.30), channel_id=1, source_target_pairs={{0,2},{2,0},{1,3},{3,1},{4,6},{6,4},{5,7},{7,5},{8,10},{10,8},{9,1... | collective-permute-start | bytes 1572872 | tf_op jit(solution)/shard_map/ppermute | solution.py:35
  159.1 66.1 %collective-permute-start.22 = (bf16[128,2048]{1,0:T(8,128)(2,1)S(1)}, bf16[128,2048]{1,0:T(8,128)(2,1)}, u32[]{:S(2)}, u32[]{:S(2)}) collective-permute-start(bf16[128,2048]{1,0:T(8,128)(2,1)S(1)} %copy-done.30), channel_id=1, source_target_pairs={{0,4},{4,0},{1,5},{5,1},{2,6},{6,2},{3,7},{7,3},{8,12},{12,8},{9,1... | collective-permute-start | bytes 1572872 | tf_op jit(solution)/shard_map/ppermute | solution.py:35
  191.6 19.1 %collective-permute-start.27 = (bf16[512,256]{1,0:T(8,128)(2,1)S(1)}, bf16[512,256]{1,0:T(8,128)(2,1)S(1)}, u32[]{:S(2)}, u32[]{:S(2)}) collective-permute-start(bf16[512,256]{1,0:T(8,128)(2,1)S(1)} %get-tuple-element.197), channel_id=1, source_target_pairs={{0,8},{8,16},{16,24},{1,9},{9,17},{17,25},{2,10},{10,18},{18,26},{... | collective-permute-start | bytes 786440 | tf_op jit(solution)/shard_map/ppermute | solution.py:71
  210.7 25.3 %collective-permute-start.29 = (bf16[512,256]{1,0:T(8,128)(2,1)S(1)}, bf16[512,256]{1,0:T(8,128)(2,1)S(1)}, u32[]{:S(2)}, u32[]{:S(2)}) collective-permute-start(bf16[512,256]{1,0:T(8,128)(2,1)S(1)} %collective-permute-done.27), channel_id=1, source_target_pairs={{8,16},{16,24},{9,17},{17,25},{10,18},{18,26},{11,19},{19,27},{12,... | collective-permute-start | bytes 786440 | tf_op jit(solution)/shard_map/ppermute | solution.py:71
  211.5 24.4 %collective-permute-start.30 = (bf16[256,384]{1,0:T(8,128)(2,1)S(1)}, bf16[256,384]{1,0:T(8,128)(2,1)S(1)}, u32[]{:S(2)}, u32[]{:S(2)}) collective-permute-start(bf16[256,384]{1,0:T(8,128)(2,1)S(1)} %convert_element_type.391), channel_id=1, source_target_pairs={{0,8},{8,16},{16,24},{1,9},{9,17},{17,25},{2,10},{10,18},{18,26},{... | collective-permute-start | bytes 589832 | tf_op jit(solution)/shard_map/ppermute | solution.py:813
  235.9 41.1 %collective-permute-start.25 = (bf16[512,2048]{1,0:T(8,128)(2,1)}, bf16[512,2048]{1,0:T(8,128)(2,1)}, u32[]{:S(2)}, u32[]{:S(2)}) collective-permute-start(bf16[512,2048]{1,0:T(8,128)(2,1)} %constant_dynamic-update-slice_fusion.10), channel_id=1, source_target_pairs={{0,1},{1,0},{2,3},{3,2},{4,5},{5,4},{6,7},{7,6},{8,9},{9,8},{10,11... | collective-permute-start | bytes 6291464 | tf_op jit(solution)/shard_map/ppermute | solution.py:35
  236.0 18.1 %collective-permute-start.31 = (bf16[512,256]{1,0:T(8,128)(2,1)S(1)}, bf16[512,256]{1,0:T(8,128)(2,1)S(1)}, u32[]{:S(2)}, u32[]{:S(2)}) collective-permute-start(bf16[512,256]{1,0:T(8,128)(2,1)S(1)} %collective-permute-done.29), channel_id=1, source_target_pairs={{16,24},{17,25},{18,26},{19,27},{20,28},{21,29},{22,30},{23,31}} | collective-permute-start | bytes 786440 | tf_op jit(solution)/shard_map/ppermute | solution.py:71
  236.9 20.6 %collective-permute-start.33 = (bf16[256,384]{1,0:T(8,128)(2,1)S(1)}, bf16[256,384]{1,0:T(8,128)(2,1)S(1)}, u32[]{:S(2)}, u32[]{:S(2)}) collective-permute-start(bf16[256,384]{1,0:T(8,128)(2,1)S(1)} %add_convert_fusion.6), channel_id=1, source_target_pairs={{0,8},{8,16},{16,24},{1,9},{9,17},{17,25},{2,10},{10,18},{18,26},{... | collective-permute-start | bytes 589832 | tf_op jit(solution)/shard_map/ppermute | solution.py:813
  254.2 22.8 %collective-permute-start.32 = (bf16[4,512,256]{2,1,0:T(8,128)(2,1)S(1)}, bf16[4,512,256]{2,1,0:T(8,128)(2,1)S(1)}, u32[]{:S(2)}, u32[]{:S(2)}) collective-permute-start(bf16[4,512,256]{2,1,0:T(8,128)(2,1)S(1)} %bitcast_dynamic-update-slice_fusion.2), channel_id=1, source_target_pairs={{0,1},{1,0},{2,3},{3,2},{4,5},{5,4},{6,7},{7,6},{8,9},{9,8},{10,11... | collective-permute-start | bytes 3145736 | tf_op jit(solution)/shard_map/ppermute | solution.py:35
  314.9 160.8 %reduce-scatter.7.cloned.1.call-start = ((), (), s32[]{:S(2)}) async-start(), calls=%async_computation.11 | async-start | bytes 2621440 | tf_op jit(solution)/shard_map/reduce_scatter | solution.py:257
  345.5 27.1 %collective-permute-start.48 = (bf16[512,2048]{1,0:T(8,128)(2,1)}, bf16[512,2048]{1,0:T(8,128)(2,1)}, u32[]{:S(2)}, u32[]{:S(2)}) collective-permute-start(bf16[512,2048]{1,0:T(8,128)(2,1)} %constant_dynamic-update-slice_fusion.15), channel_id=1, source_target_pairs={{0,1},{1,0},{2,3},{3,2},{4,5},{5,4},{6,7},{7,6},{8,9},{9,8},{10,11... | collective-permute-start | bytes 6291464 | tf_op jit(solution)/shard_map/ppermute | solution.py:35
  388.6 231.0 %reduce-scatter.9.cloned.1.call-start = ((), (), s32[]{:S(2)}) async-start(), calls=%async_computation.12 | async-start | bytes 5242880 | tf_op jit(solution)/shard_map/reduce_scatter | solution.py:257
  395.8 15.9 %collective-permute-start.49 = (bf16[4,128,2048]{2,1,0:T(8,128)(2,1)}, bf16[4,128,2048]{2,1,0:T(8,128)(2,1)S(1)}, u32[]{:S(2)}, u32[]{:S(2)}) collective-permute-start(bf16[4,128,2048]{2,1,0:T(8,128)(2,1)} %bitcast.65), channel_id=1, source_target_pairs={{0,1},{1,0},{2,3},{3,2},{4,5},{5,4},{6,7},{7,6},{8,9},{9,8},{10,11... | collective-permute-start | bytes 6291464 | tf_op jit(solution)/shard_map/ppermute | solution.py:35
  406.3 253.9 %reduce-scatter.11.cloned.1.call-start = ((), (), s32[]{:S(2)}) async-start(), calls=%async_computation.13 | async-start | bytes 2621440 | tf_op jit(solution)/shard_map/reduce_scatter | solution.py:257
  465.6 33.6 %collective-permute-start.60 = (bf16[4,128,2048]{2,1,0:T(8,128)(2,1)}, bf16[4,128,2048]{2,1,0:T(8,128)(2,1)}, u32[]{:S(2)}, u32[]{:S(2)}) collective-permute-start(bf16[4,128,2048]{2,1,0:T(8,128)(2,1)} %bitcast.74), channel_id=1, source_target_pairs={{0,1},{1,0},{2,3},{3,2},{4,5},{5,4},{6,7},{7,6},{8,9},{9,8},{10,11... | collective-permute-start | bytes 6291464 | tf_op jit(solution)/shard_map/ppermute | solution.py:35
  471.8 197.7 %reduce-scatter.13.cloned.1.call-start = ((), (), s32[]{:S(2)}) async-start(), calls=%async_computation.14 | async-start | bytes 2621440 | tf_op jit(solution)/shard_map/reduce_scatter | solution.py:257
  502.6 69.0 %collective-permute-start.64 = (bf16[64,2048]{1,0:T(8,128)(2,1)}, bf16[64,2048]{1,0:T(8,128)(2,1)}, u32[]{:S(2)}, u32[]{:S(2)}) collective-permute-start(bf16[64,2048]{1,0:T(8,128)(2,1)} %get-tuple-element.222), channel_id=1, source_target_pairs={{0,4},{4,0},{1,5},{5,1},{2,6},{6,2},{3,7},{7,3},{8,12},{12,8},{9,1... | collective-permute-start | bytes 786440 | tf_op jit(solution)/shard_map/ppermute | solution.py:35
  503.6 68.1 %collective-permute-start.62 = (bf16[64,2048]{1,0:T(8,128)(2,1)}, bf16[64,2048]{1,0:T(8,128)(2,1)}, u32[]{:S(2)}, u32[]{:S(2)}) collective-permute-start(bf16[64,2048]{1,0:T(8,128)(2,1)} %get-tuple-element.224), channel_id=1, source_target_pairs={{0,2},{2,0},{1,3},{3,1},{4,6},{6,4},{5,7},{7,5},{8,10},{10,8},{9,1... | collective-permute-start | bytes 786440 | tf_op jit(solution)/shard_map/ppermute | solution.py:35
  505.0 80.4 %collective-permute-start.61 = (bf16[64,2048]{1,0:T(8,128)(2,1)}, bf16[64,2048]{1,0:T(8,128)(2,1)}, u32[]{:S(2)}, u32[]{:S(2)}) collective-permute-start(bf16[64,2048]{1,0:T(8,128)(2,1)} %get-tuple-element.225), channel_id=1, source_target_pairs={{0,4},{4,0},{1,5},{5,1},{2,6},{6,2},{3,7},{7,3},{8,12},{12,8},{9,1... | collective-permute-start | bytes 786440 | tf_op jit(solution)/shard_map/ppermute | solution.py:35
  526.1 23.4 %collective-permute-start.69 = (bf16[4,512,256]{2,1,0:T(8,128)(2,1)}, bf16[4,512,256]{2,1,0:T(8,128)(2,1)}, u32[]{:S(2)}, u32[]{:S(2)}) collective-permute-start(bf16[4,512,256]{2,1,0:T(8,128)(2,1)} %dynamic-slice_bitcast_fusion), channel_id=1, source_target_pairs={{0,1},{1,0},{2,3},{3,2},{4,5},{5,4},{6,7},{7,6},{8,9},{9,8},{10,11... | collective-permute-start | bytes 3145736 | tf_op jit(solution)/shard_map/ppermute | solution.py:35
  526.1 22.3 %collective-permute-start.70 = (bf16[256,384]{1,0:T(8,128)(2,1)}, bf16[256,384]{1,0:T(8,128)(2,1)}, u32[]{:S(2)}, u32[]{:S(2)}) collective-permute-start(bf16[256,384]{1,0:T(8,128)(2,1)} %convert_element_type.440), channel_id=1, source_target_pairs={{24,16},{16,8},{8,0},{25,17},{17,9},{9,1},{26,18},{18,10},{10,2},{... | collective-permute-start | bytes 589832 | tf_op jit(solution)/shard_map/ppermute | solution.py:928
  552.9 15.4 %collective-permute-start.71 = (bf16[512,256]{1,0:T(8,128)(2,1)}, bf16[512,256]{1,0:T(8,128)(2,1)}, u32[]{:S(2)}, u32[]{:S(2)}) collective-permute-start(bf16[512,256]{1,0:T(8,128)(2,1)} %dynamic-slice_bitcast_fusion.12), channel_id=1, source_target_pairs={{24,16},{25,17},{26,18},{27,19},{28,20},{29,21},{30,22},{31,23}} | collective-permute-start | bytes 786440 | tf_op jit(solution)/shard_map/ppermute | solution.py:959
  562.8 225.3 %reduce-scatter.17.cloned.1.call-start = ((), (), s32[]{:S(2)}) async-start(), calls=%async_computation.16 | async-start | bytes 1966080 | tf_op jit(solution)/shard_map/reduce_scatter | solution.py:257
  565.4 21.2 %collective-permute-start.66 = (bf16[64,2048]{1,0:T(8,128)(2,1)}, bf16[64,2048]{1,0:T(8,128)(2,1)S(1)}, u32[]{:S(2)}, u32[]{:S(2)}) collective-permute-start(bf16[64,2048]{1,0:T(8,128)(2,1)} %get-tuple-element.223), channel_id=1, source_target_pairs={{0,2},{2,0},{1,3},{3,1},{4,6},{6,4},{5,7},{7,5},{8,10},{10,8},{9,1... | collective-permute-start | bytes 786440 | tf_op jit(solution)/shard_map/ppermute | solution.py:35
  583.0 28.4 %collective-permute-start.73 = (bf16[256,384]{1,0:T(8,128)(2,1)}, bf16[256,384]{1,0:T(8,128)(2,1)S(1)}, u32[]{:S(2)}, u32[]{:S(2)}) collective-permute-start(bf16[256,384]{1,0:T(8,128)(2,1)} %add_convert_fusion.3), channel_id=1, source_target_pairs={{24,16},{16,8},{8,0},{25,17},{17,9},{9,1},{26,18},{18,10},{10,2},{... | collective-permute-start | bytes 589832 | tf_op jit(solution)/shard_map/ppermute | solution.py:957
  585.3 33.2 %collective-permute-start.77 = (bf16[512,256]{1,0:T(8,128)(2,1)S(1)}, bf16[512,256]{1,0:T(8,128)(2,1)S(1)}, u32[]{:S(2)}, u32[]{:S(2)}) collective-permute-start(bf16[512,256]{1,0:T(8,128)(2,1)S(1)} %bitcast_add_fusion.1), channel_id=1, source_target_pairs={{24,16},{16,8},{8,0},{25,17},{17,9},{9,1},{26,18},{18,10},{10,2},{... | collective-permute-start | bytes 786440 | tf_op jit(solution)/shard_map/ppermute | solution.py:959
  671.6 59.7 %collective-permute-start.91 = (bf16[256,512]{1,0:T(8,128)(2,1)}, bf16[256,512]{1,0:T(8,128)(2,1)}, u32[]{:S(2)}, u32[]{:S(2)}) collective-permute-start(bf16[256,512]{1,0:T(8,128)(2,1)} %dynamic-slice_bitcast_fusion.10), channel_id=1, source_target_pairs={{0,4},{4,0},{1,5},{5,1},{2,6},{6,2},{3,7},{7,3},{8,12},{12,8},{9,1... | collective-permute-start | bytes 786440 | tf_op jit(solution)/shard_map/ppermute | solution.py:35
  696.2 49.8 %collective-permute-start.78 = (bf16[4,128,2048]{2,1,0:T(8,128)(2,1)}, bf16[4,128,2048]{2,1,0:T(8,128)(2,1)}, u32[]{:S(2)}, u32[]{:S(2)}) collective-permute-start(bf16[4,128,2048]{2,1,0:T(8,128)(2,1)} %bitcast.106), channel_id=1, source_target_pairs={{0,1},{1,0},{2,3},{3,2},{4,5},{5,4},{6,7},{7,6},{8,9},{9,8},{10,11... | collective-permute-start | bytes 6291464 | tf_op jit(solution)/shard_map/ppermute | solution.py:35
  721.6 32.4 %collective-permute-start.92 = (bf16[4,4,64,1024]{3,2,1,0:T(8,128)(2,1)}, bf16[4,4,64,1024]{3,2,1,0:T(8,128)(2,1)}, u32[]{:S(2)}, u32[]{:S(2)}) collective-permute-start(bf16[4,4,64,1024]{3,2,1,0:T(8,128)(2,1)} %pad_maximum_fusion.1), channel_id=1, source_target_pairs={{0,1},{1,0},{2,3},{3,2},{4,5},{5,4},{6,7},{7,6},{8,9},{9,8},{10,11... | collective-permute-start | bytes 6291464 | tf_op jit(solution)/shard_map/ppermute | solution.py:35
  734.2 75.1 %reduce-scatter.15.cloned.1.call-start = ((), (), s32[]{:S(2)}) async-start(), calls=%async_computation.15 | async-start | bytes 655360 | tf_op jit(solution)/shard_map/reduce_scatter | solution.py:1022
  749.9 25.2 %collective-permute-start.84 = (bf16[64,2048]{1,0:T(8,128)(2,1)}, bf16[64,2048]{1,0:T(8,128)(2,1)}, u32[]{:S(2)}, u32[]{:S(2)}) collective-permute-start(bf16[64,2048]{1,0:T(8,128)(2,1)} %get-tuple-element.215), channel_id=1, source_target_pairs={{0,2},{2,0},{1,3},{3,1},{4,6},{6,4},{5,7},{7,5},{8,10},{10,8},{9,1... | collective-permute-start | bytes 786440 | tf_op jit(solution)/shard_map/ppermute | solution.py:35
  753.4 22.4 %collective-permute-start.79 = (bf16[64,2048]{1,0:T(8,128)(2,1)}, bf16[64,2048]{1,0:T(8,128)(2,1)}, u32[]{:S(2)}, u32[]{:S(2)}) collective-permute-start(bf16[64,2048]{1,0:T(8,128)(2,1)} %get-tuple-element.214), channel_id=1, source_target_pairs={{0,4},{4,0},{1,5},{5,1},{2,6},{6,2},{3,7},{7,3},{8,12},{12,8},{9,1... | collective-permute-start | bytes 786440 | tf_op jit(solution)/shard_map/ppermute | solution.py:35
  (156 other events, 1867.3 us)
Sparse Core Ops, SparseCore 0:
  20.9 54.1 all-gather.5
  76.7 35.1 all-gather.9
  114.1 44.7 all-gather.7
  160.3 85.2 all-gather.11
  315.0 52.4 all-gather.13
  388.7 42.5 reduce-scatter.6
  433.7 76.0 reduce-scatter.8
  512.1 48.5 reduce-scatter.10
  563.1 62.3 reduce-scatter.12
  734.4 35.6 reduce-scatter.16
  788.2 21.0 reduce-scatter.14

commit v3 on v2

v3 whole, which is shorter than its diff:
```python
import functools
import math

import jax
import jax.numpy as jnp
from jax import lax
from jax.experimental import pallas as pl
from jax.experimental.pallas import tpu as pltpu
from jax.sharding import Mesh
from jax.sharding import PartitionSpec as P

QH = 8
KVH = 2
HD = 128
MP = 64
CHUNK = 256
KEYS = 512
EPS = 1e-05
THETA = 100000000000.0
NEGATIVE = -1e30
EXACT = lax.Precision.HIGHEST
F32 = jnp.float32
BF16 = jnp.bfloat16
VMEM_BYTES = 56 * 1024 * 1024
SWAP = [(0, 1), (1, 0)]


def mm(a, b, ca, cb, precision=None):
    return lax.dot_general(
        a, b, (((ca,), (cb,)), ((), ())), preferred_element_type=F32, precision=precision
    )


def scoped(function):
    def named(name, *args, **kwargs):
        with jax.named_scope(name):
            return function(*args, **kwargs)

    return named


def swap(a, axis):
    return lax.ppermute(a, axis, SWAP)


def after(value, *earlier):
    return lax.optimization_barrier((value,) + earlier)[0]


@scoped
def from_below(values):
    count = lax.axis_size("z")
    return [
        lax.ppermute(values[far], "z", [(i, i + far) for i in range(count - far)])
        for far in range(1, count)
    ]


@scoped
def from_above(values):
    count = lax.axis_size("z")
    return [
        lax.ppermute(values[far], "z", [(i + far, i) for i in range(count - far)])
        for far in range(1, count)
    ]


@scoped
def from_ring(value):
    count = lax.axis_size("z")
    return [
        lax.ppermute(value, "z", [(i, (i + far) % count) for i in range(count)])
        for far in range(1, count)
    ]


def spots(dx, dy, dc):
    x, y, c = (lax.axis_index(name) for name in "xyc")
    return ((x ^ dx) * 2 + (y ^ dy)) * 2 + (c ^ dc)


@scoped
def cube_gather(piece, split=0, gate=None):
    by_x, by_y = swap(piece, "x"), swap(piece, "y")
    if gate is not None:
        by_x, by_y = after(by_x, gate), after(by_y, gate)
    low = swap(jnp.split(by_x, 2, split)[0], "y")
    high = swap(jnp.split(by_y, 2, split)[1], "x")
    far = [low, high] if split == 0 else [jnp.concatenate([low, high], axis=split)]
    own = jnp.concatenate([piece, by_y, by_x] + far, axis=0)
    return own, swap(own, "c"), by_x, low


@scoped
def cube_scatter(mine, other, gate=None):
    mine = mine + swap(other, "c")
    if gate is not None:
        mine = after(mine, gate)
    here, to_y, to_x, far = mine[0], mine[1], mine[2], mine[3]
    half = far.shape[0] // 2
    from_x, from_y = swap(far[:half], "x"), swap(far[half:], "y")
    x_low, y_high = swap(to_x[:half], "x"), swap(to_y[half:], "y")
    x_high = swap(to_x[half:] + from_y, "x")
    y_low = swap(to_y[:half] + from_x, "y")
    by_x = jnp.concatenate([x_low, x_high], 0).astype(F32)
    by_y = jnp.concatenate([y_low, y_high], 0).astype(F32)
    return here.astype(F32) + by_x + by_y, from_x


def place_ref():
    x, y, c = (lax.axis_index(name) for name in "xyc")
    return jnp.stack([x * 2 + y, c]).astype(jnp.int32)


def core_order(place, own, other):
    first = place[1] == 0
    return jnp.concatenate([jnp.where(first, own, other), jnp.where(first, other, own)], axis=0)


def core_split(place, values):
    half = values.shape[0] // 2
    first = place[1] == 0
    low, high = values[:half], values[half:]
    return jnp.where(first, low, high), jnp.where(first, high, low)


def near_spec(rows, cols):
    return pl.BlockSpec((rows, cols), lambda i, place: (i ^ place[0], 0))


def here_spec(rows, cols):
    return pl.BlockSpec((rows, cols), lambda i, place: (i, 0))


def settle_kernel(place, own_ref, other_ref, *out_refs):
    values = core_order(place, own_ref[...], other_ref[...])
    start = 0
    for out_ref in out_refs:
        out_ref[...] = values[:, start : start + out_ref.shape[1]]
        start += out_ref.shape[1]


def settle(own, other, rows, cuts):
    cols = own.shape[1]
    return call(
        settle_kernel,
        tuple(shape((8 * rows, n), own.dtype) for n in cuts),
        (4,),
        [near_spec(rows, cols)] * 2,
        tuple(here_spec(2 * rows, n) for n in cuts),
        prefetch=1,
    )(place_ref(), own, other)


def unsettle_kernel(place, *refs):
    values = jnp.concatenate([ref[...].astype(BF16) for ref in refs[:-2]], axis=1)
    refs[-2][...], refs[-1][...] = core_split(place, values)


def unsettle(parts, rows):
    cols = sum(a.shape[1] for a in parts)
    return call(
        unsettle_kernel,
        (shape((4 * rows, cols), BF16),) * 2,
        (4,),
        [near_spec(2 * rows, a.shape[1]) for a in parts],
        (here_spec(rows, cols),) * 2,
        prefetch=1,
    )(place_ref(), *parts)


def settle_groups_kernel(place, own_ref, other_ref, main_ref, misc_ref):
    groups, rows = own_ref.shape[1], own_ref.shape[2]
    first = place[1] == 0
    main = main_ref.shape[-1]
    for far in range(groups):
        own, other = own_ref[0, far], other_ref[0, far]
        at = lax.rem(place[2] - far + groups, groups)
        for core in range(2):
            values = jnp.where(first, own, other) if core == 0 else jnp.where(first, other, own)
            main_ref[pl.ds(at, 1), core] = values[None, :, :main]
            misc_ref[pl.ds(at, 1), core] = values[None, :, main:]


def settle_groups(own, other, main):
    _, groups, rows, cols = own.shape
    spec = pl.BlockSpec((1, groups, rows, cols), lambda i, place: (i ^ place[0], 0, 0, 0))
    outs = call(
        settle_groups_kernel,
        tuple(shape((groups, 8, rows, n), own.dtype) for n in (main, cols - main)),
        (4,),
        [spec, spec],
        tuple(
            pl.BlockSpec((groups, 2, rows, n), lambda i, place: (0, i, 0, 0))
            for n in (main, cols - main)
        ),
        prefetch=1,
    )(jnp.concatenate([place_ref(), lax.axis_index("z")[None]]), own, other)
    return tuple(out.reshape(groups * 8 * rows, -1) for out in outs)


def project_kernel(
    place, own_ref, other_ref, gain_ref, one_ref, two_ref, step_ref, cos_ref, sin_ref,
    normed_ref, q_ref, x_ref, kv_ref, bc_ref, dt_ref,
):
    rows = own_ref.shape[0] // 2
    flip = (place[0] & 1) == 1
    pieces = []
    own_low, own_high = own_ref[:rows], own_ref[rows:]
    other_low, other_high = other_ref[:rows], other_ref[rows:]
    pieces.append(
        core_order(
            place, jnp.where(flip, own_high, own_low), jnp.where(flip, other_high, other_low)
        )
    )
    pieces.append(
        core_order(
            place, jnp.where(flip, own_low, own_high), jnp.where(flip, other_low, other_high)
        )
    )
    values = jnp.concatenate(pieces, axis=0).astype(F32)
    scale = lax.rsqrt(jnp.mean(values * values, axis=1, keepdims=True) + EPS)
    normed = (values * scale * gain_ref[...]).astype(BF16)
    normed_ref[...] = normed
    cosine, sine = cos_ref[...], sin_ref[...]

    def turned(v):
        return (v * cosine + pltpu.roll(v, HD // 2, 1) * sine).astype(BF16)

    one = mm(normed, one_ref[...], 1, 0)
    q_ref[...] = turned(one[:, :HD])
    x_ref[...] = one[:, HD:].astype(BF16)
    at = pl.multiple_of(place[2] * HD, HD)
    lead = KVH * HD
    kv_w = jnp.concatenate([two_ref[:, pl.ds(at, HD)], two_ref[:, pl.ds(lead + at, HD)]], axis=1)
    kv = mm(normed, kv_w, 1, 0)
    kv_ref[:, :HD] = turned(kv[:, :HD])
    kv_ref[:, HD:] = kv[:, HD:].astype(BF16)
    bc_ref[...] = mm(normed, two_ref[:, 2 * lead :], 1, 0).astype(BF16)
    dt_ref[...] = mm(normed, step_ref[...], 1, 0).astype(BF16)


def project(kv_head, own, other, gain, w_one, w_two, w_dt, tables, rows):
    total = 8 * rows
    width = own.shape[1]
    cut = total // 2
    widths = (width, HD, w_one.shape[1] - HD, 2 * HD, w_two.shape[1] - 2 * KVH * HD, 128)
    near = pl.BlockSpec((2 * rows, width), lambda i, place: (i ^ (place[0] // 2), 0))

    def fixed(a):
        return pl.BlockSpec(a.shape, lambda i, place: (0, 0))

    return call(
        project_kernel,
        tuple(shape((total, n), BF16) for n in widths),
        (2,),
        [near, near, fixed(gain), fixed(w_one), fixed(w_two), fixed(w_dt)]
        + [here_spec(cut, HD)] * 2,
        tuple(here_spec(cut, n) for n in widths),
        prefetch=1,
    )(
        jnp.concatenate([place_ref(), kv_head[None].astype(jnp.int32)]),
        own, other, gain, w_one, w_two, w_dt, *tables,
    )


def grad_early_kernel(normed_ref, q_ref, z_ref, w_ref, out_ref, gain_ref):
    grad = jnp.concatenate([q_ref[...], z_ref[...]], axis=1)
    grad = mm(normed_ref[...], grad, 0, 0)
    out_ref[...] = grad.astype(BF16)
    q_cols, z_cols = q_ref.shape[1], z_ref.shape[1]
    w = jnp.concatenate([w_ref[:, :q_cols], w_ref[:, w_ref.shape[1] - z_cols :]], axis=1)
    gain = jnp.sum(grad * w.astype(F32), axis=1, keepdims=True)
    gain_ref[...] = jnp.broadcast_to(gain, gain_ref.shape)


def grad_early(groups, normed, q, z, w_all):
    total, width = normed.shape
    rows = width // groups

    def fixed(a):
        return pl.BlockSpec(a.shape, lambda i: (0, 0))

    def flow(cols):
        return pl.BlockSpec((rows, cols), lambda i: (i, 0))

    cols = q.shape[1] + z.shape[1]
    return call(
        grad_early_kernel,
        (shape((width, cols), BF16), shape((width, 128))),
        (groups,),
        [pl.BlockSpec((total, rows), lambda i: (0, i)), fixed(q), fixed(z), flow(w_all.shape[1])],
        (flow(cols), flow(128)),
    )(normed, q, z, w_all)


def grad_late_kernel(
    place, normed_ref, x_ref, kv_ref, bc_ref, dt_ref, w_ref, gain_ref, gain_two_ref,
    x_out_ref, own_ref, other_ref,
):
    rows = own_ref.shape[2]
    head = place[2]
    first = place[1] == 0
    normed = normed_ref[...]
    x_cols, bc_cols = x_ref.shape[1], bc_ref.shape[1]
    lead = 2 * KVH * HD
    start = w_ref.shape[1] - x_cols - 128 - bc_cols - lead
    grad_x = mm(normed, x_ref[...], 0, 0)
    x_out_ref[...] = grad_x.astype(BF16)
    gain = jnp.sum(grad_x * w_ref[:, start - x_cols : start].astype(F32), axis=1, keepdims=True)
    kv = mm(normed, kv_ref[...], 0, 0)
    zero = jnp.zeros((kv.shape[0], HD), F32)
    parts = []
    for part in (kv[:, :HD], kv[:, HD:]):
        parts += [jnp.where(head == i, part, zero) for i in range(KVH)]
    two = jnp.concatenate(parts + [mm(normed, bc_ref[...], 0, 0)], axis=1)
    wide = lead + bc_cols
    gain = gain + jnp.sum(two * w_ref[:, start : start + wide].astype(F32), axis=1, keepdims=True)
    dt = mm(normed, dt_ref[...], 0, 0) * w_ref[:, start + wide : start + wide + 128].astype(F32)
    gain = gain + jnp.sum(dt, axis=1, keepdims=True) + gain_ref[:, 0:1]
    lane = lax.broadcasted_iota(jnp.int32, (gain.shape[0], 128), 1)
    gains = jnp.where(lane == 0, gain, jnp.where(lane == 1, gain_two_ref[...], 0.0))
    grad = jnp.concatenate([two.astype(BF16), gains.astype(BF16)], axis=1)
    for spot in range(4):
        low = grad[2 * spot * rows : (2 * spot + 1) * rows]
        high = grad[(2 * spot + 1) * rows : (2 * spot + 2) * rows]
        at = pl.ds(spot ^ place[0], 1)
        own_ref[at, 0] = jnp.where(first, low, high)[None]
        other_ref[at, 0] = jnp.where(first, high, low)[None]


def grad_late(kv_head, groups, normed, x, kv, bc, dt, w_all, gain, gain_two):
    total, width = normed.shape
    block = width // groups
    rows = block // 8
    cols = 2 * KVH * HD + bc.shape[1] + 128

    def fixed(a):
        return pl.BlockSpec(a.shape, lambda i, place: (0, 0))

    def flow(n):
        return pl.BlockSpec((block, n), lambda i, place: (i, 0))

    return call(
        grad_late_kernel,
        (shape((width, x.shape[1]), BF16),) + (shape((4, groups, rows, cols), BF16),) * 2,
        (groups,),
        [pl.BlockSpec((total, block), lambda i, place: (0, i))]
        + [fixed(a) for a in (x, kv, bc, dt)]
        + [flow(w_all.shape[1]), flow(128), flow(1)],
        (flow(x.shape[1]),)
        + (pl.BlockSpec((4, 1, rows, cols), lambda i, place: (0, i, 0, 0)),) * 2,
        prefetch=1,
    )(
        jnp.concatenate([place_ref(), kv_head[None].astype(jnp.int32)]),
        normed, x, kv, bc, dt, w_all, gain, gain_two,
    )


def assemble_kernel(place, q_ref, x_ref, kv_ref, bc_ref, dt_ref, z_ref, own_ref, other_ref):
    head = place[2]
    zero = jnp.zeros((kv_ref.shape[0], HD), BF16)
    parts = []
    for part in (kv_ref[:, :HD], kv_ref[:, HD:]):
        parts += [jnp.where(head == i, part, zero) for i in range(KVH)]
    wide = jnp.concatenate(
        [q_ref[...], x_ref[...]] + parts + [bc_ref[...], dt_ref[...], z_ref[...]], axis=1
    )
    own_ref[...], other_ref[...] = core_split(place, wide)


def assemble(kv_head, rows, *parts):
    total = parts[0].shape[0]
    wide = sum(a.shape[1] for a in parts) + 2 * (KVH - 1) * HD
    return call(
        assemble_kernel,
        (shape((total // 2, wide), BF16),) * 2,
        (4,),
        [near_spec(2 * rows, a.shape[1]) for a in parts],
        (here_spec(rows, wide),) * 2,
        prefetch=1,
    )(jnp.concatenate([place_ref(), kv_head[None].astype(jnp.int32)]), *parts)


def halves(pack):
    x = lax.axis_index("x")
    own = lax.dynamic_index_in_dim(pack, x, 0, False)
    return own, lax.dynamic_index_in_dim(pack, x ^ 1, 0, False)


@scoped
def weight_gather(own, got):
    x = lax.axis_index("x")
    both = jnp.concatenate([jnp.where(x == 0, own, got), jnp.where(x == 0, got, own)], axis=0)
    return lax.all_gather(both, "z", axis=0, tiled=True)


def halves_in_order(own, got, axis):
    x = lax.axis_index("x")
    return jnp.concatenate([jnp.where(x == 0, own, got), jnp.where(x == 0, got, own)], axis=axis)


def both_halves(own, got):
    return halves_in_order(own, got, 1)


@scoped
def line_scatter(grad):
    return lax.psum_scatter(grad, "z", scatter_dimension=0, tiled=True)


@scoped
def own_and_got(part):
    x = lax.axis_index("x")
    part = part.reshape(2, -1, part.shape[1])
    got = swap(lax.dynamic_index_in_dim(part, x ^ 1, 0, False), "x")
    return lax.dynamic_index_in_dim(part, x, 0, False).astype(F32), got.astype(F32)


def lanes_of(cols, heads):
    rows = cols.shape[0]
    low = lax.broadcasted_iota(jnp.int32, (rows, 2 * MP), 1) < MP
    return jnp.concatenate(
        [
            jnp.where(low, cols[:, 2 * j : 2 * j + 1], cols[:, 2 * j + 1 : 2 * j + 2])
            for j in range(heads // 2)
        ],
        axis=1,
    )


def head_sums(values):
    wide = values.shape[1]
    lane = lax.broadcasted_iota(jnp.int32, (wide, 128), 0) // MP
    pick = (lane == lax.broadcasted_iota(jnp.int32, (wide, 128), 1)).astype(F32)
    return mm(values, pick, 1, 0, EXACT)


def softplus(v):
    return jnp.maximum(v, 0.0) + jnp.log1p(jnp.exp(-jnp.abs(v)))


def sigmoid(v):
    return 1.0 / (1.0 + jnp.exp(-v))


def chunk_common(bc_ref, dt_in_ref, dt_row_ref, par_ref, par_col_ref, seg_col_ref, seg_row_ref, wide):
    heads = wide // MP
    states = bc_ref.shape[1] // 2
    b_val = bc_ref[:, :states]
    c_val = bc_ref[:, states:]
    raw = dt_in_ref[...].astype(F32) + par_ref[0:1, :]
    dt = softplus(raw)
    rate = par_ref[1:2, :]
    raw_row = dt_row_ref[...].astype(F32) + par_col_ref[:, 0:1]
    e_row = -softplus(raw_row) * par_col_ref[:, 1:2]
    first = lax.broadcasted_iota(jnp.int32, (CHUNK, CHUNK), 0)
    second = lax.broadcasted_iota(jnp.int32, (CHUNK, CHUNK), 1)
    lower = (first >= second).astype(F32)
    run = mm(lower, -dt * rate, 1, 0, EXACT)
    run_row = mm(e_row, lower, 1, 1, EXACT)
    bias = jnp.where((first >= second) & (seg_col_ref[...] == seg_row_ref[0]), 0.0, NEGATIVE)
    return heads, b_val, c_val, raw, dt, rate, run, run_row, bias, lower


def mamba_local_kernel(
    x_in_ref, bc_in_ref, dt_in_ref, dt_row_ref, par_ref, par_col_ref, skip_ref, seg_col_ref, seg_row_ref, marks_ref,
    y_ref, run_ref, held_ref, total_ref, starts_ref, state, base_run,
):
    step = pl.program_id(0)
    wide = skip_ref.shape[1]
    heads, b_val, c_val, raw, dt, rate, run, run_row, bias, _ = chunk_common(
        bc_in_ref, dt_in_ref, dt_row_ref, par_ref, par_col_ref, seg_col_ref, seg_row_ref, wide
    )

    @pl.when(step == 0)
    def _():
        state[...] = jnp.zeros_like(state)
        base_run[...] = jnp.zeros_like(base_run)

    x_val = x_in_ref[...].astype(F32)
    seg = seg_col_ref[...]
    label = marks_ref[step]
    final = marks_ref[step + 1]
    held = state[...]
    starts_ref[0] = held
    x_dt = x_val * lanes_of(dt, heads)
    x_dt_b = x_dt.astype(BF16)
    entry = jnp.where(seg == label, jnp.exp(run), 0.0)
    last = run[CHUNK - 1 : CHUNK, :]
    tail = jnp.where(seg == final, jnp.exp(last - run), 0.0)
    y_val = skip_ref[...] * x_val
    y_val = y_val + lanes_of(entry, heads) * mm(c_val, held.astype(BF16), 1, 0)
    gram = mm(c_val, b_val, 1, 1)
    low = lax.broadcasted_iota(jnp.int32, (CHUNK, 2 * MP), 1) < MP
    parts = []
    for pair in range(heads // 2):
        both = x_dt_b[:, pair * 2 * MP : (pair + 1) * 2 * MP]
        outs = []
        for h in (2 * pair, 2 * pair + 1):
            decay = jnp.exp(run[:, h : h + 1] - run_row[h : h + 1, :] + bias)
            outs.append(mm((decay * gram).astype(BF16), both, 1, 0))
        parts.append(jnp.where(low, outs[0], outs[1]))
    y_ref[...] = y_val + jnp.concatenate(parts, axis=1)
    fresh = mm(b_val, (x_dt * lanes_of(tail, heads)).astype(BF16), 0, 0)
    kept = jnp.where(label == final, jnp.exp(last), 0.0)
    new = lanes_of(jnp.broadcast_to(kept, (8, 128)), heads)[0:1] * held + fresh
    state[...] = new
    held_ref[...] = new
    run_all = run + base_run[0:1, :]
    run_ref[...] = run_all
    base_run[...] = jnp.broadcast_to(run_all[CHUNK - 1 : CHUNK, :], base_run.shape)
    total_ref[...] = jnp.exp(base_run[...])


def mamba_close_kernel(bc_in_ref, gate_ref, y_ref, run_ref, seg_col_ref, held_ref, marks_ref, out_ref, full_ref):
    wide = y_ref.shape[1]
    heads = wide // MP
    states = held_ref.shape[0]
    c_val = bc_in_ref[:, states:]
    entry = jnp.where(seg_col_ref[...] == marks_ref[0], jnp.exp(run_ref[...]), 0.0)
    y_val = y_ref[...] + lanes_of(entry, heads) * mm(c_val, held_ref[...].astype(BF16), 1, 0)
    full_ref[...] = y_val
    z_val = gate_ref[...].astype(F32)
    out_ref[...] = (y_val * z_val * sigmoid(z_val)).astype(BF16)


def mamba_grad_state_kernel(
    bc_in_ref, gate_ref, y_ref, grad_ref, run_ref, seg_col_ref, marks_ref, out_ref, gate_grad_ref
):
    wide = grad_ref.shape[1]
    heads = wide // MP
    states = out_ref.shape[0]
    c_val = bc_in_ref[:, states:]
    z_val = gate_ref[...].astype(F32)
    entry = jnp.where(seg_col_ref[...] == marks_ref[0], jnp.exp(run_ref[...]), 0.0)
    grad = grad_ref[...].astype(F32)
    sig = sigmoid(z_val)
    grad_y = grad * z_val * sig
    gate_grad_ref[...] = (grad * y_ref[...] * (sig * (1.0 + z_val * (1.0 - sig)))).astype(BF16)

    @pl.when(pl.program_id(0) == 0)
    def _():
        out_ref[...] = jnp.zeros_like(out_ref)

    out_ref[...] += mm(c_val, (grad_y * lanes_of(entry, heads)).astype(BF16), 0, 0)


def mamba_grad_near_kernel(
    x_in_ref, bc_in_ref, dt_in_ref, dt_row_ref, par_ref, par_col_ref, skip_ref, seg_col_ref, seg_row_ref, marks_ref,
    gate_ref, run_ref, starts_ref, held_ref, grad_ref,
    x_grad_ref, b_ref, c_ref, e_ref, carry_ref, skip_sum_ref,
):
    step = pl.program_id(0)
    wide = skip_ref.shape[1]
    heads, b_val, c_val, raw, dt, rate, run, run_row, bias, lower = chunk_common(
        bc_in_ref, dt_in_ref, dt_row_ref, par_ref, par_col_ref, seg_col_ref, seg_row_ref, wide
    )

    @pl.when(step == 0)
    def _():
        skip_sum_ref[...] = jnp.zeros_like(skip_sum_ref)

    z_val = gate_ref[...].astype(F32)
    x_val = x_in_ref[...].astype(F32)
    label = marks_ref[step]
    before = run_ref[0:1, :] - run[0:1, :]
    carry = jnp.where(label == marks_ref[0], jnp.exp(before), 0.0)
    held = starts_ref[0] + lanes_of(jnp.broadcast_to(carry, (8, 128)), heads)[0:1] * held_ref[...]
    held_b = held.astype(BF16)
    grad_y = grad_ref[...].astype(F32) * z_val * sigmoid(z_val)
    dt_wide = lanes_of(dt, heads)
    x_dt_b = (x_val * dt_wide).astype(BF16)
    entry = lanes_of(jnp.where(seg_col_ref[...] == label, jnp.exp(run), 0.0), heads)
    grad_in = (entry * grad_y).astype(BF16)
    run_grad = head_sums(grad_y * entry * mm(c_val, held_b, 1, 0))
    grad_c = mm(grad_in, held_b, 1, 1)
    carry_ref[0] = mm(c_val, grad_in, 0, 0)
    gram = mm(c_val, b_val, 1, 1)
    low = lax.broadcasted_iota(jnp.int32, (CHUNK, 2 * MP), 1) < MP
    lane = lax.broadcasted_iota(jnp.int32, (CHUNK, 128), 1)
    grad_y_b = grad_y.astype(BF16)
    none = jnp.zeros((CHUNK, 2 * MP), BF16)
    gram_grad = None
    parts, cols = [], []
    for pair in range(heads // 2):
        span = slice(pair * 2 * MP, (pair + 1) * 2 * MP)
        outs = []
        for h in (2 * pair, 2 * pair + 1):
            mask = low if h % 2 == 0 else ~low
            decay = jnp.exp(run[:, h : h + 1] - run_row[h : h + 1, :] + bias)
            mixing = (decay * gram).astype(BF16)
            outs.append(mm(mixing, grad_y_b[:, span], 0, 0))
            mixing_grad = mm(jnp.where(mask, grad_y_b[:, span], none), x_dt_b[:, span], 1, 1)
            weighted = mixing_grad * decay
            gram_grad = weighted if gram_grad is None else gram_grad + weighted
            weighted = weighted * gram
            run_grad = run_grad + jnp.where(
                lane == h, jnp.sum(weighted, axis=1, keepdims=True), 0.0
            )
            cols.append(jnp.sum(weighted, axis=0, keepdims=True))
        parts.append(jnp.where(low, outs[0], outs[1]))
    gram_grad_b = gram_grad.astype(BF16)
    c_ref[...] = (grad_c + mm(gram_grad_b, b_val, 1, 0)).astype(BF16)
    b_ref[...] = mm(gram_grad_b, c_val, 0, 0)
    x_grad_ref[...] = jnp.concatenate(parts, axis=1)
    col_grad = jnp.concatenate(cols + [jnp.zeros((128 - heads, CHUNK), F32)], axis=0)
    e_ref[...] = mm(lower, run_grad, 0, 0, EXACT) - mm(lower, col_grad, 0, 1, EXACT)
    skip_sum_ref[0:1, :] += jnp.sum(grad_y * x_val, axis=0, keepdims=True)


def mamba_grad_kernel(
    x_in_ref, bc_in_ref, dt_in_ref, dt_row_ref, par_ref, par_col_ref, skip_ref, seg_col_ref, seg_row_ref, marks_ref,
    gate_ref, run_ref, starts_ref, held_ref, grad_ref,
    x_grad_ref, b_grad_ref, c_grad_ref, e_grad_ref, carry_ref, deep_ref,
    x_ref, bc_ref, dt_ref, sums_ref, deep,
):
    step = pl.num_programs(0) - 1 - pl.program_id(0)
    wide = skip_ref.shape[1]
    heads = wide // MP
    states = b_grad_ref.shape[1]
    b_val = bc_in_ref[:, :states]
    raw = dt_in_ref[...].astype(F32) + par_ref[0:1, :]
    dt = softplus(raw)
    rate = par_ref[1:2, :]
    first = lax.broadcasted_iota(jnp.int32, (CHUNK, CHUNK), 0)
    second = lax.broadcasted_iota(jnp.int32, (CHUNK, CHUNK), 1)
    lower = (first >= second).astype(F32)
    run = run_ref[...]

    @pl.when(pl.program_id(0) == 0)
    def _():
        deep[...] = deep_ref[...]
        sums_ref[...] = jnp.zeros_like(sums_ref)

    z_val = gate_ref[...].astype(F32)
    x_val = x_in_ref[...].astype(F32)
    seg = seg_col_ref[...]
    label = marks_ref[step]
    final = marks_ref[step + 1]
    last = run[CHUNK - 1 : CHUNK, :]
    e_first = -dt[0:1, :] * rate
    before = run[0:1, :] - e_first
    carry = jnp.where(label == marks_ref[0], jnp.exp(before), 0.0)
    held = starts_ref[0] + lanes_of(jnp.broadcast_to(carry, (8, 128)), heads)[0:1] * held_ref[...]
    after_b = deep[...].astype(BF16)
    grad_y = grad_ref[...].astype(F32) * z_val * sigmoid(z_val)
    dt_wide = lanes_of(dt, heads)
    tail = lanes_of(jnp.where(seg == final, jnp.exp(last - run), 0.0), heads)
    x_tail = x_val * dt_wide * tail
    back = mm(b_val, after_b, 1, 0)
    bc_ref[:, :states] = (b_grad_ref[...] + mm(x_tail.astype(BF16), after_b, 1, 1)).astype(BF16)
    bc_ref[:, states:] = c_grad_ref[...]
    tail_grad = head_sums(x_tail * back)
    kept = jnp.where(label == final, jnp.exp(last - before), 0.0)
    kept_wide = lanes_of(jnp.broadcast_to(kept, (8, 128)), heads)[0:1]
    kept_grad = head_sums(
        jnp.broadcast_to(kept_wide * jnp.sum(deep[...] * held, axis=0, keepdims=True), (8, wide))
    )
    last_grad = jnp.sum(tail_grad, axis=0, keepdims=True) + kept_grad[0:1]
    deep[...] = kept_wide * deep[...] + carry_ref[0]
    x_dt_grad = x_grad_ref[...] + tail * back
    x_ref[...] = (x_dt_grad * dt_wide + skip_ref[...] * grad_y).astype(BF16)
    e_grad = e_grad_ref[...] - mm(lower, tail_grad, 0, 0, EXACT) + last_grad
    dt_grad = head_sums(x_dt_grad * x_val) - rate * e_grad
    raw_grad = dt_grad * sigmoid(raw)
    lane = lax.broadcasted_iota(jnp.int32, (CHUNK, 128), 1)
    dt_ref[...] = jnp.where(lane < heads, raw_grad, 0.0).astype(BF16)
    sums_ref[0:1, :] += jnp.sum(-rate * dt * e_grad, axis=0, keepdims=True)
    sums_ref[1:2, :] += jnp.sum(raw_grad, axis=0, keepdims=True)


def seen(kseg_ref, qseg, first_query, block):
    rows = qseg.shape[0]
    key_pos = block * KEYS + lax.broadcasted_iota(jnp.int32, (rows, KEYS), 1)
    query_pos = first_query + lax.broadcasted_iota(jnp.int32, (rows, KEYS), 0)
    return (key_pos <= query_pos) & (kseg_ref[pl.ds(block, 1), :] == qseg)


def key_span(block, where_ref, groups):
    far = where_ref[0] - block // 2
    at = jnp.where((block & 1) == where_ref[1], far, groups + far)
    return pl.ds(pl.multiple_of(at * KEYS, KEYS), KEYS)


def attend_kernel(low_ref, high_ref, start_ref, where_ref, q_ref, kv_ref, kseg_ref, qseg_ref, att_ref, log_ref):
    step = pl.program_id(0)
    rows = q_ref.shape[0]
    query = q_ref[...]
    qseg = qseg_ref[...]
    first_query = start_ref[0] + step * rows
    scale = HD**-0.5

    def visit(block, state):
        peak, total, acc = state
        span = key_span(block, where_ref, kv_ref.shape[0] // (2 * KEYS))
        scores = mm(query, kv_ref[span, :HD], 1, 1) * scale
        scores = jnp.where(seen(kseg_ref, qseg, first_query, block), scores, NEGATIVE)
        new_peak = jnp.maximum(peak, jnp.max(scores, axis=1, keepdims=True))
        weights = jnp.exp(scores - new_peak)
        rescale = jnp.exp(peak - new_peak)
        total = total * rescale + jnp.sum(weights, axis=1, keepdims=True)
        acc = acc * rescale + mm(weights.astype(BF16), kv_ref[span, HD:], 1, 0)
        return new_peak, total, acc

    peak, total, acc = lax.fori_loop(
        low_ref[step],
        high_ref[step],
        visit,
        (
            jnp.full((rows, 1), NEGATIVE, F32),
            jnp.zeros((rows, 1), F32),
            jnp.zeros((rows, HD), F32),
        ),
    )
    att_ref[...] = acc / total
    log_ref[...] = jnp.broadcast_to(peak + jnp.log(total), log_ref.shape)


def attend_grad_kernel(
    low_ref, high_ref, start_ref, where_ref, q_ref, kv_ref, kseg_ref, qseg_ref, att_ref, log_ref,
    grad_ref, dq_ref, dkv_ref, sums,
):
    step = pl.program_id(0)
    rows = q_ref.shape[0]
    query = q_ref[...]
    grad = grad_ref[...]
    qseg = qseg_ref[...]
    log_total = log_ref[:, 0:1]
    first_query = start_ref[0] + step * rows
    scale = HD**-0.5
    delta = jnp.sum(grad.astype(F32) * att_ref[...], axis=1, keepdims=True)

    @pl.when(step == 0)
    def _():
        sums[...] = jnp.zeros_like(sums)

    def visit(block, acc):
        span = key_span(block, where_ref, kv_ref.shape[0] // (2 * KEYS))
        keys = kv_ref[span, :HD]
        scores = mm(query, keys, 1, 1) * scale - log_total
        scores = jnp.where(seen(kseg_ref, qseg, first_query, block), scores, NEGATIVE)
        probs = jnp.exp(scores)
        probs_grad = mm(grad, kv_ref[span, HD:], 1, 1)
        scores_grad = (probs * (probs_grad - delta)).astype(BF16)
        sums[span, :HD] += mm(scores_grad, query, 0, 0)
        sums[span, HD:] += mm(probs.astype(BF16), grad, 0, 0)
        return acc + mm(scores_grad, keys, 1, 0)

    acc = lax.fori_loop(low_ref[step], high_ref[step], visit, jnp.zeros((rows, HD), F32))
    dq_ref[...] = acc * scale

    @pl.when(step == pl.num_programs(0) - 1)
    def _():
        dkv_ref[:, :HD] = (sums[:, :HD] * scale).astype(BF16)
        dkv_ref[:, HD:] = sums[:, HD:].astype(BF16)


def call(kernel, out_shape, grid, in_specs, out_specs, scratch=(), prefetch=0, cost=None):
    return pl.pallas_call(
        kernel,
        out_shape=out_shape,
        grid_spec=pltpu.PrefetchScalarGridSpec(
            num_scalar_prefetch=prefetch,
            grid=grid,
            in_specs=in_specs,
            out_specs=out_specs,
            scratch_shapes=list(scratch),
        ),
        compiler_params=pltpu.CompilerParams(
            vmem_limit_bytes=VMEM_BYTES, dimension_semantics=("arbitrary",) * len(grid)
        ),
        cost_estimate=cost,
        name=kernel.__name__,
    )


def shape(dims, dtype=F32):
    return jax.ShapeDtypeStruct(dims, dtype)


def rope_tables(positions):
    half = HD // 2
    frequency = jnp.exp(jnp.arange(half, dtype=F32) * (-2.0 * math.log(THETA) / HD))
    angle = positions.astype(F32)[:, None] * frequency[None, :]
    cosine, sine = jnp.cos(angle), jnp.sin(angle)
    return jnp.concatenate([cosine, cosine], 1), jnp.concatenate([-sine, sine], 1)


def rope(values, tables):
    cosine, sine = tables
    return values * cosine + jnp.concatenate([values[:, HD // 2 :], values[:, : HD // 2]], 1) * sine


def rope_back(values, tables):
    cosine, sine = tables
    return values * cosine - jnp.concatenate([values[:, HD // 2 :], values[:, : HD // 2]], 1) * sine


def unit(values):
    return values * lax.rsqrt(jnp.mean(values * values, axis=-1, keepdims=True) + EPS)


def norm_back(values, gain, grad):
    scale = lax.rsqrt(jnp.mean(values * values, axis=-1, keepdims=True) + EPS)
    u = values * scale
    inner = jnp.mean(grad * gain * u, axis=-1, keepdims=True)
    return scale * (grad * gain - u * inner), jnp.sum(grad * u, axis=0)


def shards(
    tokens, seg_ids, cotangent, gain_mix, q_w, kv_w, zx_w, dt_w, bc_w,
    a_log, dt_bias, skip, wo_w, wm_w, gain_ff, gu_w, down_w,
):
    groups = lax.axis_size("z")
    z, x, y, c = (lax.axis_index(name) for name in "zxyc")
    own_rows, width = tokens.shape
    group = 8 * own_rows
    rows_w = q_w.shape[0]
    part = kv_w.shape[0]
    ratio = rows_w // part
    heads = dt_w.shape[1] // 2
    wide = heads * MP
    states = bc_w.shape[1] // 2
    ff = gu_w.shape[2] // 2
    inner = q_w.shape[1] // 2
    steps = group // CHUNK

    zx_cut = zx_w.reshape(rows_w, 2, 2, wide).transpose(1, 2, 0, 3)
    pack_z = zx_cut[0]
    pack_one = jnp.concatenate([q_w.reshape(rows_w, 2, inner).transpose(1, 0, 2), zx_cut[1]], axis=2)
    pack_out = jnp.concatenate(
        [
            wo_w.reshape(rows_w, 2, inner).transpose(1, 0, 2),
            wm_w.reshape(rows_w, 2, wide).transpose(1, 0, 2),
        ],
        axis=2,
    )
    pack_gu = gu_w.reshape(rows_w, 2, 2, ff).transpose(2, 0, 1, 3).reshape(2, rows_w, 2 * ff)
    pack_down = down_w.reshape(rows_w, 2, ff).transpose(1, 0, 2)
    kv_cols = kv_w.shape[1] * kv_w.shape[2]
    bc_cols = bc_w.shape[1]
    lead = kv_cols + bc_cols
    dt_cols = dt_w.shape[1]
    dt_part = dt_w.reshape(ratio, part, dt_cols).transpose(1, 0, 2).reshape(part, ratio * dt_cols)
    pack_two = jnp.concatenate(
        [kv_w.reshape(part, kv_cols), bc_w, gain_mix[:, None], gain_ff[:, None], dt_part], axis=1
    )
    used = pack_two.shape[1]
    total_cols = -(-used // 128) * 128
    pack_two = jnp.pad(pack_two, ((0, 0), (0, total_cols - used)))

    def put_two(out, at, number, value):
        return lax.dynamic_update_slice(out, value[None], (at, 0, 0))

    own_one, give_one = halves(pack_one)
    own_out, give_out = halves(jnp.concatenate([pack_out, pack_z], axis=2))
    own_ff, give_ff = halves(jnp.concatenate([pack_gu, pack_down], axis=2))
    two_far = from_ring("whole_rows", pack_two)
    seg_pair = jnp.zeros((2, seg_ids.shape[0]), jnp.int32)
    seg_pair = lax.dynamic_update_index_in_dim(seg_pair, seg_ids, x, 0)
    seg_pair = lax.dynamic_update_index_in_dim(seg_pair, swap(seg_ids, "x"), x ^ 1, 0)
    seg_own = seg_pair.reshape(1, group)
    seg_far = from_ring("ids", seg_own)
    two = jnp.stack([pack_two] + two_far)[None]
    got_one = swap(give_one, "x")
    own_one, got_one, two, *seg_far = lax.optimization_barrier((own_one, got_one, two, *seg_far))
    seg_all = jnp.zeros((groups, group), jnp.int32)
    for far, got in enumerate([seg_own, *seg_far]):
        seg_all = lax.dynamic_update_slice(seg_all, got, ((z - far + groups) % groups, 0))
    w_one = weight_gather("w_one", own_one, got_one)
    two_own, two_other, _, two_low = cube_gather("whole_rows", two, 1)
    rows_own, rows_other, *_ = cube_gather("tokens", after(tokens, two_low))
    w_two, misc = settle_groups(two_own, two_other, lead)
    w_mix = weight_gather("w_mix", own_out, swap(after(give_out, rows_own), "x"))
    w_out, w_z = w_mix[:, : inner + wide], w_mix[:, inner + wide :]
    got_ff = swap(after(give_ff, rows_own), "x")
    w_ff = weight_gather("w_ff", own_ff, got_ff)
    w_gu, w_down = w_ff[:, : 2 * ff], w_ff[:, 2 * ff :]
    segment = seg_own.astype(F32)
    seg_col = segment.reshape(group, 1)
    seg_row = segment.reshape(steps, 1, CHUNK)
    previous = lax.dynamic_index_in_dim(seg_all, jnp.maximum(z - 1, 0), 0, False)[group - 1]
    in_label = jnp.where(z > 0, previous, -1).astype(F32)
    marks = jnp.concatenate([in_label[None], segment[0, CHUNK - 1 :: CHUNK]])

    gain_one = misc[:, 0].astype(F32)
    gain_two = misc[:, 1].astype(F32)
    dt_all = misc[:, 2 : 2 + ratio * dt_cols].reshape(
        groups, 2, 4, part, ratio, 2, heads
    )
    dt_own = lax.dynamic_index_in_dim(dt_all, y * 2 + c, 2, False)
    dt_own = lax.dynamic_index_in_dim(dt_own, x, 4, False)
    w_dt = dt_own.transpose(0, 1, 3, 2, 4).reshape(width, heads)
    kv_head = ((y * 2 + c) * 2 + x) * (inner // HD) // (QH // KVH)
    w_dt = jnp.pad(w_dt, ((0, 0), (0, 128 - heads)))

    positions = z * group + jnp.arange(group, dtype=jnp.int32)
    tables = rope_tables(positions)
    normed, query, x_in, kv_own, bc_in, dt_in = project(
        kv_head, rows_own, rows_other, gain_one[None, :], w_one, w_two, w_dt, tables, own_rows
    )
    half, quarter = group // 2, group // 4
    kv_half = lax.dynamic_slice_in_dim(kv_own, c * half, half, 0)
    kv_quarter = lax.dynamic_slice_in_dim(kv_own, c * half + x * quarter, quarter, 0)
    kv_far = from_below("kv", [kv_quarter] * groups)
    x_in = after(x_in, got_ff)
    gate_in = mm(normed, w_z, 1, 0).astype(BF16)

    dt_row = jnp.pad(dt_in[:, :8].T, ((0, 8), (0, 0)))
    pad = ((0, 128 - heads),)

    def pick(values):
        return lax.dynamic_slice_in_dim(values, x * heads, heads, 0)

    rates = jnp.exp(pick(a_log))
    params = jnp.stack([jnp.pad(pick(dt_bias), pad), jnp.pad(rates, pad)])
    params = jnp.pad(params, ((0, 6), (0, 0)))
    params_col = jnp.pad(
        jnp.stack([pick(dt_bias), rates], axis=1), ((0, 16 - heads), (0, 126))
    )
    skip_wide = jnp.repeat(pick(skip), MP)[None, :]

    def flow(cols, back=False):
        at = (lambda i: (steps - 1 - i, 0)) if back else (lambda i: (i, 0))
        return pl.BlockSpec((CHUNK, cols), at)

    def chunk_specs(back=False):
        def turn(i):
            return steps - 1 - i if back else i

        return [
            flow(wide, back),
            flow(2 * states, back),
            flow(128, back),
            pl.BlockSpec((16, CHUNK), lambda i: (0, turn(i))),
            pl.BlockSpec((8, 128), lambda i: (0, 0)),
            pl.BlockSpec((16, 128), lambda i: (0, 0)),
            pl.BlockSpec((1, wide), lambda i: (0, 0)),
            flow(1, back),
            pl.BlockSpec((1, 1, CHUNK), lambda i: (turn(i), 0, 0)),
            pl.BlockSpec(memory_space=pltpu.SMEM),
        ]

    whole = pl.BlockSpec((states, wide), lambda i: (0, 0))
    smem = pl.BlockSpec(memory_space=pltpu.SMEM)
    chunk_args = (x_in, bc_in, dt_in, dt_row, params, params_col, skip_wide, seg_col, seg_row, marks)
    y_local, run, held_own, total, starts = call(
        mamba_local_kernel,
        (
            shape((group, wide)),
            shape((group, 128)),
            shape((states, wide)),
            shape((8, 128)),
            shape((steps, states, wide)),
        ),
        (steps,),
        chunk_specs(),
        (
            flow(wide),
            flow(128),
            whole,
            pl.BlockSpec((8, 128), lambda i: (0, 0)),
            pl.BlockSpec((1, states, wide), lambda i: (i, 0, 0)),
        ),
        [pltpu.VMEM((states, wide), F32), pltpu.VMEM((8, 128), F32)],
    )(*chunk_args)
    joined = jnp.where(in_label == segment[0, group - 1], 1.0, 0.0)
    factor = jnp.repeat(total[0, :heads] * joined, MP)[None, :]
    factor_rows = jnp.broadcast_to(factor, (16, wide))
    held_sent = jnp.concatenate([held_own, factor_rows], axis=0).astype(BF16)
    held_sent, *kv_far = lax.optimization_barrier((held_sent, *kv_far))
    held_far = from_below("held", [held_sent] * groups)
    kv_far = jnp.stack(kv_far)
    kv_far = halves_in_order(kv_far, swap(kv_far, "x"), 1).reshape(-1, 2 * HD)
    kv_near = jnp.concatenate([kv_half, kv_far], axis=0)
    cot_own, cot_other, *_ = cube_gather("cotangent", after(cotangent, kv_near))
    kv_all = jnp.concatenate([kv_near, swap(kv_near, "c")], axis=0)
    w_all = jnp.concatenate([w_one, w_two, w_dt, w_z], axis=1)
    query, w_all, *held_far = lax.optimization_barrier((query, w_all, *held_far))
    in_held = jnp.zeros((states, wide), F32)
    for got in reversed(held_far):
        got = got.astype(F32)
        in_held = got[:states] + got[states : states + 1] * in_held

    q_rows = CHUNK
    blocks = group // q_rows
    first_rows = z * group + q_rows * jnp.arange(blocks, dtype=jnp.int32)
    first_seg = seg_own[0, ::q_rows]
    reached = jnp.arange(groups * group, dtype=jnp.int32)[None, :] < (z + 1) * group
    earlier = (seg_all.reshape(1, -1) < first_seg[:, None]) & reached
    low = jnp.sum(earlier, axis=1, dtype=jnp.int32) // KEYS
    high = (first_rows + q_rows - 1) // KEYS + 1
    start = (z * group)[None].astype(jnp.int32)
    where = jnp.stack([z, c]).astype(jnp.int32)
    key_seg = seg_all.astype(F32).reshape(groups * group // KEYS, KEYS)

    def rows_spec(cols):
        return pl.BlockSpec((q_rows, cols), lambda i, *_: (i, 0))

    def full_spec(a):
        return pl.BlockSpec(a.shape, lambda i, *_: (0, 0))

    att_full, log_total = call(
        attend_kernel,
        (shape((group, HD)), shape((group, 128))),
        (blocks,),
        [rows_spec(HD), full_spec(kv_all), full_spec(key_seg), rows_spec(1)],
        (rows_spec(HD), rows_spec(128)),
        prefetch=4,
    )(low, high, start, where, query, kv_all, key_seg, seg_col)

    ssm_out, y_full = call(
        mamba_close_kernel,
        (shape((group, wide), BF16), shape((group, wide))),
        (steps,),
        [flow(2 * states), flow(wide), flow(wide), flow(128), flow(1), whole, smem],
        (flow(wide), flow(wide)),
    )(bc_in, gate_in, y_local, run, seg_col, after(in_held, att_full), marks)

    def row_term(a, w):
        return mm(a, w, 1, 1).astype(BF16).reshape(4, own_rows, width)

    def weight_grad(pairs):
        total = None
        for a, g in pairs:
            value = mm(a, g, 0, 0)
            total = value if total is None else total + value
        return total.astype(BF16)

    stream_own = tokens.astype(F32)
    ssm_out, cot_own, cot_other = lax.optimization_barrier((ssm_out, cot_own, cot_other))
    mixer_own, mixer_other = unsettle([att_full, ssm_out], own_rows)
    term_other = row_term(mixer_other, w_out)
    middle = stream_own + cube_scatter("mixed", row_term(mixer_own, w_out), term_other)[0]
    normed_two = (unit(middle) * gain_two).astype(BF16)
    two_rows = cube_gather("normed_two", normed_two)[:2]

    def forward(rows):
        gate_up = mm(rows, w_gu, 1, 0).astype(BF16)
        gate = gate_up[:, :ff].astype(F32)
        up = gate_up[:, ff:].astype(F32)
        sig = jax.nn.sigmoid(gate)
        return gate, up, sig, (gate * sig * up).astype(BF16)

    def backward(rows, gate, up, sig):
        grad_hidden = mm(rows, w_down, 1, 0).astype(BF16).astype(F32)
        grad_gate = grad_hidden * up * (sig * (1.0 + gate * (1.0 - sig)))
        return jnp.concatenate([grad_gate, grad_hidden * gate * sig], axis=1).astype(BF16)

    *kept_own, hidden_own = forward(two_rows[0])
    *kept_other, hidden_other = forward(two_rows[1])
    gu_other = backward(cot_other, *kept_other)
    gu_own = backward(cot_own, *kept_own)
    term_other = row_term(gu_other, w_gu)
    down_w = weight_grad(
        [(after(cot_own, term_other), hidden_own), (after(cot_other, term_other), hidden_other)]
    )
    down_part = line_scatter("down", down_w)
    term, down_w = lax.optimization_barrier((row_term(gu_own, w_gu), down_w))
    grad_normed_two, far = cube_scatter("grad_normed_two", term, term_other)
    gu_w = weight_grad([(after(two_rows[0], far), gu_own), (after(two_rows[1], far), gu_other)])
    middle_part, gain_two_part = norm_back(middle, gain_two, grad_normed_two)
    grad_middle = cotangent.astype(F32) + middle_part
    mixed_own, mixed_other, *_ = cube_gather("grad_middle", grad_middle.astype(BF16))
    mixed_own, gu_w = lax.optimization_barrier((mixed_own, gu_w))
    gu_part = line_scatter("gu", gu_w)
    grad_att, grad_ssm = settle(
        mm(mixed_own, w_out, 1, 0).astype(BF16),
        mm(mixed_other, w_out, 1, 0).astype(BF16),
        own_rows,
        (inner, wide),
    )

    state_grad, grad_z = call(
        mamba_grad_state_kernel,
        (shape((states, wide)), shape((group, wide), BF16)),
        (steps,),
        [flow(2 * states), flow(wide), flow(wide), flow(wide), flow(128), flow(1), smem],
        (whole, flow(wide)),
    )(bc_in, gate_in, y_full, grad_ssm, run, seg_col, marks)
    grad_sent = jnp.concatenate([state_grad, factor_rows], axis=0).astype(BF16)
    grad_att, grad_sent, down_part = lax.optimization_barrier((grad_att, grad_sent, down_part))
    held_far = from_above("grad_held", [grad_sent] * groups)
    grad_query, grad_kv_all = call(
        attend_grad_kernel,
        (shape((group, HD)), shape((groups * group, 2 * HD), BF16)),
        (blocks,),
        [
            rows_spec(HD), full_spec(kv_all), full_spec(key_seg), rows_spec(1),
            rows_spec(HD), rows_spec(128), rows_spec(HD),
        ],
        (rows_spec(HD), full_spec(kv_all)),
        [pltpu.VMEM((groups * group, 2 * HD), F32)],
        prefetch=4,
    )(low, high, start, where, query, kv_all, key_seg, seg_col, att_full, log_total, grad_att)
    kv_terms = grad_kv_all.reshape(2, groups, half, 2 * HD)
    kv_terms = (kv_terms[0] + swap(kv_terms[1], "c")).reshape(groups, 2, quarter, 2 * HD)
    kv_terms = lax.dynamic_index_in_dim(kv_terms, x, 1, False) + swap(
        lax.dynamic_index_in_dim(kv_terms, x ^ 1, 1, False), "x"
    )
    kv_terms, *held_far = lax.optimization_barrier((kv_terms, *held_far))
    kv_far = from_above("grad_kv", kv_terms)
    grad_q = rope_back(grad_query, tables).astype(BF16)
    chunk_more = (gate_in, run, starts, in_held, after(grad_ssm, kv_terms))

    def more_specs(back=False):
        return [
            flow(wide, back),
            flow(128, back),
            pl.BlockSpec((1, states, wide), lambda i: (steps - 1 - i if back else i, 0, 0)),
            whole,
            flow(wide, back),
        ]

    near_out = call(
        mamba_grad_near_kernel,
        (
            shape((group, wide)),
            shape((group, states)),
            shape((group, states), BF16),
            shape((group, 128)),
            shape((steps, states, wide)),
            shape((8, wide)),
        ),
        (steps,),
        chunk_specs() + more_specs(),
        (
            flow(wide),
            flow(states),
            flow(states),
            flow(128),
            pl.BlockSpec((1, states, wide), lambda i: (i, 0, 0)),
            pl.BlockSpec((8, wide), lambda i: (0, 0)),
        ),
    )(*chunk_args, *chunk_more)
    skip_sums = near_out[5]
    near, *kv_far = lax.optimization_barrier((near_out[3], *kv_far))
    qz_w, gain_early = grad_early(groups, normed, after(grad_q, near), grad_z, w_all)
    qz_part = line_scatter("qz", qz_w)
    out_w = weight_grad([(after(mixed_own, near), mixer_own), (mixed_other, mixer_other)])
    out_part = line_scatter("out", out_w)
    hidden_own, hidden_other = after(hidden_own, near), after(hidden_other, near)
    layer_other = row_term(hidden_other, w_down)
    layer_own = row_term(hidden_own, w_down)
    layer_out = middle + cube_scatter("layer_out", layer_own, layer_other)[0]
    layer_out = layer_out.astype(BF16)
    deep = jnp.zeros((states, wide), F32)
    for got in reversed(held_far):
        got = got.astype(F32)
        deep = got[:states] + got[states : states + 1] * deep
    grad_kv_part = kv_terms[0].astype(F32)
    for got in kv_far:
        grad_kv_part = grad_kv_part + got.astype(F32)
    down_own, down_got = own_and_got("down", down_part)
    deep = after(deep, grad_kv_part, down_got, layer_out)
    part_tables = tuple(
        lax.dynamic_slice_in_dim(table, c * half + x * quarter, quarter, 0) for table in tables
    )
    grad_kv_part = jnp.concatenate(
        [rope_back(grad_kv_part[:, :HD], part_tables), grad_kv_part[:, HD:]], axis=1
    ).astype(BF16)
    grad_kv = lax.dynamic_update_slice(
        jnp.zeros((group, 2 * HD), BF16), grad_kv_part, (c * half + x * quarter, 0)
    )
    grad_x, grad_bc, grad_dt, sums = call(
        mamba_grad_kernel,
        (
            shape((group, wide), BF16),
            shape((group, 2 * states), BF16),
            shape((group, 128), BF16),
            shape((8, 128)),
        ),
        (steps,),
        chunk_specs(True)
        + more_specs(True)
        + [
            flow(wide, True),
            flow(states, True),
            flow(states, True),
            flow(128, True),
            pl.BlockSpec((1, states, wide), lambda i: (steps - 1 - i, 0, 0)),
            whole,
        ],
        (
            flow(wide, True),
            flow(2 * states, True),
            flow(128, True),
            pl.BlockSpec((8, 128), lambda i: (0, 0)),
        ),
        [pltpu.VMEM((states, wide), F32)],
    )(*chunk_args, *chunk_more, *near_out[:5], deep)

    gu_own, gu_got = own_and_got("gu", gu_part)
    grad_x, gu_got = lax.optimization_barrier((grad_x, gu_got))
    x_w, two_own, two_other = grad_late(
        kv_head, groups, normed, grad_x, grad_kv, grad_bc, grad_dt, w_all, gain_early,
        gain_two_part[:, None],
    )
    x_part = line_scatter("x", x_w)
    grad_own, grad_other = assemble(
        kv_head, own_rows, grad_q, after(grad_x, x_w), grad_kv, grad_bc, grad_dt, grad_z
    )
    in_other = row_term(grad_other, w_all)
    grad_own, out_part = lax.optimization_barrier((after(grad_own, in_other), out_part))
    in_own = row_term(grad_own, w_all)
    two_part, two_far = cube_scatter("grad_two", two_own, two_other)
    in_grad, in_far = cube_scatter("grad_in", in_own, in_other, gate=two_far)
    in_grad, qz_part = lax.optimization_barrier((in_grad, qz_part))
    qz_own, qz_got = own_and_got("qz", after(qz_part, in_grad))
    out_own, out_got = own_and_got("out", after(out_part, in_grad))
    input_part, _ = norm_back(stream_own, gain_one, in_grad)
    input_grad = grad_middle + input_part
    two_part = after(two_part.astype(BF16), in_grad)
    ahead = [lax.dynamic_index_in_dim(two_part, (z + i) % groups, 0, False) for i in range(groups)]
    back = [lax.dynamic_index_in_dim(two_part, (z - i) % groups, 0, False) for i in range(groups)]
    from_others = from_above("grad_two", back) + from_below("grad_two", ahead)
    two_part = lax.dynamic_index_in_dim(two_part, z, 0, False).astype(F32)
    for got in from_others:
        two_part = two_part + got.astype(F32)
    kv_grad = two_part[:, :kv_cols].reshape(kv_w.shape)
    bc_grad = two_part[:, kv_cols:lead]
    small = jnp.concatenate(
        [sums[0, :heads], sums[1, :heads], jnp.sum(skip_sums[0].reshape(heads, MP), axis=1)]
    )
    small = jnp.pad(small, (0, width - small.shape[0]))
    dt_w_grad = mm(after(grad_dt, in_own), normed, 0, 0)[:heads]
    tiny = jnp.concatenate([dt_w_grad, small[None]], axis=0)
    for got in from_ring("tiny", tiny):
        tiny = tiny + got
    tiny_other = swap(tiny, "x")
    dt_grad = both_halves(
        *(
            lax.dynamic_slice_in_dim(a[:heads], (z * 2 + x) * rows_w, rows_w, 1).T
            for a in (tiny, tiny_other)
        )
    )
    small_sum = both_halves(*(a[heads, : 3 * heads].reshape(3, heads) for a in (tiny, tiny_other)))
    return (
        layer_out,
        input_grad,
        two_part[:, lead] / gain_mix.astype(F32),
        both_halves(qz_own[:, :inner], qz_got[:, :inner]),
        kv_grad,
        jnp.stack(
            [both_halves(qz_own[:, inner:], qz_got[:, inner:]), both_halves(*own_and_got("x", x_part))],
            axis=1,
        ),
        dt_grad,
        bc_grad,
        small_sum[0],
        small_sum[1],
        small_sum[2],
        both_halves(out_own[:, :inner], out_got[:, :inner]),
        both_halves(out_own[:, inner:], out_got[:, inner:]),
        two_part[:, lead + 1],
        jnp.stack(
            [both_halves(gu_own[:, :ff], gu_got[:, :ff]), both_halves(gu_own[:, ff:], gu_got[:, ff:])],
            axis=1,
        ),
        both_halves(down_own, down_got),
    )


def solution(mesh):
    groups = mesh.shape["blk"] // 2
    fine = Mesh(mesh.devices.reshape(groups, 2, 2, mesh.shape["head"] // 2), ("z", "x", "y", "c"))
    blk, head = ("z", "x"), ("y", "c")
    every = blk + head
    rows = P(every, None)
    return jax.shard_map(
        shards,
        mesh=fine,
        in_specs=(
            rows,
            P(blk),
            rows,
            P(every),
            P(blk, head),
            P(every, None, None),
            P(blk, None, head),
            P(blk, head),
            rows,
            P(head),
            P(head),
            P(head),
            P(blk, head),
            P(blk, head),
            P(every),
            P(blk, None, head),
            P(blk, head),
        ),
        out_specs=(
            rows,
            rows,
            P(every),
            P(blk, head),
            P(every, None, None),
            P(blk, None, head),
            P(blk, head),
            rows,
            P(head),
            P(head),
            P(head),
            P(blk, head),
            P(blk, head),
            P(every),
            P(blk, None, head),
            P(blk, head),
        ),
        check_vma=False,
    )
```

time: 830 us -> 727 us (0.88)
  local copies, waits for them, and re-layouts: 125 us -> 72.9 us
  matrix products: 125 us -> 83.9 us
  Pallas kernels: 96.8 us -> 124 us
  waiting for transfers between devices: 228 us -> 209 us
  starting transfers between devices: 146 us -> 132 us
    dot_general x28 -> x22, matrix products: 125 us -> 83.9 us  [mm(): lax.dot_general(a, b, (((ca,), (cb,)), ((), ())), preferred_element_type=...]
    pallas_call x4 -> x7, Pallas kernels: 28.8 us -> 67 us  [the longest x1 16.4 us: shards(): call(mamba_grad_near_kernel, (shape((group, wide)), shape((group, states)...]
    ppermute x76 -> x74, waiting for transfers between devices: 124 us -> 152 us  [swap(): return lax.ppermute(a, axis, SWAP)]
    unnamed x221 -> x226, local copies, waits for them, and re-layouts: 53.7 us -> 29.3 us
    ppermute x24 -> x27, waiting for transfers between devices: 75.7 us -> 52 us  [the longest x9 44.4 us: from_above(): lax.ppermute(values[far], 'z', [(i + far, i) for i in range(count - far)])]
    concatenate x4 -> x19, other arithmetic: 1.78 us -> 19.3 us  [the longest x1 6.26 us: shards(): w_all = jnp.concatenate([w_one, w_two, w_dt, w_z], axis=1)]
    ppermute x24 -> x27, starting transfers between devices: 76.7 us -> 62 us  [the longest x9 32.7 us: from_below(): lax.ppermute(values[far], 'z', [(i, i + far) for i in range(count - far)])]
    slice x34 -> x8, local copies, waits for them, and re-layouts: 18 us -> 4.86 us  [the longest x1 1.73 us: shards(): w_out, w_z = (w_mix[:, :inner + wide], w_mix[:, inner + wide:])]
  transfers between devices with their start and end apart: 111 -> 109, of which waited for: 51 -> 52; matrix products, arithmetic and copies ran while one was open for 36% -> 28% of each run, Pallas kernels for 12% -> 17%
where the time goes in v3:
time: 727 us; the launch traced here: 717 us
  waiting for transfers between devices  209 us (29%)
  starting transfers between devices  132 us (18%)
  Pallas kernels  124 us (17%)
  matrix products  83.9 us (12%)
  other arithmetic  76.6 us (11%)
  local copies, waits for them, and re-layouts  72.9 us (10%)
  between operations  17.8 us (2%)
    ppermute x74, waiting for transfers between devices, swap(): return lax.ppermute(a, axis, SWAP)  152 us
    dot_general x22, matrix products, mm(): lax.dot_general(a, b, (((ca,), (cb,)), ((), ())), preferred_element_type=...  83.9 us
    ppermute x74, starting transfers between devices, swap(): return lax.ppermute(a, axis, SWAP)  69.2 us
    ppermute x9, waiting for transfers between devices, from_above(): lax.ppermute(values[far], 'z', [(i + far, i) for i in range(count - far)])  44.4 us
    ppermute x9, starting transfers between devices, from_below(): lax.ppermute(values[far], 'z', [(i, i + far) for i in range(count - far)])  32.7 us
    unnamed x226, local copies, waits for them, and re-layouts  29.3 us
    ppermute x9, starting transfers between devices, from_ring(): lax.ppermute(value, 'z', [(i, (i + far) % count) for i in range(count)])  17.6 us
    pallas_call x1, Pallas kernels, shards(): call(mamba_grad_near_kernel, (shape((group, wide)), shape((group, states)...  16.4 us
  transfers between devices with their start and end apart: 109, of which 52 were waited for; matrix products, arithmetic and copies ran while one was open for 28% of the time, Pallas kernels for 17%

profile of v3, /device:TPU:0, one launch (start us, length us, event | category | flops | bytes accessed | tf_op | source)
XLA Modules:
  0.0 716.7 jit_solution(17751800536276096435)
XLA Ops:
  11.5 5.1 collective-permute-start.4
  23.0 5.2 collective-permute-done
  41.4 7.3 %collective-permute-done.8 = bf16[1,4,64,1152]{3,2,1,0:T(8,128)(2,1)S(1)} collective-permute-done((bf16[1,4,64,1152]{3,2,1,0:T(8,128)(2,1)S(1)}, bf16[1,4,64,1152]{3,2,1,0:T(8,128)(2,1)S(1)}, u32[]{:S(2)}, u32[]{:S(2)}) %collective-permute-start.8) | collective-permute-done | bytes 589856 | tf_op jit(solution)/shard_map/whole_rows/ppermute | solution.py:43
  52.4 6.3 collective-permute-done.9
  62.0 9.4 %collective-permute-done.15 = bf16[1,4,64,1152]{3,2,1,0:T(8,128)(2,1)S(1)} collective-permute-done((bf16[1,4,64,1152]{3,2,1,0:T(8,128)(2,1)S(1)}, bf16[1,4,64,1152]{3,2,1,0:T(8,128)(2,1)S(1)}, u32[]{:S(2)}, u32[]{:S(2)}) %collective-permute-start.15) | collective-permute-done | bytes 589856 | tf_op jit(solution)/shard_map/whole_rows/ppermute | solution.py:43
  75.7 4.5 collective-permute-done.10
  85.0 5.5 collective-permute-done.13
  93.6 5.5 collective-permute-done.18
  123.9 5.7 settle_groups_kernel.1
  136.2 13.8 %project_kernel.1 = (bf16[1024,2048]{1,0:T(8,128)(2,1)}, bf16[1024,128]{1,0:T(8,128)(2,1)}, bf16[1024,384]{1,0:T(8,128)(2,1)}, bf16[1024,256]{1,0:T(8,128)(2,1)}...) custom-call(s32[3]{0:T(128)} %pad_add_fusion.2.place, bf16[512,2048]{1,0:T(8,128)(2,1)} %copy-done.27, ...), custom_call_target="tpu_custom_call" | custom-call | tf_op jit(solution)/shard_map/project_kernel/pallas_call | solution.py:253
  153.0 5.6 collective-permute-start.21
  161.6 10.6 %mamba_local_kernel.1 = (f32[1024,384]{1,0:T(8,128)}, f32[1024,128]{1,0:T(8,128)}, f32[256,384]{1,0:T(8,128)}, f32[8,128]{1,0:T(8,128)}, f32[4,256,384]{2,1,0:T(8,128)}) custom-call(bf16[1024,384]{1,0:T(8,128)(2,1)} %get-tuple-element.132.x_in_ref, bf16[1024,512]{1,0:T(8,128)(2,1)} %get-tuple-element.133.bc_in_ref, ...), custom_call_target="tpu_custom_call" | custom-call | tf_op jit(solution)/shard_map/mamba_local_kernel/pallas_call | solution.py:948
  176.9 8.8 %collective-permute-done.26 = bf16[3,256,256]{2,1,0:T(8,128)(2,1)S(1)} collective-permute-done((bf16[3,256,256]{2,1,0:T(8,128)(2,1)S(1)}, bf16[3,256,256]{2,1,0:T(8,128)(2,1)S(1)}, u32[]{:S(2)}, u32[]{:S(2)}) %collective-permute-start.26) | collective-permute-done | bytes 393248 | tf_op jit(solution)/shard_map/ppermute | solution.py:43
  191.7 6.8 collective-permute-start.23
  198.5 5.6 collective-permute-start.24
  223.3 6.3 pad_maximum_fusion.w_ref
  232.5 7.8 %attend_kernel.1 = (f32[1024,128]{1,0:T(8,128)}, f32[1024,128]{1,0:T(8,128)}) custom-call(s32[4]{0:T(128)} %and_select_fusion.1.low_ref, s32[4]{0:T(128)} %fusion.118.high_ref, s32[1]{0:T(128)} %bitcast.18.start_ref, s32[2]{0:T(128)} %pad_add_fusion.1.where_ref, bf16[1024,128]{1,0:T(8,128)(2,1)} %get-tuple-element.139.q_ref, ...), custom_call_target="tpu_custom_call" | custom-call | tf_op jit(solution)/shard_map/attend_kernel/pallas_call | solution.py:1004
  241.2 4.7 convolution_convert_fusion.8.gate_ref
  245.8 5.4 mamba_close_kernel.1
  251.2 4.6 unsettle_kernel.1
  268.4 5.1 collective-permute-done.35
  289.2 10.8 %collective-permute-done.41 = bf16[128,2048]{1,0:T(8,128)(2,1)S(1)} collective-permute-done((bf16[128,2048]{1,0:T(8,128)(2,1)S(1)}, bf16[128,2048]{1,0:T(8,128)(2,1)S(1)}, u32[]{:S(2)}, u32[]{:S(2)}) %collective-permute-start.41) | collective-permute-done | bytes 524320 | tf_op jit(solution)/shard_map/normed_two/ppermute | solution.py:43
  302.5 4.5 collective-permute-done.42
  308.1 5.1 all-gather.8.cloned.1.call-done
  313.2 5.3 fusion.9
  338.1 4.3 add_convert_fusion.2
  349.1 5.1 collective-permute-done.47
  371.6 4.7 add_convert_fusion
  376.3 7.1 collective-permute-done.53
  394.1 4.4 fusion.24.own_ref
  404.8 6.3 mamba_grad_state_kernel.1
  412.8 10.1 %attend_grad_kernel.1 = (f32[1024,128]{1,0:T(8,128)}, bf16[4096,256]{1,0:T(8,128)(2,1)}) custom-call(s32[4]{0:T(128)} %and_select_fusion.1.low_ref, s32[4]{0:T(128)} %fusion.118.high_ref, s32[1]{0:T(128)} %bitcast.18.start_ref, s32[2]{0:T(128)} %pad_add_fusion.1.where_ref, bf16[1024,128]{1,0:T(8,128)(2,1)} %get-tuple-element.139.q_ref, ...), custom_call_target="tpu_custom_call" | custom-call | tf_op jit(solution)/shard_map/attend_grad_kernel/pallas_call | solution.py:1085
  433.3 8.7 %collective-permute-done.58 = bf16[4,256,256]{2,1,0:T(8,128)(2,1)S(1)} collective-permute-done((bf16[4,256,256]{2,1,0:T(8,128)(2,1)S(1)}, bf16[4,256,256]{2,1,0:T(8,128)(2,1)S(1)}, u32[]{:S(2)}, u32[]{:S(2)}) %collective-permute-start.58) | collective-permute-done | bytes 524320 | tf_op jit(solution)/shard_map/ppermute | solution.py:43
  442.1 13.3 %collective-permute-done.59 = bf16[272,384]{1,0:T(8,128)(2,1)S(1)} collective-permute-done((bf16[272,384]{1,0:T(8,128)(2,1)S(1)}, bf16[272,384]{1,0:T(8,128)(2,1)S(1)}, u32[]{:S(2)}, u32[]{:S(2)}) %collective-permute-start.59) | collective-permute-done | bytes 208928 | tf_op jit(solution)/shard_map/grad_held/ppermute | solution.py:63
  455.4 26.4 %collective-permute-done.60 = bf16[272,384]{1,0:T(8,128)(2,1)S(1)} collective-permute-done((bf16[272,384]{1,0:T(8,128)(2,1)S(1)}, bf16[272,384]{1,0:T(8,128)(2,1)S(1)}, u32[]{:S(2)}, u32[]{:S(2)}) %collective-permute-start.60) | collective-permute-done | bytes 208928 | tf_op jit(solution)/shard_map/grad_held/ppermute | solution.py:63
  485.8 16.4 %mamba_grad_near_kernel.1 = (f32[1024,384]{1,0:T(8,128)}, f32[1024,256]{1,0:T(8,128)}, bf16[1024,256]{1,0:T(8,128)(2,1)}, f32[1024,128]{1,0:T(8,128)}, f32[4,256,384]{2,1,0:T(8,128)}, /*index=5*/f32[8,384]{1,0:T(8,128)}) custom-call(bf16[1024,384]{1,0:T(8,128)(2,1)} %get-tuple-element.132.x_in_ref, bf16[1024,512]{1,0:T(8,128)(2,1)} %get-tuple-element.133.bc_in_ref, ...), custom_call_target="tpu_custom_call" | custom-call | tf_op jit(solution)/shard_map/mamba_grad_near_kernel/pallas_call | solution.py:1116
  502.3 4.3 convolution_convert_fusion.4
  539.7 8.4 %grad_early_kernel.1 = (bf16[2048,512]{1,0:T(8,128)(2,1)}, f32[2048,128]{1,0:T(8,128)}) custom-call(bf16[1024,2048]{1,0:T(8,128)(2,1)} %get-tuple-element.144.normed_ref, bf16[1024,128]{1,0:T(8,128)(2,1)} %fusion.77.q_ref, bf16[1024,384]{1,0:T(8,128)(2,1)} %get-tuple-element.199.z_ref, bf16[2048,2048]{1,0:T(8,128)(2,1)} %pad_maximum_fusion.w_ref), custom_call_target="tpu_custom_call" | custom-call | tf_op jit(solution)/shard_map/grad_early_kernel/pallas_call | solution.py:288
  550.2 11.2 %mamba_grad_kernel.1 = (bf16[1024,384]{1,0:T(8,128)(2,1)}, bf16[1024,512]{1,0:T(8,128)(2,1)}, bf16[1024,128]{1,0:T(8,128)(2,1)}, f32[8,128]{1,0:T(8,128)}) custom-call(bf16[1024,384]{1,0:T(8,128)(2,1)} %get-tuple-element.132.x_in_ref, bf16[1024,512]{1,0:T(8,128)(2,1)} %get-tuple-element.133.bc_in_ref, bf16[1024,128]{1,0:T(8,128)(2,1)} %get-tuple-element.134.dt_in_ref, ...), custom_call_target="tpu_custom_call" | custom-call | tf_op jit(solution)/shard_map/mamba_grad_kernel/pallas_call | solution.py:1166
  561.6 14.2 %grad_late_kernel.1 = (bf16[2048,384]{1,0:T(8,128)(2,1)}, bf16[4,4,64,1152]{3,2,1,0:T(8,128)(2,1)}, bf16[4,4,64,1152]{3,2,1,0:T(8,128)(2,1)}) custom-call(s32[3]{0:T(128)} %pad_add_fusion.2.place, bf16[1024,2048]{1,0:T(8,128)(2,1)} %get-tuple-element.144.normed_ref, bf16[1024,384]{1,0:T(8,128)(2,1)} %get-tuple-element.202.x_ref, ...), custom_call_target="tpu_custom_call" | custom-call | tf_op jit(solution)/shard_map/grad_late_kernel/pallas_call | solution.py:344
  576.7 5.9 collective-permute-done.72
  585.5 5.4 assemble_kernel.1
  590.9 10.1 %convolution_convert_fusion.3 = bf16[512,2048]{1,0:T(8,128)(2,1)} fusion(bf16[512,2048]{1,0:T(8,128)(2,1)} %get-tuple-element.204, bf16[2048,2048]{1,0:T(8,128)(2,1)} %pad_maximum_fusion.w_ref), kind=kOutput, calls=%fused_computation.7 | convolution fusion | flops 4296015872 | bytes 12582912 | tf_op jit(solution)/shard_map/dot_general | solution.py:29
  601.6 9.4 %convolution_convert_fusion.2 = bf16[512,2048]{1,0:T(8,128)(2,1)} fusion(bf16[512,2048]{1,0:T(8,128)(2,1)S(1)} %copy-done.88, bf16[2048,2048]{1,0:T(8,128)(2,1)} %pad_maximum_fusion.w_ref), kind=kOutput, calls=%fused_computation.6 | convolution fusion | flops 4296015872 | bytes 12582912 | tf_op jit(solution)/shard_map/dot_general | solution.py:29
  611.7 5.5 collective-permute-start.98
  646.9 6.1 collective-permute-done.80
  658.1 6.9 collective-permute-done.85
  676.0 4.3 collective-permute-start.93
  (652 shorter events, 335.4 us)
Async XLA Ops:
  7.2 129.0 %all-gather.4.cloned.1.call-start = ((), (), s32[]{:S(2)}) async-start(), calls=%async_computation.5 | async-start | bytes 2621440 | tf_op jit(solution)/shard_map/w_one/all_gather | solution.py:395
  11.5 19.2 %collective-permute-start.4 = (bf16[64,1152]{1,0:T(8,128)(2,1)S(1)}, bf16[64,1152]{1,0:T(8,128)(2,1)S(1)}, u32[]{:S(2)}, u32[]{:S(2)}) collective-permute-start(bf16[64,1152]{1,0:T(8,128)(2,1)S(1)} %get-tuple-element.406), channel_id=1, source_target_pairs={{0,24},{8,0},{16,8},{24,16},{1,25},{9,1},{17,9},{25,17},{2,26},{10... | collective-permute-start | bytes 442376 | tf_op jit(solution)/shard_map/whole_rows/ppermute | solution.py:72
  16.6 15.3 %collective-permute-start.3 = (bf16[64,1152]{1,0:T(8,128)(2,1)S(1)}, bf16[64,1152]{1,0:T(8,128)(2,1)S(1)}, u32[]{:S(2)}, u32[]{:S(2)}) collective-permute-start(bf16[64,1152]{1,0:T(8,128)(2,1)S(1)} %get-tuple-element.406), channel_id=1, source_target_pairs={{0,16},{8,24},{16,0},{24,8},{1,17},{9,25},{17,1},{25,9},{2,18},{10... | collective-permute-start | bytes 442376 | tf_op jit(solution)/shard_map/whole_rows/ppermute | solution.py:72
  16.6 16.8 %collective-permute-start.2 = (bf16[64,1152]{1,0:T(8,128)(2,1)S(1)}, bf16[64,1152]{1,0:T(8,128)(2,1)S(1)}, u32[]{:S(2)}, u32[]{:S(2)}) collective-permute-start(bf16[64,1152]{1,0:T(8,128)(2,1)S(1)} %get-tuple-element.406), channel_id=1, source_target_pairs={{0,8},{8,16},{16,24},{24,0},{1,9},{9,17},{17,25},{25,1},{2,10},{10... | collective-permute-start | bytes 442376 | tf_op jit(solution)/shard_map/whole_rows/ppermute | solution.py:72
  20.9 14.7 %collective-permute-start.1 = (bf16[256,512]{1,0:T(8,128)(2,1)S(1)}, bf16[256,512]{1,0:T(8,128)(2,1)S(1)}, u32[]{:S(2)}, u32[]{:S(2)}) collective-permute-start(bf16[256,512]{1,0:T(8,128)(2,1)S(1)} %get-tuple-element.399), channel_id=1, source_target_pairs={{0,4},{4,0},{1,5},{5,1},{2,6},{6,2},{3,7},{7,3},{8,12},{12,8},{9,1... | collective-permute-start | bytes 786440 | tf_op jit(solution)/shard_map/ppermute | solution.py:43
  40.2 180.9 %all-gather.6.cloned.1.call-start = ((), (), s32[]{:S(2)}) async-start(), calls=%async_computation.6 | async-start | bytes 4587520 | tf_op jit(solution)/shard_map/w_mix/all_gather | solution.py:395
  51.0 20.4 %collective-permute-start.15 = (bf16[1,4,64,1152]{3,2,1,0:T(8,128)(2,1)S(1)}, bf16[1,4,64,1152]{3,2,1,0:T(8,128)(2,1)S(1)}, u32[]{:S(2)}, u32[]{:S(2)}) collective-permute-start(bf16[1,4,64,1152]{3,2,1,0:T(8,128)(2,1)S(1)} %maximum_bitcast_fusion.4), channel_id=1, source_target_pairs={{0,2},{2,0},{1,3},{3,1},{4,6},{6,4},{5,7},{7,5},{8,10},{10,8},{9,1... | collective-permute-start | bytes 1769480 | tf_op jit(solution)/shard_map/whole_rows/ppermute | solution.py:43
  58.8 21.5 %collective-permute-start.10 = (bf16[128,2048]{1,0:T(8,128)(2,1)S(1)}, bf16[128,2048]{1,0:T(8,128)(2,1)}, u32[]{:S(2)}, u32[]{:S(2)}) collective-permute-start(bf16[128,2048]{1,0:T(8,128)(2,1)S(1)} %copy-done.14), channel_id=1, source_target_pairs={{0,2},{2,0},{1,3},{3,1},{4,6},{6,4},{5,7},{7,5},{8,10},{10,8},{9,1... | collective-permute-start | bytes 1572872 | tf_op jit(solution)/shard_map/tokens/ppermute | solution.py:43
  71.4 20.6 %collective-permute-start.16 = (bf16[1,2,64,1152]{3,2,1,0:T(8,128)(2,1)S(1)}, bf16[1,2,64,1152]{3,2,1,0:T(8,128)(2,1)S(1)}, u32[]{:S(2)}, u32[]{:S(2)}) collective-permute-start(bf16[1,2,64,1152]{3,2,1,0:T(8,128)(2,1)S(1)} %split.43), channel_id=1, source_target_pairs={{0,4},{4,0},{1,5},{5,1},{2,6},{6,2},{3,7},{7,3},{8,12},{12,8},{9,1... | collective-permute-start | bytes 884744 | tf_op jit(solution)/shard_map/whole_rows/ppermute | solution.py:43
  93.5 30.4 %collective-permute-start.17 = (bf16[4,4,64,1152]{3,2,1,0:T(8,128)(2,1)S(1)}, bf16[4,4,64,1152]{3,2,1,0:T(8,128)(2,1)}, u32[]{:S(2)}, u32[]{:S(2)}) collective-permute-start(bf16[4,4,64,1152]{3,2,1,0:T(8,128)(2,1)S(1)} %maximum_maximum_fusion.own_ref), channel_id=1, source_target_pairs={{0,1},{1,0},{2,3},{3,2},{4,5},{5,4},{6,7},{7,6},{8,9},{9,8},{10,11... | collective-permute-start | bytes 7077896 | tf_op jit(solution)/shard_map/whole_rows/ppermute | solution.py:43
  100.2 213.0 %all-gather.8.cloned.1.call-start = ((), (), s32[]{:S(2)}) async-start(), calls=%async_computation.7 | async-start | bytes 7864320 | tf_op jit(solution)/shard_map/w_ff/all_gather | solution.py:395
  101.1 35.1 %collective-permute-start.14 = (bf16[512,2048]{1,0:T(8,128)(2,1)}, bf16[512,2048]{1,0:T(8,128)(2,1)}, u32[]{:S(2)}, u32[]{:S(2)}) collective-permute-start(bf16[512,2048]{1,0:T(8,128)(2,1)} %copy-done.27), channel_id=1, source_target_pairs={{0,1},{1,0},{2,3},{3,2},{4,5},{5,4},{6,7},{7,6},{8,9},{9,8},{10,11... | collective-permute-start | bytes 6291464 | tf_op jit(solution)/shard_map/tokens/ppermute | solution.py:43
  120.5 39.4 %collective-permute-start.19 = (bf16[256,1536]{0,1:T(8,128)(2,1)}, bf16[256,1536]{0,1:T(8,128)(2,1)}, u32[]{:S(2)}, u32[]{:S(2)}) collective-permute-start(bf16[256,1536]{0,1:T(8,128)(2,1)} %fusion.74), channel_id=1, source_target_pairs={{0,4},{4,0},{1,5},{5,1},{2,6},{6,2},{3,7},{7,3},{8,12},{12,8},{9,1... | collective-permute-start | bytes 2359304 | tf_op jit(solution)/shard_map/ppermute | solution.py:43
  150.9 23.9 %collective-permute-start.20 = (bf16[256,256]{1,0:T(8,128)(2,1)S(1)}, bf16[256,256]{1,0:T(8,128)(2,1)S(1)}, u32[]{:S(2)}, u32[]{:S(2)}) collective-permute-start(bf16[256,256]{1,0:T(8,128)(2,1)S(1)} %constant_dynamic-slice_fusion.3), channel_id=1, source_target_pairs={{0,8},{8,16},{16,24},{1,9},{9,17},{17,25},{2,10},{10,18},{18,26},{... | collective-permute-start | bytes 393224 | tf_op jit(solution)/shard_map/kv/ppermute | solution.py:54
  153.0 21.8 %collective-permute-start.21 = (bf16[256,256]{1,0:T(8,128)(2,1)S(1)}, bf16[256,256]{1,0:T(8,128)(2,1)S(1)}, u32[]{:S(2)}, u32[]{:S(2)}) collective-permute-start(bf16[256,256]{1,0:T(8,128)(2,1)S(1)} %constant_dynamic-slice_fusion.3), channel_id=1, source_target_pairs={{0,16},{8,24},{1,17},{9,25},{2,18},{10,26},{3,19},{11,27},{4,20},{... | collective-permute-start | bytes 393224 | tf_op jit(solution)/shard_map/kv/ppermute | solution.py:54
  158.6 16.3 %collective-permute-start.22 = (bf16[256,256]{1,0:T(8,128)(2,1)S(1)}, bf16[256,256]{1,0:T(8,128)(2,1)S(1)}, u32[]{:S(2)}, u32[]{:S(2)}) collective-permute-start(bf16[256,256]{1,0:T(8,128)(2,1)S(1)} %constant_dynamic-slice_fusion.3), channel_id=1, source_target_pairs={{0,24},{1,25},{2,26},{3,27},{4,28},{5,29},{6,30},{7,31}} | collective-permute-start | bytes 393224 | tf_op jit(solution)/shard_map/kv/ppermute | solution.py:54
  186.9 20.9 %collective-permute-start.28 = (bf16[128,2048]{1,0:T(8,128)(2,1)}, bf16[128,2048]{1,0:T(8,128)(2,1)}, u32[]{:S(2)}, u32[]{:S(2)}) collective-permute-start(bf16[128,2048]{1,0:T(8,128)(2,1)} %param.19), channel_id=1, source_target_pairs={{0,2},{2,0},{1,3},{3,1},{4,6},{6,4},{5,7},{7,5},{8,10},{10,8},{9,1... | collective-permute-start | bytes 1572872 | tf_op jit(solution)/shard_map/cotangent/ppermute | solution.py:43
  188.4 17.7 %collective-permute-start.29 = (bf16[128,2048]{1,0:T(8,128)(2,1)}, bf16[128,2048]{1,0:T(8,128)(2,1)}, u32[]{:S(2)}, u32[]{:S(2)}) collective-permute-start(bf16[128,2048]{1,0:T(8,128)(2,1)} %param.19), channel_id=1, source_target_pairs={{0,4},{4,0},{1,5},{5,1},{2,6},{6,2},{3,7},{7,3},{8,12},{12,8},{9,1... | collective-permute-start | bytes 1572872 | tf_op jit(solution)/shard_map/cotangent/ppermute | solution.py:43
  191.7 221.2 %reduce-scatter.6.cloned.1.call-start = ((), (), s32[]{:S(2)}) async-start(), calls=%async_computation.8 | async-start | bytes 2621440 | tf_op jit(solution)/shard_map/down/reduce_scatter | solution.py:409
  191.7 37.9 %collective-permute-start.23 = (bf16[272,384]{1,0:T(8,128)(2,1)}, bf16[272,384]{1,0:T(8,128)(2,1)}, u32[]{:S(2)}, u32[]{:S(2)}) collective-permute-start(bf16[272,384]{1,0:T(8,128)(2,1)} %pad_maximum_fusion.22), channel_id=1, source_target_pairs={{0,8},{8,16},{16,24},{1,9},{9,17},{17,25},{2,10},{10,18},{18,26},{... | collective-permute-start | bytes 626696 | tf_op jit(solution)/shard_map/held/ppermute | solution.py:54
  198.5 31.1 %collective-permute-start.24 = (bf16[272,384]{1,0:T(8,128)(2,1)}, bf16[272,384]{1,0:T(8,128)(2,1)}, u32[]{:S(2)}, u32[]{:S(2)}) collective-permute-start(bf16[272,384]{1,0:T(8,128)(2,1)} %pad_maximum_fusion.22), channel_id=1, source_target_pairs={{0,16},{8,24},{1,17},{9,25},{2,18},{10,26},{3,19},{11,27},{4,20},{... | collective-permute-start | bytes 626696 | tf_op jit(solution)/shard_map/held/ppermute | solution.py:54
  204.1 15.5 %collective-permute-start.27 = (bf16[2048,256]{1,0:T(8,128)(2,1)S(1)}, bf16[2048,256]{1,0:T(8,128)(2,1)S(1)}, u32[]{:S(2)}, u32[]{:S(2)}) collective-permute-start(bf16[2048,256]{1,0:T(8,128)(2,1)S(1)} %copy-done.36), channel_id=1, source_target_pairs={{0,1},{1,0},{2,3},{3,2},{4,5},{5,4},{6,7},{7,6},{8,9},{9,8},{10,11... | collective-permute-start | bytes 3145736 | tf_op jit(solution)/shard_map/ppermute | solution.py:43
  215.9 13.7 %collective-permute-start.25 = (bf16[272,384]{1,0:T(8,128)(2,1)}, bf16[272,384]{1,0:T(8,128)(2,1)}, u32[]{:S(2)}, u32[]{:S(2)}) collective-permute-start(bf16[272,384]{1,0:T(8,128)(2,1)} %pad_maximum_fusion.22), channel_id=1, source_target_pairs={{0,24},{1,25},{2,26},{3,27},{4,28},{5,29},{6,30},{7,31}} | collective-permute-start | bytes 626696 | tf_op jit(solution)/shard_map/held/ppermute | solution.py:54
  219.7 31.5 %collective-permute-start.32 = (bf16[512,2048]{1,0:T(8,128)(2,1)}, bf16[512,2048]{1,0:T(8,128)(2,1)}, u32[]{:S(2)}, u32[]{:S(2)}) collective-permute-start(bf16[512,2048]{1,0:T(8,128)(2,1)} %constant_dynamic-update-slice_fusion.5), channel_id=1, source_target_pairs={{0,1},{1,0},{2,3},{3,2},{4,5},{5,4},{6,7},{7,6},{8,9},{9,8},{10,11... | collective-permute-start | bytes 6291464 | tf_op jit(solution)/shard_map/cotangent/ppermute | solution.py:43
  325.6 16.9 %collective-permute-start.45 = (bf16[4,128,2048]{2,1,0:T(8,128)(2,1)}, bf16[4,128,2048]{2,1,0:T(8,128)(2,1)S(1)}, u32[]{:S(2)}, u32[]{:S(2)}) collective-permute-start(bf16[4,128,2048]{2,1,0:T(8,128)(2,1)} %bitcast.64), channel_id=1, source_target_pairs={{0,1},{1,0},{2,3},{3,2},{4,5},{5,4},{6,7},{7,6},{8,9},{9,8},{10,11... | collective-permute-start | bytes 6291464 | tf_op jit(solution)/shard_map/grad_normed_two/ppermute | solution.py:43
  342.4 193.3 %reduce-scatter.8.cloned.1.call-start = ((), (), s32[]{:S(2)}) async-start(), calls=%async_computation.9 | async-start | bytes 5242880 | tf_op jit(solution)/shard_map/gu/reduce_scatter | solution.py:409
  347.1 14.9 %collective-permute-start.51 = (bf16[64,2048]{1,0:T(8,128)(2,1)S(1)}, bf16[64,2048]{1,0:T(8,128)(2,1)S(1)}, u32[]{:S(2)}, u32[]{:S(2)}) collective-permute-start(bf16[64,2048]{1,0:T(8,128)(2,1)S(1)} %get-tuple-element.342), channel_id=1, source_target_pairs={{0,2},{2,0},{1,3},{3,1},{4,6},{6,4},{5,7},{7,5},{8,10},{10,8},{9,1... | collective-permute-start | bytes 786440 | tf_op jit(solution)/shard_map/grad_normed_two/ppermute | solution.py:43
  368.6 16.4 %collective-permute-start.52 = (bf16[128,2048]{1,0:T(8,128)(2,1)}, bf16[128,2048]{1,0:T(8,128)(2,1)}, u32[]{:S(2)}, u32[]{:S(2)}) collective-permute-start(bf16[128,2048]{1,0:T(8,128)(2,1)} %get-tuple-element.309), channel_id=1, source_target_pairs={{0,2},{2,0},{1,3},{3,1},{4,6},{6,4},{5,7},{7,5},{8,10},{10,8},{9,1... | collective-permute-start | bytes 1572872 | tf_op jit(solution)/shard_map/grad_middle/ppermute | solution.py:43
  393.8 207.3 %reduce-scatter.10.cloned.1.call-start = ((), (), s32[]{:S(2)}) async-start(), calls=%async_computation.10 | async-start | bytes 2621440 | tf_op jit(solution)/shard_map/out/reduce_scatter | solution.py:409
  427.8 14.2 %collective-permute-start.58 = (bf16[4,256,256]{2,1,0:T(8,128)(2,1)S(1)}, bf16[4,256,256]{2,1,0:T(8,128)(2,1)S(1)}, u32[]{:S(2)}, u32[]{:S(2)}) collective-permute-start(bf16[4,256,256]{2,1,0:T(8,128)(2,1)S(1)} %dynamic-slice_bitcast_fusion.1), channel_id=1, source_target_pairs={{0,4},{4,0},{1,5},{5,1},{2,6},{6,2},{3,7},{7,3},{8,12},{12,8},{9,1... | collective-permute-start | bytes 1572872 | tf_op jit(solution)/shard_map/ppermute | solution.py:43
  429.4 26.0 %collective-permute-start.59 = (bf16[272,384]{1,0:T(8,128)(2,1)S(1)}, bf16[272,384]{1,0:T(8,128)(2,1)S(1)}, u32[]{:S(2)}, u32[]{:S(2)}) collective-permute-start(bf16[272,384]{1,0:T(8,128)(2,1)S(1)} %copy-done.63), channel_id=1, source_target_pairs={{8,0},{16,8},{24,16},{9,1},{17,9},{25,17},{10,2},{18,10},{26,18},{... | collective-permute-start | bytes 626696 | tf_op jit(solution)/shard_map/grad_held/ppermute | solution.py:63
  430.7 51.1 %collective-permute-start.60 = (bf16[272,384]{1,0:T(8,128)(2,1)S(1)}, bf16[272,384]{1,0:T(8,128)(2,1)S(1)}, u32[]{:S(2)}, u32[]{:S(2)}) collective-permute-start(bf16[272,384]{1,0:T(8,128)(2,1)S(1)} %copy-done.63), channel_id=1, source_target_pairs={{16,0},{24,8},{17,1},{25,9},{18,2},{26,10},{19,3},{27,11},{20,4},{... | collective-permute-start | bytes 626696 | tf_op jit(solution)/shard_map/grad_held/ppermute | solution.py:63
  432.0 49.8 %collective-permute-start.61 = (bf16[272,384]{1,0:T(8,128)(2,1)S(1)}, bf16[272,384]{1,0:T(8,128)(2,1)S(1)}, u32[]{:S(2)}, u32[]{:S(2)}) collective-permute-start(bf16[272,384]{1,0:T(8,128)(2,1)S(1)} %copy-done.63), channel_id=1, source_target_pairs={{24,0},{25,1},{26,2},{27,3},{28,4},{29,5},{30,6},{31,7}} | collective-permute-start | bytes 626696 | tf_op jit(solution)/shard_map/grad_held/ppermute | solution.py:63
  481.9 20.3 %collective-permute-start.62 = (bf16[256,256]{1,0:T(8,128)(2,1)S(1)}, bf16[256,256]{1,0:T(8,128)(2,1)S(1)}, u32[]{:S(2)}, u32[]{:S(2)}) collective-permute-start(bf16[256,256]{1,0:T(8,128)(2,1)S(1)} %get-tuple-element.394), channel_id=1, source_target_pairs={{8,0},{16,8},{24,16},{9,1},{17,9},{25,17},{10,2},{18,10},{26,18},{... | collective-permute-start | bytes 393224 | tf_op jit(solution)/shard_map/grad_kv/ppermute | solution.py:63
  483.2 19.0 %collective-permute-start.63 = (bf16[256,256]{1,0:T(8,128)(2,1)S(1)}, bf16[256,256]{1,0:T(8,128)(2,1)S(1)}, u32[]{:S(2)}, u32[]{:S(2)}) collective-permute-start(bf16[256,256]{1,0:T(8,128)(2,1)S(1)} %get-tuple-element.393), channel_id=1, source_target_pairs={{16,0},{24,8},{17,1},{25,9},{18,2},{26,10},{19,3},{27,11},{20,4},{... | collective-permute-start | bytes 393224 | tf_op jit(solution)/shard_map/grad_kv/ppermute | solution.py:63
  484.5 17.8 %collective-permute-start.64 = (bf16[256,256]{1,0:T(8,128)(2,1)S(1)}, bf16[256,256]{1,0:T(8,128)(2,1)S(1)}, u32[]{:S(2)}, u32[]{:S(2)}) collective-permute-start(bf16[256,256]{1,0:T(8,128)(2,1)S(1)} %get-tuple-element.392), channel_id=1, source_target_pairs={{24,0},{25,1},{26,2},{27,3},{28,4},{29,5},{30,6},{31,7}} | collective-permute-start | bytes 393224 | tf_op jit(solution)/shard_map/grad_kv/ppermute | solution.py:63
  510.8 155.5 %reduce-scatter.14.cloned.1.call-start = ((), (), s32[]{:S(2)}) async-start(), calls=%async_computation.12 | async-start | bytes 1966080 | tf_op jit(solution)/shard_map/x/reduce_scatter | solution.py:409
  526.8 21.3 %collective-permute-start.66 = (bf16[64,2048]{1,0:T(8,128)(2,1)}, bf16[64,2048]{1,0:T(8,128)(2,1)S(1)}, u32[]{:S(2)}, u32[]{:S(2)}) collective-permute-start(bf16[64,2048]{1,0:T(8,128)(2,1)} %get-tuple-element.338), channel_id=1, source_target_pairs={{0,4},{4,0},{1,5},{5,1},{2,6},{6,2},{3,7},{7,3},{8,12},{12,8},{9,1... | collective-permute-start | bytes 786440 | tf_op jit(solution)/shard_map/layer_out/ppermute | solution.py:43
  527.4 20.7 %collective-permute-start.71 = (bf16[64,2048]{1,0:T(8,128)(2,1)}, bf16[64,2048]{1,0:T(8,128)(2,1)}, u32[]{:S(2)}, u32[]{:S(2)}) collective-permute-start(bf16[64,2048]{1,0:T(8,128)(2,1)} %get-tuple-element.336), channel_id=1, source_target_pairs={{0,2},{2,0},{1,3},{3,1},{4,6},{6,4},{5,7},{7,5},{8,10},{10,8},{9,1... | collective-permute-start | bytes 786440 | tf_op jit(solution)/shard_map/layer_out/ppermute | solution.py:43
  533.8 14.3 %collective-permute-start.68 = (bf16[64,2048]{1,0:T(8,128)(2,1)}, bf16[64,2048]{1,0:T(8,128)(2,1)}, u32[]{:S(2)}, u32[]{:S(2)}) collective-permute-start(bf16[64,2048]{1,0:T(8,128)(2,1)} %get-tuple-element.334), channel_id=1, source_target_pairs={{0,4},{4,0},{1,5},{5,1},{2,6},{6,2},{3,7},{7,3},{8,12},{12,8},{9,1... | collective-permute-start | bytes 786440 | tf_op jit(solution)/shard_map/layer_out/ppermute | solution.py:43
  538.1 23.3 %collective-permute-start.73 = (bf16[256,1024]{1,0:T(8,128)(2,1)S(1)}, bf16[256,1024]{1,0:T(8,128)(2,1)S(1)}, u32[]{:S(2)}, u32[]{:S(2)}) collective-permute-start(bf16[256,1024]{1,0:T(8,128)(2,1)S(1)} %get-tuple-element.360), channel_id=1, source_target_pairs={{0,4},{4,0},{1,5},{5,1},{2,6},{6,2},{3,7},{7,3},{8,12},{12,8},{9,1... | collective-permute-start | bytes 1572872 | tf_op jit(solution)/shard_map/gu/ppermute | solution.py:43
  575.8 97.4 %reduce-scatter.12.cloned.1.call-start = ((), (), s32[]{:S(2)}) async-start(), calls=%async_computation.11 | async-start | bytes 2621440 | tf_op jit(solution)/shard_map/qz/reduce_scatter | solution.py:409
  601.0 32.4 %collective-permute-start.74 = (bf16[4,128,2048]{2,1,0:T(8,128)(2,1)}, bf16[4,128,2048]{2,1,0:T(8,128)(2,1)}, u32[]{:S(2)}, u32[]{:S(2)}) collective-permute-start(bf16[4,128,2048]{2,1,0:T(8,128)(2,1)} %bitcast.95), channel_id=1, source_target_pairs={{0,1},{1,0},{2,3},{3,2},{4,5},{5,4},{6,7},{7,6},{8,9},{9,8},{10,11... | collective-permute-start | bytes 6291464 | tf_op jit(solution)/shard_map/grad_in/ppermute | solution.py:43
  601.1 28.2 %collective-permute-start.75 = (bf16[4,4,64,1152]{3,2,1,0:T(8,128)(2,1)}, bf16[4,4,64,1152]{3,2,1,0:T(8,128)(2,1)}, u32[]{:S(2)}, u32[]{:S(2)}) collective-permute-start(bf16[4,4,64,1152]{3,2,1,0:T(8,128)(2,1)} %get-tuple-element.209), channel_id=1, source_target_pairs={{0,1},{1,0},{2,3},{3,2},{4,5},{5,4},{6,7},{7,6},{8,9},{9,8},{10,11... | collective-permute-start | bytes 7077896 | tf_op jit(solution)/shard_map/grad_two/ppermute | solution.py:43
  635.9 19.1 %collective-permute-start.83 = (bf16[2,64,1152]{2,1,0:T(8,128)(2,1)S(1)}, bf16[2,64,1152]{2,1,0:T(8,128)(2,1)S(1)}, u32[]{:S(2)}, u32[]{:S(2)}) collective-permute-start(bf16[2,64,1152]{2,1,0:T(8,128)(2,1)S(1)} %get-tuple-element.319), channel_id=1, source_target_pairs={{0,4},{4,0},{1,5},{5,1},{2,6},{6,2},{3,7},{7,3},{8,12},{12,8},{9,1... | collective-permute-start | bytes 884744 | tf_op jit(solution)/shard_map/grad_two/ppermute | solution.py:43
  637.0 20.0 %collective-permute-start.87 = (bf16[2,64,1152]{2,1,0:T(8,128)(2,1)S(1)}, bf16[2,64,1152]{2,1,0:T(8,128)(2,1)S(1)}, u32[]{:S(2)}, u32[]{:S(2)}) collective-permute-start(bf16[2,64,1152]{2,1,0:T(8,128)(2,1)S(1)} %get-tuple-element.317), channel_id=1, source_target_pairs={{0,2},{2,0},{1,3},{3,1},{4,6},{6,4},{5,7},{7,5},{8,10},{10,8},{9,1... | collective-permute-start | bytes 884744 | tf_op jit(solution)/shard_map/grad_two/ppermute | solution.py:43
  645.8 22.1 %collective-permute-start.77 = (bf16[64,2048]{1,0:T(8,128)(2,1)}, bf16[64,2048]{1,0:T(8,128)(2,1)S(1)}, u32[]{:S(2)}, u32[]{:S(2)}) collective-permute-start(bf16[64,2048]{1,0:T(8,128)(2,1)} %get-tuple-element.332), channel_id=1, source_target_pairs={{0,4},{4,0},{1,5},{5,1},{2,6},{6,2},{3,7},{7,3},{8,12},{12,8},{9,1... | collective-permute-start | bytes 786440 | tf_op jit(solution)/shard_map/grad_in/ppermute | solution.py:43
  655.0 13.9 %collective-permute-start.82 = (bf16[64,2048]{1,0:T(8,128)(2,1)}, bf16[64,2048]{1,0:T(8,128)(2,1)S(1)}, u32[]{:S(2)}, u32[]{:S(2)}) collective-permute-start(bf16[64,2048]{1,0:T(8,128)(2,1)} %get-tuple-element.330), channel_id=1, source_target_pairs={{0,2},{2,0},{1,3},{3,1},{4,6},{6,4},{5,7},{7,5},{8,10},{10,8},{9,1... | collective-permute-start | bytes 786440 | tf_op jit(solution)/shard_map/grad_in/ppermute | solution.py:43
  (161 other events, 1361.6 us)
Sparse Core Ops, SparseCore 0:
  40.3 45.8 all-gather.3
  100.3 77.5 all-gather.5
  191.8 121.3 all-gather.7
  342.6 47.2 reduce-scatter.5
  392.6 94.2 reduce-scatter.7
  510.9 46.9 reduce-scatter.9
  575.9 36.5 reduce-scatter.13
  614.9 43.4 reduce-scatter.11

commit v4 on v3

--- a/solution.py
+++ b/solution.py
@@ -80,31 +80,49 @@
 
 
 @scoped
-def cube_gather(piece, split=0, gate=None):
+def cube_gather(piece, split=0, gate=None, last_gate=None):
     by_x, by_y = swap(piece, "x"), swap(piece, "y")
     if gate is not None:
         by_x, by_y = after(by_x, gate), after(by_y, gate)
     low = swap(jnp.split(by_x, 2, split)[0], "y")
     high = swap(jnp.split(by_y, 2, split)[1], "x")
+    if last_gate is not None:
+        low, high = after(low, last_gate), after(high, last_gate)
     far = [low, high] if split == 0 else [jnp.concatenate([low, high], axis=split)]
     own = jnp.concatenate([piece, by_y, by_x] + far, axis=0)
     return own, swap(own, "c"), by_x, low
 
 
 @scoped
-def cube_scatter(mine, other, gate=None):
-    mine = mine + swap(other, "c")
+def cube_scatter(mine, other=None, gate=None, far_gate=None):
+    if other is not None:
+        mine = mine + swap(other, "c")
     if gate is not None:
         mine = after(mine, gate)
     here, to_y, to_x, far = mine[0], mine[1], mine[2], mine[3]
     half = far.shape[0] // 2
     from_x, from_y = swap(far[:half], "x"), swap(far[half:], "y")
     x_low, y_high = swap(to_x[:half], "x"), swap(to_y[half:], "y")
-    x_high = swap(to_x[half:] + from_y, "x")
+    if far_gate is not None:
+        to_x, to_y = after(to_x, far_gate), after(to_y, far_gate)
+    last = to_x[half:] + from_y
+    x_high = swap(last, "x")
     y_low = swap(to_y[:half] + from_x, "y")
     by_x = jnp.concatenate([x_low, x_high], 0).astype(F32)
     by_y = jnp.concatenate([y_low, y_high], 0).astype(F32)
-    return here.astype(F32) + by_x + by_y, from_x
+    return here.astype(F32) + by_x + by_y, from_x, last
+
+
+@scoped
+def cube_scatter_direct(mine, other, gate):
+    if other is not None:
+        mine = mine + swap(other, "c")
+    if gate is not None:
+        mine = after(mine, gate)
+    across = [(0, 3), (1, 2), (2, 1), (3, 0)]
+    by_y, by_x = swap(mine[1], "y"), swap(mine[2], "x")
+    by_both = lax.ppermute(mine[3], ("x", "y"), across)
+    return mine[0], by_y, by_x, by_both
 
 
 def place_ref():
@@ -401,7 +419,7 @@
 
 
 def both_halves(own, got):
-    return halves_in_order(own, got, 1)
+    return halves_in_order(own, got, 1).astype(F32)
 
 
 @scoped
@@ -414,7 +432,7 @@
     x = lax.axis_index("x")
     part = part.reshape(2, -1, part.shape[1])
     got = swap(lax.dynamic_index_in_dim(part, x ^ 1, 0, False), "x")
-    return lax.dynamic_index_in_dim(part, x, 0, False).astype(F32), got.astype(F32)
+    return lax.dynamic_index_in_dim(part, x, 0, False), got
 
 
 def lanes_of(cols, heads):
@@ -874,9 +892,6 @@
     w_two, misc = settle_groups(two_own, two_other, lead)
     w_mix = weight_gather("w_mix", own_out, swap(after(give_out, rows_own), "x"))
     w_out, w_z = w_mix[:, : inner + wide], w_mix[:, inner + wide :]
-    got_ff = swap(after(give_ff, rows_own), "x")
-    w_ff = weight_gather("w_ff", own_ff, got_ff)
-    w_gu, w_down = w_ff[:, : 2 * ff], w_ff[:, 2 * ff :]
     segment = seg_own.astype(F32)
     seg_col = segment.reshape(group, 1)
     seg_row = segment.reshape(steps, 1, CHUNK)
@@ -904,7 +919,6 @@
     kv_half = lax.dynamic_slice_in_dim(kv_own, c * half, half, 0)
     kv_quarter = lax.dynamic_slice_in_dim(kv_own, c * half + x * quarter, quarter, 0)
     kv_far = from_below("kv", [kv_quarter] * groups)
-    x_in = after(x_in, got_ff)
     gate_in = mm(normed, w_z, 1, 0).astype(BF16)
 
     dt_row = jnp.pad(dt_in[:, :8].T, ((0, 8), (0, 0)))
@@ -970,14 +984,16 @@
     factor_rows = jnp.broadcast_to(factor, (16, wide))
     held_sent = jnp.concatenate([held_own, factor_rows], axis=0).astype(BF16)
     held_sent, *kv_far = lax.optimization_barrier((held_sent, *kv_far))
+    w_ff = weight_gather("w_ff", own_ff, swap(after(give_ff, held_sent), "x"))
+    w_gu, w_down = w_ff[:, : 2 * ff], w_ff[:, 2 * ff :]
     held_far = from_below("held", [held_sent] * groups)
     kv_far = jnp.stack(kv_far)
     kv_far = halves_in_order(kv_far, swap(kv_far, "x"), 1).reshape(-1, 2 * HD)
     kv_near = jnp.concatenate([kv_half, kv_far], axis=0)
-    cot_own, cot_other, *_ = cube_gather("cotangent", after(cotangent, kv_near))
+    kv_near, *held_far = lax.optimization_barrier((kv_near, *held_far))
     kv_all = jnp.concatenate([kv_near, swap(kv_near, "c")], axis=0)
     w_all = jnp.concatenate([w_one, w_two, w_dt, w_z], axis=1)
-    query, w_all, *held_far = lax.optimization_barrier((query, w_all, *held_far))
+    query, w_all = lax.optimization_barrier((query, w_all))
     in_held = jnp.zeros((states, wide), F32)
     for got in reversed(held_far):
         got = got.astype(F32)
@@ -1029,12 +1045,12 @@
         return total.astype(BF16)
 
     stream_own = tokens.astype(F32)
-    ssm_out, cot_own, cot_other = lax.optimization_barrier((ssm_out, cot_own, cot_other))
     mixer_own, mixer_other = unsettle([att_full, ssm_out], own_rows)
     term_other = row_term(mixer_other, w_out)
     middle = stream_own + cube_scatter("mixed", row_term(mixer_own, w_out), term_other)[0]
     normed_two = (unit(middle) * gain_two).astype(BF16)
     two_rows = cube_gather("normed_two", normed_two)[:2]
+    cot_own, cot_other, *_ = cube_gather("cotangent", after(cotangent, two_rows[0]))
 
     def forward(rows):
         gate_up = mm(rows, w_gu, 1, 0).astype(BF16)
@@ -1058,12 +1074,20 @@
     )
     down_part = line_scatter("down", down_w)
     term, down_w = lax.optimization_barrier((row_term(gu_own, w_gu), down_w))
-    grad_normed_two, far = cube_scatter("grad_normed_two", term, term_other)
+    grad_normed_two, far, _ = cube_scatter("grad_normed_two", term, term_other)
     gu_w = weight_grad([(after(two_rows[0], far), gu_own), (after(two_rows[1], far), gu_other)])
     middle_part, gain_two_part = norm_back(middle, gain_two, grad_normed_two)
     grad_middle = cotangent.astype(F32) + middle_part
-    mixed_own, mixed_other, *_ = cube_gather("grad_middle", grad_middle.astype(BF16))
-    mixed_own, gu_w = lax.optimization_barrier((mixed_own, gu_w))
+    grad_middle, gu_w = lax.optimization_barrier((grad_middle, gu_w))
+    hidden_own, hidden_other = after(hidden_own, grad_middle), after(hidden_other, grad_middle)
+    layer_other = row_term(hidden_other, w_down)
+    layer_own = row_term(hidden_own, w_down)
+    mixed_own, mixed_other, *_ = cube_gather(
+        "grad_middle", grad_middle.astype(BF16), gate=layer_other, last_gate=layer_own
+    )
+    layer_terms = cube_scatter_direct("layer_out", layer_own, layer_other, mixed_own)
+    layer_out = middle + sum(a.astype(F32) for a in layer_terms)
+    layer_out = layer_out.astype(BF16)
     gu_part = line_scatter("gu", gu_w)
     grad_att, grad_ssm = settle(
         mm(mixed_own, w_out, 1, 0).astype(BF16),
@@ -1072,16 +1096,7 @@
         (inner, wide),
     )
 
-    state_grad, grad_z = call(
-        mamba_grad_state_kernel,
-        (shape((states, wide)), shape((group, wide), BF16)),
-        (steps,),
-        [flow(2 * states), flow(wide), flow(wide), flow(wide), flow(128), flow(1), smem],
-        (whole, flow(wide)),
-    )(bc_in, gate_in, y_full, grad_ssm, run, seg_col, marks)
-    grad_sent = jnp.concatenate([state_grad, factor_rows], axis=0).astype(BF16)
-    grad_att, grad_sent, down_part = lax.optimization_barrier((grad_att, grad_sent, down_part))
-    held_far = from_above("grad_held", [grad_sent] * groups)
+    grad_att, down_part = lax.optimization_barrier((grad_att, down_part))
     grad_query, grad_kv_all = call(
         attend_grad_kernel,
         (shape((group, HD)), shape((groups * group, 2 * HD), BF16)),
@@ -1094,15 +1109,18 @@
         [pltpu.VMEM((groups * group, 2 * HD), F32)],
         prefetch=4,
     )(low, high, start, where, query, kv_all, key_seg, seg_col, att_full, log_total, grad_att)
-    kv_terms = grad_kv_all.reshape(2, groups, half, 2 * HD)
-    kv_terms = (kv_terms[0] + swap(kv_terms[1], "c")).reshape(groups, 2, quarter, 2 * HD)
-    kv_terms = lax.dynamic_index_in_dim(kv_terms, x, 1, False) + swap(
-        lax.dynamic_index_in_dim(kv_terms, x ^ 1, 1, False), "x"
-    )
-    kv_terms, *held_far = lax.optimization_barrier((kv_terms, *held_far))
-    kv_far = from_above("grad_kv", kv_terms)
+    grad_ssm = after(grad_ssm, grad_query, layer_out)
+    state_grad, grad_z = call(
+        mamba_grad_state_kernel,
+        (shape((states, wide)), shape((group, wide), BF16)),
+        (steps,),
+        [flow(2 * states), flow(wide), flow(wide), flow(wide), flow(128), flow(1), smem],
+        (whole, flow(wide)),
+    )(bc_in, gate_in, y_full, grad_ssm, run, seg_col, marks)
+    grad_sent = jnp.concatenate([state_grad, factor_rows], axis=0).astype(BF16)
+    held_far = from_above("grad_held", [grad_sent] * groups)
     grad_q = rope_back(grad_query, tables).astype(BF16)
-    chunk_more = (gate_in, run, starts, in_held, after(grad_ssm, kv_terms))
+    chunk_more = (gate_in, run, starts, in_held, after(grad_ssm, grad_sent))
 
     def more_specs(back=False):
         return [
@@ -1134,17 +1152,23 @@
             pl.BlockSpec((8, wide), lambda i: (0, 0)),
         ),
     )(*chunk_args, *chunk_more)
+    kv_terms = grad_kv_all.reshape(2, groups, half, 2 * HD)
+    kv_mine, *held_far = lax.optimization_barrier(
+        (after(kv_terms[0], near_out[0]), *held_far)
+    )
+    kv_both = kv_mine + swap(kv_terms[1], "c")
+    kv_terms = kv_both.reshape(groups, 2, quarter, 2 * HD)
+    kv_terms = lax.dynamic_index_in_dim(kv_terms, x, 1, False) + swap(
+        lax.dynamic_index_in_dim(kv_terms, x ^ 1, 1, False), "x"
+    )
+    kv_far = from_above("grad_kv", kv_terms)
     skip_sums = near_out[5]
-    near, *kv_far = lax.optimization_barrier((near_out[3], *kv_far))
-    qz_w, gain_early = grad_early(groups, normed, after(grad_q, near), grad_z, w_all)
+    down_own, down_got = own_and_got("down", after(down_part, kv_terms))
+    grad_q, gu_part, *kv_far = lax.optimization_barrier((grad_q, gu_part, *kv_far))
+    qz_w, gain_early = grad_early(groups, normed, grad_q, grad_z, w_all)
     qz_part = line_scatter("qz", qz_w)
-    out_w = weight_grad([(after(mixed_own, near), mixer_own), (mixed_other, mixer_other)])
+    out_w = weight_grad([(after(mixed_own, kv_both), mixer_own), (mixed_other, mixer_other)])
     out_part = line_scatter("out", out_w)
-    hidden_own, hidden_other = after(hidden_own, near), after(hidden_other, near)
-    layer_other = row_term(hidden_other, w_down)
-    layer_own = row_term(hidden_own, w_down)
-    layer_out = middle + cube_scatter("layer_out", layer_own, layer_other)[0]
-    layer_out = layer_out.astype(BF16)
     deep = jnp.zeros((states, wide), F32)
     for got in reversed(held_far):
         got = got.astype(F32)
@@ -1152,8 +1176,7 @@
     grad_kv_part = kv_terms[0].astype(F32)
     for got in kv_far:
         grad_kv_part = grad_kv_part + got.astype(F32)
-    down_own, down_got = own_and_got("down", down_part)
-    deep = after(deep, grad_kv_part, down_got, layer_out)
+    deep = after(deep, grad_kv_part, qz_w, down_got)
     part_tables = tuple(
         lax.dynamic_slice_in_dim(table, c * half + x * quarter, quarter, 0) for table in tables
     )
@@ -1191,8 +1214,7 @@
         [pltpu.VMEM((states, wide), F32)],
     )(*chunk_args, *chunk_more, *near_out[:5], deep)
 
-    gu_own, gu_got = own_and_got("gu", gu_part)
-    grad_x, gu_got = lax.optimization_barrier((grad_x, gu_got))
+    grad_x, out_part = lax.optimization_barrier((grad_x, out_part))
     x_w, two_own, two_other = grad_late(
         kv_head, groups, normed, grad_x, grad_kv, grad_bc, grad_dt, w_all, gain_early,
         gain_two_part[:, None],
@@ -1201,31 +1223,31 @@
     grad_own, grad_other = assemble(
         kv_head, own_rows, grad_q, after(grad_x, x_w), grad_kv, grad_bc, grad_dt, grad_z
     )
+    two_mine = two_own + swap(two_other, "c")
+    grad_other = after(grad_other, two_mine)
     in_other = row_term(grad_other, w_all)
-    grad_own, out_part = lax.optimization_barrier((after(grad_own, in_other), out_part))
+    two_terms = cube_scatter_direct("grad_two", two_mine, None, None)
+    grad_own, qz_part = lax.optimization_barrier((after(grad_own, in_other), qz_part))
     in_own = row_term(grad_own, w_all)
-    two_part, two_far = cube_scatter("grad_two", two_own, two_other)
-    in_grad, in_far = cube_scatter("grad_in", in_own, in_other, gate=two_far)
-    in_grad, qz_part = lax.optimization_barrier((in_grad, qz_part))
-    qz_own, qz_got = own_and_got("qz", after(qz_part, in_grad))
-    out_own, out_got = own_and_got("out", after(out_part, in_grad))
+    in_sum, in_far, in_last = cube_scatter("grad_in", in_own, in_other)
+    two_terms = lax.optimization_barrier((*two_terms, in_far))[:4]
+    two_part = sum(a.astype(F32) for a in two_terms)
+    out_own, out_got = own_and_got("out", after(out_part, in_sum))
+    gu_own, gu_got = own_and_got("gu", after(gu_part, in_sum))
+    qz_own, qz_got = own_and_got("qz", after(qz_part, in_sum))
+    in_grad = in_sum
     input_part, _ = norm_back(stream_own, gain_one, in_grad)
     input_grad = grad_middle + input_part
-    two_part = after(two_part.astype(BF16), in_grad)
-    ahead = [lax.dynamic_index_in_dim(two_part, (z + i) % groups, 0, False) for i in range(groups)]
-    back = [lax.dynamic_index_in_dim(two_part, (z - i) % groups, 0, False) for i in range(groups)]
-    from_others = from_above("grad_two", back) + from_below("grad_two", ahead)
-    two_part = lax.dynamic_index_in_dim(two_part, z, 0, False).astype(F32)
-    for got in from_others:
-        two_part = two_part + got.astype(F32)
+    two_part = lax.psum_scatter(two_part.astype(BF16), "z", scatter_dimension=0).astype(F32)
     kv_grad = two_part[:, :kv_cols].reshape(kv_w.shape)
     bc_grad = two_part[:, kv_cols:lead]
     small = jnp.concatenate(
         [sums[0, :heads], sums[1, :heads], jnp.sum(skip_sums[0].reshape(heads, MP), axis=1)]
     )
     small = jnp.pad(small, (0, width - small.shape[0]))
-    dt_w_grad = mm(after(grad_dt, in_own), normed, 0, 0)[:heads]
+    dt_w_grad = mm(after(grad_dt, in_other), normed, 0, 0)[:heads]
     tiny = jnp.concatenate([dt_w_grad, small[None]], axis=0)
+    tiny = after(tiny, in_sum)
     for got in from_ring("tiny", tiny):
         tiny = tiny + got
     tiny_other = swap(tiny, "x")
@@ -1243,7 +1265,7 @@
         both_halves(qz_own[:, :inner], qz_got[:, :inner]),
         kv_grad,
         jnp.stack(
-            [both_halves(qz_own[:, inner:], qz_got[:, inner:]), both_halves(*own_and_got("x", x_part))],
+            [both_halves(qz_own[:, inner:], qz_got[:, inner:]), both_halves(*own_and_got("x", after(x_part, in_sum)))],
             axis=1,
         ),
         dt_grad,

time: 727 us -> 689 us (0.948)
  starting transfers between devices: 132 us -> 110 us
    ppermute x74 -> x66, waiting for transfers between devices: 152 us -> 140 us  [swap(): return lax.ppermute(a, axis, SWAP)]
    all_gather x3, waiting for transfers between devices: 5.08 us -> 14.4 us  [weight_gather(): return lax.all_gather(both, 'z', axis=0, tiled=True)]
    ppermute x74 -> x66, starting transfers between devices: 69.2 us -> 60.1 us  [swap(): return lax.ppermute(a, axis, SWAP)]
    ppermute x9 -> x6, starting transfers between devices: 32.7 us -> 25.3 us  [from_below(): lax.ppermute(values[far], 'z', [(i, i + far) for i in range(count - far)])]
    ppermute x9 -> x6, waiting for transfers between devices: 44.4 us -> 37 us  [from_above(): lax.ppermute(values[far], 'z', [(i + far, i) for i in range(count - far)])]
    unnamed x226 -> x203, local copies, waits for them, and re-layouts: 29.3 us -> 26.8 us
  transfers between devices with their start and end apart: 109 -> 98, of which waited for: 52 -> 46; matrix products, arithmetic and copies ran while one was open for 28% -> 30% of each run, Pallas kernels for 17% -> 18%
where the time goes in v4:
time: 689 us; the launch traced here: 679 us
  waiting for transfers between devices  202 us (29%)
  Pallas kernels  123 us (18%)
  starting transfers between devices  110 us (16%)
  other arithmetic  81.3 us (12%)
  matrix products  77.1 us (11%)
  local copies, waits for them, and re-layouts  68.5 us (10%)
  between operations  17.3 us (3%)
    ppermute x66, waiting for transfers between devices, swap(): return lax.ppermute(a, axis, SWAP)  140 us
    dot_general x22, matrix products, mm(): lax.dot_general(a, b, (((ca,), (cb,)), ((), ())), preferred_element_type=...  77.1 us
    ppermute x66, starting transfers between devices, swap(): return lax.ppermute(a, axis, SWAP)  60.1 us
    ppermute x6, waiting for transfers between devices, from_above(): lax.ppermute(values[far], 'z', [(i + far, i) for i in range(count - far)])  37 us
    unnamed x203, local copies, waits for them, and re-layouts  26.8 us
    ppermute x6, starting transfers between devices, from_below(): lax.ppermute(values[far], 'z', [(i, i + far) for i in range(count - far)])  25.3 us
    pallas_call x1, Pallas kernels, shards(): call(mamba_grad_near_kernel, (shape((group, wide)), shape((group, states)...  16.3 us
    all_gather x3, waiting for transfers between devices, weight_gather(): return lax.all_gather(both, 'z', axis=0, tiled=True)  14.4 us
  transfers between devices with their start and end apart: 98, of which 46 were waited for; matrix products, arithmetic and copies ran while one was open for 30% of the time, Pallas kernels for 18%

profile of v4, /device:TPU:0, one launch (start us, length us, event | category | flops | bytes accessed | tf_op | source)
XLA Modules:
  0.0 679.3 jit_solution(14714753976159716764)
XLA Ops:
  11.5 5.1 collective-permute-start.4
  38.7 8.6 %collective-permute-done.8 = bf16[1,4,64,1152]{3,2,1,0:T(8,128)(2,1)S(1)} collective-permute-done((bf16[1,4,64,1152]{3,2,1,0:T(8,128)(2,1)S(1)}, bf16[1,4,64,1152]{3,2,1,0:T(8,128)(2,1)S(1)}, u32[]{:S(2)}, u32[]{:S(2)}) %collective-permute-start.8) | collective-permute-done | bytes 589856 | tf_op jit(solution)/shard_map/whole_rows/ppermute | solution.py:43
  60.2 7.5 %collective-permute-done.11 = bf16[128,2048]{1,0:T(8,128)(2,1)S(1)} collective-permute-done((bf16[128,2048]{1,0:T(8,128)(2,1)S(1)}, bf16[128,2048]{1,0:T(8,128)(2,1)S(1)}, u32[]{:S(2)}, u32[]{:S(2)}) %collective-permute-start.11) | collective-permute-done | bytes 524320 | tf_op jit(solution)/shard_map/tokens/ppermute | solution.py:43
  102.1 5.7 settle_groups_kernel.1
  114.3 13.9 %project_kernel.1 = (bf16[1024,2048]{1,0:T(8,128)(2,1)}, bf16[1024,128]{1,0:T(8,128)(2,1)}, bf16[1024,384]{1,0:T(8,128)(2,1)}, bf16[1024,256]{1,0:T(8,128)(2,1)}...) custom-call(s32[3]{0:T(128)} %pad_add_fusion.2.place, ...), custom_call_target="tpu_custom_call" | custom-call | tf_op jit(solution)/shard_map/project_kernel/pallas_call | solution.py:271
  130.7 6.3 collective-permute-start.20
  140.1 10.6 %mamba_local_kernel.1 = (f32[1024,384]{1,0:T(8,128)}, f32[1024,128]{1,0:T(8,128)}, f32[256,384]{1,0:T(8,128)}, f32[8,128]{1,0:T(8,128)}, f32[4,256,384]{2,1,0:T(8,128)}) custom-call(bf16[1024,384]{1,0:T(8,128)(2,1)} %get-tuple-element.140.x_in_ref, bf16[1024,512]{1,0:T(8,128)(2,1)} %get-tuple-element.141.bc_in_ref, ...), custom_call_target="tpu_custom_call" | custom-call | tf_op jit(solution)/shard_map/mamba_local_kernel/pallas_call | solution.py:962
  154.6 9.2 %collective-permute-start.23 = (bf16[272,384]{1,0:T(8,128)(2,1)S(1)}, bf16[272,384]{1,0:T(8,128)(2,1)S(1)}, u32[]{:S(2)}, u32[]{:S(2)}) collective-permute-start(bf16[272,384]{1,0:T(8,128)(2,1)S(1)} %pad_maximum_fusion.17), channel_id=1, source_target_pairs={{0,8},{8,16},{16,24},{1,9},{9,17},{17,25},{2,10},{10,18},{18,26},{... | collective-permute-start | bytes 626696 | tf_op jit(solution)/shard_map/held/ppermute | solution.py:54
  163.8 5.5 collective-permute-start.24
  180.1 6.8 collective-permute-done.38
  192.9 8.3 %pad_maximum_fusion.w_ref = bf16[2048,2048]{1,0:T(8,128)(2,1)} fusion(bf16[2048,384]{1,0:T(8,128)(2,1)S(1)} %slice.506, bf16[2048,128]{1,0:T(8,128)(2,1)S(1)} %copy-done.22, bf16[2048,1024]{1,0:T(8,128)(2,1)} %bitcast.339, bf16[2048,512]{1,0:T(8,128)(2,1)S(1)} %copy-done.12), kind=kLoop, calls=%fused_computation | loop fusion | flops 33554432 | bytes 16777216 | tf_op jit(solution)/shard_map/concatenate | solution.py:995
  201.2 3.2 convolution_convert_fusion.8.gate_ref
  204.4 7.2 %attend_kernel.1 = (f32[1024,128]{1,0:T(8,128)}, f32[1024,128]{1,0:T(8,128)}) custom-call(s32[4]{0:T(128)} %and_select_fusion.1.low_ref, s32[4]{0:T(128)} %fusion.112.high_ref, s32[1]{0:T(128)} %bitcast.18.start_ref, s32[2]{0:T(128)} %pad_add_fusion.1.where_ref, bf16[1024,128]{1,0:T(8,128)(2,1)} %get-tuple-element.138.q_ref, bf16[4096,256]{1,0:T(8,128)(2,1)} %copy-done.4, ...), custom_call_target="tpu_custom_call" | custom-call | tf_op jit(solution)/shard_map/attend_kernel/pallas_call | solution.py:1020
  211.6 5.2 mamba_close_kernel.1
  216.8 4.6 unsettle_kernel.1
  233.9 5.1 collective-permute-done.29
  244.9 4.6 collective-permute-done.32
  253.6 11.1 %collective-permute-done.35 = bf16[128,2048]{1,0:T(8,128)(2,1)S(1)} collective-permute-done((bf16[128,2048]{1,0:T(8,128)(2,1)S(1)}, bf16[128,2048]{1,0:T(8,128)(2,1)S(1)}, u32[]{:S(2)}, u32[]{:S(2)}) %collective-permute-start.35) | collective-permute-done | bytes 524320 | tf_op jit(solution)/shard_map/normed_two/ppermute | solution.py:43
  267.0 4.5 collective-permute-done.36
  274.5 9.4 %collective-permute-done.40 = bf16[128,2048]{1,0:T(8,128)(2,1)S(1)} collective-permute-done((bf16[128,2048]{1,0:T(8,128)(2,1)S(1)}, bf16[128,2048]{1,0:T(8,128)(2,1)S(1)}, u32[]{:S(2)}, u32[]{:S(2)}) %collective-permute-start.40) | collective-permute-done | bytes 524320 | tf_op jit(solution)/shard_map/cotangent/ppermute | solution.py:43
  287.1 3.3 collective-permute-done.41
  292.3 14.4 %all-gather.8.cloned.1.call-done = bf16[2048,1536]{0,1:T(8,128)(2,1)} async-done(((bf16[512,1536]{0,1:T(8,128)(2,1)}), bf16[2048,1536]{0,1:T(8,128)(2,1)}) %all-gather.8.cloned.1.call-update) | async-done | bytes 6291472 | tf_op jit(solution)/shard_map/w_ff/all_gather | solution.py:413
  306.7 5.3 fusion.9
  312.0 3.3 fusion.46
  315.4 3.7 convolution_convert_fusion
  331.9 4.5 convolution_convert_fusion.1
  343.8 5.1 collective-permute-done.47
  353.3 4.0 fusion.74
  357.4 4.6 add_convert_fusion
  376.2 3.9 collective-permute-done.53
  383.5 4.1 collective-permute-done.55
  399.6 4.1 settle_kernel.1
  403.7 10.1 %attend_grad_kernel.1 = (f32[1024,128]{1,0:T(8,128)}, bf16[4096,256]{1,0:T(8,128)(2,1)}) custom-call(s32[4]{0:T(128)} %and_select_fusion.1.low_ref, s32[4]{0:T(128)} %fusion.112.high_ref, s32[1]{0:T(128)} %bitcast.18.start_ref, s32[2]{0:T(128)} %pad_add_fusion.1.where_ref, bf16[1024,128]{1,0:T(8,128)(2,1)} %get-tuple-element.138.q_ref, ...), custom_call_target="tpu_custom_call" | custom-call | tf_op jit(solution)/shard_map/attend_grad_kernel/pallas_call | solution.py:1100
  422.2 6.3 mamba_grad_state_kernel.1
  434.5 16.3 %mamba_grad_near_kernel.1 = (f32[1024,384]{1,0:T(8,128)}, f32[1024,256]{1,0:T(8,128)}, bf16[1024,256]{1,0:T(8,128)(2,1)}, f32[1024,128]{1,0:T(8,128)}, f32[4,256,384]{2,1,0:T(8,128)}, /*index=5*/f32[8,384]{1,0:T(8,128)}) custom-call(bf16[1024,384]{1,0:T(8,128)(2,1)} %get-tuple-element.140.x_in_ref, bf16[1024,512]{1,0:T(8,128)(2,1)} %get-tuple-element.141.bc_in_ref, ...), custom_call_target="tpu_custom_call" | custom-call | tf_op jit(solution)/shard_map/mamba_grad_near_kernel/pallas_call | solution.py:1134
  453.7 15.2 %collective-permute-done.62 = bf16[272,384]{1,0:T(8,128)(2,1)} collective-permute-done((bf16[272,384]{1,0:T(8,128)(2,1)}, bf16[272,384]{1,0:T(8,128)(2,1)}, u32[]{:S(2)}, u32[]{:S(2)}) %collective-permute-start.62) | collective-permute-done | bytes 208928 | tf_op jit(solution)/shard_map/grad_held/ppermute | solution.py:63
  480.5 9.3 %collective-permute-done.65 = bf16[4,256,256]{2,1,0:T(8,128)(2,1)S(1)} collective-permute-done((bf16[4,256,256]{2,1,0:T(8,128)(2,1)S(1)}, bf16[4,256,256]{2,1,0:T(8,128)(2,1)S(1)}, u32[]{:S(2)}, u32[]{:S(2)}) %collective-permute-start.65) | collective-permute-done | bytes 524320 | tf_op jit(solution)/shard_map/ppermute | solution.py:43
  496.2 6.7 collective-permute-done.66
  502.9 15.0 %collective-permute-done.67 = bf16[256,256]{1,0:T(8,128)(2,1)S(1)} collective-permute-done((bf16[256,256]{1,0:T(8,128)(2,1)S(1)}, bf16[256,256]{1,0:T(8,128)(2,1)S(1)}, u32[]{:S(2)}, u32[]{:S(2)}) %collective-permute-start.67) | collective-permute-done | bytes 131104 | tf_op jit(solution)/shard_map/grad_kv/ppermute | solution.py:63
  518.0 8.2 %grad_early_kernel.1 = (bf16[2048,512]{1,0:T(8,128)(2,1)}, f32[2048,128]{1,0:T(8,128)}) custom-call(bf16[1024,2048]{1,0:T(8,128)(2,1)} %get-tuple-element.151.normed_ref, bf16[1024,128]{1,0:T(8,128)(2,1)} %fusion.76.q_ref, bf16[1024,384]{1,0:T(8,128)(2,1)} %get-tuple-element.202.z_ref, bf16[2048,2048]{1,0:T(8,128)(2,1)} %pad_maximum_fusion.w_ref), custom_call_target="tpu_custom_call" | custom-call | tf_op jit(solution)/shard_map/grad_early_kernel/pallas_call | solution.py:306
  527.0 11.2 %mamba_grad_kernel.1 = (bf16[1024,384]{1,0:T(8,128)(2,1)}, bf16[1024,512]{1,0:T(8,128)(2,1)}, bf16[1024,128]{1,0:T(8,128)(2,1)}, f32[8,128]{1,0:T(8,128)}) custom-call(bf16[1024,384]{1,0:T(8,128)(2,1)} %get-tuple-element.140.x_in_ref, bf16[1024,512]{1,0:T(8,128)(2,1)} %get-tuple-element.141.bc_in_ref, bf16[1024,128]{1,0:T(8,128)(2,1)} %get-tuple-element.142.dt_in_ref, ...), custom_call_target="tpu_custom_call" | custom-call | tf_op jit(solution)/shard_map/mamba_grad_kernel/pallas_call | solution.py:1189
  539.4 14.2 %grad_late_kernel.1 = (bf16[2048,384]{1,0:T(8,128)(2,1)}, bf16[4,4,64,1152]{3,2,1,0:T(8,128)(2,1)}, bf16[4,4,64,1152]{3,2,1,0:T(8,128)(2,1)}) custom-call(s32[3]{0:T(128)} %pad_add_fusion.2.place, bf16[1024,2048]{1,0:T(8,128)(2,1)} %get-tuple-element.151.normed_ref, bf16[1024,384]{1,0:T(8,128)(2,1)} %get-tuple-element.215.x_ref, ...), custom_call_target="tpu_custom_call" | custom-call | tf_op jit(solution)/shard_map/grad_late_kernel/pallas_call | solution.py:362
  555.5 5.5 assemble_kernel.1
  562.4 3.3 add.416
  565.7 9.2 %convolution_convert_fusion.3 = bf16[512,2048]{1,0:T(8,128)(2,1)} fusion(bf16[512,2048]{1,0:T(8,128)(2,1)S(1)} %copy-done.75, bf16[2048,2048]{1,0:T(8,128)(2,1)} %pad_maximum_fusion.w_ref), kind=kOutput, calls=%fused_computation.7 | convolution fusion | flops 4296015872 | bytes 12582912 | tf_op jit(solution)/shard_map/dot_general | solution.py:29
  582.4 8.7 %convolution_convert_fusion.2 = bf16[512,2048]{1,0:T(8,128)(2,1)S(1)} fusion(bf16[512,2048]{1,0:T(8,128)(2,1)} %get-tuple-element.222, bf16[2048,2048]{1,0:T(8,128)(2,1)} %pad_maximum_fusion.w_ref), kind=kOutput, calls=%fused_computation.6 | convolution fusion | flops 4296015872 | bytes 12582912 | tf_op jit(solution)/shard_map/dot_general | solution.py:29
  598.3 15.3 %collective-permute-done.73 = bf16[64,2048]{1,0:T(8,128)(2,1)S(1)} collective-permute-done((bf16[64,2048]{1,0:T(8,128)(2,1)S(1)}, bf16[64,2048]{1,0:T(8,128)(2,1)S(1)}, u32[]{:S(2)}, u32[]{:S(2)}) %collective-permute-start.73) | collective-permute-done | bytes 262176 | tf_op jit(solution)/shard_map/grad_in/ppermute | solution.py:43
  645.3 9.4 %collective-permute-done.86 = f32[7,2048]{1,0:T(8,128)S(1)} collective-permute-done((f32[7,2048]{1,0:T(8,128)S(1)}, f32[7,2048]{1,0:T(8,128)S(1)}, u32[]{:S(2)}, u32[]{:S(2)}) %collective-permute-start.86) | collective-permute-done | bytes 57376 | tf_op jit(solution)/shard_map/ppermute | solution.py:43
  (597 shorter events, 295.4 us)
Async XLA Ops:
  7.2 107.1 %all-gather.4.cloned.1.call-start = ((), (), s32[]{:S(2)}) async-start(), calls=%async_computation.6 | async-start | bytes 2621440 | tf_op jit(solution)/shard_map/w_one/all_gather | solution.py:413
  11.5 15.5 %collective-permute-start.4 = (bf16[64,1152]{1,0:T(8,128)(2,1)S(1)}, bf16[64,1152]{1,0:T(8,128)(2,1)S(1)}, u32[]{:S(2)}, u32[]{:S(2)}) collective-permute-start(bf16[64,1152]{1,0:T(8,128)(2,1)S(1)} %get-tuple-element.412), channel_id=1, source_target_pairs={{0,24},{8,0},{16,8},{24,16},{1,25},{9,1},{17,9},{25,17},{2,26},{10... | collective-permute-start | bytes 442376 | tf_op jit(solution)/shard_map/whole_rows/ppermute | solution.py:72
  35.2 14.3 %collective-permute-start.15 = (bf16[1,4,64,1152]{3,2,1,0:T(8,128)(2,1)S(1)}, bf16[1,4,64,1152]{3,2,1,0:T(8,128)(2,1)S(1)}, u32[]{:S(2)}, u32[]{:S(2)}) collective-permute-start(bf16[1,4,64,1152]{3,2,1,0:T(8,128)(2,1)S(1)} %maximum_bitcast_fusion), channel_id=1, source_target_pairs={{0,2},{2,0},{1,3},{3,1},{4,6},{6,4},{5,7},{7,5},{8,10},{10,8},{9,1... | collective-permute-start | bytes 1769480 | tf_op jit(solution)/shard_map/whole_rows/ppermute | solution.py:43
  38.5 151.4 %all-gather.6.cloned.1.call-start = ((), (), s32[]{:S(2)}) async-start(), calls=%async_computation.7 | async-start | bytes 4587520 | tf_op jit(solution)/shard_map/w_mix/all_gather | solution.py:413
  54.9 14.3 %collective-permute-start.10 = (bf16[128,2048]{1,0:T(8,128)(2,1)S(1)}, bf16[128,2048]{1,0:T(8,128)(2,1)S(1)}, u32[]{:S(2)}, u32[]{:S(2)}) collective-permute-start(bf16[128,2048]{1,0:T(8,128)(2,1)S(1)} %copy-done.10), channel_id=1, source_target_pairs={{0,2},{2,0},{1,3},{3,1},{4,6},{6,4},{5,7},{7,5},{8,10},{10,8},{9,1... | collective-permute-start | bytes 1572872 | tf_op jit(solution)/shard_map/tokens/ppermute | solution.py:43
  59.1 43.0 %collective-permute-start.17 = (bf16[4,4,64,1152]{3,2,1,0:T(8,128)(2,1)S(1)}, bf16[4,4,64,1152]{3,2,1,0:T(8,128)(2,1)}, u32[]{:S(2)}, u32[]{:S(2)}) collective-permute-start(bf16[4,4,64,1152]{3,2,1,0:T(8,128)(2,1)S(1)} %maximum_maximum_fusion.own_ref), channel_id=1, source_target_pairs={{0,1},{1,0},{2,3},{3,2},{4,5},{5,4},{6,7},{7,6},{8,9},{9,8},{10,11... | collective-permute-start | bytes 7077896 | tf_op jit(solution)/shard_map/whole_rows/ppermute | solution.py:43
  84.2 30.1 %collective-permute-start.14 = (bf16[512,2048]{1,0:T(8,128)(2,1)}, bf16[512,2048]{1,0:T(8,128)(2,1)}, u32[]{:S(2)}, u32[]{:S(2)}) collective-permute-start(bf16[512,2048]{1,0:T(8,128)(2,1)} %constant_dynamic-update-slice_fusion.own_ref), channel_id=1, source_target_pairs={{0,1},{1,0},{2,3},{3,2},{4,5},{5,4},{6,7},{7,6},{8,9},{9,8},{10,11... | collective-permute-start | bytes 6291464 | tf_op jit(solution)/shard_map/tokens/ppermute | solution.py:43
  87.9 218.8 %all-gather.8.cloned.1.call-start = ((), (), s32[]{:S(2)}) async-start(), calls=%async_computation.8 | async-start | bytes 7864320 | tf_op jit(solution)/shard_map/w_ff/all_gather | solution.py:413
  129.1 23.5 %collective-permute-start.19 = (bf16[256,256]{1,0:T(8,128)(2,1)S(1)}, bf16[256,256]{1,0:T(8,128)(2,1)S(1)}, u32[]{:S(2)}, u32[]{:S(2)}) collective-permute-start(bf16[256,256]{1,0:T(8,128)(2,1)S(1)} %constant_dynamic-slice_fusion.2), channel_id=1, source_target_pairs={{0,8},{8,16},{16,24},{1,9},{9,17},{17,25},{2,10},{10,18},{18,26},{... | collective-permute-start | bytes 393224 | tf_op jit(solution)/shard_map/kv/ppermute | solution.py:54
  130.7 21.9 %collective-permute-start.20 = (bf16[256,256]{1,0:T(8,128)(2,1)S(1)}, bf16[256,256]{1,0:T(8,128)(2,1)S(1)}, u32[]{:S(2)}, u32[]{:S(2)}) collective-permute-start(bf16[256,256]{1,0:T(8,128)(2,1)S(1)} %constant_dynamic-slice_fusion.2), channel_id=1, source_target_pairs={{0,16},{8,24},{1,17},{9,25},{2,18},{10,26},{3,19},{11,27},{4,20},{... | collective-permute-start | bytes 393224 | tf_op jit(solution)/shard_map/kv/ppermute | solution.py:54
  137.1 15.6 %collective-permute-start.21 = (bf16[256,256]{1,0:T(8,128)(2,1)S(1)}, bf16[256,256]{1,0:T(8,128)(2,1)S(1)}, u32[]{:S(2)}, u32[]{:S(2)}) collective-permute-start(bf16[256,256]{1,0:T(8,128)(2,1)S(1)} %constant_dynamic-slice_fusion.2), channel_id=1, source_target_pairs={{0,24},{1,25},{2,26},{3,27},{4,28},{5,29},{6,30},{7,31}} | collective-permute-start | bytes 393224 | tf_op jit(solution)/shard_map/kv/ppermute | solution.py:54
  152.8 18.9 %collective-permute-start.22 = (bf16[3,256,256]{2,1,0:T(8,128)(2,1)S(1)}, bf16[3,256,256]{2,1,0:T(8,128)(2,1)S(1)}, u32[]{:S(2)}, u32[]{:S(2)}) collective-permute-start(bf16[3,256,256]{2,1,0:T(8,128)(2,1)S(1)} %pad_maximum_fusion.15), channel_id=1, source_target_pairs={{0,4},{4,0},{1,5},{5,1},{2,6},{6,2},{3,7},{7,3},{8,12},{12,8},{9,1... | collective-permute-start | bytes 1179656 | tf_op jit(solution)/shard_map/ppermute | solution.py:43
  154.6 18.2 %collective-permute-start.23 = (bf16[272,384]{1,0:T(8,128)(2,1)S(1)}, bf16[272,384]{1,0:T(8,128)(2,1)S(1)}, u32[]{:S(2)}, u32[]{:S(2)}) collective-permute-start(bf16[272,384]{1,0:T(8,128)(2,1)S(1)} %pad_maximum_fusion.17), channel_id=1, source_target_pairs={{0,8},{8,16},{16,24},{1,9},{9,17},{17,25},{2,10},{10,18},{18,26},{... | collective-permute-start | bytes 626696 | tf_op jit(solution)/shard_map/held/ppermute | solution.py:54
  170.6 16.2 %collective-permute-start.38 = (bf16[256,1536]{0,1:T(8,128)(2,1)}, bf16[256,1536]{0,1:T(8,128)(2,1)S(1)}, u32[]{:S(2)}, u32[]{:S(2)}) collective-permute-start(bf16[256,1536]{0,1:T(8,128)(2,1)} %fusion.71), channel_id=1, source_target_pairs={{0,4},{4,0},{1,5},{5,1},{2,6},{6,2},{3,7},{7,3},{8,12},{12,8},{9,1... | collective-permute-start | bytes 2359304 | tf_op jit(solution)/shard_map/ppermute | solution.py:43
  188.5 215.1 %reduce-scatter.7.cloned.1.call-start = ((), (), s32[]{:S(2)}) async-start(), calls=%async_computation.9 | async-start | bytes 2621440 | tf_op jit(solution)/shard_map/down/reduce_scatter | solution.py:427
  230.5 14.1 %collective-permute-start.33 = (bf16[64,2048]{1,0:T(8,128)(2,1)}, bf16[64,2048]{1,0:T(8,128)(2,1)S(1)}, u32[]{:S(2)}, u32[]{:S(2)}) collective-permute-start(bf16[64,2048]{1,0:T(8,128)(2,1)} %get-tuple-element.356), channel_id=1, source_target_pairs={{0,2},{2,0},{1,3},{3,1},{4,6},{6,4},{5,7},{7,5},{8,10},{10,8},{9,1... | collective-permute-start | bytes 786440 | tf_op jit(solution)/shard_map/mixed/ppermute | solution.py:43
  251.9 14.2 %collective-permute-start.34 = (bf16[128,2048]{1,0:T(8,128)(2,1)S(1)}, bf16[128,2048]{1,0:T(8,128)(2,1)S(1)}, u32[]{:S(2)}, u32[]{:S(2)}) collective-permute-start(bf16[128,2048]{1,0:T(8,128)(2,1)S(1)} %get-tuple-element.329), channel_id=1, source_target_pairs={{0,2},{2,0},{1,3},{3,1},{4,6},{6,4},{5,7},{7,5},{8,10},{10,8},{9,1... | collective-permute-start | bytes 1572872 | tf_op jit(solution)/shard_map/normed_two/ppermute | solution.py:43
  274.5 17.8 %collective-permute-start.44 = (bf16[512,2048]{1,0:T(8,128)(2,1)S(1)}, bf16[512,2048]{1,0:T(8,128)(2,1)}, u32[]{:S(2)}, u32[]{:S(2)}) collective-permute-start(bf16[512,2048]{1,0:T(8,128)(2,1)S(1)} %constant_dynamic-update-slice_fusion.7), channel_id=1, source_target_pairs={{0,1},{1,0},{2,3},{3,2},{4,5},{5,4},{6,7},{7,6},{8,9},{9,8},{10,11... | collective-permute-start | bytes 6291464 | tf_op jit(solution)/shard_map/normed_two/ppermute | solution.py:43
  292.2 19.8 %collective-permute-start.43 = (bf16[512,2048]{1,0:T(8,128)(2,1)S(1)}, bf16[512,2048]{1,0:T(8,128)(2,1)}, u32[]{:S(2)}, u32[]{:S(2)}) collective-permute-start(bf16[512,2048]{1,0:T(8,128)(2,1)S(1)} %constant_dynamic-update-slice_fusion.12), channel_id=1, source_target_pairs={{0,1},{1,0},{2,3},{3,2},{4,5},{5,4},{6,7},{7,6},{8,9},{9,8},{10,11... | collective-permute-start | bytes 6291464 | tf_op jit(solution)/shard_map/cotangent/ppermute | solution.py:43
  319.0 17.4 %collective-permute-start.45 = (bf16[4,128,2048]{2,1,0:T(8,128)(2,1)}, bf16[4,128,2048]{2,1,0:T(8,128)(2,1)}, u32[]{:S(2)}, u32[]{:S(2)}) collective-permute-start(bf16[4,128,2048]{2,1,0:T(8,128)(2,1)} %bitcast.64), channel_id=1, source_target_pairs={{0,1},{1,0},{2,3},{3,2},{4,5},{5,4},{6,7},{7,6},{8,9},{9,8},{10,11... | collective-permute-start | bytes 6291464 | tf_op jit(solution)/shard_map/grad_normed_two/ppermute | solution.py:43
  330.8 187.2 %reduce-scatter.9.cloned.1.call-start = ((), (), s32[]{:S(2)}) async-start(), calls=%async_computation.10 | async-start | bytes 5242880 | tf_op jit(solution)/shard_map/gu/reduce_scatter | solution.py:427
  342.7 19.3 %collective-permute-start.51 = (bf16[64,2048]{1,0:T(8,128)(2,1)}, bf16[64,2048]{1,0:T(8,128)(2,1)S(1)}, u32[]{:S(2)}, u32[]{:S(2)}) collective-permute-start(bf16[64,2048]{1,0:T(8,128)(2,1)} %get-tuple-element.350), channel_id=1, source_target_pairs={{0,2},{2,0},{1,3},{3,1},{4,6},{6,4},{5,7},{7,5},{8,10},{10,8},{9,1... | collective-permute-start | bytes 786440 | tf_op jit(solution)/shard_map/grad_normed_two/ppermute | solution.py:43
  343.3 18.7 %collective-permute-start.46 = (bf16[64,2048]{1,0:T(8,128)(2,1)}, bf16[64,2048]{1,0:T(8,128)(2,1)}, u32[]{:S(2)}, u32[]{:S(2)}) collective-permute-start(bf16[64,2048]{1,0:T(8,128)(2,1)} %get-tuple-element.349), channel_id=1, source_target_pairs={{0,4},{4,0},{1,5},{5,1},{2,6},{6,2},{3,7},{7,3},{8,12},{12,8},{9,1... | collective-permute-start | bytes 786440 | tf_op jit(solution)/shard_map/grad_normed_two/ppermute | solution.py:43
  366.3 171.9 %reduce-scatter.11.cloned.1.call-start = ((), (), s32[]{:S(2)}) async-start(), calls=%async_computation.11 | async-start | bytes 2621440 | tf_op jit(solution)/shard_map/out/reduce_scatter | solution.py:427
  373.2 17.3 %collective-permute-start.52 = (bf16[4,128,2048]{2,1,0:T(8,128)(2,1)S(1)}, bf16[4,128,2048]{2,1,0:T(8,128)(2,1)S(1)}, u32[]{:S(2)}, u32[]{:S(2)}) collective-permute-start(bf16[4,128,2048]{2,1,0:T(8,128)(2,1)S(1)} %bitcast.404), channel_id=1, source_target_pairs={{0,1},{1,0},{2,3},{3,2},{4,5},{5,4},{6,7},{7,6},{8,9},{9,8},{10,11... | collective-permute-start | bytes 6291464 | tf_op jit(solution)/shard_map/layer_out/ppermute | solution.py:43
  392.7 23.7 %collective-permute-start.59 = (bf16[128,2048]{1,0:T(8,128)(2,1)}, bf16[128,2048]{1,0:T(8,128)(2,1)}, u32[]{:S(2)}, u32[]{:S(2)}) collective-permute-start(bf16[128,2048]{1,0:T(8,128)(2,1)} %get-tuple-element.347), channel_id=1, source_target_pairs={{0,6},{2,4},{4,2},{6,0},{1,7},{3,5},{5,3},{7,1},{8,14},{10,12},{12... | collective-permute-start | bytes 1572872 | tf_op jit(solution)/shard_map/layer_out/ppermute | solution.py:124
  394.2 25.2 %collective-permute-start.58 = (bf16[128,2048]{1,0:T(8,128)(2,1)}, bf16[128,2048]{1,0:T(8,128)(2,1)}, u32[]{:S(2)}, u32[]{:S(2)}) collective-permute-start(bf16[128,2048]{1,0:T(8,128)(2,1)} %get-tuple-element.348), channel_id=1, source_target_pairs={{0,4},{4,0},{1,5},{5,1},{2,6},{6,2},{3,7},{7,3},{8,12},{12,8},{9,1... | collective-permute-start | bytes 1572872 | tf_op jit(solution)/shard_map/layer_out/ppermute | solution.py:43
  395.5 24.0 %collective-permute-start.57 = (bf16[128,2048]{1,0:T(8,128)(2,1)}, bf16[128,2048]{1,0:T(8,128)(2,1)}, u32[]{:S(2)}, u32[]{:S(2)}) collective-permute-start(bf16[128,2048]{1,0:T(8,128)(2,1)} %get-tuple-element.346), channel_id=1, source_target_pairs={{0,2},{2,0},{1,3},{3,1},{4,6},{6,4},{5,7},{7,5},{8,10},{10,8},{9,1... | collective-permute-start | bytes 1572872 | tf_op jit(solution)/shard_map/layer_out/ppermute | solution.py:43
  416.4 52.6 %collective-permute-start.64 = (bf16[4,512,256]{2,1,0:T(8,128)(2,1)}, bf16[4,512,256]{2,1,0:T(8,128)(2,1)}, u32[]{:S(2)}, u32[]{:S(2)}) collective-permute-start(bf16[4,512,256]{2,1,0:T(8,128)(2,1)} %bitcast.79), channel_id=1, source_target_pairs={{0,1},{1,0},{2,3},{3,2},{4,5},{5,4},{6,7},{7,6},{8,9},{9,8},{10,11... | collective-permute-start | bytes 3145736 | tf_op jit(solution)/shard_map/ppermute | solution.py:43
  430.2 23.5 %collective-permute-start.61 = (bf16[272,384]{1,0:T(8,128)(2,1)}, bf16[272,384]{1,0:T(8,128)(2,1)S(1)}, u32[]{:S(2)}, u32[]{:S(2)}) collective-permute-start(bf16[272,384]{1,0:T(8,128)(2,1)} %pad_maximum_fusion.16), channel_id=1, source_target_pairs={{8,0},{16,8},{24,16},{9,1},{17,9},{25,17},{10,2},{18,10},{26,18},{... | collective-permute-start | bytes 626696 | tf_op jit(solution)/shard_map/grad_held/ppermute | solution.py:63
  431.5 37.5 %collective-permute-start.62 = (bf16[272,384]{1,0:T(8,128)(2,1)}, bf16[272,384]{1,0:T(8,128)(2,1)}, u32[]{:S(2)}, u32[]{:S(2)}) collective-permute-start(bf16[272,384]{1,0:T(8,128)(2,1)} %pad_maximum_fusion.16), channel_id=1, source_target_pairs={{16,0},{24,8},{17,1},{25,9},{18,2},{26,10},{19,3},{27,11},{20,4},{... | collective-permute-start | bytes 626696 | tf_op jit(solution)/shard_map/grad_held/ppermute | solution.py:63
  432.8 36.2 %collective-permute-start.63 = (bf16[272,384]{1,0:T(8,128)(2,1)}, bf16[272,384]{1,0:T(8,128)(2,1)}, u32[]{:S(2)}, u32[]{:S(2)}) collective-permute-start(bf16[272,384]{1,0:T(8,128)(2,1)} %pad_maximum_fusion.16), channel_id=1, source_target_pairs={{24,0},{25,1},{26,2},{27,3},{28,4},{29,5},{30,6},{31,7}} | collective-permute-start | bytes 626696 | tf_op jit(solution)/shard_map/grad_held/ppermute | solution.py:63
  474.1 108.3 %reduce-scatter.13.cloned.1.call-start = ((), (), s32[]{:S(2)}) async-start(), calls=%async_computation.12 | async-start | bytes 2621440 | tf_op jit(solution)/shard_map/qz/reduce_scatter | solution.py:427
  491.2 26.7 %collective-permute-start.67 = (bf16[256,256]{1,0:T(8,128)(2,1)S(1)}, bf16[256,256]{1,0:T(8,128)(2,1)S(1)}, u32[]{:S(2)}, u32[]{:S(2)}) collective-permute-start(bf16[256,256]{1,0:T(8,128)(2,1)S(1)} %get-tuple-element.396), channel_id=1, source_target_pairs={{16,0},{24,8},{17,1},{25,9},{18,2},{26,10},{19,3},{27,11},{20,4},{... | collective-permute-start | bytes 393224 | tf_op jit(solution)/shard_map/grad_kv/ppermute | solution.py:63
  492.5 25.4 %collective-permute-start.68 = (bf16[256,256]{1,0:T(8,128)(2,1)S(1)}, bf16[256,256]{1,0:T(8,128)(2,1)S(1)}, u32[]{:S(2)}, u32[]{:S(2)}) collective-permute-start(bf16[256,256]{1,0:T(8,128)(2,1)S(1)} %get-tuple-element.395), channel_id=1, source_target_pairs={{24,0},{25,1},{26,2},{27,3},{28,4},{29,5},{30,6},{31,7}} | collective-permute-start | bytes 393224 | tf_op jit(solution)/shard_map/grad_kv/ppermute | solution.py:63
  493.8 32.4 %collective-permute-start.69 = (bf16[256,512]{1,0:T(8,128)(2,1)S(1)}, bf16[256,512]{1,0:T(8,128)(2,1)S(1)}, u32[]{:S(2)}, u32[]{:S(2)}) collective-permute-start(bf16[256,512]{1,0:T(8,128)(2,1)S(1)} %dynamic-slice_bitcast_fusion.8), channel_id=1, source_target_pairs={{0,4},{4,0},{1,5},{5,1},{2,6},{6,2},{3,7},{7,3},{8,12},{12,8},{9,1... | collective-permute-start | bytes 786440 | tf_op jit(solution)/shard_map/down/ppermute | solution.py:43
  526.3 109.4 %reduce-scatter.17.cloned.1.call-start = ((), (), s32[]{:S(2)}) async-start(), calls=%async_computation.14 | async-start | bytes 1966080 | tf_op jit(solution)/shard_map/x/reduce_scatter | solution.py:427
  574.9 16.1 %collective-permute-start.71 = (bf16[4,128,2048]{2,1,0:T(8,128)(2,1)}, bf16[4,128,2048]{2,1,0:T(8,128)(2,1)}, u32[]{:S(2)}, u32[]{:S(2)}) collective-permute-start(bf16[4,128,2048]{2,1,0:T(8,128)(2,1)} %bitcast.90), channel_id=1, source_target_pairs={{0,1},{1,0},{2,3},{3,2},{4,5},{5,4},{6,7},{7,6},{8,9},{9,8},{10,11... | collective-permute-start | bytes 6291464 | tf_op jit(solution)/shard_map/grad_in/ppermute | solution.py:43
  576.5 92.4 %reduce-scatter.15.cloned.1.call-start = ((), (), s32[]{:S(2)}) async-start(), calls=%async_computation.13 | async-start | bytes 737280 | tf_op jit(solution)/shard_map/reduce_scatter | solution.py:1241
  578.9 38.6 %collective-permute-start.78 = (bf16[4,64,1152]{2,1,0:T(8,128)(2,1)}, bf16[4,64,1152]{2,1,0:T(8,128)(2,1)}, u32[]{:S(2)}, u32[]{:S(2)}) collective-permute-start(bf16[4,64,1152]{2,1,0:T(8,128)(2,1)} %get-tuple-element.334), channel_id=1, source_target_pairs={{0,2},{2,0},{1,3},{3,1},{4,6},{6,4},{5,7},{7,5},{8,10},{10,8},{9,1... | collective-permute-start | bytes 1769480 | tf_op jit(solution)/shard_map/grad_two/ppermute | solution.py:43
  580.4 37.7 %collective-permute-start.79 = (bf16[4,64,1152]{2,1,0:T(8,128)(2,1)}, bf16[4,64,1152]{2,1,0:T(8,128)(2,1)}, u32[]{:S(2)}, u32[]{:S(2)}) collective-permute-start(bf16[4,64,1152]{2,1,0:T(8,128)(2,1)} %get-tuple-element.333), channel_id=1, source_target_pairs={{0,4},{4,0},{1,5},{5,1},{2,6},{6,2},{3,7},{7,3},{8,12},{12,8},{9,1... | collective-permute-start | bytes 1769480 | tf_op jit(solution)/shard_map/grad_two/ppermute | solution.py:43
  581.9 36.6 %collective-permute-start.80 = (bf16[4,64,1152]{2,1,0:T(8,128)(2,1)}, bf16[4,64,1152]{2,1,0:T(8,128)(2,1)}, u32[]{:S(2)}, u32[]{:S(2)}) collective-permute-start(bf16[4,64,1152]{2,1,0:T(8,128)(2,1)} %get-tuple-element.332), channel_id=1, source_target_pairs={{0,6},{2,4},{4,2},{6,0},{1,7},{3,5},{5,3},{7,1},{8,14},{10,12},{12... | collective-permute-start | bytes 1769480 | tf_op jit(solution)/shard_map/grad_two/ppermute | solution.py:124
  594.5 19.1 %collective-permute-start.73 = (bf16[64,2048]{1,0:T(8,128)(2,1)S(1)}, bf16[64,2048]{1,0:T(8,128)(2,1)S(1)}, u32[]{:S(2)}, u32[]{:S(2)}) collective-permute-start(bf16[64,2048]{1,0:T(8,128)(2,1)S(1)} %get-tuple-element.341), channel_id=1, source_target_pairs={{0,2},{2,0},{1,3},{3,1},{4,6},{6,4},{5,7},{7,5},{8,10},{10,8},{9,1... | collective-permute-start | bytes 786440 | tf_op jit(solution)/shard_map/grad_in/ppermute | solution.py:43
  596.0 19.2 %collective-permute-start.75 = (bf16[64,2048]{1,0:T(8,128)(2,1)S(1)}, bf16[64,2048]{1,0:T(8,128)(2,1)S(1)}, u32[]{:S(2)}, u32[]{:S(2)}) collective-permute-start(bf16[64,2048]{1,0:T(8,128)(2,1)S(1)} %get-tuple-element.340), channel_id=1, source_target_pairs={{0,4},{4,0},{1,5},{5,1},{2,6},{6,2},{3,7},{7,3},{8,12},{12,8},{9,1... | collective-permute-start | bytes 786440 | tf_op jit(solution)/shard_map/grad_in/ppermute | solution.py:43
  634.3 22.9 %collective-permute-start.81 = (bf16[256,512]{1,0:T(8,128)(2,1)S(1)}, bf16[256,512]{1,0:T(8,128)(2,1)}, u32[]{:S(2)}, u32[]{:S(2)}) collective-permute-start(bf16[256,512]{1,0:T(8,128)(2,1)S(1)} %get-tuple-element.394), channel_id=1, source_target_pairs={{0,4},{4,0},{1,5},{5,1},{2,6},{6,2},{3,7},{7,3},{8,12},{12,8},{9,1... | collective-permute-start | bytes 786440 | tf_op jit(solution)/shard_map/qz/ppermute | solution.py:43
  637.3 18.8 %collective-permute-start.82 = (bf16[256,384]{1,0:T(8,128)(2,1)}, bf16[256,384]{1,0:T(8,128)(2,1)}, u32[]{:S(2)}, u32[]{:S(2)}) collective-permute-start(bf16[256,384]{1,0:T(8,128)(2,1)} %dynamic-slice_bitcast_fusion.9), channel_id=1, source_target_pairs={{0,4},{4,0},{1,5},{5,1},{2,6},{6,2},{3,7},{7,3},{8,12},{12,8},{9,1... | collective-permute-start | bytes 589832 | tf_op jit(solution)/shard_map/x/ppermute | solution.py:43
  638.8 20.2 %collective-permute-start.87 = (bf16[256,512]{1,0:T(8,128)(2,1)}, bf16[256,512]{1,0:T(8,128)(2,1)}, u32[]{:S(2)}, u32[]{:S(2)}) collective-permute-start(bf16[256,512]{1,0:T(8,128)(2,1)} %get-tuple-element.388), channel_id=1, source_target_pairs={{0,4},{4,0},{1,5},{5,1},{2,6},{6,2},{3,7},{7,3},{8,12},{12,8},{9,1... | collective-permute-start | bytes 786440 | tf_op jit(solution)/shard_map/out/ppermute | solution.py:43
  644.5 21.2 %collective-permute-start.88 = (bf16[256,1024]{1,0:T(8,128)(2,1)S(1)}, bf16[256,1024]{1,0:T(8,128)(2,1)S(1)}, u32[]{:S(2)}, u32[]{:S(2)}) collective-permute-start(bf16[256,1024]{1,0:T(8,128)(2,1)S(1)} %get-tuple-element.372), channel_id=1, source_target_pairs={{0,4},{4,0},{1,5},{5,1},{2,6},{6,2},{3,7},{7,3},{8,12},{12,8},{9,1... | collective-permute-start | bytes 1572872 | tf_op jit(solution)/shard_map/gu/ppermute | solution.py:43
  (138 other events, 1184.9 us)
Sparse Core Ops, SparseCore 0:
  38.7 44.7 all-gather.3
  88.0 78.4 all-gather.5
  188.6 117.9 all-gather.7
  330.9 42.1 reduce-scatter.6
  375.3 84.1 reduce-scatter.8
  474.2 50.3 reduce-scatter.10
  527.0 44.7 reduce-scatter.12
  576.6 33.5 reduce-scatter.16
  621.2 22.7 reduce-scatter.14

commit v5 on v4

--- a/solution.py
+++ b/solution.py
@@ -1232,9 +1232,9 @@
     in_sum, in_far, in_last = cube_scatter("grad_in", in_own, in_other)
     two_terms = lax.optimization_barrier((*two_terms, in_far))[:4]
     two_part = sum(a.astype(F32) for a in two_terms)
-    out_own, out_got = own_and_got("out", after(out_part, in_sum))
-    gu_own, gu_got = own_and_got("gu", after(gu_part, in_sum))
-    qz_own, qz_got = own_and_got("qz", after(qz_part, in_sum))
+    out_own, out_got = own_and_got("out", after(out_part, in_last))
+    gu_own, gu_got = own_and_got("gu", after(gu_part, in_last))
+    qz_own, qz_got = own_and_got("qz", after(qz_part, in_last))
     in_grad = in_sum
     input_part, _ = norm_back(stream_own, gain_one, in_grad)
     input_grad = grad_middle + input_part
@@ -1265,7 +1265,7 @@
         both_halves(qz_own[:, :inner], qz_got[:, :inner]),
         kv_grad,
         jnp.stack(
-            [both_halves(qz_own[:, inner:], qz_got[:, inner:]), both_halves(*own_and_got("x", after(x_part, in_sum)))],
+            [both_halves(qz_own[:, inner:], qz_got[:, inner:]), both_halves(*own_and_got("x", after(x_part, in_last)))],
             axis=1,
         ),
         dt_grad,

time: 689 us -> 683 us (level)
    unnamed x203 -> x199, local copies, waits for them, and re-layouts: 26.8 us -> 26.7 us
  transfers between devices with their start and end apart: 98 -> 98, of which waited for: 46 -> 43; matrix products, arithmetic and copies ran while one was open for 30% -> 30% of each run, Pallas kernels for 18% -> 18%
where the time goes in v5:
time: 683 us; the launch traced here: 674 us
  waiting for transfers between devices  202 us (30%)
  Pallas kernels  123 us (18%)
  starting transfers between devices  109 us (16%)
  matrix products  77.1 us (11%)
  other arithmetic  75.9 us (11%)
  local copies, waits for them, and re-layouts  70.2 us (10%)
  between operations  17.3 us (3%)
    ppermute x66, waiting for transfers between devices, swap(): return lax.ppermute(a, axis, SWAP)  137 us
    dot_general x22, matrix products, mm(): lax.dot_general(a, b, (((ca,), (cb,)), ((), ())), preferred_element_type=...  77.1 us
    ppermute x66, starting transfers between devices, swap(): return lax.ppermute(a, axis, SWAP)  61.3 us
    ppermute x6, waiting for transfers between devices, from_above(): lax.ppermute(values[far], 'z', [(i + far, i) for i in range(count - far)])  37 us
    unnamed x199, local copies, waits for them, and re-layouts  26.7 us
    ppermute x6, starting transfers between devices, from_below(): lax.ppermute(values[far], 'z', [(i, i + far) for i in range(count - far)])  25.2 us
    pallas_call x1, Pallas kernels, shards(): call(mamba_grad_near_kernel, (shape((group, wide)), shape((group, states)...  16.3 us
    all_gather x3, waiting for transfers between devices, weight_gather(): return lax.all_gather(both, 'z', axis=0, tiled=True)  14.4 us
  transfers between devices with their start and end apart: 98, of which 43 were waited for; matrix products, arithmetic and copies ran while one was open for 30% of the time, Pallas kernels for 18%

profile of v5, /device:TPU:0, one launch (start us, length us, event | category | flops | bytes accessed | tf_op | source)
XLA Modules:
  0.0 673.9 jit_solution(1003695015961389221)
XLA Ops:
  11.5 5.1 collective-permute-start.4
  38.7 8.6 %collective-permute-done.8 = bf16[1,4,64,1152]{3,2,1,0:T(8,128)(2,1)S(1)} collective-permute-done((bf16[1,4,64,1152]{3,2,1,0:T(8,128)(2,1)S(1)}, bf16[1,4,64,1152]{3,2,1,0:T(8,128)(2,1)S(1)}, u32[]{:S(2)}, u32[]{:S(2)}) %collective-permute-start.8) | collective-permute-done | bytes 589856 | tf_op jit(solution)/shard_map/whole_rows/ppermute | solution.py:43
  60.2 7.5 %collective-permute-done.11 = bf16[128,2048]{1,0:T(8,128)(2,1)S(1)} collective-permute-done((bf16[128,2048]{1,0:T(8,128)(2,1)S(1)}, bf16[128,2048]{1,0:T(8,128)(2,1)S(1)}, u32[]{:S(2)}, u32[]{:S(2)}) %collective-permute-start.11) | collective-permute-done | bytes 524320 | tf_op jit(solution)/shard_map/tokens/ppermute | solution.py:43
  102.1 5.7 settle_groups_kernel.1
  114.4 13.9 %project_kernel.1 = (bf16[1024,2048]{1,0:T(8,128)(2,1)}, bf16[1024,128]{1,0:T(8,128)(2,1)}, bf16[1024,384]{1,0:T(8,128)(2,1)}, bf16[1024,256]{1,0:T(8,128)(2,1)}...) custom-call(s32[3]{0:T(128)} %pad_add_fusion.2.place, ...), custom_call_target="tpu_custom_call" | custom-call | tf_op jit(solution)/shard_map/project_kernel/pallas_call | solution.py:271
  130.8 6.3 collective-permute-start.20
  140.2 10.6 %mamba_local_kernel.1 = (f32[1024,384]{1,0:T(8,128)}, f32[1024,128]{1,0:T(8,128)}, f32[256,384]{1,0:T(8,128)}, f32[8,128]{1,0:T(8,128)}, f32[4,256,384]{2,1,0:T(8,128)}) custom-call(bf16[1024,384]{1,0:T(8,128)(2,1)} %get-tuple-element.140.x_in_ref, bf16[1024,512]{1,0:T(8,128)(2,1)} %get-tuple-element.141.bc_in_ref, ...), custom_call_target="tpu_custom_call" | custom-call | tf_op jit(solution)/shard_map/mamba_local_kernel/pallas_call | solution.py:962
  154.5 9.2 %collective-permute-start.23 = (bf16[272,384]{1,0:T(8,128)(2,1)S(1)}, bf16[272,384]{1,0:T(8,128)(2,1)S(1)}, u32[]{:S(2)}, u32[]{:S(2)}) collective-permute-start(bf16[272,384]{1,0:T(8,128)(2,1)S(1)} %pad_maximum_fusion.17), channel_id=1, source_target_pairs={{0,8},{8,16},{16,24},{1,9},{9,17},{17,25},{2,10},{10,18},{18,26},{... | collective-permute-start | bytes 626696 | tf_op jit(solution)/shard_map/held/ppermute | solution.py:54
  163.7 5.5 collective-permute-start.24
  180.1 6.8 %collective-permute-done.38 = bf16[256,1536]{0,1:T(8,128)(2,1)S(1)} collective-permute-done((bf16[256,1536]{0,1:T(8,128)(2,1)}, bf16[256,1536]{0,1:T(8,128)(2,1)S(1)}, u32[]{:S(2)}, u32[]{:S(2)}) %collective-permute-start.38) | collective-permute-done | bytes 786464 | tf_op jit(solution)/shard_map/ppermute | solution.py:43
  192.9 8.3 %pad_maximum_fusion.w_ref = bf16[2048,2048]{1,0:T(8,128)(2,1)} fusion(bf16[2048,384]{1,0:T(8,128)(2,1)S(1)} %slice.506, bf16[2048,128]{1,0:T(8,128)(2,1)S(1)} %copy-done.22, bf16[2048,1024]{1,0:T(8,128)(2,1)} %bitcast.339, bf16[2048,512]{1,0:T(8,128)(2,1)S(1)} %copy-done.12), kind=kLoop, calls=%fused_computation | loop fusion | flops 33554432 | bytes 16777216 | tf_op jit(solution)/shard_map/concatenate | solution.py:995
  204.4 7.2 %attend_kernel.1 = (f32[1024,128]{1,0:T(8,128)}, f32[1024,128]{1,0:T(8,128)}) custom-call(s32[4]{0:T(128)} %and_select_fusion.1.low_ref, s32[4]{0:T(128)} %fusion.112.high_ref, s32[1]{0:T(128)} %bitcast.18.start_ref, s32[2]{0:T(128)} %pad_add_fusion.1.where_ref, bf16[1024,128]{1,0:T(8,128)(2,1)} %get-tuple-element.138.q_ref, bf16[4096,256]{1,0:T(8,128)(2,1)} %copy-done.4, ...), custom_call_target="tpu_custom_call" | custom-call | tf_op jit(solution)/shard_map/attend_kernel/pallas_call | solution.py:1020
  211.6 5.2 mamba_close_kernel.1
  216.8 4.6 unsettle_kernel.1
  233.9 5.1 collective-permute-done.29
  244.8 4.7 collective-permute-done.32
  253.5 11.1 %collective-permute-done.35 = bf16[128,2048]{1,0:T(8,128)(2,1)S(1)} collective-permute-done((bf16[128,2048]{1,0:T(8,128)(2,1)S(1)}, bf16[128,2048]{1,0:T(8,128)(2,1)S(1)}, u32[]{:S(2)}, u32[]{:S(2)}) %collective-permute-start.35) | collective-permute-done | bytes 524320 | tf_op jit(solution)/shard_map/normed_two/ppermute | solution.py:43
  266.9 4.5 collective-permute-done.36
  274.5 9.4 %collective-permute-done.40 = bf16[128,2048]{1,0:T(8,128)(2,1)S(1)} collective-permute-done((bf16[128,2048]{1,0:T(8,128)(2,1)S(1)}, bf16[128,2048]{1,0:T(8,128)(2,1)S(1)}, u32[]{:S(2)}, u32[]{:S(2)}) %collective-permute-start.40) | collective-permute-done | bytes 524320 | tf_op jit(solution)/shard_map/cotangent/ppermute | solution.py:43
  287.1 3.3 collective-permute-done.41
  292.3 14.4 %all-gather.8.cloned.1.call-done = bf16[2048,1536]{0,1:T(8,128)(2,1)} async-done(((bf16[512,1536]{0,1:T(8,128)(2,1)}), bf16[2048,1536]{0,1:T(8,128)(2,1)}) %all-gather.8.cloned.1.call-update) | async-done | bytes 6291472 | tf_op jit(solution)/shard_map/w_ff/all_gather | solution.py:413
  306.6 5.3 fusion.9
  312.0 3.3 fusion.46
  315.3 3.7 convolution_convert_fusion
  331.9 4.5 convolution_convert_fusion.1
  343.7 5.1 collective-permute-done.47
  353.2 4.0 fusion.74
  357.3 4.6 add_convert_fusion
  376.1 3.9 collective-permute-done.53
  383.4 4.1 collective-permute-done.55
  399.5 4.1 settle_kernel.1
  403.5 10.1 %attend_grad_kernel.1 = (f32[1024,128]{1,0:T(8,128)}, bf16[4096,256]{1,0:T(8,128)(2,1)}) custom-call(s32[4]{0:T(128)} %and_select_fusion.1.low_ref, s32[4]{0:T(128)} %fusion.112.high_ref, s32[1]{0:T(128)} %bitcast.18.start_ref, s32[2]{0:T(128)} %pad_add_fusion.1.where_ref, bf16[1024,128]{1,0:T(8,128)(2,1)} %get-tuple-element.138.q_ref, ...), custom_call_target="tpu_custom_call" | custom-call | tf_op jit(solution)/shard_map/attend_grad_kernel/pallas_call | solution.py:1100
  422.0 6.3 mamba_grad_state_kernel.1
  434.4 16.3 %mamba_grad_near_kernel.1 = (f32[1024,384]{1,0:T(8,128)}, f32[1024,256]{1,0:T(8,128)}, bf16[1024,256]{1,0:T(8,128)(2,1)}, f32[1024,128]{1,0:T(8,128)}, f32[4,256,384]{2,1,0:T(8,128)}, /*index=5*/f32[8,384]{1,0:T(8,128)}) custom-call(bf16[1024,384]{1,0:T(8,128)(2,1)} %get-tuple-element.140.x_in_ref, bf16[1024,512]{1,0:T(8,128)(2,1)} %get-tuple-element.141.bc_in_ref, ...), custom_call_target="tpu_custom_call" | custom-call | tf_op jit(solution)/shard_map/mamba_grad_near_kernel/pallas_call | solution.py:1134
  453.6 15.3 %collective-permute-done.62 = bf16[272,384]{1,0:T(8,128)(2,1)} collective-permute-done((bf16[272,384]{1,0:T(8,128)(2,1)}, bf16[272,384]{1,0:T(8,128)(2,1)}, u32[]{:S(2)}, u32[]{:S(2)}) %collective-permute-start.62) | collective-permute-done | bytes 208928 | tf_op jit(solution)/shard_map/grad_held/ppermute | solution.py:63
  480.5 9.3 %collective-permute-done.65 = bf16[4,256,256]{2,1,0:T(8,128)(2,1)S(1)} collective-permute-done((bf16[4,256,256]{2,1,0:T(8,128)(2,1)S(1)}, bf16[4,256,256]{2,1,0:T(8,128)(2,1)S(1)}, u32[]{:S(2)}, u32[]{:S(2)}) %collective-permute-start.65) | collective-permute-done | bytes 524320 | tf_op jit(solution)/shard_map/ppermute | solution.py:43
  496.1 6.7 %collective-permute-done.66 = bf16[256,256]{1,0:T(8,128)(2,1)S(1)} collective-permute-done((bf16[256,256]{1,0:T(8,128)(2,1)S(1)}, bf16[256,256]{1,0:T(8,128)(2,1)S(1)}, u32[]{:S(2)}, u32[]{:S(2)}) %collective-permute-start.66) | collective-permute-done | bytes 131104 | tf_op jit(solution)/shard_map/grad_kv/ppermute | solution.py:63
  502.9 15.0 %collective-permute-done.67 = bf16[256,256]{1,0:T(8,128)(2,1)S(1)} collective-permute-done((bf16[256,256]{1,0:T(8,128)(2,1)S(1)}, bf16[256,256]{1,0:T(8,128)(2,1)S(1)}, u32[]{:S(2)}, u32[]{:S(2)}) %collective-permute-start.67) | collective-permute-done | bytes 131104 | tf_op jit(solution)/shard_map/grad_kv/ppermute | solution.py:63
  517.9 8.2 %grad_early_kernel.1 = (bf16[2048,512]{1,0:T(8,128)(2,1)}, f32[2048,128]{1,0:T(8,128)}) custom-call(bf16[1024,2048]{1,0:T(8,128)(2,1)} %get-tuple-element.151.normed_ref, bf16[1024,128]{1,0:T(8,128)(2,1)} %fusion.76.q_ref, bf16[1024,384]{1,0:T(8,128)(2,1)} %get-tuple-element.202.z_ref, bf16[2048,2048]{1,0:T(8,128)(2,1)} %pad_maximum_fusion.w_ref), custom_call_target="tpu_custom_call" | custom-call | tf_op jit(solution)/shard_map/grad_early_kernel/pallas_call | solution.py:306
  526.9 11.2 %mamba_grad_kernel.1 = (bf16[1024,384]{1,0:T(8,128)(2,1)}, bf16[1024,512]{1,0:T(8,128)(2,1)}, bf16[1024,128]{1,0:T(8,128)(2,1)}, f32[8,128]{1,0:T(8,128)}) custom-call(bf16[1024,384]{1,0:T(8,128)(2,1)} %get-tuple-element.140.x_in_ref, bf16[1024,512]{1,0:T(8,128)(2,1)} %get-tuple-element.141.bc_in_ref, bf16[1024,128]{1,0:T(8,128)(2,1)} %get-tuple-element.142.dt_in_ref, ...), custom_call_target="tpu_custom_call" | custom-call | tf_op jit(solution)/shard_map/mamba_grad_kernel/pallas_call | solution.py:1189
  539.3 14.2 %grad_late_kernel.1 = (bf16[2048,384]{1,0:T(8,128)(2,1)}, bf16[4,4,64,1152]{3,2,1,0:T(8,128)(2,1)}, bf16[4,4,64,1152]{3,2,1,0:T(8,128)(2,1)}) custom-call(s32[3]{0:T(128)} %pad_add_fusion.2.place, bf16[1024,2048]{1,0:T(8,128)(2,1)} %get-tuple-element.151.normed_ref, bf16[1024,384]{1,0:T(8,128)(2,1)} %get-tuple-element.215.x_ref, ...), custom_call_target="tpu_custom_call" | custom-call | tf_op jit(solution)/shard_map/grad_late_kernel/pallas_call | solution.py:362
  555.5 5.5 assemble_kernel.1
  565.7 9.3 %convolution_convert_fusion.3 = bf16[512,2048]{1,0:T(8,128)(2,1)} fusion(bf16[512,2048]{1,0:T(8,128)(2,1)S(1)} %copy-done.73, bf16[2048,2048]{1,0:T(8,128)(2,1)} %pad_maximum_fusion.w_ref), kind=kOutput, calls=%fused_computation.7 | convolution fusion | flops 4296015872 | bytes 12582912 | tf_op jit(solution)/shard_map/dot_general | solution.py:29
  582.4 8.7 %convolution_convert_fusion.2 = bf16[512,2048]{1,0:T(8,128)(2,1)S(1)} fusion(bf16[512,2048]{1,0:T(8,128)(2,1)} %get-tuple-element.222, bf16[2048,2048]{1,0:T(8,128)(2,1)} %pad_maximum_fusion.w_ref), kind=kOutput, calls=%fused_computation.6 | convolution fusion | flops 4296015872 | bytes 12582912 | tf_op jit(solution)/shard_map/dot_general | solution.py:29
  598.2 15.3 %collective-permute-done.73 = bf16[64,2048]{1,0:T(8,128)(2,1)S(1)} collective-permute-done((bf16[64,2048]{1,0:T(8,128)(2,1)S(1)}, bf16[64,2048]{1,0:T(8,128)(2,1)S(1)}, u32[]{:S(2)}, u32[]{:S(2)}) %collective-permute-start.73) | collective-permute-done | bytes 262176 | tf_op jit(solution)/shard_map/grad_in/ppermute | solution.py:43
  627.0 5.8 collective-permute-done.82
  639.7 8.0 %collective-permute-done.87 = bf16[256,512]{1,0:T(8,128)(2,1)S(1)} collective-permute-done((bf16[256,512]{1,0:T(8,128)(2,1)S(1)}, bf16[256,512]{1,0:T(8,128)(2,1)S(1)}, u32[]{:S(2)}, u32[]{:S(2)}) %collective-permute-start.87) | collective-permute-done | bytes 262176 | tf_op jit(solution)/shard_map/out/ppermute | solution.py:43
  649.9 4.1 collective-permute-done.83
  (593 shorter events, 287.7 us)
Async XLA Ops:
  7.2 107.2 %all-gather.4.cloned.1.call-start = ((), (), s32[]{:S(2)}) async-start(), calls=%async_computation.6 | async-start | bytes 2621440 | tf_op jit(solution)/shard_map/w_one/all_gather | solution.py:413
  11.5 15.4 %collective-permute-start.4 = (bf16[64,1152]{1,0:T(8,128)(2,1)S(1)}, bf16[64,1152]{1,0:T(8,128)(2,1)S(1)}, u32[]{:S(2)}, u32[]{:S(2)}) collective-permute-start(bf16[64,1152]{1,0:T(8,128)(2,1)S(1)} %get-tuple-element.412), channel_id=1, source_target_pairs={{0,24},{8,0},{16,8},{24,16},{1,25},{9,1},{17,9},{25,17},{2,26},{10... | collective-permute-start | bytes 442376 | tf_op jit(solution)/shard_map/whole_rows/ppermute | solution.py:72
  35.2 14.3 %collective-permute-start.15 = (bf16[1,4,64,1152]{3,2,1,0:T(8,128)(2,1)S(1)}, bf16[1,4,64,1152]{3,2,1,0:T(8,128)(2,1)S(1)}, u32[]{:S(2)}, u32[]{:S(2)}) collective-permute-start(bf16[1,4,64,1152]{3,2,1,0:T(8,128)(2,1)S(1)} %maximum_bitcast_fusion), channel_id=1, source_target_pairs={{0,2},{2,0},{1,3},{3,1},{4,6},{6,4},{5,7},{7,5},{8,10},{10,8},{9,1... | collective-permute-start | bytes 1769480 | tf_op jit(solution)/shard_map/whole_rows/ppermute | solution.py:43
  38.5 151.4 %all-gather.6.cloned.1.call-start = ((), (), s32[]{:S(2)}) async-start(), calls=%async_computation.7 | async-start | bytes 4587520 | tf_op jit(solution)/shard_map/w_mix/all_gather | solution.py:413
  54.9 14.3 %collective-permute-start.10 = (bf16[128,2048]{1,0:T(8,128)(2,1)S(1)}, bf16[128,2048]{1,0:T(8,128)(2,1)S(1)}, u32[]{:S(2)}, u32[]{:S(2)}) collective-permute-start(bf16[128,2048]{1,0:T(8,128)(2,1)S(1)} %copy-done.10), channel_id=1, source_target_pairs={{0,2},{2,0},{1,3},{3,1},{4,6},{6,4},{5,7},{7,5},{8,10},{10,8},{9,1... | collective-permute-start | bytes 1572872 | tf_op jit(solution)/shard_map/tokens/ppermute | solution.py:43
  59.1 43.0 %collective-permute-start.17 = (bf16[4,4,64,1152]{3,2,1,0:T(8,128)(2,1)S(1)}, bf16[4,4,64,1152]{3,2,1,0:T(8,128)(2,1)}, u32[]{:S(2)}, u32[]{:S(2)}) collective-permute-start(bf16[4,4,64,1152]{3,2,1,0:T(8,128)(2,1)S(1)} %maximum_maximum_fusion.own_ref), channel_id=1, source_target_pairs={{0,1},{1,0},{2,3},{3,2},{4,5},{5,4},{6,7},{7,6},{8,9},{9,8},{10,11... | collective-permute-start | bytes 7077896 | tf_op jit(solution)/shard_map/whole_rows/ppermute | solution.py:43
  84.2 30.2 %collective-permute-start.14 = (bf16[512,2048]{1,0:T(8,128)(2,1)}, bf16[512,2048]{1,0:T(8,128)(2,1)}, u32[]{:S(2)}, u32[]{:S(2)}) collective-permute-start(bf16[512,2048]{1,0:T(8,128)(2,1)} %constant_dynamic-update-slice_fusion.own_ref), channel_id=1, source_target_pairs={{0,1},{1,0},{2,3},{3,2},{4,5},{5,4},{6,7},{7,6},{8,9},{9,8},{10,11... | collective-permute-start | bytes 6291464 | tf_op jit(solution)/shard_map/tokens/ppermute | solution.py:43
  87.9 218.7 %all-gather.8.cloned.1.call-start = ((), (), s32[]{:S(2)}) async-start(), calls=%async_computation.8 | async-start | bytes 7864320 | tf_op jit(solution)/shard_map/w_ff/all_gather | solution.py:413
  129.2 23.5 %collective-permute-start.19 = (bf16[256,256]{1,0:T(8,128)(2,1)S(1)}, bf16[256,256]{1,0:T(8,128)(2,1)S(1)}, u32[]{:S(2)}, u32[]{:S(2)}) collective-permute-start(bf16[256,256]{1,0:T(8,128)(2,1)S(1)} %constant_dynamic-slice_fusion.2), channel_id=1, source_target_pairs={{0,8},{8,16},{16,24},{1,9},{9,17},{17,25},{2,10},{10,18},{18,26},{... | collective-permute-start | bytes 393224 | tf_op jit(solution)/shard_map/kv/ppermute | solution.py:54
  130.8 21.9 %collective-permute-start.20 = (bf16[256,256]{1,0:T(8,128)(2,1)S(1)}, bf16[256,256]{1,0:T(8,128)(2,1)S(1)}, u32[]{:S(2)}, u32[]{:S(2)}) collective-permute-start(bf16[256,256]{1,0:T(8,128)(2,1)S(1)} %constant_dynamic-slice_fusion.2), channel_id=1, source_target_pairs={{0,16},{8,24},{1,17},{9,25},{2,18},{10,26},{3,19},{11,27},{4,20},{... | collective-permute-start | bytes 393224 | tf_op jit(solution)/shard_map/kv/ppermute | solution.py:54
  137.1 15.6 %collective-permute-start.21 = (bf16[256,256]{1,0:T(8,128)(2,1)S(1)}, bf16[256,256]{1,0:T(8,128)(2,1)S(1)}, u32[]{:S(2)}, u32[]{:S(2)}) collective-permute-start(bf16[256,256]{1,0:T(8,128)(2,1)S(1)} %constant_dynamic-slice_fusion.2), channel_id=1, source_target_pairs={{0,24},{1,25},{2,26},{3,27},{4,28},{5,29},{6,30},{7,31}} | collective-permute-start | bytes 393224 | tf_op jit(solution)/shard_map/kv/ppermute | solution.py:54
  152.8 18.8 %collective-permute-start.22 = (bf16[3,256,256]{2,1,0:T(8,128)(2,1)S(1)}, bf16[3,256,256]{2,1,0:T(8,128)(2,1)S(1)}, u32[]{:S(2)}, u32[]{:S(2)}) collective-permute-start(bf16[3,256,256]{2,1,0:T(8,128)(2,1)S(1)} %pad_maximum_fusion.15), channel_id=1, source_target_pairs={{0,4},{4,0},{1,5},{5,1},{2,6},{6,2},{3,7},{7,3},{8,12},{12,8},{9,1... | collective-permute-start | bytes 1179656 | tf_op jit(solution)/shard_map/ppermute | solution.py:43
  154.5 18.2 %collective-permute-start.23 = (bf16[272,384]{1,0:T(8,128)(2,1)S(1)}, bf16[272,384]{1,0:T(8,128)(2,1)S(1)}, u32[]{:S(2)}, u32[]{:S(2)}) collective-permute-start(bf16[272,384]{1,0:T(8,128)(2,1)S(1)} %pad_maximum_fusion.17), channel_id=1, source_target_pairs={{0,8},{8,16},{16,24},{1,9},{9,17},{17,25},{2,10},{10,18},{18,26},{... | collective-permute-start | bytes 626696 | tf_op jit(solution)/shard_map/held/ppermute | solution.py:54
  170.5 16.3 %collective-permute-start.38 = (bf16[256,1536]{0,1:T(8,128)(2,1)}, bf16[256,1536]{0,1:T(8,128)(2,1)S(1)}, u32[]{:S(2)}, u32[]{:S(2)}) collective-permute-start(bf16[256,1536]{0,1:T(8,128)(2,1)} %fusion.71), channel_id=1, source_target_pairs={{0,4},{4,0},{1,5},{5,1},{2,6},{6,2},{3,7},{7,3},{8,12},{12,8},{9,1... | collective-permute-start | bytes 2359304 | tf_op jit(solution)/shard_map/ppermute | solution.py:43
  188.5 215.0 %reduce-scatter.7.cloned.1.call-start = ((), (), s32[]{:S(2)}) async-start(), calls=%async_computation.9 | async-start | bytes 2621440 | tf_op jit(solution)/shard_map/down/reduce_scatter | solution.py:427
  274.5 17.8 %collective-permute-start.44 = (bf16[512,2048]{1,0:T(8,128)(2,1)S(1)}, bf16[512,2048]{1,0:T(8,128)(2,1)}, u32[]{:S(2)}, u32[]{:S(2)}) collective-permute-start(bf16[512,2048]{1,0:T(8,128)(2,1)S(1)} %constant_dynamic-update-slice_fusion.7), channel_id=1, source_target_pairs={{0,1},{1,0},{2,3},{3,2},{4,5},{5,4},{6,7},{7,6},{8,9},{9,8},{10,11... | collective-permute-start | bytes 6291464 | tf_op jit(solution)/shard_map/normed_two/ppermute | solution.py:43
  292.2 19.8 %collective-permute-start.43 = (bf16[512,2048]{1,0:T(8,128)(2,1)S(1)}, bf16[512,2048]{1,0:T(8,128)(2,1)}, u32[]{:S(2)}, u32[]{:S(2)}) collective-permute-start(bf16[512,2048]{1,0:T(8,128)(2,1)S(1)} %constant_dynamic-update-slice_fusion.12), channel_id=1, source_target_pairs={{0,1},{1,0},{2,3},{3,2},{4,5},{5,4},{6,7},{7,6},{8,9},{9,8},{10,11... | collective-permute-start | bytes 6291464 | tf_op jit(solution)/shard_map/cotangent/ppermute | solution.py:43
  319.0 17.4 %collective-permute-start.45 = (bf16[4,128,2048]{2,1,0:T(8,128)(2,1)}, bf16[4,128,2048]{2,1,0:T(8,128)(2,1)}, u32[]{:S(2)}, u32[]{:S(2)}) collective-permute-start(bf16[4,128,2048]{2,1,0:T(8,128)(2,1)} %bitcast.64), channel_id=1, source_target_pairs={{0,1},{1,0},{2,3},{3,2},{4,5},{5,4},{6,7},{7,6},{8,9},{9,8},{10,11... | collective-permute-start | bytes 6291464 | tf_op jit(solution)/shard_map/grad_normed_two/ppermute | solution.py:43
  330.7 187.1 %reduce-scatter.9.cloned.1.call-start = ((), (), s32[]{:S(2)}) async-start(), calls=%async_computation.10 | async-start | bytes 5242880 | tf_op jit(solution)/shard_map/gu/reduce_scatter | solution.py:427
  342.6 19.3 %collective-permute-start.51 = (bf16[64,2048]{1,0:T(8,128)(2,1)}, bf16[64,2048]{1,0:T(8,128)(2,1)S(1)}, u32[]{:S(2)}, u32[]{:S(2)}) collective-permute-start(bf16[64,2048]{1,0:T(8,128)(2,1)} %get-tuple-element.350), channel_id=1, source_target_pairs={{0,2},{2,0},{1,3},{3,1},{4,6},{6,4},{5,7},{7,5},{8,10},{10,8},{9,1... | collective-permute-start | bytes 786440 | tf_op jit(solution)/shard_map/grad_normed_two/ppermute | solution.py:43
  343.2 18.7 %collective-permute-start.46 = (bf16[64,2048]{1,0:T(8,128)(2,1)}, bf16[64,2048]{1,0:T(8,128)(2,1)}, u32[]{:S(2)}, u32[]{:S(2)}) collective-permute-start(bf16[64,2048]{1,0:T(8,128)(2,1)} %get-tuple-element.349), channel_id=1, source_target_pairs={{0,4},{4,0},{1,5},{5,1},{2,6},{6,2},{3,7},{7,3},{8,12},{12,8},{9,1... | collective-permute-start | bytes 786440 | tf_op jit(solution)/shard_map/grad_normed_two/ppermute | solution.py:43
  366.2 171.9 %reduce-scatter.11.cloned.1.call-start = ((), (), s32[]{:S(2)}) async-start(), calls=%async_computation.11 | async-start | bytes 2621440 | tf_op jit(solution)/shard_map/out/reduce_scatter | solution.py:427
  373.1 17.4 %collective-permute-start.52 = (bf16[4,128,2048]{2,1,0:T(8,128)(2,1)S(1)}, bf16[4,128,2048]{2,1,0:T(8,128)(2,1)S(1)}, u32[]{:S(2)}, u32[]{:S(2)}) collective-permute-start(bf16[4,128,2048]{2,1,0:T(8,128)(2,1)S(1)} %bitcast.404), channel_id=1, source_target_pairs={{0,1},{1,0},{2,3},{3,2},{4,5},{5,4},{6,7},{7,6},{8,9},{9,8},{10,11... | collective-permute-start | bytes 6291464 | tf_op jit(solution)/shard_map/layer_out/ppermute | solution.py:43
  392.6 23.7 %collective-permute-start.59 = (bf16[128,2048]{1,0:T(8,128)(2,1)}, bf16[128,2048]{1,0:T(8,128)(2,1)}, u32[]{:S(2)}, u32[]{:S(2)}) collective-permute-start(bf16[128,2048]{1,0:T(8,128)(2,1)} %get-tuple-element.347), channel_id=1, source_target_pairs={{0,6},{2,4},{4,2},{6,0},{1,7},{3,5},{5,3},{7,1},{8,14},{10,12},{12... | collective-permute-start | bytes 1572872 | tf_op jit(solution)/shard_map/layer_out/ppermute | solution.py:124
  394.1 25.1 %collective-permute-start.58 = (bf16[128,2048]{1,0:T(8,128)(2,1)}, bf16[128,2048]{1,0:T(8,128)(2,1)}, u32[]{:S(2)}, u32[]{:S(2)}) collective-permute-start(bf16[128,2048]{1,0:T(8,128)(2,1)} %get-tuple-element.348), channel_id=1, source_target_pairs={{0,4},{4,0},{1,5},{5,1},{2,6},{6,2},{3,7},{7,3},{8,12},{12,8},{9,1... | collective-permute-start | bytes 1572872 | tf_op jit(solution)/shard_map/layer_out/ppermute | solution.py:43
  395.4 24.0 %collective-permute-start.57 = (bf16[128,2048]{1,0:T(8,128)(2,1)}, bf16[128,2048]{1,0:T(8,128)(2,1)}, u32[]{:S(2)}, u32[]{:S(2)}) collective-permute-start(bf16[128,2048]{1,0:T(8,128)(2,1)} %get-tuple-element.346), channel_id=1, source_target_pairs={{0,2},{2,0},{1,3},{3,1},{4,6},{6,4},{5,7},{7,5},{8,10},{10,8},{9,1... | collective-permute-start | bytes 1572872 | tf_op jit(solution)/shard_map/layer_out/ppermute | solution.py:43
  416.3 52.6 %collective-permute-start.64 = (bf16[4,512,256]{2,1,0:T(8,128)(2,1)}, bf16[4,512,256]{2,1,0:T(8,128)(2,1)}, u32[]{:S(2)}, u32[]{:S(2)}) collective-permute-start(bf16[4,512,256]{2,1,0:T(8,128)(2,1)} %bitcast.79), channel_id=1, source_target_pairs={{0,1},{1,0},{2,3},{3,2},{4,5},{5,4},{6,7},{7,6},{8,9},{9,8},{10,11... | collective-permute-start | bytes 3145736 | tf_op jit(solution)/shard_map/ppermute | solution.py:43
  430.1 23.5 %collective-permute-start.61 = (bf16[272,384]{1,0:T(8,128)(2,1)}, bf16[272,384]{1,0:T(8,128)(2,1)S(1)}, u32[]{:S(2)}, u32[]{:S(2)}) collective-permute-start(bf16[272,384]{1,0:T(8,128)(2,1)} %pad_maximum_fusion.16), channel_id=1, source_target_pairs={{8,0},{16,8},{24,16},{9,1},{17,9},{25,17},{10,2},{18,10},{26,18},{... | collective-permute-start | bytes 626696 | tf_op jit(solution)/shard_map/grad_held/ppermute | solution.py:63
  431.4 37.6 %collective-permute-start.62 = (bf16[272,384]{1,0:T(8,128)(2,1)}, bf16[272,384]{1,0:T(8,128)(2,1)}, u32[]{:S(2)}, u32[]{:S(2)}) collective-permute-start(bf16[272,384]{1,0:T(8,128)(2,1)} %pad_maximum_fusion.16), channel_id=1, source_target_pairs={{16,0},{24,8},{17,1},{25,9},{18,2},{26,10},{19,3},{27,11},{20,4},{... | collective-permute-start | bytes 626696 | tf_op jit(solution)/shard_map/grad_held/ppermute | solution.py:63
  432.7 36.3 %collective-permute-start.63 = (bf16[272,384]{1,0:T(8,128)(2,1)}, bf16[272,384]{1,0:T(8,128)(2,1)}, u32[]{:S(2)}, u32[]{:S(2)}) collective-permute-start(bf16[272,384]{1,0:T(8,128)(2,1)} %pad_maximum_fusion.16), channel_id=1, source_target_pairs={{24,0},{25,1},{26,2},{27,3},{28,4},{29,5},{30,6},{31,7}} | collective-permute-start | bytes 626696 | tf_op jit(solution)/shard_map/grad_held/ppermute | solution.py:63
  474.0 108.4 %reduce-scatter.13.cloned.1.call-start = ((), (), s32[]{:S(2)}) async-start(), calls=%async_computation.12 | async-start | bytes 2621440 | tf_op jit(solution)/shard_map/qz/reduce_scatter | solution.py:427
  491.1 26.7 %collective-permute-start.67 = (bf16[256,256]{1,0:T(8,128)(2,1)S(1)}, bf16[256,256]{1,0:T(8,128)(2,1)S(1)}, u32[]{:S(2)}, u32[]{:S(2)}) collective-permute-start(bf16[256,256]{1,0:T(8,128)(2,1)S(1)} %get-tuple-element.396), channel_id=1, source_target_pairs={{16,0},{24,8},{17,1},{25,9},{18,2},{26,10},{19,3},{27,11},{20,4},{... | collective-permute-start | bytes 393224 | tf_op jit(solution)/shard_map/grad_kv/ppermute | solution.py:63
  492.4 25.4 %collective-permute-start.68 = (bf16[256,256]{1,0:T(8,128)(2,1)S(1)}, bf16[256,256]{1,0:T(8,128)(2,1)S(1)}, u32[]{:S(2)}, u32[]{:S(2)}) collective-permute-start(bf16[256,256]{1,0:T(8,128)(2,1)S(1)} %get-tuple-element.395), channel_id=1, source_target_pairs={{24,0},{25,1},{26,2},{27,3},{28,4},{29,5},{30,6},{31,7}} | collective-permute-start | bytes 393224 | tf_op jit(solution)/shard_map/grad_kv/ppermute | solution.py:63
  493.8 32.4 %collective-permute-start.69 = (bf16[256,512]{1,0:T(8,128)(2,1)S(1)}, bf16[256,512]{1,0:T(8,128)(2,1)S(1)}, u32[]{:S(2)}, u32[]{:S(2)}) collective-permute-start(bf16[256,512]{1,0:T(8,128)(2,1)S(1)} %dynamic-slice_bitcast_fusion.8), channel_id=1, source_target_pairs={{0,4},{4,0},{1,5},{5,1},{2,6},{6,2},{3,7},{7,3},{8,12},{12,8},{9,1... | collective-permute-start | bytes 786440 | tf_op jit(solution)/shard_map/down/ppermute | solution.py:43
  526.2 94.9 %reduce-scatter.17.cloned.1.call-start = ((), (), s32[]{:S(2)}) async-start(), calls=%async_computation.14 | async-start | bytes 1966080 | tf_op jit(solution)/shard_map/x/reduce_scatter | solution.py:427
  575.0 16.1 %collective-permute-start.71 = (bf16[4,128,2048]{2,1,0:T(8,128)(2,1)}, bf16[4,128,2048]{2,1,0:T(8,128)(2,1)}, u32[]{:S(2)}, u32[]{:S(2)}) collective-permute-start(bf16[4,128,2048]{2,1,0:T(8,128)(2,1)} %bitcast.90), channel_id=1, source_target_pairs={{0,1},{1,0},{2,3},{3,2},{4,5},{5,4},{6,7},{7,6},{8,9},{9,8},{10,11... | collective-permute-start | bytes 6291464 | tf_op jit(solution)/shard_map/grad_in/ppermute | solution.py:43
  576.6 86.9 %reduce-scatter.15.cloned.1.call-start = ((), (), s32[]{:S(2)}) async-start(), calls=%async_computation.13 | async-start | bytes 737280 | tf_op jit(solution)/shard_map/reduce_scatter | solution.py:1241
  578.9 38.6 %collective-permute-start.78 = (bf16[4,64,1152]{2,1,0:T(8,128)(2,1)}, bf16[4,64,1152]{2,1,0:T(8,128)(2,1)}, u32[]{:S(2)}, u32[]{:S(2)}) collective-permute-start(bf16[4,64,1152]{2,1,0:T(8,128)(2,1)} %get-tuple-element.334), channel_id=1, source_target_pairs={{0,2},{2,0},{1,3},{3,1},{4,6},{6,4},{5,7},{7,5},{8,10},{10,8},{9,1... | collective-permute-start | bytes 1769480 | tf_op jit(solution)/shard_map/grad_two/ppermute | solution.py:43
  580.5 37.5 %collective-permute-start.79 = (bf16[4,64,1152]{2,1,0:T(8,128)(2,1)}, bf16[4,64,1152]{2,1,0:T(8,128)(2,1)}, u32[]{:S(2)}, u32[]{:S(2)}) collective-permute-start(bf16[4,64,1152]{2,1,0:T(8,128)(2,1)} %get-tuple-element.333), channel_id=1, source_target_pairs={{0,4},{4,0},{1,5},{5,1},{2,6},{6,2},{3,7},{7,3},{8,12},{12,8},{9,1... | collective-permute-start | bytes 1769480 | tf_op jit(solution)/shard_map/grad_two/ppermute | solution.py:43
  581.9 36.6 %collective-permute-start.80 = (bf16[4,64,1152]{2,1,0:T(8,128)(2,1)}, bf16[4,64,1152]{2,1,0:T(8,128)(2,1)}, u32[]{:S(2)}, u32[]{:S(2)}) collective-permute-start(bf16[4,64,1152]{2,1,0:T(8,128)(2,1)} %get-tuple-element.332), channel_id=1, source_target_pairs={{0,6},{2,4},{4,2},{6,0},{1,7},{3,5},{5,3},{7,1},{8,14},{10,12},{12... | collective-permute-start | bytes 1769480 | tf_op jit(solution)/shard_map/grad_two/ppermute | solution.py:124
  594.5 19.1 %collective-permute-start.73 = (bf16[64,2048]{1,0:T(8,128)(2,1)S(1)}, bf16[64,2048]{1,0:T(8,128)(2,1)S(1)}, u32[]{:S(2)}, u32[]{:S(2)}) collective-permute-start(bf16[64,2048]{1,0:T(8,128)(2,1)S(1)} %get-tuple-element.341), channel_id=1, source_target_pairs={{0,2},{2,0},{1,3},{3,1},{4,6},{6,4},{5,7},{7,5},{8,10},{10,8},{9,1... | collective-permute-start | bytes 786440 | tf_op jit(solution)/shard_map/grad_in/ppermute | solution.py:43
  596.1 19.1 %collective-permute-start.75 = (bf16[64,2048]{1,0:T(8,128)(2,1)S(1)}, bf16[64,2048]{1,0:T(8,128)(2,1)S(1)}, u32[]{:S(2)}, u32[]{:S(2)}) collective-permute-start(bf16[64,2048]{1,0:T(8,128)(2,1)S(1)} %get-tuple-element.340), channel_id=1, source_target_pairs={{0,4},{4,0},{1,5},{5,1},{2,6},{6,2},{3,7},{7,3},{8,12},{12,8},{9,1... | collective-permute-start | bytes 786440 | tf_op jit(solution)/shard_map/grad_in/ppermute | solution.py:43
  613.6 20.9 %collective-permute-start.77 = (bf16[64,2048]{1,0:T(8,128)(2,1)}, bf16[64,2048]{1,0:T(8,128)(2,1)S(1)}, u32[]{:S(2)}, u32[]{:S(2)}) collective-permute-start(bf16[64,2048]{1,0:T(8,128)(2,1)} %get-tuple-element.339), channel_id=1, source_target_pairs={{0,2},{2,0},{1,3},{3,1},{4,6},{6,4},{5,7},{7,5},{8,10},{10,8},{9,1... | collective-permute-start | bytes 786440 | tf_op jit(solution)/shard_map/grad_in/ppermute | solution.py:43
  615.2 19.8 %collective-permute-start.72 = (bf16[64,2048]{1,0:T(8,128)(2,1)}, bf16[64,2048]{1,0:T(8,128)(2,1)}, u32[]{:S(2)}, u32[]{:S(2)}) collective-permute-start(bf16[64,2048]{1,0:T(8,128)(2,1)} %get-tuple-element.338), channel_id=1, source_target_pairs={{0,4},{4,0},{1,5},{5,1},{2,6},{6,2},{3,7},{7,3},{8,12},{12,8},{9,1... | collective-permute-start | bytes 786440 | tf_op jit(solution)/shard_map/grad_in/ppermute | solution.py:43
  617.5 19.1 %collective-permute-start.76 = (bf16[64,2048]{1,0:T(8,128)(2,1)}, bf16[64,2048]{1,0:T(8,128)(2,1)}, u32[]{:S(2)}, u32[]{:S(2)}) collective-permute-start(bf16[64,2048]{1,0:T(8,128)(2,1)} %get-tuple-element.343), channel_id=1, source_target_pairs={{0,2},{2,0},{1,3},{3,1},{4,6},{6,4},{5,7},{7,5},{8,10},{10,8},{9,1... | collective-permute-start | bytes 786440 | tf_op jit(solution)/shard_map/grad_in/ppermute | solution.py:43
  618.0 18.6 %collective-permute-start.74 = (bf16[64,2048]{1,0:T(8,128)(2,1)}, bf16[64,2048]{1,0:T(8,128)(2,1)}, u32[]{:S(2)}, u32[]{:S(2)}) collective-permute-start(bf16[64,2048]{1,0:T(8,128)(2,1)} %get-tuple-element.342), channel_id=1, source_target_pairs={{0,4},{4,0},{1,5},{5,1},{2,6},{6,2},{3,7},{7,3},{8,12},{12,8},{9,1... | collective-permute-start | bytes 786440 | tf_op jit(solution)/shard_map/grad_in/ppermute | solution.py:43
  632.8 16.1 %collective-permute-start.81 = (bf16[256,512]{1,0:T(8,128)(2,1)S(1)}, bf16[256,512]{1,0:T(8,128)(2,1)S(1)}, u32[]{:S(2)}, u32[]{:S(2)}) collective-permute-start(bf16[256,512]{1,0:T(8,128)(2,1)S(1)} %get-tuple-element.394), channel_id=1, source_target_pairs={{0,4},{4,0},{1,5},{5,1},{2,6},{6,2},{3,7},{7,3},{8,12},{12,8},{9,1... | collective-permute-start | bytes 786440 | tf_op jit(solution)/shard_map/qz/ppermute | solution.py:43
  635.0 25.2 %collective-permute-start.88 = (bf16[256,1024]{1,0:T(8,128)(2,1)}, bf16[256,1024]{1,0:T(8,128)(2,1)S(1)}, u32[]{:S(2)}, u32[]{:S(2)}) collective-permute-start(bf16[256,1024]{1,0:T(8,128)(2,1)} %get-tuple-element.372), channel_id=1, source_target_pairs={{0,4},{4,0},{1,5},{5,1},{2,6},{6,2},{3,7},{7,3},{8,12},{12,8},{9,1... | collective-permute-start | bytes 1572872 | tf_op jit(solution)/shard_map/gu/ppermute | solution.py:43
  (136 other events, 1167.8 us)
Sparse Core Ops, SparseCore 0:
  38.7 44.7 all-gather.3
  88.1 78.2 all-gather.5
  188.6 117.9 all-gather.7
  330.8 42.1 reduce-scatter.6
  375.3 84.1 reduce-scatter.8
  474.1 50.3 reduce-scatter.10
  526.9 44.7 reduce-scatter.12
  576.7 33.4 reduce-scatter.16
  621.2 20.2 reduce-scatter.14
